TPU v7x, 32 devices: a whole 2x2x4 slice. The times are simulated.
32 devices in a mesh: tm: 4 (over z), height: 8 (over y, x, core).
Axes of the slice: x: 2, y: 2, z: 4, core: 2. Of those that a mesh axis runs over, the one named last changes fastest.
Arguments:
- tokens: bfloat16 [8, 16, 64, 1536], P('tm', 'height'), may hold values from -6 to 6
- norm_gain: float32 [1536], replicated, may hold values from 0.5 to 1.5
- in_weight: bfloat16 [1536, 3072], replicated, may hold values from -0.15625 to 0.15625
- bc_weight: bfloat16 [1536, 512], replicated, may hold values from -0.15625 to 0.15625
- dt_weight: bfloat16 [1536, 48], replicated, may hold values from -0.15625 to 0.15625
- dt_bias: float32 [48], replicated, may hold values from -1 to 1
- decay_rate: float32 [2, 24], replicated, may hold values from 0.0006510417 to 0.05
- out_gain: float32 [1536], replicated, may hold values from 0.5 to 1.5
- out_weight: bfloat16 [1536, 1536], replicated, may hold values from -0.15625 to 0.15625
Outputs:
- mixed: bfloat16 [8, 16, 64, 1536], P('tm', 'height')
All inputs are finite; a program needn't handle non-finite values.
Results may differ from a plain program's by a relative error of at most 0.02.
Values may be sent and summed in bfloat16 or wider, within the bound.
No kernel may reach another device: no remote copies, remote signals or barrier semaphores. Data moves between devices by JAX's collectives and lax.ppermute only.
A program may use at most 192 MiB of HBM per device.

v0:
```python
import math

import jax
import jax.numpy as jnp
from jax import lax
from jax.sharding import PartitionSpec as P

PRECISE = lax.Precision.HIGH
EPSILON = 1e-05


def passed_along(value, axis, steps):
    count = lax.axis_size(axis)
    initial, last = (max(0, -steps), min(count, count - steps))
    return lax.ppermute(value, axis, [(source, source + steps) for source in range(initial, last)])


def carried_in(value, axis, combine, identity):
    count, here = (lax.axis_size(axis), lax.axis_index(axis))
    everything = jax.tree.map(
        lambda part, kind: lax.all_gather(part.astype(kind), axis),
        value,
        (jnp.bfloat16, jnp.bfloat16),
    )
    start = jax.tree.map(
        lambda part, zero: jnp.broadcast_to(jnp.asarray(zero, part.dtype), part.shape),
        value,
        identity,
    )

    def step(k, before):
        reached = k < here
        new = combine(
            before, jax.tree.map(lambda part, own: part[k].astype(own.dtype), everything, value)
        )
        return jax.tree.map(lambda a, b: jnp.where(reached, a, b), new, before)

    return lax.fori_loop(0, count, step, start)


def stored(values):
    return lax.optimization_barrier(values.astype(jnp.bfloat16))


def rms_scale(values, scaling):
    mean_square = jnp.mean(values * values, axis=-1, keepdims=True)
    return values * lax.rsqrt(mean_square + EPSILON) * scaling


def project(left, right):
    return jnp.dot(left, right, preferred_element_type=jnp.float32)


def block_step(carried, pieces):
    inputs, b_proj, c_proj, dt_values, log_decay = pieces
    running = jnp.cumsum(log_decay, axis=0)
    length = inputs.shape[0]
    causal = jnp.arange(length)[:, None] >= jnp.arange(length)[None, :]
    spread = running[:, None, :] - running[None, :, :]
    decays = jnp.exp(jnp.where(causal[:, :, None], spread, -jnp.inf))
    scores = jnp.dot(
        c_proj.astype(jnp.bfloat16),
        b_proj.astype(jnp.bfloat16).T,
        preferred_element_type=jnp.float32,
    )
    weights = scores[:, :, None] * decays * dt_values[None, :, :]
    within = jnp.einsum("ijh,jhp->ihp", weights, inputs, precision=PRECISE)
    earlier = jnp.einsum("in,hpn->ihp", c_proj, carried, precision=PRECISE)
    outputs = within + jnp.exp(running)[:, :, None] * earlier
    to_end = jnp.exp(running[-1][None, :] - running) * dt_values
    fresh_state = jnp.einsum("jh,jhp,jn->hpn", to_end, inputs, b_proj, precision=PRECISE)
    carried = jnp.exp(running[-1])[:, None, None] * carried + fresh_state
    return (carried, outputs)


def run_blocks(inputs, b_proj, c_proj, dt_values, log_decay, initial, block_len):
    blocks = inputs.shape[0] // block_len

    def split_blocks(operand):
        return operand.reshape((blocks, block_len) + operand.shape[1:])

    final_state, outputs = lax.scan(
        block_step,
        initial,
        (
            split_blocks(inputs),
            split_blocks(b_proj),
            split_blocks(c_proj),
            split_blocks(dt_values),
            split_blocks(log_decay),
        ),
    )
    return (outputs.reshape(inputs.shape), final_state)


def local_scan(inputs, b_proj, c_proj, dt_values, log_decay):
    length = inputs.shape[1]
    block_len = math.gcd(256, length)
    initial = jnp.zeros((inputs.shape[2], inputs.shape[3], b_proj.shape[2]), jnp.float32)

    def single(inputs_one, b_one, c_one, dt_one, decay_one):
        return run_blocks(inputs_one, b_one, c_one, dt_one, decay_one, initial, block_len)

    outputs, local_state = jax.vmap(single)(inputs, b_proj, c_proj, dt_values, log_decay)
    running = jnp.cumsum(log_decay, axis=1)
    return (outputs, local_state, running)


def add_incoming(outputs, c_proj, running, incoming):
    earlier = jnp.einsum("bln,bhpn->blhp", c_proj, incoming, precision=PRECISE)
    return outputs + jnp.exp(running)[..., None] * earlier


def link(earlier, later):
    return (earlier[0] * later[0], later[0][..., None, None] * earlier[1] + later[1])


def per_device(
    tokens, norm_gain, in_weight, bc_weight, dt_weight, dt_bias, decay_rate, out_gain, out_weight
):
    frames_dev, rows_dev, columns, model_width = tokens.shape
    heads = decay_rate.shape[1]
    inner = out_weight.shape[0]
    head_dim = inner // heads
    state_dim = bc_weight.shape[1] // 4
    tm_count = lax.axis_size("tm")
    col_block = columns // tm_count
    all_frames = frames_dev * tm_count
    grid_dev = (frames_dev, rows_dev, columns)
    normed = stored(rms_scale(tokens.reshape(-1, model_width).astype(jnp.float32), norm_gain))
    projected = stored(project(normed, in_weight))
    bc_values = stored(project(normed, bc_weight))
    dt_logits = stored(project(normed, dt_weight))
    tm_inputs, tm_bc, tm_logits = (
        lax.all_to_all(
            projected[:, :inner].reshape(grid_dev + (inner,)),
            "tm",
            split_axis=2,
            concat_axis=0,
            tiled=True,
        ),
        lax.all_to_all(
            bc_values[:, 2 * state_dim :].reshape(grid_dev + (2 * state_dim,)),
            "tm",
            split_axis=2,
            concat_axis=0,
            tiled=True,
        ),
        lax.all_to_all(
            dt_logits[:, heads:].reshape(grid_dev + (heads,)),
            "tm",
            split_axis=2,
            concat_axis=0,
            tiled=True,
        ),
    )
    spatial_len = rows_dev * columns
    sp_inputs = (
        projected[:, :inner].astype(jnp.float32).reshape(frames_dev, spatial_len, heads, head_dim)
    )
    sp_bc = (
        bc_values[:, : 2 * state_dim]
        .astype(jnp.float32)
        .reshape(frames_dev, spatial_len, 2 * state_dim)
    )
    sp_dt = jax.nn.softplus(dt_logits[:, :heads].astype(jnp.float32) + dt_bias[:heads]).reshape(
        frames_dev, spatial_len, heads
    )
    sp_decay = -sp_dt * decay_rate[0]
    sp_out, sp_local, sp_running = local_scan(
        sp_inputs, sp_bc[..., :state_dim], sp_bc[..., state_dim:], sp_dt, sp_decay
    )
    sp_total = jnp.exp(sp_running[:, -1])

    def relay(position, incoming):
        return passed_along(
            (sp_total[..., None, None] * incoming + sp_local).astype(jnp.bfloat16), "height", 1
        ).astype(jnp.float32)

    sp_incoming = lax.fori_loop(0, lax.axis_size("height") - 1, relay, jnp.zeros_like(sp_local))
    sp_out = add_incoming(sp_out, sp_bc[..., state_dim:], sp_running, sp_incoming)
    tm_len = col_block * all_frames

    def row_order(operand):
        moved = jnp.transpose(operand, (1, 2, 0, 3))
        return moved.reshape(rows_dev, tm_len, operand.shape[3])

    tm_values = row_order(tm_inputs).astype(jnp.float32).reshape(rows_dev, tm_len, heads, head_dim)
    tm_bcf = row_order(tm_bc).astype(jnp.float32)
    tm_dt = jax.nn.softplus(row_order(tm_logits).astype(jnp.float32) + dt_bias[heads:])
    tm_decay = -tm_dt * decay_rate[1]
    tm_out, tm_local, tm_running = local_scan(
        tm_values, tm_bcf[..., :state_dim], tm_bcf[..., state_dim:], tm_dt, tm_decay
    )
    tm_total = jnp.exp(tm_running[:, -1])
    _, tm_incoming = carried_in(
        (tm_total, tm_local), "tm", link, (jnp.ones_like(tm_total), jnp.zeros_like(tm_local))
    )
    tm_out = add_incoming(tm_out, tm_bcf[..., state_dim:], tm_running, tm_incoming)
    tm_out = stored(
        jnp.transpose(tm_out.reshape(rows_dev, col_block, all_frames, inner), (2, 0, 1, 3))
    )
    returned = lax.all_to_all(tm_out, "tm", split_axis=0, concat_axis=2, tiled=True)
    gate_values = projected[:, inner:].astype(jnp.float32)
    combined = sp_out.reshape(-1, inner) + returned.reshape(-1, inner).astype(jnp.float32)
    gated = combined * jax.nn.silu(gate_values)
    normed_out = stored(rms_scale(gated, out_gain))
    mixed = project(normed_out, out_weight)
    return mixed.astype(jnp.bfloat16).reshape(frames_dev, rows_dev, columns, model_width)


def solution(mesh):
    in_specs = (P("tm", "height", None, None), P(), P(), P(), P(), P(), P(), P(), P())
    out_specs = P("tm", "height", None, None)
    return jax.shard_map(
        per_device, mesh=mesh, in_specs=in_specs, out_specs=out_specs, check_vma=False
    )
```

profile of v0, /device:TPU:12, one launch (start us, length us, event | category | flops | bytes accessed | tf_op | source)
XLA Modules:
  0.0 299.8 jit_solution(438397001234543736)
XLA Ops:
  10.8 5.3 %all-to-all-start.2 = ((bf16[4,2,768]{2,1,0:T(2,128)(2,1)}), bf16[4,2,768]{2,1,0:T(2,128)(2,1)S(1)}, u32[]{:S(2)}, u32[]{:S(2)}) async-start(bf16[4,2,768]{2,1,0:T(2,128)(2,1)} %reshape.201), calls=%async_computation.2 | async-start | bytes 24576 | tf_op jit(solution)/shard_map/all_to_all | solution.py:149
  16.1 6.3 %convolution_convert_fusion = bf16[256,3072]{1,0:T(8,128)(2,1)S(1)} fusion(bf16[256,1536]{1,0:T(8,128)(2,1)S(1)} %fusion.25, bf16[1536,3072]{1,0:T(8,128)(2,1)} %param.15), kind=kOutput, calls=%fused_computation.6 | convolution fusion | flops 2416705536 | bytes 11796480 | tf_op jit(solution)/shard_map/dot_general | solution.py:51
  26.2 5.1 %all-to-all-start.1 = ((bf16[2,2,64,256]{3,1,0,2:T(2,128)(2,1)}), bf16[2,2,64,256]{3,1,0,2:T(2,128)(2,1)S(1)}, u32[]{:S(2)}, u32[]{:S(2)}) async-start(bf16[2,2,64,256]{3,1,0,2:T(2,128)(2,1)} %copy.91), calls=%async_computation.1 | async-start | bytes 262144 | tf_op jit(solution)/shard_map/all_to_all | solution.py:142
  32.0 4.5 %all-to-all-done.1 = bf16[2,2,64,256]{3,1,0,2:T(2,128)(2,1)S(1)} async-done(((bf16[2,2,64,256]{3,1,0,2:T(2,128)(2,1)}), bf16[2,2,64,256]{3,1,0,2:T(2,128)(2,1)S(1)}, u32[]{:S(2)}, u32[]{:S(2)}) %all-to-all-start.1) | async-done | bytes 131104 | tf_op jit(solution)/shard_map/all_to_all | solution.py:142
  36.4 4.2 %all-to-all-start = ((bf16[2,2,64,1536]{3,1,0,2:T(2,128)(2,1)}), bf16[2,2,64,1536]{3,1,0,2:T(2,128)(2,1)S(1)}, u32[]{:S(2)}, u32[]{:S(2)}) async-start(bf16[2,2,64,1536]{3,1,0,2:T(2,128)(2,1)} %copy.87), calls=%async_computation | async-start | bytes 1572864 | tf_op jit(solution)/shard_map/all_to_all | solution.py:135
  43.5 12.3 %all-to-all-done = bf16[2,2,64,1536]{3,1,0,2:T(2,128)(2,1)S(1)} async-done(((bf16[2,2,64,1536]{3,1,0,2:T(2,128)(2,1)}), bf16[2,2,64,1536]{3,1,0,2:T(2,128)(2,1)S(1)}, u32[]{:S(2)}, u32[]{:S(2)}) %all-to-all-start) | async-done | bytes 786464 | tf_op jit(solution)/shard_map/all_to_all | solution.py:135
  68.0 11.0 %all-gather = bf16[8,1,24]{2,1,0:T(2,128)(2,1)S(1)} all-gather(bf16[2,1,24]{2,1,0:T(2,128)(2,1)S(1)} %copy-done.16), channel_id=2, replica_groups=mesh['tm'=4,'height'=8] {'tm'}, dimensions={0}, use_global_device_ids=true | all-gather | bytes 480 | tf_op jit(solution)/shard_map/all_gather | solution.py:21
  80.1 3.4 %fusion.11 = f32[2,24,64,128]{3,2,1,0:T(8,128)} fusion(f32[2,128,24]{1,2,0:T(8,128)S(1)} %bitcast.148, f32[2,128,24]{1,2,0:T(8,128)S(1)} %copy.78, f32[2,128,128]{2,1,0:T(8,128)S(1)} %fusion.61, pred[128,128]{1,0:T(8,128)(4,1)S(1)} %iota_compare_fusion, bf16[2,128,24,64]{1,0,3,2:T(2,128)(2,1)S(1)} %squeeze.45), kind=kOutput, calls=%fused_computation.16 | convolution fusion | flops 305135616 | bytes 2555904 | tf_op jit(solution)/shard_map/vmap()/while/body/eval_jaxpr/ijh,jhp->ihp/dot_general | solution.py:67
  86.1 4.0 %fusion.5 = f32[2,24,64,128]{3,2,1,0:T(8,128)} fusion(bf16[2,128,24,64]{3,2,1,0:T(8,128)(2,1)S(1)} %copy-done.3, f32[2,128,24]{1,2,0:T(8,128)S(1)} %copy.99, f32[2,128,24]{1,2,0:T(8,128)S(1)} %copy-done.14, f32[2,128,128]{2,1,0:T(8,128)S(1)} %fusion.58, pred[128,128]{1,0:T(8,128)(4,1)S(1)} %iota_compare_fusion), kind=kOutput, calls=%fused_computation.10 | convolution fusion | flops 305135616 | bytes 2555904 | tf_op jit(solution)/shard_map/vmap()/while/body/eval_jaxpr/ijh,jhp->ihp/dot_general | solution.py:67
  90.1 36.9 %all-gather.4.cloned.1.call-done = bf16[8,24,64,128]{3,2,1,0:T(8,128)(2,1)} async-done(((bf16[2,24,64,128]{3,2,1,0:T(8,128)(2,1)}), bf16[8,24,64,128]{3,2,1,0:T(8,128)(2,1)}) %all-gather.4.cloned.1.call-update) | async-done | bytes 3145744 | tf_op jit(solution)/shard_map/all_gather | solution.py:21
  126.9 11.9 %while.17 = (s32[]{:T(128)}, f32[2,24,64,128]{3,2,1,0:T(8,128)}, s32[]{:T(128)}, bf16[4,2,24]{2,1,0:T(2,128)(2,1)S(1)}, bf16[4,2,24,64,128]{4,3,2,1,0:T(8,128)(2,1)}, /*index=5*/s32[]{:T(128)}, s32[]{:T(128)}) while((s32[]{:T(128)}, f32[2,24,64,128]{3,2,1,0:T(8,128)}, s32[]{:T(128)}, bf16[4,2,24]{2,1,0:T(2,128)(2,1)S(1)}, ...), condition=%wide.region_6.7_spmd.clone, body=%wide.region_5.6_spmd.clone.sunk | while | flops 1966132 | bytes 3932745 | solution.py:38
  129.5 3.1 %fusion.93 = f32[2,24,64,128]{3,2,1,0:T(8,128)} fusion(f32[2,24,64,128]{3,2,1,0:T(8,128)} %get-tuple-element.325, bf16[4,2,24,64,128]{4,3,2,1,0:T(8,128)(2,1)} %get-tuple-element.335, s32[]{:T(128)} %get-tuple-element.324, f32[2,24]{1,0:T(2,128)S(1)} %bitcast_convert_fusion.2, pred[]{:T(512)S(6)} %compare.7, pred[]{:T(512)S(6)} %lt.29), kind=kLoop, calls=%fused_computation.4.clone.1 | loop fusion | flops 1966080 | bytes 3932358 | tf_op jit(solution)/shard_map/while/body/eval_jaxpr/jit(_where)/select_n | solution.py:36
  138.8 4.0 %fusion.22 = bf16[2,128,24,64]{1,3,2,0:T(8,128)(2,1)} fusion(f32[2,24,64,128]{3,2,1,0:T(8,128)} %fusion.5, f32[2,128,24,64]{1,3,2,0:T(8,128)} %fusion.47, f32[2,24,64,128]{3,2,1,0:T(8,128)} %get-tuple-element.170, f32[2,128,24]{1,2,0:T(8,128)S(1)} %copy.101, bf16[2,128,256]{2,1,0:T(8,128)(2,1)S(1)} %bitcast.135), kind=kOutput, calls=%fused_computation.33 | convolution fusion | flops 303955968 | bytes 5595136 | tf_op jit(solution)/shard_map/bln,bhpn->blhp/dot_general | solution.py:110
  145.5 3.4 %convert_element_type.148 = bf16[2,16,8,1536]{3,2,1,0:T(8,128)(2,1)} reshape(bf16[2,128,24,64]{3,2,1,0:T(8,128)(2,1)} %copy.103) | data formatting | bytes 1572864 | tf_op jit(solution)/shard_map/convert_element_type | solution.py:42
  151.1 6.9 %all-to-all-start.3 = ((bf16[8,2,16,1536]{3,2,1,0:T(8,128)(2,1)}), bf16[8,2,16,1536]{3,2,1,0:T(8,128)(2,1)}, u32[]{:S(2)}, u32[]{:S(2)}) async-start(bf16[8,2,16,1536]{3,2,1,0:T(8,128)(2,1)} %copy.104), calls=%async_computation.3 | async-start | bytes 1572864 | tf_op jit(solution)/shard_map/all_to_all | solution.py:203
  158.1 118.8 %while.16 = (s32[]{:T(128)}, f32[2,24,64,128]{3,2,1,0:T(8,128)S(1)}, f32[2,24]{1,0:T(2,128)S(1)}, f32[2,24,64,128]{3,2,1,0:T(8,128)S(1)}, s32[]{:T(128)}, /*index=5*/s32[]{:T(128)}) while((s32[]{:T(128)}, f32[2,24,64,128]{3,2,1,0:T(8,128)S(1)}, f32[2,24]{1,0:T(2,128)S(1)}, f32[2,24,64,128]{3,2,1,0:T(8,128)S(1)}, s32[]{:T(128)}, ...), condition=%wide.region_3.4_spmd.clone, body=%wide.region_2.3_spmd.clone.sunk | while | flops 1966083 | bytes 9437495 | solution.py:180
  161.1 12.6 %collective-permute-done = bf16[2,24,64,128]{3,2,1,0:T(8,128)(2,1)} collective-permute-done((bf16[2,24,64,128]{3,2,1,0:T(8,128)(2,1)}, bf16[2,24,64,128]{3,2,1,0:T(8,128)(2,1)}, u32[]{:S(2)}, u32[]{:S(2)}) %collective-permute-start) | collective-permute-done | bytes 786464 | tf_op jit(solution)/shard_map/while/body/eval_jaxpr/ppermute | solution.py:15
  178.1 12.6 %collective-permute-done = bf16[2,24,64,128]{3,2,1,0:T(8,128)(2,1)} collective-permute-done((bf16[2,24,64,128]{3,2,1,0:T(8,128)(2,1)}, bf16[2,24,64,128]{3,2,1,0:T(8,128)(2,1)}, u32[]{:S(2)}, u32[]{:S(2)}) %collective-permute-start) | collective-permute-done | bytes 786464 | tf_op jit(solution)/shard_map/while/body/eval_jaxpr/ppermute | solution.py:15
  195.1 12.6 %collective-permute-done = bf16[2,24,64,128]{3,2,1,0:T(8,128)(2,1)} collective-permute-done((bf16[2,24,64,128]{3,2,1,0:T(8,128)(2,1)}, bf16[2,24,64,128]{3,2,1,0:T(8,128)(2,1)}, u32[]{:S(2)}, u32[]{:S(2)}) %collective-permute-start) | collective-permute-done | bytes 786464 | tf_op jit(solution)/shard_map/while/body/eval_jaxpr/ppermute | solution.py:15
  212.1 12.6 %collective-permute-done = bf16[2,24,64,128]{3,2,1,0:T(8,128)(2,1)} collective-permute-done((bf16[2,24,64,128]{3,2,1,0:T(8,128)(2,1)}, bf16[2,24,64,128]{3,2,1,0:T(8,128)(2,1)}, u32[]{:S(2)}, u32[]{:S(2)}) %collective-permute-start) | collective-permute-done | bytes 786464 | tf_op jit(solution)/shard_map/while/body/eval_jaxpr/ppermute | solution.py:15
  229.0 12.6 %collective-permute-done = bf16[2,24,64,128]{3,2,1,0:T(8,128)(2,1)} collective-permute-done((bf16[2,24,64,128]{3,2,1,0:T(8,128)(2,1)}, bf16[2,24,64,128]{3,2,1,0:T(8,128)(2,1)}, u32[]{:S(2)}, u32[]{:S(2)}) %collective-permute-start) | collective-permute-done | bytes 786464 | tf_op jit(solution)/shard_map/while/body/eval_jaxpr/ppermute | solution.py:15
  246.0 12.6 %collective-permute-done = bf16[2,24,64,128]{3,2,1,0:T(8,128)(2,1)} collective-permute-done((bf16[2,24,64,128]{3,2,1,0:T(8,128)(2,1)}, bf16[2,24,64,128]{3,2,1,0:T(8,128)(2,1)}, u32[]{:S(2)}, u32[]{:S(2)}) %collective-permute-start) | collective-permute-done | bytes 786464 | tf_op jit(solution)/shard_map/while/body/eval_jaxpr/ppermute | solution.py:15
  263.0 12.6 %collective-permute-done = bf16[2,24,64,128]{3,2,1,0:T(8,128)(2,1)} collective-permute-done((bf16[2,24,64,128]{3,2,1,0:T(8,128)(2,1)}, bf16[2,24,64,128]{3,2,1,0:T(8,128)(2,1)}, u32[]{:S(2)}, u32[]{:S(2)}) %collective-permute-start) | collective-permute-done | bytes 786464 | tf_op jit(solution)/shard_map/while/body/eval_jaxpr/ppermute | solution.py:15
  288.3 4.7 %convolution_convert_fusion.1 = bf16[256,1536]{1,0:T(8,128)(2,1)} fusion(bf16[256,1536]{1,0:T(8,128)(2,1)S(1)} %multiply_convert_fusion, bf16[1536,1536]{1,0:T(8,128)(2,1)} %param.21), kind=kOutput, calls=%fused_computation.22 | convolution fusion | flops 1208352768 | bytes 6291456 | tf_op jit(solution)/shard_map/dot_general | solution.py:51
  (138 shorter events, 82.5 us)
Async XLA Ops:
  6.5 15.9 %copy-start = (bf16[1536,512]{1,0:T(8,128)(2,1)S(1)}, bf16[1536,512]{1,0:T(8,128)(2,1)}, u32[]{:S(2)}) copy-start(bf16[1536,512]{1,0:T(8,128)(2,1)} %param.16) | copy-start | bytes 4718596
  6.5 3.0 %copy-start.13 = (bf16[1536,48]{0,1:T(8,128)(2,1)S(1)}, bf16[1536,48]{0,1:T(8,128)(2,1)}, u32[]{:S(2)}) copy-start(bf16[1536,48]{0,1:T(8,128)(2,1)} %param.17) | copy-start | bytes 442372
  10.8 15.3 %all-to-all-start.2 = ((bf16[4,2,768]{2,1,0:T(2,128)(2,1)}), bf16[4,2,768]{2,1,0:T(2,128)(2,1)S(1)}, u32[]{:S(2)}, u32[]{:S(2)}) async-start(bf16[4,2,768]{2,1,0:T(2,128)(2,1)} %reshape.201), calls=%async_computation.2 | async-start | bytes 24576 | tf_op jit(solution)/shard_map/all_to_all | solution.py:149
  23.7 17.0 %copy-start.18 = (f32[2,24]{1,0:T(2,128)S(1)}, f32[2,24]{1,0:T(2,128)}, u32[]{:S(2)}) copy-start(f32[2,24]{1,0:T(2,128)} %param.19) | copy-start | bytes 580
  26.2 10.3 %all-to-all-start.1 = ((bf16[2,2,64,256]{3,1,0,2:T(2,128)(2,1)}), bf16[2,2,64,256]{3,1,0,2:T(2,128)(2,1)S(1)}, u32[]{:S(2)}, u32[]{:S(2)}) async-start(bf16[2,2,64,256]{3,1,0,2:T(2,128)(2,1)} %copy.91), calls=%async_computation.1 | async-start | bytes 262144 | tf_op jit(solution)/shard_map/all_to_all | solution.py:142
  36.4 19.4 %all-to-all-start = ((bf16[2,2,64,1536]{3,1,0,2:T(2,128)(2,1)}), bf16[2,2,64,1536]{3,1,0,2:T(2,128)(2,1)S(1)}, u32[]{:S(2)}, u32[]{:S(2)}) async-start(bf16[2,2,64,1536]{3,1,0,2:T(2,128)(2,1)} %copy.87), calls=%async_computation | async-start | bytes 1572864 | tf_op jit(solution)/shard_map/all_to_all | solution.py:135
  40.7 86.3 %all-gather.4.cloned.1.call-start = ((), (), s32[]{:S(2)}) async-start(), calls=%async_computation.4 | async-start | bytes 3932160 | tf_op jit(solution)/shard_map/all_gather | solution.py:21
  40.8 15.2 %copy-start.6 = (f32[256,24]{1,0:T(8,128)}, f32[256,24]{1,0:T(8,128)S(1)}, u32[]{:S(2)}) copy-start(f32[256,24]{1,0:T(8,128)S(1)} %copy.131) | copy-start | bytes 73732
  41.7 14.3 %copy-start.8 = (f32[2,128,24]{2,1,0:T(8,128)}, f32[2,128,24]{2,1,0:T(8,128)S(1)}, u32[]{:S(2)}) copy-start(f32[2,128,24]{2,1,0:T(8,128)S(1)} %get-tuple-element.225) | copy-start | bytes 73732
  57.3 2.4 copy-start.10
  64.1 3.5 %copy-start.9 = (f32[2,128,24]{2,1,0:T(8,128)S(1)}, f32[2,128,24]{2,1,0:T(8,128)}, u32[]{:S(2)}) copy-start(f32[2,128,24]{2,1,0:T(8,128)} %copy-done.8) | copy-start | bytes 73732
  64.2 3.6 %copy-start.11 = (f32[2,128,24]{2,1,0:T(8,128)S(1)}, f32[2,128,24]{2,1,0:T(8,128)}, u32[]{:S(2)}) copy-start(f32[2,128,24]{2,1,0:T(8,128)} %get-tuple-element.242) | copy-start | bytes 73732
  64.2 3.8 %copy-start.16 = (bf16[2,1,24]{2,1,0:T(2,128)(2,1)S(1)}, bf16[2,1,24]{2,1,0:T(2,128)(2,1)}, u32[]{:S(2)}) copy-start(bf16[2,1,24]{2,1,0:T(2,128)(2,1)} %get-tuple-element.231) | copy-start | bytes 292
  64.2 14.9 %copy-start.12 = (f32[2,128,24]{2,1,0:T(8,128)S(1)}, f32[2,128,24]{2,1,0:T(8,128)}, u32[]{:S(2)}) copy-start(f32[2,128,24]{2,1,0:T(8,128)} %get-tuple-element.228) | copy-start | bytes 73732
  64.2 14.9 %copy-start.7 = (f32[256,24]{1,0:T(8,128)S(1)}, f32[256,24]{1,0:T(8,128)}, u32[]{:S(2)}) copy-start(f32[256,24]{1,0:T(8,128)} %copy-done.6) | copy-start | bytes 73732
  151.1 133.5 %all-to-all-start.3 = ((bf16[8,2,16,1536]{3,2,1,0:T(8,128)(2,1)}), bf16[8,2,16,1536]{3,2,1,0:T(8,128)(2,1)}, u32[]{:S(2)}, u32[]{:S(2)}) async-start(bf16[8,2,16,1536]{3,2,1,0:T(8,128)(2,1)} %copy.104), calls=%async_computation.3 | async-start | bytes 1572864 | tf_op jit(solution)/shard_map/all_to_all | solution.py:203
  159.2 14.5 %collective-permute-start = (bf16[2,24,64,128]{3,2,1,0:T(8,128)(2,1)}, bf16[2,24,64,128]{3,2,1,0:T(8,128)(2,1)}, u32[]{:S(2)}, u32[]{:S(2)}) collective-permute-start(bf16[2,24,64,128]{3,2,1,0:T(8,128)(2,1)} %fusion.92), channel_id=1, source_target_pairs={{0,1},{1,2},{2,3},{3,4},{4,5},{5,6},{6,7},{8,9},{9,10},{10,11},{11... | collective-permute-start | bytes 2359304 | tf_op jit(solution)/shard_map/while/body/eval_jaxpr/ppermute | solution.py:15
  176.2 14.5 %collective-permute-start = (bf16[2,24,64,128]{3,2,1,0:T(8,128)(2,1)}, bf16[2,24,64,128]{3,2,1,0:T(8,128)(2,1)}, u32[]{:S(2)}, u32[]{:S(2)}) collective-permute-start(bf16[2,24,64,128]{3,2,1,0:T(8,128)(2,1)} %fusion.92), channel_id=1, source_target_pairs={{0,1},{1,2},{2,3},{3,4},{4,5},{5,6},{6,7},{8,9},{9,10},{10,11},{11... | collective-permute-start | bytes 2359304 | tf_op jit(solution)/shard_map/while/body/eval_jaxpr/ppermute | solution.py:15
  193.2 14.5 %collective-permute-start = (bf16[2,24,64,128]{3,2,1,0:T(8,128)(2,1)}, bf16[2,24,64,128]{3,2,1,0:T(8,128)(2,1)}, u32[]{:S(2)}, u32[]{:S(2)}) collective-permute-start(bf16[2,24,64,128]{3,2,1,0:T(8,128)(2,1)} %fusion.92), channel_id=1, source_target_pairs={{0,1},{1,2},{2,3},{3,4},{4,5},{5,6},{6,7},{8,9},{9,10},{10,11},{11... | collective-permute-start | bytes 2359304 | tf_op jit(solution)/shard_map/while/body/eval_jaxpr/ppermute | solution.py:15
  210.1 14.5 %collective-permute-start = (bf16[2,24,64,128]{3,2,1,0:T(8,128)(2,1)}, bf16[2,24,64,128]{3,2,1,0:T(8,128)(2,1)}, u32[]{:S(2)}, u32[]{:S(2)}) collective-permute-start(bf16[2,24,64,128]{3,2,1,0:T(8,128)(2,1)} %fusion.92), channel_id=1, source_target_pairs={{0,1},{1,2},{2,3},{3,4},{4,5},{5,6},{6,7},{8,9},{9,10},{10,11},{11... | collective-permute-start | bytes 2359304 | tf_op jit(solution)/shard_map/while/body/eval_jaxpr/ppermute | solution.py:15
  227.1 14.5 %collective-permute-start = (bf16[2,24,64,128]{3,2,1,0:T(8,128)(2,1)}, bf16[2,24,64,128]{3,2,1,0:T(8,128)(2,1)}, u32[]{:S(2)}, u32[]{:S(2)}) collective-permute-start(bf16[2,24,64,128]{3,2,1,0:T(8,128)(2,1)} %fusion.92), channel_id=1, source_target_pairs={{0,1},{1,2},{2,3},{3,4},{4,5},{5,6},{6,7},{8,9},{9,10},{10,11},{11... | collective-permute-start | bytes 2359304 | tf_op jit(solution)/shard_map/while/body/eval_jaxpr/ppermute | solution.py:15
  244.1 14.5 %collective-permute-start = (bf16[2,24,64,128]{3,2,1,0:T(8,128)(2,1)}, bf16[2,24,64,128]{3,2,1,0:T(8,128)(2,1)}, u32[]{:S(2)}, u32[]{:S(2)}) collective-permute-start(bf16[2,24,64,128]{3,2,1,0:T(8,128)(2,1)} %fusion.92), channel_id=1, source_target_pairs={{0,1},{1,2},{2,3},{3,4},{4,5},{5,6},{6,7},{8,9},{9,10},{10,11},{11... | collective-permute-start | bytes 2359304 | tf_op jit(solution)/shard_map/while/body/eval_jaxpr/ppermute | solution.py:15
  261.1 14.5 %collective-permute-start = (bf16[2,24,64,128]{3,2,1,0:T(8,128)(2,1)}, bf16[2,24,64,128]{3,2,1,0:T(8,128)(2,1)}, u32[]{:S(2)}, u32[]{:S(2)}) collective-permute-start(bf16[2,24,64,128]{3,2,1,0:T(8,128)(2,1)} %fusion.92), channel_id=1, source_target_pairs={{0,1},{1,2},{2,3},{3,4},{4,5},{5,6},{6,7},{8,9},{9,10},{10,11},{11... | collective-permute-start | bytes 2359304 | tf_op jit(solution)/shard_map/while/body/eval_jaxpr/ppermute | solution.py:15
  288.2 4.7 %copy-start.1 = (bf16[1536,512]{1,0:T(8,128)(2,1)S(1)}, bf16[1536,512]{1,0:T(8,128)(2,1)}, u32[]{:S(2)}) copy-start(bf16[1536,512]{1,0:T(8,128)(2,1)} %param.16) | copy-start | bytes 4718596
  (7 other events, 9.1 us)
Sparse Core Ops, SparseCore 0:
  63.8 63.0 all-gather.3
where the time goes:
time: 301 us; the launch traced here: 300 us
  waiting for transfers between devices  142 us (47%)
  other arithmetic  39 us (13%)
  starting transfers between devices  34.9 us (12%)
  matrix products  33.2 us (11%)
  local copies, waits for them, and re-layouts  25.8 us (9%)
  between operations  13.8 us (5%)
  blocking collectives  11 us (4%)
    ppermute x7, waiting for transfers between devices, passed_along(): lax.ppermute(value, axis, [(source, source + steps) for source in range(i...  88.2 us
    all_gather x1, waiting for transfers between devices, carried_in(): lax.all_gather(part.astype(kind), axis)  36.9 us
    ppermute x7, starting transfers between devices, passed_along(): lax.ppermute(value, axis, [(source, source + steps) for source in range(i...  13.4 us
    all_to_all x1, waiting for transfers between devices, per_device(): lax.all_to_all(projected[:, :inner].reshape(grid_dev + (inner,)), 'tm', s...  12.3 us
    dot_general x4, matrix products, project(): return jnp.dot(left, right, preferred_element_type=jnp.float32)  11.9 us
    select_n x4, other arithmetic, step(): return jax.tree.map(lambda a, b: jnp.where(reached, a, b), new, before)  11.9 us
    all_gather x1, blocking collectives, carried_in(): lax.all_gather(part.astype(kind), axis)  11 us
    convert_element_type x7, other arithmetic, relay(): return passed_along((sp_total[..., None, None] * incoming + sp_local).ast...  9.07 us
  transfers between devices with their start and end apart: 12, of which 10 were waited for; matrix products, arithmetic and copies ran while one was open for 18% of the time, Pallas kernels for 0%

commit v1 on v0

v1 whole, which is shorter than its diff:
```python
import functools
import math

import jax
import jax.numpy as jnp
from jax import lax
from jax.experimental import pallas as pl
from jax.experimental.pallas import tpu as pltpu
from jax.sharding import PartitionSpec as P

EPSILON = 1e-05
LANES = 128
TAIL = 16
F32 = jnp.float32
BF16 = jnp.bfloat16
EXACT = lax.Precision.HIGHEST
LARGE = 56 * 1024 * 1024
SMALL = 24 * 1024 * 1024

ANY = pl.BlockSpec(memory_space=pl.ANY)
HBM = pl.BlockSpec(memory_space=pltpu.HBM)
SCALAR = pl.BlockSpec(memory_space=pltpu.SMEM)
WHOLE = pl.BlockSpec(memory_space=pltpu.VMEM)


def call(kernel, name, out_shape, in_specs, limit=SMALL, outs=None, **options):
    return pl.pallas_call(
        kernel,
        out_shape=out_shape,
        in_specs=in_specs,
        out_specs=jax.tree.map(lambda _: WHOLE, out_shape) if outs is None else outs,
        compiler_params=pltpu.CompilerParams(vmem_limit_bytes=limit),
        cost_estimate=pl.CostEstimate(flops=1, bytes_accessed=1, transcendentals=0),
        name=name,
        **options,
    )


def shape_of(shape, dtype):
    return jax.ShapeDtypeStruct(shape, dtype)


def dot(left, right, **options):
    return jnp.dot(left, right, preferred_element_type=F32, **options)


def dot_tn(left, right):
    return lax.dot_general(left, right, (((0,), (0,)), ((), ())), preferred_element_type=F32)


def dot_nt(left, right):
    return lax.dot_general(left, right, (((1,), (1,)), ((), ())), preferred_element_type=F32)


def softplus(values):
    return jnp.maximum(values, 0.0) + jnp.log1p(jnp.exp(-jnp.abs(values)))


def iota(shape, dim):
    return lax.broadcasted_iota(jnp.int32, shape, dim)


def spread_matrix(first_head, width, head_dim):
    return (iota((LANES, width), 0) - first_head == iota((LANES, width), 1) // head_dim).astype(BF16)


def spread(values, matrix):
    high = values.astype(BF16)
    low = (values - high.astype(F32)).astype(BF16)
    return dot(high, matrix) + dot(low, matrix)


def head_mixes(scores, running, running_t, dt_t, x, first_head, heads, head_dim):
    length = scores.shape[0]
    outs = []

    def weights(head):
        spreads = running[:, head : head + 1] - running_t[head : head + 1, :]
        return (scores * jnp.exp(jnp.minimum(spreads, 0.0)) * dt_t[head : head + 1, :]).astype(BF16)

    head = 0
    while head < heads:
        here = first_head + head
        if head + 1 < heads and 2 * head_dim == LANES:
            both = x[:, head * head_dim : (head + 2) * head_dim]
            first = iota((length, LANES), 1) < head_dim
            zero = jnp.zeros_like(both)
            stacked = jnp.concatenate([jnp.where(first, both, zero), jnp.where(first, zero, both)], axis=0)
            pair = jnp.concatenate([weights(here), weights(here + 1)], axis=1)
            outs.append(dot(pair, stacked))
            head += 2
        else:
            outs.append(dot(weights(here), x[:, head * head_dim : (head + 1) * head_dim]))
            head += 1
    return outs[0] if len(outs) == 1 else jnp.concatenate(outs, axis=1)


def column_copies(weight, scratch, sems, first, offset, blocks):
    width = scratch.shape[1] // blocks
    return [
        pltpu.make_async_copy(
            weight.at[:, pl.ds(offset + index * width, width)],
            scratch.at[:, pl.ds(index * width, width)],
            sems.at[first + index],
        )
        for index in range(blocks)
    ]


def packing(length, group):
    columns = group // LANES
    rest = -(-(2 * length + TAIL) // columns)
    return length, -(-rest // TAIL) * TAIL


def pack_rest(ref, length, b_proj, c_proj, dt):
    columns, rest = ref.shape[1] // LANES, ref.shape[0] - length
    blank = jnp.zeros((columns * rest - 2 * length - TAIL, LANES), BF16)
    stacked = jnp.concatenate([b_proj, c_proj, dt, blank], axis=0)
    for column in range(columns):
        ref[length:, column * LANES : (column + 1) * LANES] = stacked[column * rest : (column + 1) * rest]


def unpacked_rest(ref, length):
    columns = ref.shape[1] // LANES
    stacked = jnp.concatenate(
        [ref[length:, column * LANES : (column + 1) * LANES] for column in range(columns)], axis=0
    )
    return stacked[:length], stacked[length : 2 * length], stacked[2 * length : 2 * length + TAIL]


def entry_kernel(shares, heads, state, blocks, *refs):
    here_ref, band, tokens, gain, bias, rates, dt_weight, bc_weight, weight = refs[:9]
    normed_out, payload_out, bc_own, logits, params, own_states, other_states = refs[9:16]
    held, dt_held, bc_held, held_weight, table, normed, payload, sems, out_sems = refs[16:]
    frames, rows, columns, width = tokens.shape
    length = frames * columns
    count = rows * length
    groups = shares // rows
    per_group = heads // groups
    group = held_weight.shape[1] // groups

    token_copies = [
        pltpu.make_async_copy(tokens.at[frame, row], held.at[row, frame], sems.at[row * frames + frame])
        for row in range(rows)
        for frame in range(frames)
    ]
    for copy in token_copies:
        copy.start()
    first = rows * frames
    dt_copy = pltpu.make_async_copy(dt_weight, dt_held, sems.at[first])
    dt_copy.start()
    bc_copy = pltpu.make_async_copy(bc_weight, bc_held, sems.at[first + 1])
    bc_copy.start()
    copies = column_copies(weight, held_weight, sems, first + 2, 0, blocks)
    for copy in copies:
        copy.start()

    table[...] = jnp.zeros_like(table)
    table[0:1, : 2 * heads] = bias[...].reshape(1, 2 * heads)
    table[1:2, :heads] = rates[0:1, :]
    table[1:2, heads : 2 * heads] = rates[1:2, :]
    first_head = heads + here_ref[0] // rows * per_group
    lane_in, lane_out = iota((LANES, LANES), 0), iota((LANES, LANES), 1)
    own = ((lane_in == lane_out + first_head) & (lane_out < per_group)).astype(F32)
    params[0:8, :] = table[...]
    params[8:16, :] = dot(table[...], own, precision=EXACT)
    logits[...] = jnp.zeros_like(logits)

    gains = gain[...].reshape(1, width)
    for index, copy in enumerate(token_copies):
        copy.wait()
        values = held[index // frames, index % frames].astype(F32)
        mean_square = jnp.mean(values * values, axis=-1, keepdims=True)
        normed[index * columns : (index + 1) * columns, :] = (
            values * lax.rsqrt(mean_square + EPSILON) * gains
        ).astype(BF16)
    outgoing = [pltpu.make_async_copy(normed, normed_out, out_sems.at[0])]
    outgoing[0].start()
    dt_copy.wait()
    logits[:, : 2 * heads] = dot_nt(normed[...], dt_held[...]).astype(BF16).astype(F32)
    dt_heads = dot_nt(dt_held[heads:, :], normed[...])
    dt_heads = jnp.concatenate([dt_heads, jnp.zeros((TAIL, count), F32)], axis=0).astype(BF16)
    bc_copy.wait()
    bc = dot(normed[...], bc_held[...]).astype(BF16)
    bc_own[...] = bc[:, : 2 * state]
    scan = [
        end_factors(frame_of(logits, frame, rows, frames, columns), params, rows * columns)
        for frame in range(frames)
    ]

    block = held_weight.shape[1] // blocks
    for index, copy in enumerate(copies):
        copy.wait()
        at = index * block
        values = dot(normed[...], held_weight[:, at : at + block]).astype(BF16)
        for inside in range(0, block, group):
            part = (at + inside) // group
            for row in range(rows):
                piece = part * rows + row
                here = slice(row * length, (row + 1) * length)
                payload[piece, :length, :] = values[here, inside : inside + group]
                pack_rest(
                    payload.at[piece],
                    length,
                    bc[here, 2 * state : 3 * state],
                    bc[here, 3 * state :],
                    dt_heads[part * per_group : part * per_group + TAIL, here],
                )
                outgoing.append(
                    pltpu.make_async_copy(
                        payload.at[piece], payload_out.at[piece], out_sems.at[1 + piece]
                    )
                )
                outgoing[-1].start()
    half = state // 2
    head_dim = groups * group // heads
    mine = band[0] % 2 == 0
    for frame in range(frames):
        b_proj = frame_of(bc_own, frame, rows, frames, columns)[:, :state]
        for part in range(groups):
            at = slice(part * group, (part + 1) * group)
            values = frame_x(payload, part, frame, rows, columns)
            matrix = spread_matrix(part * per_group, group, head_dim)
            scaled = (values.astype(F32) * dot(scan[frame][0], matrix)).astype(BF16)
            fresh = dot_tn(b_proj, scaled).astype(BF16)
            at_rows = slice(frame * half, (frame + 1) * half)
            own_states[at_rows, at] = jnp.where(mine, fresh[:half], fresh[half:])
            other_states[at_rows, at] = jnp.where(mine, fresh[half:], fresh[:half])
    whole = [decay for _, decay in scan] + [jnp.zeros((8 - frames, LANES), F32)]
    decays = spread(jnp.concatenate(whole, axis=0), spread_matrix(0, groups * group, head_dim))
    tail = tail_of(decays)
    own_states[frames * half :, :] = tail
    other_states[frames * half :, :] = tail
    for copy in outgoing:
        copy.wait()


def gate_kernel(blocks, after, normed, weight, out, held_weight, sems):
    inner = held_weight.shape[1]
    copies = column_copies(weight, held_weight, sems, 0, inner, blocks)
    for copy in copies:
        copy.start()
    block = inner // blocks
    for index, copy in enumerate(copies):
        copy.wait()
        at = slice(index * block, (index + 1) * block)
        out[:, at] = dot(normed[...], held_weight[:, at]).astype(BF16)


def frame_of(ref, frame, rows, frames, columns):
    return jnp.concatenate(
        [
            ref[(row * frames + frame) * columns : (row * frames + frame + 1) * columns, :]
            for row in range(rows)
        ],
        axis=0,
    )


def frame_x(payload, part, frame, rows, columns):
    return jnp.concatenate(
        [
            payload[part * rows + row, frame * columns : (frame + 1) * columns, :]
            for row in range(rows)
        ],
        axis=0,
    )


def scan_terms(logits, params, causal):
    dt = softplus(logits + params[0:1, :])
    running = dot(causal.astype(F32), -dt * params[1:2, :], precision=EXACT)
    return dt, running, jnp.min(running, axis=0, keepdims=True)


def end_factors(logits, params, length):
    causal = iota((length, length), 0) >= iota((length, length), 1)
    dt, running, last = scan_terms(logits, params, causal)
    return (jnp.exp(last - running) * dt).astype(BF16), jnp.exp(last)


def local_kernel(frames, rows, columns, head_dim, groups, *refs):
    after, bc, logits, params, x, out, reach = refs
    length = rows * columns
    group = x.shape[2]
    state = bc.shape[1] // 2
    per_group = group // head_dim
    causal = iota((length, length), 0) >= iota((length, length), 1)

    def stored(ref, values, frame, at):
        for row in range(rows):
            to = (row * frames + frame) * columns
            ref[to : to + columns, at] = values[row * columns : (row + 1) * columns]

    for frame in range(frames):
        dt, running, _ = scan_terms(frame_of(logits, frame, rows, frames, columns), params, causal)
        running_t, dt_t = jnp.transpose(running), jnp.transpose(dt)
        bc_rows = frame_of(bc, frame, rows, frames, columns)
        scores = jnp.where(causal, dot_nt(bc_rows[:, state:], bc_rows[:, :state]), 0.0)
        stored(reach, jnp.exp(running), frame, slice(None))
        for piece in range(groups):
            values = frame_x(x, piece, frame, rows, columns)
            mixed = head_mixes(
                scores, running, running_t, dt_t, values, piece * per_group, per_group, head_dim
            )
            stored(out, mixed, frame, slice(piece * group, (piece + 1) * group))


def tail_of(decays):
    high = decays.astype(BF16)
    return jnp.concatenate([high, (decays - high.astype(F32)).astype(BF16)], axis=0)


def pair_kernel(frames, band, own, far, total):
    rows = (own.shape[0] - TAIL) // frames
    own_decay = own[-TAIL:-8, :].astype(F32) + own[-8:, :].astype(F32)
    far_decay = far[-TAIL:-8, :].astype(F32) + far[-8:, :].astype(F32)
    lower = band[0] % 2 == 0
    through = jnp.where(lower, far_decay, own_decay)
    for frame in range(frames):
        at = slice(frame * rows, (frame + 1) * rows)
        first = jnp.where(lower, own[at, :], far[at, :]).astype(F32)
        second = jnp.where(lower, far[at, :], own[at, :]).astype(F32)
        total[at, :] = (through[frame : frame + 1, :] * first + second).astype(BF16)
    total[frames * rows :, :] = tail_of(own_decay * far_decay)


def merge_kernel(frames, distance, finish, *refs):
    _, band, own, far = refs[:4]
    start = distance == 2
    rest = list(refs[4:])
    before_in = None if start else rest.pop(0)
    band_own, band_far = (rest.pop(0), rest.pop(0)) if finish else (None, None)
    rows = (own.shape[0] - TAIL) // frames
    upper, lower_band = (band[0] // distance) % 2 == 1, band[0] % 2 == 0
    own_decay = own[-TAIL:-8, :].astype(F32) + own[-8:, :].astype(F32)
    far_decay = far[-TAIL:-8, :].astype(F32) + far[-8:, :].astype(F32)
    if start:
        before_decay = jnp.ones_like(own_decay)
    else:
        before_decay = before_in[-8:, :]
    if finish:
        first_decay = jnp.where(
            lower_band,
            band_own[-TAIL:-8, :].astype(F32) + band_own[-8:, :].astype(F32),
            band_far[-TAIL:-8, :].astype(F32) + band_far[-8:, :].astype(F32),
        )
    through = jnp.where(upper, own_decay, far_decay)
    for frame in range(frames):
        at = slice(frame * rows, (frame + 1) * rows)
        row = slice(frame, frame + 1)
        far_state = far[at, :].astype(F32)
        came = before_decay[row, :] * far_state
        if not start:
            came = came + before_in[at, :]
        before = jnp.where(upper, came, 0.0 if start else before_in[at, :])
        if finish:
            keep, give = rest
            first = jnp.where(lower_band, band_own[at, :], band_far[at, :]).astype(F32)
            after = first_decay[row, :] * before + first
            keep[at, :] = jnp.where(lower_band, before, after).astype(BF16)
            give[at, :] = jnp.where(lower_band, after, before).astype(BF16)
        else:
            total, before_out = rest
            own_state = own[at, :].astype(F32)
            early = jnp.where(upper, far_state, own_state)
            late = jnp.where(upper, own_state, far_state)
            total[at, :] = (through[row, :] * early + late).astype(BF16)
            before_out[at, :] = before
    if not finish:
        total[frames * rows :, :] = tail_of(own_decay * far_decay)
        before_out[frames * rows :, :] = jnp.where(upper, before_decay * far_decay, before_decay)


def incoming_kernel(frames, rows, columns, head_dim, band, out_local, bc, reach, own, other, out):
    state = bc.shape[1] // 2
    half = state // 2
    inner = out.shape[1]
    mine = band[0] % 2 == 0
    matrix = spread_matrix(0, inner, head_dim)
    for frame in range(frames):
        at = slice(frame * half, (frame + 1) * half)
        low = jnp.where(mine, own[at, :], other[at, :])
        high = jnp.where(mine, other[at, :], own[at, :])
        carried = jnp.concatenate([low, high], axis=0)
        for row in range(rows):
            to = (row * frames + frame) * columns
            here = slice(to, to + columns)
            factor = spread(reach[here, :], matrix)
            out[here, :] = out_local[here, :] + factor * dot(bc[here, state:], carried)


def temporal_kernel(
    part, parts, per_group, head_dim, rows, frames, columns, chunk_cols, shares, state, *refs
):
    here_ref, params, payload = refs[:3]
    rest = list(refs[3:])
    carried_in = rest.pop(0) if part > 0 else None
    outs, rest = rest[:shares], rest[shares:]
    carried_out = rest.pop(0) if part + 1 < parts else None
    b_all, c_all, dt_all, decay_all = rest
    here = here_ref[0]
    length = frames * columns
    part_cols = columns // parts
    group = outs[0].shape[1]
    eye = (iota((TAIL, LANES), 0) == iota((TAIL, LANES), 1)) & (iota((TAIL, LANES), 1) < per_group)
    eye = eye.astype(BF16)

    def came(distance):
        return payload.at[here ^ distance]

    for distance in range(shares):
        b_proj, c_proj, logits = unpacked_rest(came(distance), length)
        logits = dot_tn(logits, eye)
        for frame in range(frames):
            at = slice(frame * columns + part * part_cols, frame * columns + (part + 1) * part_cols)
            to = slice(frame * part_cols, (frame + 1) * part_cols)
            b_all[distance, to] = b_proj[at]
            c_all[distance, to] = c_proj[at]
            dt = softplus(logits[at] + params[8:9, :])
            dt_all[distance, to] = dt
            decay_all[distance, to] = -dt * params[9:10, :]

    all_frames = shares * frames
    size = all_frames * chunk_cols

    def order_key(dim):
        index = iota((size, size), dim)
        source = here ^ (index // (frames * chunk_cols))
        frame = source * frames + (index // chunk_cols) % frames
        return (index % chunk_cols) * all_frames + frame

    causal = order_key(0) >= order_key(1)
    order = causal.astype(F32)
    matrix = spread_matrix(0, group, head_dim)
    carried = jnp.zeros((state, group), F32) if part == 0 else carried_in[...]
    places = [(source, frame) for source in range(shares) for frame in range(frames)]
    for chunk in range(part_cols // chunk_cols):

        def gathered(ref_of, pitch=part_cols, offset=0):
            return jnp.concatenate(
                [
                    ref_of(source)[pl.ds(frame * pitch + offset + chunk * chunk_cols, chunk_cols), :]
                    for source, frame in places
                ],
                axis=0,
            )

        values = gathered(came, columns, part * part_cols)
        b_proj = gathered(lambda source: b_all.at[source])
        c_proj = gathered(lambda source: c_all.at[source])
        dt = gathered(lambda source: dt_all.at[source])
        running = dot(order, gathered(lambda source: decay_all.at[source]), precision=EXACT)
        running_t, dt_t = jnp.transpose(running), jnp.transpose(dt)
        scores = jnp.where(causal, dot_nt(c_proj, b_proj), 0.0)
        last = jnp.min(running, axis=0, keepdims=True)
        mixed = head_mixes(scores, running, running_t, dt_t, values, 0, per_group, head_dim)
        ends = jnp.concatenate([running, jnp.broadcast_to(last, (8, LANES))], axis=0)
        reach = spread(jnp.exp(ends), matrix)
        mixed = mixed + reach[:size] * dot(c_proj, carried.astype(BF16))
        to_end = (jnp.exp(last - running) * dt).astype(BF16)
        scaled = (values.astype(F32) * dot(to_end, matrix)).astype(BF16)
        carried = reach[size : size + 1, :] * carried + dot_tn(b_proj, scaled)
        mixed = mixed.astype(BF16)
        for index, (source, frame) in enumerate(places):
            to = frame * part_cols + chunk * chunk_cols
            outs[source][to : to + chunk_cols, :] = mixed[index * chunk_cols : (index + 1) * chunk_cols]
    if carried_out is not None:
        carried_out[...] = carried


def exit_kernel(part, parts, shares, *refs):
    here, spatial, gate, gain, weight = refs[:5]
    out, temporal, normed, mixed, sems = refs[-5:]
    frames, rows, columns, _ = out.shape
    part_cols = columns // parts
    _, part_len, group = temporal.shape
    groups = shares // rows
    inner = groups * group
    for distance in range(shares):
        temporal[here[0] ^ distance] = refs[5 + distance][...]

    def own(ref, row, at):
        return jnp.concatenate(
            [
                ref[pl.ds((row * frames + frame) * columns + part * part_cols, part_cols), at]
                for frame in range(frames)
            ],
            axis=0,
        )

    gains = gain[...].reshape(1, inner)
    for row in range(rows):
        total = jnp.zeros((part_len, 1), F32)
        kept = []
        for index in range(groups):
            at = slice(index * group, (index + 1) * group)
            gates = own(gate, row, at).astype(F32)
            gated = own(spatial, row, at) + temporal[index * rows + row].astype(F32)
            gated = gated * (gates / (1.0 + jnp.exp(-gates)))
            total = total + jnp.sum(gated * gated, axis=1, keepdims=True)
            kept.append(gated)
        scale = lax.rsqrt(total / inner + EPSILON)
        for index, gated in enumerate(kept):
            at = slice(index * group, (index + 1) * group)
            normed[row * part_len : (row + 1) * part_len, at] = (gated * scale * gains[:, at]).astype(BF16)
    mixed[...] = dot(normed[...], weight[...]).astype(BF16)
    copies = [
        pltpu.make_async_copy(
            mixed.at[pl.ds((row * frames + frame) * part_cols, part_cols), :],
            out.at[frame, row, pl.ds(part * part_cols, part_cols), :],
            sems.at[row * frames + frame],
        )
        for row in range(rows)
        for frame in range(frames)
    ]
    for copy in copies:
        copy.start()
    for copy in copies:
        copy.wait()


def swapped(value, axis, distance):
    count = lax.axis_size(axis)
    return lax.ppermute(value, axis, [(source, source ^ distance) for source in range(count)])


def per_device(
    tokens, norm_gain, in_weight, bc_weight, dt_weight, dt_bias, decay_rate, out_gain, out_weight
):
    frames, rows, columns, width = tokens.shape
    heads = decay_rate.shape[1]
    inner = out_weight.shape[0]
    head_dim = inner // heads
    state = bc_weight.shape[1] // 4
    shares = lax.axis_size("tm")
    bands = lax.axis_size("height")
    groups = shares // rows
    group = inner // groups
    per_group = heads // groups
    length = frames * columns
    count = rows * length
    half = state // 2
    chunk_cols = 16
    blocks = parts = 2
    part_len = length // parts
    here = lax.axis_index("tm").astype(jnp.int32).reshape(1)
    band = lax.axis_index("height").astype(jnp.int32).reshape(1)

    packed = (shares, sum(packing(length, group)), group)
    normed, payload, bc_own, logits, params, own, other = call(
        functools.partial(entry_kernel, shares, heads, state, blocks),
        "entry",
        [
            shape_of((count, width), BF16),
            shape_of(packed, BF16),
            shape_of((count, 2 * state), BF16),
            shape_of((count, LANES), F32),
            shape_of((16, LANES), F32),
        ]
        + [shape_of((frames * half + TAIL, inner), BF16)] * 2,
        [SCALAR, SCALAR, HBM, WHOLE, WHOLE, WHOLE, HBM, HBM, HBM],
        limit=LARGE,
        outs=[HBM, HBM] + [WHOLE] * 5,
        scratch_shapes=[
            pltpu.VMEM((rows, frames, columns, width), BF16),
            pltpu.VMEM((2 * heads, width), BF16),
            pltpu.VMEM((width, 4 * state), BF16),
            pltpu.VMEM((width, inner), BF16),
            pltpu.VMEM((8, LANES), F32),
            pltpu.VMEM((count, width), BF16),
            pltpu.VMEM(packed, BF16),
            pltpu.SemaphoreType.DMA((rows * frames + 2 + blocks,)),
            pltpu.SemaphoreType.DMA((1 + shares,)),
        ],
    )(here, band, tokens, norm_gain, dt_bias, decay_rate, dt_weight.T, bc_weight, in_weight)

    def sent(parts):
        return [parts[0]] + [swapped(parts[d], "tm", d) for d in range(1, shares)]

    received = lax.all_to_all(payload, "tm", split_axis=0, concat_axis=0, tiled=True)
    far = swapped(other, "height", 1)
    gate = call(
        functools.partial(gate_kernel, blocks),
        "gate",
        shape_of((count, inner), BF16),
        [ANY, WHOLE, HBM],
        scratch_shapes=[
            pltpu.VMEM((width, inner), BF16),
            pltpu.SemaphoreType.DMA((blocks,)),
        ],
    )(payload, normed, in_weight)

    out_local, reach = call(
        functools.partial(local_kernel, frames, rows, columns, head_dim, groups),
        "spatial_local",
        [shape_of((count, inner), F32), shape_of((count, LANES), F32)],
        [ANY] + [WHOLE] * 4,
    )(gate, bc_own, logits, params, payload)

    total = call(
        functools.partial(pair_kernel, frames),
        "pair_total",
        shape_of((frames * half + TAIL, inner), BF16),
        [SCALAR, WHOLE, WHOLE],
    )(band, own, far)
    returned, carried = [], []
    for part in range(parts):
        more = [shape_of((state, group), F32)] if part + 1 < parts else []
        results = call(
            functools.partial(
                temporal_kernel,
                part,
                parts,
                per_group,
                head_dim,
                rows,
                frames,
                columns,
                chunk_cols,
                shares,
                state,
            ),
            "temporal",
            [shape_of((part_len, group), BF16)] * shares + more,
            [SCALAR] + [WHOLE] * (2 + len(carried)),
            scratch_shapes=[
                pltpu.VMEM((shares, part_len, state), BF16),
                pltpu.VMEM((shares, part_len, state), BF16),
                pltpu.VMEM((shares, part_len, LANES), F32),
                pltpu.VMEM((shares, part_len, LANES), F32),
            ],
        )(here, params, received, *carried)
        returned.append(sent(results[:shares]))
        carried = results[shares:]

    before = []
    distance = 2
    while distance < bands:
        far_total = swapped(total, "height", distance)
        finish = distance * 2 >= bands
        operands = [reach, band, total, far_total] + before + ([own, far] if finish else [])
        outs = (
            [shape_of((frames * half, inner), BF16)] * 2
            if finish
            else [
                shape_of((frames * half + TAIL, inner), BF16),
                shape_of((frames * half + 8, inner), F32),
            ]
        )
        results = call(
            functools.partial(merge_kernel, frames, distance, finish),
            "merge",
            outs,
            [ANY, SCALAR] + [WHOLE] * (len(operands) - 2),
        )(*operands)
        if not finish:
            total, before = results[0], [results[1]]
        distance *= 2
    keep, give = results
    came = swapped(give, "height", 1)

    spatial_out = call(
        functools.partial(incoming_kernel, frames, rows, columns, head_dim),
        "spatial_incoming",
        shape_of((count, inner), F32),
        [SCALAR] + [WHOLE] * 5,
    )(band, out_local, bc_own, reach, keep, came)

    mixed = []
    for part in range(parts):
        mixed = [
            call(
                functools.partial(exit_kernel, part, parts, shares),
                "exit",
                shape_of(tokens.shape, BF16),
                [SCALAR] + [WHOLE] * (4 + shares) + [HBM] * len(mixed),
                outs=HBM,
                scratch_shapes=[
                    pltpu.VMEM((shares, part_len, group), BF16),
                    pltpu.VMEM((rows * part_len, inner), BF16),
                    pltpu.VMEM((rows * part_len, width), BF16),
                    pltpu.SemaphoreType.DMA((rows * frames,)),
                ],
                input_output_aliases={5 + shares: 0} if mixed else {},
            )(here, spatial_out, gate, out_gain, out_weight, *returned[part], *mixed)
        ]
    return mixed[0]


def solution(mesh):
    in_specs = (P("tm", "height", None, None), P(), P(), P(), P(), P(), P(), P(), P())
    out_specs = P("tm", "height", None, None)
    return jax.shard_map(
        per_device, mesh=mesh, in_specs=in_specs, out_specs=out_specs, check_vma=False
    )
```

time: 301 us -> 65.2 us (0.22)
  the two profiles are of different devices: /device:TPU:12 before, /device:TPU:0 now
where the time goes in v1:
time: 65.2 us; the launch traced here: 64.9 us
  Pallas kernels  22.6 us (35%)
  starting transfers between devices  18.6 us (29%)
  waiting for transfers between devices  14.6 us (22%)
  local copies, waits for them, and re-layouts  8.65 us (13%)
    ppermute x10, waiting for transfers between devices, swapped(): lax.ppermute(value, axis, [(source, source ^ distance) for source in rang...  12.9 us
    ppermute x10, starting transfers between devices, swapped(): lax.ppermute(value, axis, [(source, source ^ distance) for source in rang...  12.5 us
    unnamed x28, local copies, waits for them, and re-layouts  8.65 us
    pallas_call x1, Pallas kernels, per_device(): call(functools.partial(entry_kernel, shares, heads, state, blocks), 'entr...  7.42 us
    all_to_all x1, starting transfers between devices, per_device(): lax.all_to_all(payload, 'tm', split_axis=0, concat_axis=0, tiled=True)  6.03 us
    pallas_call x2, Pallas kernels, per_device(): call(functools.partial(temporal_kernel, part, parts, per_group, head_dim,...  4.58 us
    pallas_call x2, Pallas kernels, per_device(): call(functools.partial(exit_kernel, part, parts, shares), 'exit', shape_o...  3.92 us
    pallas_call x1, Pallas kernels, per_device(): call(functools.partial(gate_kernel, blocks), 'gate', shape_of((count, inn...  2.6 us
  transfers between devices with their start and end apart: 11, of which 4 were waited for; matrix products, arithmetic and copies ran while one was open for 0% of the time, Pallas kernels for 20%

profile of v1, /device:TPU:0, one launch (start us, length us, event | category | flops | bytes accessed | tf_op | source)
XLA Modules:
  0.0 64.9 jit_solution(460641233197146638)
XLA Ops:
  0.0 7.4 %entry.1 = (bf16[256,1536]{1,0:T(8,128)(2,1)}, bf16[4,176,768]{2,1,0:T(8,128)(2,1)}, bf16[256,256]{1,0:T(8,128)(2,1)}, f32[256,128]{1,0:T(8,128)}, f32[16,128]{1...) custom-call(s32[1]{0:T(128)} %bitcast.refs_0_, s32[1]{0:T(128)} %bitcast.1.refs_1_.band, ...), custom_call_target="tpu_custom_call" | custom-call | flops 1 | bytes 1 | tf_op jit(solution)/shard_map/entry/pallas_call | solution.py:552
  8.0 6.0 %all-to-all-start = ((bf16[4,176,768]{2,1,0:T(8,128)(2,1)}), bf16[4,176,768]{2,1,0:T(8,128)(2,1)S(1)}, u32[]{:S(2)}, u32[]{:S(2)}) async-start(bf16[4,176,768]{2,1,0:T(8,128)(2,1)} %get-tuple-element.27.after.refs_4_), calls=%async_computation | async-start | bytes 2162688 | tf_op jit(solution)/shard_map/all_to_all | solution.py:582
  14.2 1.6 %collective-permute-start.1 = (bf16[144,1536]{1,0:T(8,128)(2,1)S(1)}, bf16[144,1536]{1,0:T(8,128)(2,1)S(1)}, u32[]{:S(2)}, u32[]{:S(2)}) collective-permute-start(bf16[144,1536]{1,0:T(8,128)(2,1)S(1)} %pair_total.1.refs_2_), channel_id=1, source_target_pairs={{0,2},{1,3},{2,0},{3,1},{4,6},{5,7},{6,4},{7,5},{8,10},{9,11},{10,... | collective-permute-start | bytes 1327112 | tf_op jit(solution)/shard_map/ppermute | solution.py:526
  15.8 3.7 %copy-done = bf16[1536,3072]{1,0:T(8,128)(2,1)S(1)} copy-done((bf16[1536,3072]{1,0:T(8,128)(2,1)S(1)}, bf16[1536,3072]{1,0:T(8,128)(2,1)}, u32[]{:S(2)}) %copy-start) | copy-done | bytes 9437208
  19.5 2.6 %gate.1.refs_0_.refs_2_ = bf16[256,1536]{1,0:T(8,128)(2,1)S(1)} custom-call(bf16[4,176,768]{2,1,0:T(8,128)(2,1)S(1)} %copy-done.2, bf16[256,1536]{1,0:T(8,128)(2,1)S(1)} %copy-done.8, bf16[1536,3072]{1,0:T(8,128)(2,1)S(1)} %copy-done), custom_call_target="tpu_custom_call" | custom-call | flops 1 | bytes 1 | tf_op jit(solution)/shard_map/gate/pallas_call | solution.py:584
  22.1 1.9 %spatial_local.1 = (f32[256,1536]{1,0:T(8,128)S(1)}, f32[256,128]{1,0:T(8,128)S(1)}) custom-call(bf16[256,1536]{1,0:T(8,128)(2,1)S(1)} %gate.1.refs_0_.refs_2_, bf16[256,256]{1,0:T(8,128)(2,1)S(1)} %copy-done.9, f32[256,128]{1,0:T(8,128)S(1)} %copy-done.11, f32[16,128]{1,0:T(8,128)S(1)} %copy-done.12, bf16[4,176,768]{2,1,0:T(8,128)(2,1)S(1)} %copy-done.2), custom_call_target="tpu_custom_call" | custom-call | flops 1 | bytes 1 | tf_op jit(solution)/shard_map/spatial_local/pallas_call | solution.py:595
  24.1 1.2 %copy-done.6 = f32[256,1536]{1,0:T(8,128)} copy-done((f32[256,1536]{1,0:T(8,128)}, f32[256,1536]{1,0:T(8,128)S(1)}, u32[]{:S(2)}) %copy-start.6) | copy-done | bytes 1572888
  25.2 1.3 %collective-permute-done.1.refs_3_ = bf16[144,1536]{1,0:T(8,128)(2,1)S(1)} collective-permute-done((bf16[144,1536]{1,0:T(8,128)(2,1)S(1)}, bf16[144,1536]{1,0:T(8,128)(2,1)S(1)}, u32[]{:S(2)}, u32[]{:S(2)}) %collective-permute-start.1) | collective-permute-done | bytes 442400 | tf_op jit(solution)/shard_map/ppermute | solution.py:526
  26.8 1.6 %collective-permute-start.2 = (bf16[144,1536]{1,0:T(8,128)(2,1)S(1)}, bf16[144,1536]{1,0:T(8,128)(2,1)S(1)}, u32[]{:S(2)}, u32[]{:S(2)}) collective-permute-start(bf16[144,1536]{1,0:T(8,128)(2,1)S(1)} %get-tuple-element.36.refs_2_), channel_id=1, source_target_pairs={{0,4},{1,5},{2,6},{3,7},{4,0},{5,1},{6,2},{7,3},{8,12},{9,13},{10,... | collective-permute-start | bytes 1327112 | tf_op jit(solution)/shard_map/ppermute | solution.py:526
  28.4 9.9 %collective-permute-done.2.refs_3_ = bf16[144,1536]{1,0:T(8,128)(2,1)S(1)} collective-permute-done((bf16[144,1536]{1,0:T(8,128)(2,1)S(1)}, bf16[144,1536]{1,0:T(8,128)(2,1)S(1)}, u32[]{:S(2)}, u32[]{:S(2)}) %collective-permute-start.2) | collective-permute-done | bytes 442400 | tf_op jit(solution)/shard_map/ppermute | solution.py:526
  38.3 1.0 %merge.3 = (bf16[128,1536]{1,0:T(8,128)(2,1)S(1)}, bf16[128,1536]{1,0:T(8,128)(2,1)}) custom-call(f32[256,128]{1,0:T(8,128)S(1)} %get-tuple-element.33.refs_0_.reach, s32[1]{0:T(128)} %bitcast.1.refs_1_.band, bf16[144,1536]{1,0:T(8,128)(2,1)S(1)} %get-tuple-element.36.refs_2_, bf16[144,1536]{1,0:T(8,128)(2,1)S(1)} %collective-permute-done.2.refs_3_, ...), custom_call_target="tpu_custom_call" | custom-call | flops 1 | bytes 1 | tf_op jit(solution)/shard_map/merge/pallas_call | solution.py:652
  39.3 1.7 %all-to-all-done.refs_2_ = bf16[4,176,768]{2,1,0:T(8,128)(2,1)S(1)} async-done(((bf16[4,176,768]{2,1,0:T(8,128)(2,1)}), bf16[4,176,768]{2,1,0:T(8,128)(2,1)S(1)}, u32[]{:S(2)}, u32[]{:S(2)}) %all-to-all-start) | async-done | bytes 1081376 | tf_op jit(solution)/shard_map/all_to_all | solution.py:582
  41.1 2.4 %temporal.2 = (bf16[64,768]{1,0:T(8,128)(2,1)S(1)}, bf16[64,768]{1,0:T(8,128)(2,1)S(1)}, bf16[64,768]{1,0:T(8,128)(2,1)S(1)}, bf16[64,768]{1,0:T(8,128)(2,1)S(1)}, f32[128,768]{1,0:T(8,128)S(1)}) custom-call(s32[1]{0:T(128)} %bitcast.refs_0_, f32[16,128]{1,0:T(8,128)S(1)} %copy-done.12, bf16[4,176,768]{2,1,0:T(8,128)(2,1)S(1)} %all-to-all-done.refs_2_), custom_call_target="tpu_custom_call" | custom-call | flops 1 | bytes 1 | tf_op jit(solution)/shard_map/temporal/pallas_call | solution.py:611
  43.5 2.0 %collective-permute-start.8 = (bf16[64,768]{1,0:T(8,128)(2,1)S(1)}, bf16[64,768]{1,0:T(8,128)(2,1)S(1)}, u32[]{:S(2)}, u32[]{:S(2)}) collective-permute-start(bf16[64,768]{1,0:T(8,128)(2,1)S(1)} %get-tuple-element.47), channel_id=1, source_target_pairs={{0,16},{8,24},{16,0},{24,8},{1,17},{9,25},{17,1},{25,9},{2,18},{10... | collective-permute-start | bytes 294920 | tf_op jit(solution)/shard_map/ppermute | solution.py:526
  45.5 2.3 %collective-permute-start.9 = (bf16[64,768]{1,0:T(8,128)(2,1)S(1)}, bf16[64,768]{1,0:T(8,128)(2,1)S(1)}, u32[]{:S(2)}, u32[]{:S(2)}) collective-permute-start(bf16[64,768]{1,0:T(8,128)(2,1)S(1)} %get-tuple-element.48), channel_id=1, source_target_pairs={{0,24},{8,16},{16,8},{24,0},{1,25},{9,17},{17,9},{25,1},{2,26},{10... | collective-permute-start | bytes 294920 | tf_op jit(solution)/shard_map/ppermute | solution.py:526
  47.9 2.2 %temporal.3 = (bf16[64,768]{1,0:T(8,128)(2,1)S(1)}, bf16[64,768]{1,0:T(8,128)(2,1)S(1)}, bf16[64,768]{1,0:T(8,128)(2,1)S(1)}, bf16[64,768]{1,0:T(8,128)(2,1)S(1)}) custom-call(s32[1]{0:T(128)} %bitcast.refs_0_, f32[16,128]{1,0:T(8,128)S(1)} %copy-done.12, bf16[4,176,768]{2,1,0:T(8,128)(2,1)S(1)} %all-to-all-done.refs_2_, ...), custom_call_target="tpu_custom_call" | custom-call | flops 1 | bytes 1 | tf_op jit(solution)/shard_map/temporal/pallas_call | solution.py:611
  50.2 2.0 %collective-permute-start.5 = (bf16[64,768]{1,0:T(8,128)(2,1)S(1)}, bf16[64,768]{1,0:T(8,128)(2,1)S(1)}, u32[]{:S(2)}, u32[]{:S(2)}) collective-permute-start(bf16[64,768]{1,0:T(8,128)(2,1)S(1)} %get-tuple-element.43), channel_id=1, source_target_pairs={{0,16},{8,24},{16,0},{24,8},{1,17},{9,25},{17,1},{25,9},{2,18},{10... | collective-permute-start | bytes 294920 | tf_op jit(solution)/shard_map/ppermute | solution.py:526
  52.2 2.4 %collective-permute-start.6 = (bf16[64,768]{1,0:T(8,128)(2,1)S(1)}, bf16[64,768]{1,0:T(8,128)(2,1)S(1)}, u32[]{:S(2)}, u32[]{:S(2)}) collective-permute-start(bf16[64,768]{1,0:T(8,128)(2,1)S(1)} %get-tuple-element.44), channel_id=1, source_target_pairs={{0,24},{8,16},{16,8},{24,0},{1,25},{9,17},{17,9},{25,1},{2,26},{10... | collective-permute-start | bytes 294920 | tf_op jit(solution)/shard_map/ppermute | solution.py:526
  54.6 1.4 %copy-done.7 = f32[256,1536]{1,0:T(8,128)S(1)} copy-done((f32[256,1536]{1,0:T(8,128)S(1)}, f32[256,1536]{1,0:T(8,128)}, u32[]{:S(2)}) %copy-start.7) | copy-done | bytes 1572888
  56.0 0.8 %spatial_incoming.1.refs_1_ = f32[256,1536]{1,0:T(8,128)S(1)} custom-call(s32[1]{0:T(128)} %bitcast.1.refs_1_.band, f32[256,1536]{1,0:T(8,128)S(1)} %copy-done.7, bf16[256,256]{1,0:T(8,128)(2,1)S(1)} %copy-done.10, f32[256,128]{1,0:T(8,128)S(1)} %get-tuple-element.33.refs_0_.reach, bf16[128,1536]{1,0:T(8,128)(2,1)S(1)} %get-tuple-element.38.own, ...), custom_call_target="tpu_custom_call" | custom-call | flops 1 | bytes 1 | tf_op jit(solution)/shard_map/spatial_incoming/pallas_call | solution.py:664
  56.8 2.3 %copy-done.1 = bf16[1536,1536]{1,0:T(8,128)(2,1)S(1)} copy-done((bf16[1536,1536]{1,0:T(8,128)(2,1)S(1)}, bf16[1536,1536]{1,0:T(8,128)(2,1)}, u32[]{:S(2)}) %copy-start.1) | copy-done | bytes 4718616
  59.1 2.0 %exit.2.refs_9_ = bf16[2,2,64,1536]{3,2,1,0:T(8,128)(2,1)} custom-call(s32[1]{0:T(128)} %bitcast.refs_0_, f32[256,1536]{1,0:T(8,128)S(1)} %spatial_incoming.1.refs_1_, bf16[256,1536]{1,0:T(8,128)(2,1)S(1)} %gate.1.refs_0_.refs_2_, f32[1536]{0:T(1024)S(1)} %copy-done.13, bf16[1536,1536]{1,0:T(8,128)(2,1)S(1)} %copy-done.1, ...), custom_call_target="tpu_custom_call" | custom-call | flops 1 | bytes 1 | tf_op jit(solution)/shard_map/exit/pallas_call | solution.py:674
  61.1 1.7 %collective-permute-done.5.refs_7_ = bf16[64,768]{1,0:T(8,128)(2,1)S(1)} collective-permute-done((bf16[64,768]{1,0:T(8,128)(2,1)S(1)}, bf16[64,768]{1,0:T(8,128)(2,1)S(1)}, u32[]{:S(2)}, u32[]{:S(2)}) %collective-permute-start.5) | collective-permute-done | bytes 98336 | tf_op jit(solution)/shard_map/ppermute | solution.py:526
  62.8 2.0 %exit.3 = bf16[2,2,64,1536]{3,2,1,0:T(8,128)(2,1)} custom-call(s32[1]{0:T(128)} %bitcast.refs_0_, f32[256,1536]{1,0:T(8,128)S(1)} %spatial_incoming.1.refs_1_, bf16[256,1536]{1,0:T(8,128)(2,1)S(1)} %gate.1.refs_0_.refs_2_, f32[1536]{0:T(1024)S(1)} %copy-done.13, bf16[1536,1536]{1,0:T(8,128)(2,1)S(1)} %copy-done.1, ...), custom_call_target="tpu_custom_call", output_to_operand_aliasing={{}: (9, {})} | custom-call | flops 1 | bytes 1 | tf_op jit(solution)/shard_map/exit/pallas_call | solution.py:674
  (37 shorter events, 1.1 us)
Async XLA Ops:
  7.4 6.6 %copy-start.3 = (bf16[144,1536]{1,0:T(8,128)(2,1)S(1)}, bf16[144,1536]{1,0:T(8,128)(2,1)}, u32[]{:S(2)}) copy-start(bf16[144,1536]{1,0:T(8,128)(2,1)} %get-tuple-element.34.own.refs_5_) | copy-start | bytes 1327108
  7.4 6.6 %collective-permute-start = (bf16[144,1536]{1,0:T(8,128)(2,1)}, bf16[144,1536]{1,0:T(8,128)(2,1)S(1)}, u32[]{:S(2)}, u32[]{:S(2)}) collective-permute-start(bf16[144,1536]{1,0:T(8,128)(2,1)} %get-tuple-element.35), channel_id=1, source_target_pairs={{0,1},{1,0},{2,3},{3,2},{4,5},{5,4},{6,7},{7,6},{8,9},{9,8},{10,11... | collective-permute-start | bytes 1327112 | tf_op jit(solution)/shard_map/ppermute | solution.py:526
  8.0 7.8 %copy-start.2 = (bf16[4,176,768]{2,1,0:T(8,128)(2,1)S(1)}, bf16[4,176,768]{2,1,0:T(8,128)(2,1)}, u32[]{:S(2)}) copy-start(bf16[4,176,768]{2,1,0:T(8,128)(2,1)} %get-tuple-element.27.after.refs_4_) | copy-start | bytes 3244036
  8.0 33.1 %all-to-all-start = ((bf16[4,176,768]{2,1,0:T(8,128)(2,1)}), bf16[4,176,768]{2,1,0:T(8,128)(2,1)S(1)}, u32[]{:S(2)}, u32[]{:S(2)}) async-start(bf16[4,176,768]{2,1,0:T(8,128)(2,1)} %get-tuple-element.27.after.refs_4_), calls=%async_computation | async-start | bytes 2162688 | tf_op jit(solution)/shard_map/all_to_all | solution.py:582
  14.0 1.8 %copy-start.8 = (bf16[256,1536]{1,0:T(8,128)(2,1)S(1)}, bf16[256,1536]{1,0:T(8,128)(2,1)}, u32[]{:S(2)}) copy-start(bf16[256,1536]{1,0:T(8,128)(2,1)} %get-tuple-element.28.normed) | copy-start | bytes 2359300
  14.0 1.8 %copy-start.4 = (bf16[144,1536]{1,0:T(8,128)(2,1)}, bf16[144,1536]{1,0:T(8,128)(2,1)S(1)}, u32[]{:S(2)}) copy-start(bf16[144,1536]{1,0:T(8,128)(2,1)S(1)} %collective-permute-done.far.refs_6_) | copy-start | bytes 1327108
  14.2 12.3 %collective-permute-start.1 = (bf16[144,1536]{1,0:T(8,128)(2,1)S(1)}, bf16[144,1536]{1,0:T(8,128)(2,1)S(1)}, u32[]{:S(2)}, u32[]{:S(2)}) collective-permute-start(bf16[144,1536]{1,0:T(8,128)(2,1)S(1)} %pair_total.1.refs_2_), channel_id=1, source_target_pairs={{0,2},{1,3},{2,0},{3,1},{4,6},{5,7},{6,4},{7,5},{8,10},{9,11},{10,... | collective-permute-start | bytes 1327112 | tf_op jit(solution)/shard_map/ppermute | solution.py:526
  15.8 3.7 %copy-start = (bf16[1536,3072]{1,0:T(8,128)(2,1)S(1)}, bf16[1536,3072]{1,0:T(8,128)(2,1)}, u32[]{:S(2)}) copy-start(bf16[1536,3072]{1,0:T(8,128)(2,1)} %weight.1) | copy-start | bytes 28311556
  19.4 2.6 %copy-start.9 = (bf16[256,256]{1,0:T(8,128)(2,1)S(1)}, bf16[256,256]{1,0:T(8,128)(2,1)}, u32[]{:S(2)}) copy-start(bf16[256,256]{1,0:T(8,128)(2,1)} %get-tuple-element.29.refs_1_.bc) | copy-start | bytes 393220
  19.5 2.6 %copy-start.11 = (f32[256,128]{1,0:T(8,128)S(1)}, f32[256,128]{1,0:T(8,128)}, u32[]{:S(2)}) copy-start(f32[256,128]{1,0:T(8,128)} %get-tuple-element.30.refs_2_) | copy-start | bytes 393220
  19.5 2.6 %copy-start.12 = (f32[16,128]{1,0:T(8,128)S(1)}, f32[16,128]{1,0:T(8,128)}, u32[]{:S(2)}) copy-start(f32[16,128]{1,0:T(8,128)} %get-tuple-element.31.refs_3_.refs_1_) | copy-start | bytes 24580
  22.1 16.2 %copy-start.5 = (bf16[144,1536]{1,0:T(8,128)(2,1)S(1)}, bf16[144,1536]{1,0:T(8,128)(2,1)}, u32[]{:S(2)}) copy-start(bf16[144,1536]{1,0:T(8,128)(2,1)} %copy-done.4) | copy-start | bytes 1327108
  24.0 1.2 %copy-start.6 = (f32[256,1536]{1,0:T(8,128)}, f32[256,1536]{1,0:T(8,128)S(1)}, u32[]{:S(2)}) copy-start(f32[256,1536]{1,0:T(8,128)S(1)} %get-tuple-element.32.out_local) | copy-start | bytes 4718596
  26.8 11.5 %collective-permute-start.2 = (bf16[144,1536]{1,0:T(8,128)(2,1)S(1)}, bf16[144,1536]{1,0:T(8,128)(2,1)S(1)}, u32[]{:S(2)}, u32[]{:S(2)}) collective-permute-start(bf16[144,1536]{1,0:T(8,128)(2,1)S(1)} %get-tuple-element.36.refs_2_), channel_id=1, source_target_pairs={{0,4},{1,5},{2,6},{3,7},{4,0},{5,1},{6,2},{7,3},{8,12},{9,13},{10,... | collective-permute-start | bytes 1327112 | tf_op jit(solution)/shard_map/ppermute | solution.py:526
  39.3 15.3 %copy-start.10 = (bf16[256,256]{1,0:T(8,128)(2,1)S(1)}, bf16[256,256]{1,0:T(8,128)(2,1)}, u32[]{:S(2)}) copy-start(bf16[256,256]{1,0:T(8,128)(2,1)} %get-tuple-element.29.refs_1_.bc) | copy-start | bytes 393220
  39.3 12.9 %collective-permute-start.3 = (bf16[128,1536]{1,0:T(8,128)(2,1)}, bf16[128,1536]{1,0:T(8,128)(2,1)S(1)}, u32[]{:S(2)}, u32[]{:S(2)}) collective-permute-start(bf16[128,1536]{1,0:T(8,128)(2,1)} %get-tuple-element.39), channel_id=1, source_target_pairs={{0,1},{1,0},{2,3},{3,2},{4,5},{5,4},{6,7},{7,6},{8,9},{9,8},{10,11... | collective-permute-start | bytes 1179656 | tf_op jit(solution)/shard_map/ppermute | solution.py:526
  43.4 6.7 %collective-permute-start.7 = (bf16[64,768]{1,0:T(8,128)(2,1)S(1)}, bf16[64,768]{1,0:T(8,128)(2,1)S(1)}, u32[]{:S(2)}, u32[]{:S(2)}) collective-permute-start(bf16[64,768]{1,0:T(8,128)(2,1)S(1)} %get-tuple-element.46), channel_id=1, source_target_pairs={{0,8},{8,0},{16,24},{24,16},{1,9},{9,1},{17,25},{25,17},{2,10},{10... | collective-permute-start | bytes 294920 | tf_op jit(solution)/shard_map/ppermute | solution.py:526
  43.5 13.2 %collective-permute-start.8 = (bf16[64,768]{1,0:T(8,128)(2,1)S(1)}, bf16[64,768]{1,0:T(8,128)(2,1)S(1)}, u32[]{:S(2)}, u32[]{:S(2)}) collective-permute-start(bf16[64,768]{1,0:T(8,128)(2,1)S(1)} %get-tuple-element.47), channel_id=1, source_target_pairs={{0,16},{8,24},{16,0},{24,8},{1,17},{9,25},{17,1},{25,9},{2,18},{10... | collective-permute-start | bytes 294920 | tf_op jit(solution)/shard_map/ppermute | solution.py:526
  45.5 11.2 %collective-permute-start.9 = (bf16[64,768]{1,0:T(8,128)(2,1)S(1)}, bf16[64,768]{1,0:T(8,128)(2,1)S(1)}, u32[]{:S(2)}, u32[]{:S(2)}) collective-permute-start(bf16[64,768]{1,0:T(8,128)(2,1)S(1)} %get-tuple-element.48), channel_id=1, source_target_pairs={{0,24},{8,16},{16,8},{24,0},{1,25},{9,17},{17,9},{25,1},{2,26},{10... | collective-permute-start | bytes 294920 | tf_op jit(solution)/shard_map/ppermute | solution.py:526
  50.1 11.0 %collective-permute-start.4 = (bf16[64,768]{1,0:T(8,128)(2,1)S(1)}, bf16[64,768]{1,0:T(8,128)(2,1)S(1)}, u32[]{:S(2)}, u32[]{:S(2)}) collective-permute-start(bf16[64,768]{1,0:T(8,128)(2,1)S(1)} %get-tuple-element.42), channel_id=1, source_target_pairs={{0,8},{8,0},{16,24},{24,16},{1,9},{9,1},{17,25},{25,17},{2,10},{10... | collective-permute-start | bytes 294920 | tf_op jit(solution)/shard_map/ppermute | solution.py:526
  50.2 12.6 %collective-permute-start.5 = (bf16[64,768]{1,0:T(8,128)(2,1)S(1)}, bf16[64,768]{1,0:T(8,128)(2,1)S(1)}, u32[]{:S(2)}, u32[]{:S(2)}) collective-permute-start(bf16[64,768]{1,0:T(8,128)(2,1)S(1)} %get-tuple-element.43), channel_id=1, source_target_pairs={{0,16},{8,24},{16,0},{24,8},{1,17},{9,25},{17,1},{25,9},{2,18},{10... | collective-permute-start | bytes 294920 | tf_op jit(solution)/shard_map/ppermute | solution.py:526
  52.2 10.5 %collective-permute-start.6 = (bf16[64,768]{1,0:T(8,128)(2,1)S(1)}, bf16[64,768]{1,0:T(8,128)(2,1)S(1)}, u32[]{:S(2)}, u32[]{:S(2)}) collective-permute-start(bf16[64,768]{1,0:T(8,128)(2,1)S(1)} %get-tuple-element.44), channel_id=1, source_target_pairs={{0,24},{8,16},{16,8},{24,0},{1,25},{9,17},{17,9},{25,1},{2,26},{10... | collective-permute-start | bytes 294920 | tf_op jit(solution)/shard_map/ppermute | solution.py:526
  54.6 1.4 %copy-start.7 = (f32[256,1536]{1,0:T(8,128)S(1)}, f32[256,1536]{1,0:T(8,128)}, u32[]{:S(2)}) copy-start(f32[256,1536]{1,0:T(8,128)} %copy-done.6) | copy-start | bytes 4718596
  56.8 2.3 %copy-start.1 = (bf16[1536,1536]{1,0:T(8,128)(2,1)S(1)}, bf16[1536,1536]{1,0:T(8,128)(2,1)}, u32[]{:S(2)}) copy-start(bf16[1536,1536]{1,0:T(8,128)(2,1)} %refs_4_.5) | copy-start | bytes 14155780
  (1 other events, 0.8 us)

commit v2 on v1

--- a/solution.py
+++ b/solution.py
@@ -131,8 +131,9 @@
 
 def entry_kernel(shares, heads, state, blocks, *refs):
     here_ref, band, tokens, gain, bias, rates, dt_weight, bc_weight, weight = refs[:9]
-    normed_out, payload_out, bc_own, logits, params, own_states, other_states = refs[9:16]
-    held, dt_held, bc_held, held_weight, table, normed, payload, sems, out_sems = refs[16:]
+    normed_out, x_out, bc_own, logits, params, own_states, other_states = refs[9:16]
+    payloads = refs[16 : 16 + shares]
+    held, dt_held, bc_held, held_weight, table, normed, payload, sems, out_sems = refs[-9:]
     frames, rows, columns, width = tokens.shape
     length = frames * columns
     count = rows * length
@@ -198,21 +199,23 @@
             part = (at + inside) // group
             for row in range(rows):
                 piece = part * rows + row
-                here = slice(row * length, (row + 1) * length)
-                payload[piece, :length, :] = values[here, inside : inside + group]
+                tokens_here = slice(row * length, (row + 1) * length)
+                payload[piece, :length, :] = values[tokens_here, inside : inside + group]
                 pack_rest(
                     payload.at[piece],
                     length,
-                    bc[here, 2 * state : 3 * state],
-                    bc[here, 3 * state :],
-                    dt_heads[part * per_group : part * per_group + TAIL, here],
+                    bc[tokens_here, 2 * state : 3 * state],
+                    bc[tokens_here, 3 * state :],
+                    dt_heads[part * per_group : part * per_group + TAIL, tokens_here],
                 )
-                outgoing.append(
-                    pltpu.make_async_copy(
-                        payload.at[piece], payload_out.at[piece], out_sems.at[1 + piece]
-                    )
-                )
-                outgoing[-1].start()
+    here = here_ref[0]
+    for distance in range(shares):
+        outgoing.append(
+            pltpu.make_async_copy(payload.at[here ^ distance], payloads[distance], out_sems.at[1 + distance])
+        )
+        outgoing[-1].start()
+    outgoing.append(pltpu.make_async_copy(payload, x_out, out_sems.at[1 + shares]))
+    outgoing[-1].start()
     half = state // 2
     head_dim = groups * group // heads
     mine = band[0] % 2 == 0
@@ -394,9 +397,10 @@
 def temporal_kernel(
     part, parts, per_group, head_dim, rows, frames, columns, chunk_cols, shares, state, *refs
 ):
-    here_ref, params, payload = refs[:3]
-    rest = list(refs[3:])
+    here_ref, params = refs[:2]
+    payloads, rest = refs[2 : 2 + shares], list(refs[2 + shares :])
     carried_in = rest.pop(0) if part > 0 else None
+    rest.pop(0)
     outs, rest = rest[:shares], rest[shares:]
     carried_out = rest.pop(0) if part + 1 < parts else None
     b_all, c_all, dt_all, decay_all = rest
@@ -407,11 +411,8 @@
     eye = (iota((TAIL, LANES), 0) == iota((TAIL, LANES), 1)) & (iota((TAIL, LANES), 1) < per_group)
     eye = eye.astype(BF16)
 
-    def came(distance):
-        return payload.at[here ^ distance]
-
     for distance in range(shares):
-        b_proj, c_proj, logits = unpacked_rest(came(distance), length)
+        b_proj, c_proj, logits = unpacked_rest(payloads[distance], length)
         logits = dot_tn(logits, eye)
         for frame in range(frames):
             at = slice(frame * columns + part * part_cols, frame * columns + (part + 1) * part_cols)
@@ -447,7 +448,7 @@
                 axis=0,
             )
 
-        values = gathered(came, columns, part * part_cols)
+        values = gathered(lambda source: payloads[source], columns, part * part_cols)
         b_proj = gathered(lambda source: b_all.at[source])
         c_proj = gathered(lambda source: c_all.at[source])
         dt = gathered(lambda source: dt_all.at[source])
@@ -549,7 +550,14 @@
     band = lax.axis_index("height").astype(jnp.int32).reshape(1)
 
     packed = (shares, sum(packing(length, group)), group)
-    normed, payload, bc_own, logits, params, own, other = call(
+    blanks = [
+        shape_of((frames * half, inner), BF16),
+        shape_of((frames * half, inner), BF16),
+        shape_of((count, inner), BF16),
+        shape_of((count, inner), F32),
+        shape_of((count, LANES), F32),
+    ]
+    entry = call(
         functools.partial(entry_kernel, shares, heads, state, blocks),
         "entry",
         [
@@ -559,10 +567,12 @@
             shape_of((count, LANES), F32),
             shape_of((16, LANES), F32),
         ]
-        + [shape_of((frames * half + TAIL, inner), BF16)] * 2,
+        + [shape_of((frames * half + TAIL, inner), BF16)] * 2
+        + [shape_of(packed[1:], BF16)] * shares
+        + blanks,
         [SCALAR, SCALAR, HBM, WHOLE, WHOLE, WHOLE, HBM, HBM, HBM],
         limit=LARGE,
-        outs=[HBM, HBM] + [WHOLE] * 5,
+        outs=[HBM, HBM] + [WHOLE] * 5 + [HBM] * (shares + len(blanks)),
         scratch_shapes=[
             pltpu.VMEM((rows, frames, columns, width), BF16),
             pltpu.VMEM((2 * heads, width), BF16),
@@ -572,39 +582,76 @@
             pltpu.VMEM((count, width), BF16),
             pltpu.VMEM(packed, BF16),
             pltpu.SemaphoreType.DMA((rows * frames + 2 + blocks,)),
-            pltpu.SemaphoreType.DMA((1 + shares,)),
+            pltpu.SemaphoreType.DMA((2 + shares,)),
         ],
     )(here, band, tokens, norm_gain, dt_bias, decay_rate, dt_weight.T, bc_weight, in_weight)
+    normed, x, bc_own, logits, params, own, other = entry[:7]
+    payloads, blanks = entry[7 : 7 + shares], entry[7 + shares :]
 
     def sent(parts):
         return [parts[0]] + [swapped(parts[d], "tm", d) for d in range(1, shares)]
 
-    received = lax.all_to_all(payload, "tm", split_axis=0, concat_axis=0, tiled=True)
-    far = swapped(other, "height", 1)
-    gate = call(
-        functools.partial(gate_kernel, blocks),
-        "gate",
-        shape_of((count, inner), BF16),
-        [ANY, WHOLE, HBM],
-        scratch_shapes=[
-            pltpu.VMEM((width, inner), BF16),
-            pltpu.SemaphoreType.DMA((blocks,)),
-        ],
-    )(payload, normed, in_weight)
-
-    out_local, reach = call(
-        functools.partial(local_kernel, frames, rows, columns, head_dim, groups),
-        "spatial_local",
-        [shape_of((count, inner), F32), shape_of((count, LANES), F32)],
-        [ANY] + [WHOLE] * 4,
-    )(gate, bc_own, logits, params, payload)
-
-    total = call(
-        functools.partial(pair_kernel, frames),
-        "pair_total",
-        shape_of((frames * half + TAIL, inner), BF16),
-        [SCALAR, WHOLE, WHOLE],
-    )(band, own, far)
+    received = sent(payloads)
+
+    def exchange(_, carried):
+        other = carried[-1]
+        far = swapped(other, "height", 1)
+        gate = call(
+            functools.partial(gate_kernel, blocks),
+            "gate",
+            shape_of((count, inner), BF16),
+            [ANY, WHOLE, HBM],
+            scratch_shapes=[
+                pltpu.VMEM((width, inner), BF16),
+                pltpu.SemaphoreType.DMA((blocks,)),
+            ],
+        )(other, normed, in_weight)
+
+        out_local, reach = call(
+            functools.partial(local_kernel, frames, rows, columns, head_dim, groups),
+            "spatial_local",
+            [shape_of((count, inner), F32), shape_of((count, LANES), F32)],
+            [ANY] + [WHOLE] * 4,
+        )(gate, bc_own, logits, params, x)
+
+        total = call(
+            functools.partial(pair_kernel, frames),
+            "pair_total",
+            shape_of((frames * half + TAIL, inner), BF16),
+            [SCALAR, WHOLE, WHOLE],
+        )(band, own, far)
+        before = []
+        distance = 2
+        while distance < bands:
+            far_total = swapped(total, "height", distance)
+            finish = distance * 2 >= bands
+            if distance == 2:
+                spent = total
+            operands = [reach, band, total, far_total] + before + ([own, far] if finish else [])
+            outs = (
+                [shape_of((frames * half, inner), BF16)] * 2
+                if finish
+                else [
+                    shape_of((frames * half + TAIL, inner), BF16),
+                    shape_of((frames * half + 8, inner), F32),
+                ]
+            )
+            results = call(
+                functools.partial(merge_kernel, frames, distance, finish),
+                "merge",
+                outs,
+                [ANY, SCALAR] + [WHOLE] * (len(operands) - 2),
+            )(*operands)
+            if not finish:
+                total, before = results[0], [results[1]]
+            distance *= 2
+        keep, give = results
+        return keep, give, gate, out_local, reach, spent
+
+    turns = jnp.where(band[0] < bands, 1, 2)
+    keep, give, gate, out_local, reach, _ = lax.fori_loop(0, turns, exchange, (*blanks, other))
+    came = swapped(give, "height", 1)
+
     returned, carried = [], []
     for part in range(parts):
         more = [shape_of((state, group), F32)] if part + 1 < parts else []
@@ -624,42 +671,16 @@
             ),
             "temporal",
             [shape_of((part_len, group), BF16)] * shares + more,
-            [SCALAR] + [WHOLE] * (2 + len(carried)),
+            [SCALAR] + [WHOLE] * (1 + shares + len(carried)) + [ANY],
             scratch_shapes=[
                 pltpu.VMEM((shares, part_len, state), BF16),
                 pltpu.VMEM((shares, part_len, state), BF16),
                 pltpu.VMEM((shares, part_len, LANES), F32),
                 pltpu.VMEM((shares, part_len, LANES), F32),
             ],
-        )(here, params, received, *carried)
+        )(here, params, *received, *carried, reach)
         returned.append(sent(results[:shares]))
         carried = results[shares:]
-
-    before = []
-    distance = 2
-    while distance < bands:
-        far_total = swapped(total, "height", distance)
-        finish = distance * 2 >= bands
-        operands = [reach, band, total, far_total] + before + ([own, far] if finish else [])
-        outs = (
-            [shape_of((frames * half, inner), BF16)] * 2
-            if finish
-            else [
-                shape_of((frames * half + TAIL, inner), BF16),
-                shape_of((frames * half + 8, inner), F32),
-            ]
-        )
-        results = call(
-            functools.partial(merge_kernel, frames, distance, finish),
-            "merge",
-            outs,
-            [ANY, SCALAR] + [WHOLE] * (len(operands) - 2),
-        )(*operands)
-        if not finish:
-            total, before = results[0], [results[1]]
-        distance *= 2
-    keep, give = results
-    came = swapped(give, "height", 1)
 
     spatial_out = call(
         functools.partial(incoming_kernel, frames, rows, columns, head_dim),

time: 65.2 us -> 89.7 us (1.38)
  waiting for transfers between devices: 14.6 us -> 36.4 us
  local copies, waits for them, and re-layouts: 8.65 us -> 0.06 us
  Pallas kernels: 22.6 us -> 30.1 us
  starting transfers between devices: 18.6 us -> 22.4 us
    ppermute x10 -> x13, waiting for transfers between devices: 12.9 us -> 36.4 us  [swapped(): lax.ppermute(value, axis, [(source, source ^ distance) for source in rang...]
    ppermute x10 -> x13, starting transfers between devices: 12.5 us -> 22.4 us  [swapped(): lax.ppermute(value, axis, [(source, source ^ distance) for source in rang...]
    unnamed x28 -> x12, local copies, waits for them, and re-layouts: 8.65 us -> 0.02 us
    all_to_all x1 -> x0, starting transfers between devices: 6.03 us -> none  [per_device(): lax.all_to_all(payload, 'tm', split_axis=0, concat_axis=0, tiled=True)]
    pallas_call x5, Pallas kernels: 5.96 us -> 11.1 us  [the longest x1 4.77 us: exchange(): call(functools.partial(local_kernel, frames, rows, columns, head_dim, gro...]
    all_to_all x1 -> x0, waiting for transfers between devices: 1.75 us -> none  [per_device(): lax.all_to_all(payload, 'tm', split_axis=0, concat_axis=0, tiled=True)]
    pallas_call x1, Pallas kernels: 0.76 us -> 2.24 us  [per_device(): call(functools.partial(incoming_kernel, frames, rows, columns, head_dim),...]
  transfers between devices with their start and end apart: 11 -> 13, of which waited for: 4 -> 6; matrix products, arithmetic and copies ran while one was open for 0% -> 0% of each run, Pallas kernels for 20% -> 20%
where the time goes in v2:
time: 89.7 us; the launch traced here: 89.4 us
  waiting for transfers between devices  36.4 us (41%)
  Pallas kernels  30.1 us (34%)
  starting transfers between devices  22.4 us (25%)
    ppermute x13, waiting for transfers between devices, swapped(): lax.ppermute(value, axis, [(source, source ^ distance) for source in rang...  36.4 us
    ppermute x13, starting transfers between devices, swapped(): lax.ppermute(value, axis, [(source, source ^ distance) for source in rang...  22.4 us
    pallas_call x1, Pallas kernels, per_device(): call(functools.partial(entry_kernel, shares, heads, state, blocks), 'entr...  8.25 us
    pallas_call x1, Pallas kernels, exchange(): call(functools.partial(local_kernel, frames, rows, columns, head_dim, gro...  4.77 us
    pallas_call x1, Pallas kernels, exchange(): call(functools.partial(gate_kernel, blocks), 'gate', shape_of((count, inn...  4.77 us
    pallas_call x2, Pallas kernels, per_device(): call(functools.partial(temporal_kernel, part, parts, per_group, head_dim,...  4.58 us
    pallas_call x2, Pallas kernels, per_device(): call(functools.partial(exit_kernel, part, parts, shares), 'exit', shape_o...  3.94 us
    pallas_call x1, Pallas kernels, per_device(): call(functools.partial(incoming_kernel, frames, rows, columns, head_dim),...  2.24 us
  transfers between devices with their start and end apart: 13, of which 6 were waited for; matrix products, arithmetic and copies ran while one was open for 0% of the time, Pallas kernels for 20%

profile of v2, /device:TPU:0, one launch (start us, length us, event | category | flops | bytes accessed | tf_op | source)
XLA Modules:
  0.0 89.4 jit_solution(5755750262863074962)
XLA Ops:
  0.0 8.3 %entry.1 = (bf16[256,1536]{1,0:T(8,128)(2,1)}, bf16[4,176,768]{2,1,0:T(8,128)(2,1)}, bf16[256,256]{1,0:T(8,128)(2,1)}, f32[256,128]{1,0:T(8,128)}, f32[16,128]{1...) custom-call(s32[1]{0:T(128)} %bitcast.refs_0_, ...), custom_call_target="tpu_custom_call" | custom-call | flops 1 | bytes 1 | tf_op jit(solution)/shard_map/entry/pallas_call | solution.py:560
  8.3 28.9 %while.20 = (s32[]{:T(128)}, bf16[128,1536]{1,0:T(8,128)(2,1)}, bf16[128,1536]{1,0:T(8,128)(2,1)}, bf16[256,1536]{1,0:T(8,128)(2,1)}, f32[256,1536]{1,0:T(8,128)...) while((s32[]{:T(128)}, bf16[128,1536]{1,0:T(8,128)(2,1)}, ...), condition=%wide.region_1.2_spmd, body=%wide.region_0.1_spmd.sunk | while | flops 7 | bytes 9863506 | solution.py:652
  9.0 1.4 %collective-permute-done.far.refs_6_ = bf16[144,1536]{1,0:T(8,128)(2,1)S(1)} collective-permute-done((bf16[144,1536]{1,0:T(8,128)(2,1)S(1)}, bf16[144,1536]{1,0:T(8,128)(2,1)S(1)}, u32[]{:S(2)}, u32[]{:S(2)}) %collective-permute-start) | collective-permute-done | bytes 442400 | tf_op jit(solution)/shard_map/while/body/ppermute | solution.py:527
  10.6 2.9 %collective-permute-start.1 = (bf16[144,1536]{1,0:T(8,128)(2,1)S(1)}, bf16[144,1536]{1,0:T(8,128)(2,1)S(1)}, u32[]{:S(2)}, u32[]{:S(2)}) collective-permute-start(bf16[144,1536]{1,0:T(8,128)(2,1)S(1)} %pair_total.1.refs_2_), channel_id=1, source_target_pairs={{0,2},{1,3},{2,0},{3,1},{4,6},{5,7},{6,4},{7,5},{8,10},{9,11},{10,... | collective-permute-start | bytes 1327112 | tf_op jit(solution)/shard_map/while/body/ppermute | solution.py:527
  13.5 4.8 %gate.1.refs_0_ = bf16[256,1536]{1,0:T(8,128)(2,1)S(1)} custom-call(bf16[144,1536]{1,0:T(8,128)(2,1)S(1)} %copy.24.after, bf16[256,1536]{1,0:T(8,128)(2,1)} %get-tuple-element.322.normed, bf16[1536,3072]{1,0:T(8,128)(2,1)} %get-tuple-element.323.weight), custom_call_target="tpu_custom_call" | custom-call | flops 1 | bytes 1 | tf_op jit(solution)/shard_map/while/body/gate/pallas_call | solution.py:599
  18.3 4.8 %spatial_local.1 = (f32[256,1536]{1,0:T(8,128)}, f32[256,128]{1,0:T(8,128)S(1)}) custom-call(bf16[256,1536]{1,0:T(8,128)(2,1)S(1)} %gate.1.refs_0_, bf16[256,256]{1,0:T(8,128)(2,1)} %get-tuple-element.324.refs_1_, f32[256,128]{1,0:T(8,128)} %get-tuple-element.325.refs_2_, f32[16,128]{1,0:T(8,128)S(1)} %get-tuple-element.326.refs_3_, ...), custom_call_target="tpu_custom_call" | custom-call | flops 1 | bytes 1 | tf_op jit(solution)/shard_map/while/body/spatial_local/pallas_call | solution.py:610
  24.3 1.8 %collective-permute-start.2 = (bf16[144,1536]{1,0:T(8,128)(2,1)S(1)}, bf16[144,1536]{1,0:T(8,128)(2,1)S(1)}, u32[]{:S(2)}, u32[]{:S(2)}) collective-permute-start(bf16[144,1536]{1,0:T(8,128)(2,1)S(1)} %get-tuple-element.275.refs_2_), channel_id=1, source_target_pairs={{0,4},{1,5},{2,6},{3,7},{4,0},{5,1},{6,2},{7,3},{8,12},{9,13},{10,... | collective-permute-start | bytes 1327112 | tf_op jit(solution)/shard_map/while/body/ppermute | solution.py:527
  26.1 9.9 %collective-permute-done.2.refs_3_ = bf16[144,1536]{1,0:T(8,128)(2,1)S(1)} collective-permute-done((bf16[144,1536]{1,0:T(8,128)(2,1)S(1)}, bf16[144,1536]{1,0:T(8,128)(2,1)S(1)}, u32[]{:S(2)}, u32[]{:S(2)}) %collective-permute-start.2) | collective-permute-done | bytes 442400 | tf_op jit(solution)/shard_map/while/body/ppermute | solution.py:527
  36.0 1.1 %merge.3 = (bf16[128,1536]{1,0:T(8,128)(2,1)}, bf16[128,1536]{1,0:T(8,128)(2,1)}) custom-call(f32[256,128]{1,0:T(8,128)S(1)} %get-tuple-element.319.refs_0_, s32[1]{0:T(128)} %get-tuple-element.328.band.refs_1_, bf16[144,1536]{1,0:T(8,128)(2,1)S(1)} %get-tuple-element.275.refs_2_, bf16[144,1536]{1,0:T(8,128)(2,1)S(1)} %collective-permute-done.2.refs_3_, ...), custom_call_target="tpu_custom_call" | custom-call | flops 1 | bytes 1 | tf_op jit(solution)/shard_map/while/body/merge/pallas_call | solution.py:639
  37.3 1.6 %collective-permute-start.4 = (bf16[176,768]{1,0:T(8,128)(2,1)}, bf16[176,768]{1,0:T(8,128)(2,1)S(1)}, u32[]{:S(2)}, u32[]{:S(2)}) collective-permute-start(bf16[176,768]{1,0:T(8,128)(2,1)} %get-tuple-element.136), channel_id=1, source_target_pairs={{0,8},{8,0},{16,24},{24,16},{1,9},{9,1},{17,25},{25,17},{2,10},{10... | collective-permute-start | bytes 811016 | tf_op jit(solution)/shard_map/ppermute | solution.py:527
  38.8 2.6 %collective-permute-start.5 = (bf16[176,768]{1,0:T(8,128)(2,1)}, bf16[176,768]{1,0:T(8,128)(2,1)S(1)}, u32[]{:S(2)}, u32[]{:S(2)}) collective-permute-start(bf16[176,768]{1,0:T(8,128)(2,1)} %get-tuple-element.137), channel_id=1, source_target_pairs={{0,16},{8,24},{16,0},{24,8},{1,17},{9,25},{17,1},{25,9},{2,18},{10... | collective-permute-start | bytes 811016 | tf_op jit(solution)/shard_map/ppermute | solution.py:527
  41.7 10.0 %collective-permute-done.4.refs_3_ = bf16[176,768]{1,0:T(8,128)(2,1)S(1)} collective-permute-done((bf16[176,768]{1,0:T(8,128)(2,1)}, bf16[176,768]{1,0:T(8,128)(2,1)S(1)}, u32[]{:S(2)}, u32[]{:S(2)}) %collective-permute-start.4) | collective-permute-done | bytes 270368 | tf_op jit(solution)/shard_map/ppermute | solution.py:527
  51.7 9.2 %collective-permute-done.5.refs_4_ = bf16[176,768]{1,0:T(8,128)(2,1)S(1)} collective-permute-done((bf16[176,768]{1,0:T(8,128)(2,1)}, bf16[176,768]{1,0:T(8,128)(2,1)S(1)}, u32[]{:S(2)}, u32[]{:S(2)}) %collective-permute-start.5) | collective-permute-done | bytes 270368 | tf_op jit(solution)/shard_map/ppermute | solution.py:527
  60.9 2.4 %temporal.2 = (bf16[64,768]{1,0:T(8,128)(2,1)S(1)}, bf16[64,768]{1,0:T(8,128)(2,1)S(1)}, bf16[64,768]{1,0:T(8,128)(2,1)S(1)}, bf16[64,768]{1,0:T(8,128)(2,1)S(1)}, f32[128,768]{1,0:T(8,128)S(1)}) custom-call(s32[1]{0:T(128)} %bitcast.refs_0_, f32[16,128]{1,0:T(8,128)S(1)} %get-tuple-element.353, bf16[176,768]{1,0:T(8,128)(2,1)S(1)} %copy-done.1, ...), custom_call_target="tpu_custom_call" | custom-call | flops 1 | bytes 1 | tf_op jit(solution)/shard_map/temporal/pallas_call | solution.py:658
  63.3 5.6 %collective-permute-start.10 = (bf16[64,768]{1,0:T(8,128)(2,1)S(1)}, bf16[64,768]{1,0:T(8,128)(2,1)S(1)}, u32[]{:S(2)}, u32[]{:S(2)}) collective-permute-start(bf16[64,768]{1,0:T(8,128)(2,1)S(1)} %get-tuple-element.145), channel_id=1, source_target_pairs={{0,8},{8,0},{16,24},{24,16},{1,9},{9,1},{17,25},{25,17},{2,10},{10... | collective-permute-start | bytes 294920 | tf_op jit(solution)/shard_map/ppermute | solution.py:527
  68.9 1.1 %collective-permute-start.11 = (bf16[64,768]{1,0:T(8,128)(2,1)S(1)}, bf16[64,768]{1,0:T(8,128)(2,1)S(1)}, u32[]{:S(2)}, u32[]{:S(2)}) collective-permute-start(bf16[64,768]{1,0:T(8,128)(2,1)S(1)} %get-tuple-element.146), channel_id=1, source_target_pairs={{0,16},{8,24},{16,0},{24,8},{1,17},{9,25},{17,1},{25,9},{2,18},{10... | collective-permute-start | bytes 294920 | tf_op jit(solution)/shard_map/ppermute | solution.py:527
  70.0 1.4 %collective-permute-start.12 = (bf16[64,768]{1,0:T(8,128)(2,1)S(1)}, bf16[64,768]{1,0:T(8,128)(2,1)S(1)}, u32[]{:S(2)}, u32[]{:S(2)}) collective-permute-start(bf16[64,768]{1,0:T(8,128)(2,1)S(1)} %get-tuple-element.147), channel_id=1, source_target_pairs={{0,24},{8,16},{16,8},{24,0},{1,25},{9,17},{17,9},{25,1},{2,26},{10... | collective-permute-start | bytes 294920 | tf_op jit(solution)/shard_map/ppermute | solution.py:527
  71.4 2.2 %temporal.3 = (bf16[64,768]{1,0:T(8,128)(2,1)S(1)}, bf16[64,768]{1,0:T(8,128)(2,1)S(1)}, bf16[64,768]{1,0:T(8,128)(2,1)S(1)}, bf16[64,768]{1,0:T(8,128)(2,1)S(1)}) custom-call(s32[1]{0:T(128)} %bitcast.refs_0_, f32[16,128]{1,0:T(8,128)S(1)} %get-tuple-element.353, bf16[176,768]{1,0:T(8,128)(2,1)S(1)} %copy-done.1, ...), custom_call_target="tpu_custom_call" | custom-call | flops 1 | bytes 1 | tf_op jit(solution)/shard_map/temporal/pallas_call | solution.py:658
  74.7 2.0 %collective-permute-start.8 = (bf16[64,768]{1,0:T(8,128)(2,1)S(1)}, bf16[64,768]{1,0:T(8,128)(2,1)S(1)}, u32[]{:S(2)}, u32[]{:S(2)}) collective-permute-start(bf16[64,768]{1,0:T(8,128)(2,1)S(1)} %get-tuple-element.142), channel_id=1, source_target_pairs={{0,16},{8,24},{16,0},{24,8},{1,17},{9,25},{17,1},{25,9},{2,18},{10... | collective-permute-start | bytes 294920 | tf_op jit(solution)/shard_map/ppermute | solution.py:527
  76.7 1.4 %collective-permute-start.9 = (bf16[64,768]{1,0:T(8,128)(2,1)S(1)}, bf16[64,768]{1,0:T(8,128)(2,1)S(1)}, u32[]{:S(2)}, u32[]{:S(2)}) collective-permute-start(bf16[64,768]{1,0:T(8,128)(2,1)S(1)} %get-tuple-element.143), channel_id=1, source_target_pairs={{0,24},{8,16},{16,8},{24,0},{1,25},{9,17},{17,9},{25,1},{2,26},{10... | collective-permute-start | bytes 294920 | tf_op jit(solution)/shard_map/ppermute | solution.py:527
  78.1 2.2 %spatial_incoming.1.refs_1_ = f32[256,1536]{1,0:T(8,128)S(1)} custom-call(s32[1]{0:T(128)} %bitcast.1.refs_1_.band, f32[256,1536]{1,0:T(8,128)} %get-tuple-element.130.out_local, bf16[256,256]{1,0:T(8,128)(2,1)} %get-tuple-element.290.bc, f32[256,128]{1,0:T(8,128)S(1)} %copy-done.6, bf16[128,1536]{1,0:T(8,128)(2,1)S(1)} %copy-done.7, ...), custom_call_target="tpu_custom_call" | custom-call | flops 1 | bytes 1 | tf_op jit(solution)/shard_map/spatial_incoming/pallas_call | solution.py:685
  80.4 2.0 %exit.2.refs_9_ = bf16[2,2,64,1536]{3,2,1,0:T(8,128)(2,1)} custom-call(s32[1]{0:T(128)} %bitcast.refs_0_, f32[256,1536]{1,0:T(8,128)S(1)} %spatial_incoming.1.refs_1_, bf16[256,1536]{1,0:T(8,128)(2,1)S(1)} %copy-done.4, f32[1536]{0:T(1024)S(1)} %copy-done.2, bf16[1536,1536]{1,0:T(8,128)(2,1)S(1)} %copy-done, bf16[64,768]{1,0:T(8,128)(2,1)S(1)} %get-tuple-element.144.refs_5_, ...), custom_call_target="tpu_custom_call" | custom-call | flops 1 | bytes 1 | tf_op jit(solution)/shard_map/exit/pallas_call | solution.py:695
  82.4 4.9 %collective-permute-done.8.refs_7_ = bf16[64,768]{1,0:T(8,128)(2,1)S(1)} collective-permute-done((bf16[64,768]{1,0:T(8,128)(2,1)S(1)}, bf16[64,768]{1,0:T(8,128)(2,1)S(1)}, u32[]{:S(2)}, u32[]{:S(2)}) %collective-permute-start.8) | collective-permute-done | bytes 98336 | tf_op jit(solution)/shard_map/ppermute | solution.py:527
  87.3 2.0 %exit.3 = bf16[2,2,64,1536]{3,2,1,0:T(8,128)(2,1)} custom-call(s32[1]{0:T(128)} %bitcast.refs_0_, f32[256,1536]{1,0:T(8,128)S(1)} %spatial_incoming.1.refs_1_, bf16[256,1536]{1,0:T(8,128)(2,1)S(1)} %copy-done.4, f32[1536]{0:T(1024)S(1)} %copy-done.2, bf16[1536,1536]{1,0:T(8,128)(2,1)S(1)} %copy-done, ...), custom_call_target="tpu_custom_call", output_to_operand_aliasing={{}: (9, {})} | custom-call | flops 1 | bytes 1 | tf_op jit(solution)/shard_map/exit/pallas_call | solution.py:695
  (31 shorter events, 3.3 us)
Async XLA Ops:
  8.3 52.6 %copy-start.1 = (bf16[176,768]{1,0:T(8,128)(2,1)S(1)}, bf16[176,768]{1,0:T(8,128)(2,1)}, u32[]{:S(2)}) copy-start(bf16[176,768]{1,0:T(8,128)(2,1)} %get-tuple-element.135.refs_2_) | copy-start | bytes 811012
  8.5 1.9 %collective-permute-start = (bf16[144,1536]{1,0:T(8,128)(2,1)S(1)}, bf16[144,1536]{1,0:T(8,128)(2,1)S(1)}, u32[]{:S(2)}, u32[]{:S(2)}) collective-permute-start(bf16[144,1536]{1,0:T(8,128)(2,1)S(1)} %copy.24.after), channel_id=1, source_target_pairs={{0,1},{1,0},{2,3},{3,2},{4,5},{5,4},{6,7},{7,6},{8,9},{9,8},{10,11... | collective-permute-start | bytes 1327112 | tf_op jit(solution)/shard_map/while/body/ppermute | solution.py:527
  10.6 13.4 %collective-permute-start.1 = (bf16[144,1536]{1,0:T(8,128)(2,1)S(1)}, bf16[144,1536]{1,0:T(8,128)(2,1)S(1)}, u32[]{:S(2)}, u32[]{:S(2)}) collective-permute-start(bf16[144,1536]{1,0:T(8,128)(2,1)S(1)} %pair_total.1.refs_2_), channel_id=1, source_target_pairs={{0,2},{1,3},{2,0},{3,1},{4,6},{5,7},{6,4},{7,5},{8,10},{9,11},{10,... | collective-permute-start | bytes 1327112 | tf_op jit(solution)/shard_map/while/body/ppermute | solution.py:527
  18.3 5.7 %copy-start.3 = (bf16[256,1536]{1,0:T(8,128)(2,1)}, bf16[256,1536]{1,0:T(8,128)(2,1)S(1)}, u32[]{:S(2)}) copy-start(bf16[256,1536]{1,0:T(8,128)(2,1)S(1)} %gate.1.refs_0_) | copy-start | bytes 2359300 | tf_op jit(solution)/shard_map/while
  23.1 14.1 %copy-start.5 = (f32[256,128]{1,0:T(8,128)}, f32[256,128]{1,0:T(8,128)S(1)}, u32[]{:S(2)}) copy-start(f32[256,128]{1,0:T(8,128)S(1)} %get-tuple-element.319.refs_0_) | copy-start | bytes 393220 | tf_op jit(solution)/shard_map/while
  24.3 11.8 %collective-permute-start.2 = (bf16[144,1536]{1,0:T(8,128)(2,1)S(1)}, bf16[144,1536]{1,0:T(8,128)(2,1)S(1)}, u32[]{:S(2)}, u32[]{:S(2)}) collective-permute-start(bf16[144,1536]{1,0:T(8,128)(2,1)S(1)} %get-tuple-element.275.refs_2_), channel_id=1, source_target_pairs={{0,4},{1,5},{2,6},{3,7},{4,0},{5,1},{6,2},{7,3},{8,12},{9,13},{10,... | collective-permute-start | bytes 1327112 | tf_op jit(solution)/shard_map/while/body/ppermute | solution.py:527
  37.2 40.9 %copy-start.6 = (f32[256,128]{1,0:T(8,128)S(1)}, f32[256,128]{1,0:T(8,128)}, u32[]{:S(2)}) copy-start(f32[256,128]{1,0:T(8,128)} %get-tuple-element.131.reach.refs_6_.refs_7_) | copy-start | bytes 393220
  37.2 40.9 %copy-start.7 = (bf16[128,1536]{1,0:T(8,128)(2,1)S(1)}, bf16[128,1536]{1,0:T(8,128)(2,1)}, u32[]{:S(2)}) copy-start(bf16[128,1536]{1,0:T(8,128)(2,1)} %get-tuple-element.132.own) | copy-start | bytes 1179652
  37.2 39.5 %collective-permute-start.3 = (bf16[128,1536]{1,0:T(8,128)(2,1)}, bf16[128,1536]{1,0:T(8,128)(2,1)S(1)}, u32[]{:S(2)}, u32[]{:S(2)}) collective-permute-start(bf16[128,1536]{1,0:T(8,128)(2,1)} %get-tuple-element.133), channel_id=1, source_target_pairs={{0,1},{1,0},{2,3},{3,2},{4,5},{5,4},{6,7},{7,6},{8,9},{9,8},{10,11... | collective-permute-start | bytes 1179656 | tf_op jit(solution)/shard_map/ppermute | solution.py:527
  37.3 14.5 %collective-permute-start.4 = (bf16[176,768]{1,0:T(8,128)(2,1)}, bf16[176,768]{1,0:T(8,128)(2,1)S(1)}, u32[]{:S(2)}, u32[]{:S(2)}) collective-permute-start(bf16[176,768]{1,0:T(8,128)(2,1)} %get-tuple-element.136), channel_id=1, source_target_pairs={{0,8},{8,0},{16,24},{24,16},{1,9},{9,1},{17,25},{25,17},{2,10},{10... | collective-permute-start | bytes 811016 | tf_op jit(solution)/shard_map/ppermute | solution.py:527
  38.8 22.1 %collective-permute-start.5 = (bf16[176,768]{1,0:T(8,128)(2,1)}, bf16[176,768]{1,0:T(8,128)(2,1)S(1)}, u32[]{:S(2)}, u32[]{:S(2)}) collective-permute-start(bf16[176,768]{1,0:T(8,128)(2,1)} %get-tuple-element.137), channel_id=1, source_target_pairs={{0,16},{8,24},{16,0},{24,8},{1,17},{9,25},{17,1},{25,9},{2,18},{10... | collective-permute-start | bytes 811016 | tf_op jit(solution)/shard_map/ppermute | solution.py:527
  41.4 19.5 %collective-permute-start.6 = (bf16[176,768]{1,0:T(8,128)(2,1)}, bf16[176,768]{1,0:T(8,128)(2,1)S(1)}, u32[]{:S(2)}, u32[]{:S(2)}) collective-permute-start(bf16[176,768]{1,0:T(8,128)(2,1)} %get-tuple-element.138), channel_id=1, source_target_pairs={{0,24},{8,16},{16,8},{24,0},{1,25},{9,17},{17,9},{25,1},{2,26},{10... | collective-permute-start | bytes 811016 | tf_op jit(solution)/shard_map/ppermute | solution.py:527
  63.3 11.4 %collective-permute-start.10 = (bf16[64,768]{1,0:T(8,128)(2,1)S(1)}, bf16[64,768]{1,0:T(8,128)(2,1)S(1)}, u32[]{:S(2)}, u32[]{:S(2)}) collective-permute-start(bf16[64,768]{1,0:T(8,128)(2,1)S(1)} %get-tuple-element.145), channel_id=1, source_target_pairs={{0,8},{8,0},{16,24},{24,16},{1,9},{9,1},{17,25},{25,17},{2,10},{10... | collective-permute-start | bytes 294920 | tf_op jit(solution)/shard_map/ppermute | solution.py:527
  68.9 11.4 %collective-permute-start.11 = (bf16[64,768]{1,0:T(8,128)(2,1)S(1)}, bf16[64,768]{1,0:T(8,128)(2,1)S(1)}, u32[]{:S(2)}, u32[]{:S(2)}) collective-permute-start(bf16[64,768]{1,0:T(8,128)(2,1)S(1)} %get-tuple-element.146), channel_id=1, source_target_pairs={{0,16},{8,24},{16,0},{24,8},{1,17},{9,25},{17,1},{25,9},{2,18},{10... | collective-permute-start | bytes 294920 | tf_op jit(solution)/shard_map/ppermute | solution.py:527
  70.0 10.3 %collective-permute-start.12 = (bf16[64,768]{1,0:T(8,128)(2,1)S(1)}, bf16[64,768]{1,0:T(8,128)(2,1)S(1)}, u32[]{:S(2)}, u32[]{:S(2)}) collective-permute-start(bf16[64,768]{1,0:T(8,128)(2,1)S(1)} %get-tuple-element.147), channel_id=1, source_target_pairs={{0,24},{8,16},{16,8},{24,0},{1,25},{9,17},{17,9},{25,1},{2,26},{10... | collective-permute-start | bytes 294920 | tf_op jit(solution)/shard_map/ppermute | solution.py:527
  71.4 9.0 %copy-start = (bf16[1536,1536]{1,0:T(8,128)(2,1)S(1)}, bf16[1536,1536]{1,0:T(8,128)(2,1)}, u32[]{:S(2)}) copy-start(bf16[1536,1536]{1,0:T(8,128)(2,1)} %refs_4_.5) | copy-start | bytes 14155780
  73.6 8.8 %collective-permute-start.7 = (bf16[64,768]{1,0:T(8,128)(2,1)S(1)}, bf16[64,768]{1,0:T(8,128)(2,1)S(1)}, u32[]{:S(2)}, u32[]{:S(2)}) collective-permute-start(bf16[64,768]{1,0:T(8,128)(2,1)S(1)} %get-tuple-element.141), channel_id=1, source_target_pairs={{0,8},{8,0},{16,24},{24,16},{1,9},{9,1},{17,25},{25,17},{2,10},{10... | collective-permute-start | bytes 294920 | tf_op jit(solution)/shard_map/ppermute | solution.py:527
  74.7 12.6 %collective-permute-start.8 = (bf16[64,768]{1,0:T(8,128)(2,1)S(1)}, bf16[64,768]{1,0:T(8,128)(2,1)S(1)}, u32[]{:S(2)}, u32[]{:S(2)}) collective-permute-start(bf16[64,768]{1,0:T(8,128)(2,1)S(1)} %get-tuple-element.142), channel_id=1, source_target_pairs={{0,16},{8,24},{16,0},{24,8},{1,17},{9,25},{17,1},{25,9},{2,18},{10... | collective-permute-start | bytes 294920 | tf_op jit(solution)/shard_map/ppermute | solution.py:527
  76.7 10.6 %collective-permute-start.9 = (bf16[64,768]{1,0:T(8,128)(2,1)S(1)}, bf16[64,768]{1,0:T(8,128)(2,1)S(1)}, u32[]{:S(2)}, u32[]{:S(2)}) collective-permute-start(bf16[64,768]{1,0:T(8,128)(2,1)S(1)} %get-tuple-element.143), channel_id=1, source_target_pairs={{0,24},{8,16},{16,8},{24,0},{1,25},{9,17},{17,9},{25,1},{2,26},{10... | collective-permute-start | bytes 294920 | tf_op jit(solution)/shard_map/ppermute | solution.py:527
  78.1 2.3 %copy-start.2 = (f32[1536]{0:T(1024)S(1)}, f32[1536]{0:T(1024)}, u32[]{:S(2)}) copy-start(f32[1536]{0:T(1024)} %refs_3_.5) | copy-start | bytes 18436
  78.1 2.3 %copy-start.4 = (bf16[256,1536]{1,0:T(8,128)(2,1)S(1)}, bf16[256,1536]{1,0:T(8,128)(2,1)}, u32[]{:S(2)}) copy-start(bf16[256,1536]{1,0:T(8,128)(2,1)} %get-tuple-element.134.refs_2_) | copy-start | bytes 2359300

commit v3 on v1

--- a/solution.py
+++ b/solution.py
@@ -11,6 +11,7 @@
 EPSILON = 1e-05
 LANES = 128
 TAIL = 16
+LOG2_E = 1.4426950408889634
 F32 = jnp.float32
 BF16 = jnp.bfloat16
 EXACT = lax.Precision.HIGHEST
@@ -72,11 +73,12 @@
 
 def head_mixes(scores, running, running_t, dt_t, x, first_head, heads, head_dim):
     length = scores.shape[0]
+    running, running_t = running * LOG2_E, running_t * LOG2_E
     outs = []
 
     def weights(head):
         spreads = running[:, head : head + 1] - running_t[head : head + 1, :]
-        return (scores * jnp.exp(jnp.minimum(spreads, 0.0)) * dt_t[head : head + 1, :]).astype(BF16)
+        return (scores * jnp.exp2(jnp.minimum(spreads, 0.0)) * dt_t[head : head + 1, :]).astype(BF16)
 
     head = 0
     while head < heads:
@@ -178,10 +180,12 @@
     outgoing = [pltpu.make_async_copy(normed, normed_out, out_sems.at[0])]
     outgoing[0].start()
     dt_copy.wait()
+    bc_copy.wait()
+    for copy in copies:
+        copy.wait()
     logits[:, : 2 * heads] = dot_nt(normed[...], dt_held[...]).astype(BF16).astype(F32)
     dt_heads = dot_nt(dt_held[heads:, :], normed[...])
     dt_heads = jnp.concatenate([dt_heads, jnp.zeros((TAIL, count), F32)], axis=0).astype(BF16)
-    bc_copy.wait()
     bc = dot(normed[...], bc_held[...]).astype(BF16)
     bc_own[...] = bc[:, : 2 * state]
     scan = [
@@ -189,30 +193,29 @@
         for frame in range(frames)
     ]
 
-    block = held_weight.shape[1] // blocks
-    for index, copy in enumerate(copies):
-        copy.wait()
-        at = index * block
-        values = dot(normed[...], held_weight[:, at : at + block]).astype(BF16)
-        for inside in range(0, block, group):
-            part = (at + inside) // group
+    block = 2 * LANES if group % (2 * LANES) == 0 else group
+    for part in range(groups):
+        for at in range(0, group, block):
+            from_col = part * group + at
+            values = dot(normed[...], held_weight[:, from_col : from_col + block]).astype(BF16)
             for row in range(rows):
-                piece = part * rows + row
-                here = slice(row * length, (row + 1) * length)
-                payload[piece, :length, :] = values[here, inside : inside + group]
-                pack_rest(
-                    payload.at[piece],
-                    length,
-                    bc[here, 2 * state : 3 * state],
-                    bc[here, 3 * state :],
-                    dt_heads[part * per_group : part * per_group + TAIL, here],
-                )
-                outgoing.append(
-                    pltpu.make_async_copy(
-                        payload.at[piece], payload_out.at[piece], out_sems.at[1 + piece]
-                    )
-                )
-                outgoing[-1].start()
+                payload[part * rows + row, :length, at : at + block] = values[
+                    row * length : (row + 1) * length
+                ]
+        for row in range(rows):
+            piece = part * rows + row
+            here = slice(row * length, (row + 1) * length)
+            pack_rest(
+                payload.at[piece],
+                length,
+                bc[here, 2 * state : 3 * state],
+                bc[here, 3 * state :],
+                dt_heads[part * per_group : part * per_group + TAIL, here],
+            )
+            outgoing.append(
+                pltpu.make_async_copy(payload.at[piece], payload_out.at[piece], out_sems.at[1 + piece])
+            )
+            outgoing[-1].start()
     half = state // 2
     head_dim = groups * group // heads
     mine = band[0] % 2 == 0
@@ -373,7 +376,11 @@
         before_out[frames * rows :, :] = jnp.where(upper, before_decay * far_decay, before_decay)
 
 
-def incoming_kernel(frames, rows, columns, head_dim, band, out_local, bc, reach, own, other, out):
+def incoming_kernel(
+    frames, rows, columns, head_dim, band, out_local, bc, reach, own, other, weight, out, held, sem
+):
+    fetch = pltpu.make_async_copy(weight, held, sem)
+    fetch.start()
     state = bc.shape[1] // 2
     half = state // 2
     inner = out.shape[1]
@@ -389,6 +396,7 @@
             here = slice(to, to + columns)
             factor = spread(reach[here, :], matrix)
             out[here, :] = out_local[here, :] + factor * dot(bc[here, state:], carried)
+    fetch.wait()
 
 
 def temporal_kernel(
@@ -457,7 +465,7 @@
         last = jnp.min(running, axis=0, keepdims=True)
         mixed = head_mixes(scores, running, running_t, dt_t, values, 0, per_group, head_dim)
         ends = jnp.concatenate([running, jnp.broadcast_to(last, (8, LANES))], axis=0)
-        reach = spread(jnp.exp(ends), matrix)
+        reach = dot(jnp.exp(ends).astype(BF16), matrix)
         mixed = mixed + reach[:size] * dot(c_proj, carried.astype(BF16))
         to_end = (jnp.exp(last - running) * dt).astype(BF16)
         scaled = (values.astype(F32) * dot(to_end, matrix)).astype(BF16)
@@ -661,12 +669,13 @@
     keep, give = results
     came = swapped(give, "height", 1)
 
-    spatial_out = call(
+    spatial_out, held_weight = call(
         functools.partial(incoming_kernel, frames, rows, columns, head_dim),
         "spatial_incoming",
-        shape_of((count, inner), F32),
-        [SCALAR] + [WHOLE] * 5,
-    )(band, out_local, bc_own, reach, keep, came)
+        [shape_of((count, inner), F32), shape_of((inner, width), BF16)],
+        [SCALAR] + [WHOLE] * 5 + [HBM],
+        scratch_shapes=[pltpu.SemaphoreType.DMA],
+    )(band, out_local, bc_own, reach, keep, came, out_weight)
 
     mixed = []
     for part in range(parts):
@@ -684,7 +693,7 @@
                     pltpu.SemaphoreType.DMA((rows * frames,)),
                 ],
                 input_output_aliases={5 + shares: 0} if mixed else {},
-            )(here, spatial_out, gate, out_gain, out_weight, *returned[part], *mixed)
+            )(here, spatial_out, gate, out_gain, held_weight, *returned[part], *mixed)
         ]
     return mixed[0]
 

time: 65.2 us -> 66.3 us (1.017)
  Pallas kernels: 22.6 us -> 23.9 us
    pallas_call x1, Pallas kernels: 7.42 us -> 8.65 us  [per_device(): call(functools.partial(entry_kernel, shares, heads, state, blocks), 'entr...]
where the time goes in v3:
time: 66.3 us; the launch traced here: 66 us
  Pallas kernels  23.9 us (36%)
  starting transfers between devices  18.6 us (28%)
  waiting for transfers between devices  14.5 us (22%)
  local copies, waits for them, and re-layouts  8.65 us (13%)
    ppermute x10, waiting for transfers between devices, swapped(): lax.ppermute(value, axis, [(source, source ^ distance) for source in rang...  12.7 us
    ppermute x10, starting transfers between devices, swapped(): lax.ppermute(value, axis, [(source, source ^ distance) for source in rang...  12.5 us
    pallas_call x1, Pallas kernels, per_device(): call(functools.partial(entry_kernel, shares, heads, state, blocks), 'entr...  8.65 us
    unnamed x28, local copies, waits for them, and re-layouts  8.65 us
    all_to_all x1, starting transfers between devices, per_device(): lax.all_to_all(payload, 'tm', split_axis=0, concat_axis=0, tiled=True)  6.03 us
    pallas_call x2, Pallas kernels, per_device(): call(functools.partial(temporal_kernel, part, parts, per_group, head_dim,...  4.35 us
    pallas_call x2, Pallas kernels, per_device(): call(functools.partial(exit_kernel, part, parts, shares), 'exit', shape_o...  3.93 us
    pallas_call x1, Pallas kernels, per_device(): call(functools.partial(gate_kernel, blocks), 'gate', shape_of((count, inn...  2.6 us
  transfers between devices with their start and end apart: 11, of which 4 were waited for; matrix products, arithmetic and copies ran while one was open for 0% of the time, Pallas kernels for 20%

profile of v3, /device:TPU:0, one launch (start us, length us, event | category | flops | bytes accessed | tf_op | source)
XLA Modules:
  0.0 66.0 jit_solution(14091933863751428217)
XLA Ops:
  0.0 8.7 %entry.1 = (bf16[256,1536]{1,0:T(8,128)(2,1)}, bf16[4,176,768]{2,1,0:T(8,128)(2,1)}, bf16[256,256]{1,0:T(8,128)(2,1)}, f32[256,128]{1,0:T(8,128)}, f32[16,128]{1...) custom-call(s32[1]{0:T(128)} %bitcast.refs_0_, s32[1]{0:T(128)} %bitcast.1.refs_1_.band, ...), custom_call_target="tpu_custom_call" | custom-call | flops 1 | bytes 1 | tf_op jit(solution)/shard_map/entry/pallas_call | solution.py:560
  9.2 6.0 %all-to-all-start = ((bf16[4,176,768]{2,1,0:T(8,128)(2,1)}), bf16[4,176,768]{2,1,0:T(8,128)(2,1)S(1)}, u32[]{:S(2)}, u32[]{:S(2)}) async-start(bf16[4,176,768]{2,1,0:T(8,128)(2,1)} %get-tuple-element.29.after.refs_4_), calls=%async_computation | async-start | bytes 2162688 | tf_op jit(solution)/shard_map/all_to_all | solution.py:590
  15.4 1.6 %collective-permute-start.1 = (bf16[144,1536]{1,0:T(8,128)(2,1)S(1)}, bf16[144,1536]{1,0:T(8,128)(2,1)S(1)}, u32[]{:S(2)}, u32[]{:S(2)}) collective-permute-start(bf16[144,1536]{1,0:T(8,128)(2,1)S(1)} %pair_total.1.refs_2_), channel_id=1, source_target_pairs={{0,2},{1,3},{2,0},{3,1},{4,6},{5,7},{6,4},{7,5},{8,10},{9,11},{10,... | collective-permute-start | bytes 1327112 | tf_op jit(solution)/shard_map/ppermute | solution.py:534
  17.0 3.7 %copy-done = bf16[1536,3072]{1,0:T(8,128)(2,1)S(1)} copy-done((bf16[1536,3072]{1,0:T(8,128)(2,1)S(1)}, bf16[1536,3072]{1,0:T(8,128)(2,1)}, u32[]{:S(2)}) %copy-start) | copy-done | bytes 9437208
  20.7 2.6 %gate.1.refs_0_.refs_2_ = bf16[256,1536]{1,0:T(8,128)(2,1)S(1)} custom-call(bf16[4,176,768]{2,1,0:T(8,128)(2,1)S(1)} %copy-done.1, bf16[256,1536]{1,0:T(8,128)(2,1)S(1)} %copy-done.8, bf16[1536,3072]{1,0:T(8,128)(2,1)S(1)} %copy-done), custom_call_target="tpu_custom_call" | custom-call | flops 1 | bytes 1 | tf_op jit(solution)/shard_map/gate/pallas_call | solution.py:592
  23.3 1.9 %spatial_local.1 = (f32[256,1536]{1,0:T(8,128)S(1)}, f32[256,128]{1,0:T(8,128)S(1)}) custom-call(bf16[256,1536]{1,0:T(8,128)(2,1)S(1)} %gate.1.refs_0_.refs_2_, bf16[256,256]{1,0:T(8,128)(2,1)S(1)} %copy-done.9, f32[256,128]{1,0:T(8,128)S(1)} %copy-done.11, f32[16,128]{1,0:T(8,128)S(1)} %copy-done.12, bf16[4,176,768]{2,1,0:T(8,128)(2,1)S(1)} %copy-done.1), custom_call_target="tpu_custom_call" | custom-call | flops 1 | bytes 1 | tf_op jit(solution)/shard_map/spatial_local/pallas_call | solution.py:603
  25.3 1.2 %copy-done.6 = f32[256,1536]{1,0:T(8,128)} copy-done((f32[256,1536]{1,0:T(8,128)}, f32[256,1536]{1,0:T(8,128)S(1)}, u32[]{:S(2)}) %copy-start.6) | copy-done | bytes 1572888
  26.4 1.3 %collective-permute-done.1.refs_3_ = bf16[144,1536]{1,0:T(8,128)(2,1)S(1)} collective-permute-done((bf16[144,1536]{1,0:T(8,128)(2,1)S(1)}, bf16[144,1536]{1,0:T(8,128)(2,1)S(1)}, u32[]{:S(2)}, u32[]{:S(2)}) %collective-permute-start.1) | collective-permute-done | bytes 442400 | tf_op jit(solution)/shard_map/ppermute | solution.py:534
  28.0 1.6 %collective-permute-start.2 = (bf16[144,1536]{1,0:T(8,128)(2,1)S(1)}, bf16[144,1536]{1,0:T(8,128)(2,1)S(1)}, u32[]{:S(2)}, u32[]{:S(2)}) collective-permute-start(bf16[144,1536]{1,0:T(8,128)(2,1)S(1)} %get-tuple-element.38.refs_2_), channel_id=1, source_target_pairs={{0,4},{1,5},{2,6},{3,7},{4,0},{5,1},{6,2},{7,3},{8,12},{9,13},{10,... | collective-permute-start | bytes 1327112 | tf_op jit(solution)/shard_map/ppermute | solution.py:534
  29.6 9.9 %collective-permute-done.2.refs_3_ = bf16[144,1536]{1,0:T(8,128)(2,1)S(1)} collective-permute-done((bf16[144,1536]{1,0:T(8,128)(2,1)S(1)}, bf16[144,1536]{1,0:T(8,128)(2,1)S(1)}, u32[]{:S(2)}, u32[]{:S(2)}) %collective-permute-start.2) | collective-permute-done | bytes 442400 | tf_op jit(solution)/shard_map/ppermute | solution.py:534
  39.5 1.0 %merge.3 = (bf16[128,1536]{1,0:T(8,128)(2,1)S(1)}, bf16[128,1536]{1,0:T(8,128)(2,1)}) custom-call(f32[256,128]{1,0:T(8,128)S(1)} %get-tuple-element.35.refs_0_.reach, s32[1]{0:T(128)} %bitcast.1.refs_1_.band, bf16[144,1536]{1,0:T(8,128)(2,1)S(1)} %get-tuple-element.38.refs_2_, bf16[144,1536]{1,0:T(8,128)(2,1)S(1)} %collective-permute-done.2.refs_3_, ...), custom_call_target="tpu_custom_call" | custom-call | flops 1 | bytes 1 | tf_op jit(solution)/shard_map/merge/pallas_call | solution.py:660
  40.5 1.7 %all-to-all-done.refs_2_ = bf16[4,176,768]{2,1,0:T(8,128)(2,1)S(1)} async-done(((bf16[4,176,768]{2,1,0:T(8,128)(2,1)}), bf16[4,176,768]{2,1,0:T(8,128)(2,1)S(1)}, u32[]{:S(2)}, u32[]{:S(2)}) %all-to-all-start) | async-done | bytes 1081376 | tf_op jit(solution)/shard_map/all_to_all | solution.py:590
  42.3 2.3 %temporal.2 = (bf16[64,768]{1,0:T(8,128)(2,1)S(1)}, bf16[64,768]{1,0:T(8,128)(2,1)S(1)}, bf16[64,768]{1,0:T(8,128)(2,1)S(1)}, bf16[64,768]{1,0:T(8,128)(2,1)S(1)}, f32[128,768]{1,0:T(8,128)S(1)}) custom-call(s32[1]{0:T(128)} %bitcast.refs_0_, f32[16,128]{1,0:T(8,128)S(1)} %copy-done.12, bf16[4,176,768]{2,1,0:T(8,128)(2,1)S(1)} %all-to-all-done.refs_2_), custom_call_target="tpu_custom_call" | custom-call | flops 1 | bytes 1 | tf_op jit(solution)/shard_map/temporal/pallas_call | solution.py:619
  44.6 2.0 %collective-permute-start.8 = (bf16[64,768]{1,0:T(8,128)(2,1)S(1)}, bf16[64,768]{1,0:T(8,128)(2,1)S(1)}, u32[]{:S(2)}, u32[]{:S(2)}) collective-permute-start(bf16[64,768]{1,0:T(8,128)(2,1)S(1)} %get-tuple-element.51), channel_id=1, source_target_pairs={{0,16},{8,24},{16,0},{24,8},{1,17},{9,25},{17,1},{25,9},{2,18},{10... | collective-permute-start | bytes 294920 | tf_op jit(solution)/shard_map/ppermute | solution.py:534
  46.7 2.3 %collective-permute-start.9 = (bf16[64,768]{1,0:T(8,128)(2,1)S(1)}, bf16[64,768]{1,0:T(8,128)(2,1)S(1)}, u32[]{:S(2)}, u32[]{:S(2)}) collective-permute-start(bf16[64,768]{1,0:T(8,128)(2,1)S(1)} %get-tuple-element.52), channel_id=1, source_target_pairs={{0,24},{8,16},{16,8},{24,0},{1,25},{9,17},{17,9},{25,1},{2,26},{10... | collective-permute-start | bytes 294920 | tf_op jit(solution)/shard_map/ppermute | solution.py:534
  49.0 2.1 %temporal.3 = (bf16[64,768]{1,0:T(8,128)(2,1)S(1)}, bf16[64,768]{1,0:T(8,128)(2,1)S(1)}, bf16[64,768]{1,0:T(8,128)(2,1)S(1)}, bf16[64,768]{1,0:T(8,128)(2,1)S(1)}) custom-call(s32[1]{0:T(128)} %bitcast.refs_0_, f32[16,128]{1,0:T(8,128)S(1)} %copy-done.12, bf16[4,176,768]{2,1,0:T(8,128)(2,1)S(1)} %all-to-all-done.refs_2_, ...), custom_call_target="tpu_custom_call" | custom-call | flops 1 | bytes 1 | tf_op jit(solution)/shard_map/temporal/pallas_call | solution.py:619
  51.2 2.0 %collective-permute-start.5 = (bf16[64,768]{1,0:T(8,128)(2,1)S(1)}, bf16[64,768]{1,0:T(8,128)(2,1)S(1)}, u32[]{:S(2)}, u32[]{:S(2)}) collective-permute-start(bf16[64,768]{1,0:T(8,128)(2,1)S(1)} %get-tuple-element.47), channel_id=1, source_target_pairs={{0,16},{8,24},{16,0},{24,8},{1,17},{9,25},{17,1},{25,9},{2,18},{10... | collective-permute-start | bytes 294920 | tf_op jit(solution)/shard_map/ppermute | solution.py:534
  53.2 2.3 %collective-permute-start.6 = (bf16[64,768]{1,0:T(8,128)(2,1)S(1)}, bf16[64,768]{1,0:T(8,128)(2,1)S(1)}, u32[]{:S(2)}, u32[]{:S(2)}) collective-permute-start(bf16[64,768]{1,0:T(8,128)(2,1)S(1)} %get-tuple-element.48), channel_id=1, source_target_pairs={{0,24},{8,16},{16,8},{24,0},{1,25},{9,17},{17,9},{25,1},{2,26},{10... | collective-permute-start | bytes 294920 | tf_op jit(solution)/shard_map/ppermute | solution.py:534
  55.6 2.3 %copy-done.2 = bf16[1536,1536]{1,0:T(8,128)(2,1)S(1)} copy-done((bf16[1536,1536]{1,0:T(8,128)(2,1)S(1)}, bf16[1536,1536]{1,0:T(8,128)(2,1)}, u32[]{:S(2)}) %copy-start.2) | copy-done | bytes 4718616
  57.9 1.4 %copy-done.7 = f32[256,1536]{1,0:T(8,128)S(1)} copy-done((f32[256,1536]{1,0:T(8,128)S(1)}, f32[256,1536]{1,0:T(8,128)}, u32[]{:S(2)}) %copy-start.7) | copy-done | bytes 1572888
  59.3 1.1 %spatial_incoming.1 = (f32[256,1536]{1,0:T(8,128)S(1)}, bf16[1536,1536]{1,0:T(8,128)(2,1)S(1)}) custom-call(s32[1]{0:T(128)} %bitcast.1.refs_1_.band, f32[256,1536]{1,0:T(8,128)S(1)} %copy-done.7, bf16[256,256]{1,0:T(8,128)(2,1)S(1)} %copy-done.10, f32[256,128]{1,0:T(8,128)S(1)} %get-tuple-element.35.refs_0_.reach, ...), custom_call_target="tpu_custom_call" | custom-call | flops 1 | bytes 1 | tf_op jit(solution)/shard_map/spatial_incoming/pallas_call | solution.py:672
  60.4 2.0 %exit.2.refs_9_ = bf16[2,2,64,1536]{3,2,1,0:T(8,128)(2,1)} custom-call(s32[1]{0:T(128)} %bitcast.refs_0_, f32[256,1536]{1,0:T(8,128)S(1)} %get-tuple-element.42.refs_1_, bf16[256,1536]{1,0:T(8,128)(2,1)S(1)} %gate.1.refs_0_.refs_2_, f32[1536]{0:T(1024)S(1)} %copy-done.13, bf16[1536,1536]{1,0:T(8,128)(2,1)S(1)} %get-tuple-element.43.refs_4_, ...), custom_call_target="tpu_custom_call" | custom-call | flops 1 | bytes 1 | tf_op jit(solution)/shard_map/exit/pallas_call | solution.py:683
  62.4 1.4 %collective-permute-done.5.refs_7_ = bf16[64,768]{1,0:T(8,128)(2,1)S(1)} collective-permute-done((bf16[64,768]{1,0:T(8,128)(2,1)S(1)}, bf16[64,768]{1,0:T(8,128)(2,1)S(1)}, u32[]{:S(2)}, u32[]{:S(2)}) %collective-permute-start.5) | collective-permute-done | bytes 98336 | tf_op jit(solution)/shard_map/ppermute | solution.py:534
  63.9 2.0 %exit.3 = bf16[2,2,64,1536]{3,2,1,0:T(8,128)(2,1)} custom-call(s32[1]{0:T(128)} %bitcast.refs_0_, f32[256,1536]{1,0:T(8,128)S(1)} %get-tuple-element.42.refs_1_, bf16[256,1536]{1,0:T(8,128)(2,1)S(1)} %gate.1.refs_0_.refs_2_, f32[1536]{0:T(1024)S(1)} %copy-done.13, bf16[1536,1536]{1,0:T(8,128)(2,1)S(1)} %get-tuple-element.43.refs_4_, ...), custom_call_target="tpu_custom_call", output_to_operand_aliasing={{}: (9, {})} | custom-call | flops 1 | bytes 1 | tf_op jit(solution)/shard_map/exit/pallas_call | solution.py:683
  (37 shorter events, 1.1 us)
Async XLA Ops:
  8.7 6.6 %copy-start.3 = (bf16[144,1536]{1,0:T(8,128)(2,1)S(1)}, bf16[144,1536]{1,0:T(8,128)(2,1)}, u32[]{:S(2)}) copy-start(bf16[144,1536]{1,0:T(8,128)(2,1)} %get-tuple-element.36.own.refs_5_) | copy-start | bytes 1327108
  8.7 6.6 %collective-permute-start = (bf16[144,1536]{1,0:T(8,128)(2,1)}, bf16[144,1536]{1,0:T(8,128)(2,1)S(1)}, u32[]{:S(2)}, u32[]{:S(2)}) collective-permute-start(bf16[144,1536]{1,0:T(8,128)(2,1)} %get-tuple-element.37), channel_id=1, source_target_pairs={{0,1},{1,0},{2,3},{3,2},{4,5},{5,4},{6,7},{7,6},{8,9},{9,8},{10,11... | collective-permute-start | bytes 1327112 | tf_op jit(solution)/shard_map/ppermute | solution.py:534
  9.2 7.8 %copy-start.1 = (bf16[4,176,768]{2,1,0:T(8,128)(2,1)S(1)}, bf16[4,176,768]{2,1,0:T(8,128)(2,1)}, u32[]{:S(2)}) copy-start(bf16[4,176,768]{2,1,0:T(8,128)(2,1)} %get-tuple-element.29.after.refs_4_) | copy-start | bytes 3244036
  9.2 33.1 %all-to-all-start = ((bf16[4,176,768]{2,1,0:T(8,128)(2,1)}), bf16[4,176,768]{2,1,0:T(8,128)(2,1)S(1)}, u32[]{:S(2)}, u32[]{:S(2)}) async-start(bf16[4,176,768]{2,1,0:T(8,128)(2,1)} %get-tuple-element.29.after.refs_4_), calls=%async_computation | async-start | bytes 2162688 | tf_op jit(solution)/shard_map/all_to_all | solution.py:590
  15.2 1.8 %copy-start.8 = (bf16[256,1536]{1,0:T(8,128)(2,1)S(1)}, bf16[256,1536]{1,0:T(8,128)(2,1)}, u32[]{:S(2)}) copy-start(bf16[256,1536]{1,0:T(8,128)(2,1)} %get-tuple-element.30.normed) | copy-start | bytes 2359300
  15.2 1.8 %copy-start.4 = (bf16[144,1536]{1,0:T(8,128)(2,1)}, bf16[144,1536]{1,0:T(8,128)(2,1)S(1)}, u32[]{:S(2)}) copy-start(bf16[144,1536]{1,0:T(8,128)(2,1)S(1)} %collective-permute-done.far.refs_6_) | copy-start | bytes 1327108
  15.4 12.3 %collective-permute-start.1 = (bf16[144,1536]{1,0:T(8,128)(2,1)S(1)}, bf16[144,1536]{1,0:T(8,128)(2,1)S(1)}, u32[]{:S(2)}, u32[]{:S(2)}) collective-permute-start(bf16[144,1536]{1,0:T(8,128)(2,1)S(1)} %pair_total.1.refs_2_), channel_id=1, source_target_pairs={{0,2},{1,3},{2,0},{3,1},{4,6},{5,7},{6,4},{7,5},{8,10},{9,11},{10,... | collective-permute-start | bytes 1327112 | tf_op jit(solution)/shard_map/ppermute | solution.py:534
  17.0 3.7 %copy-start = (bf16[1536,3072]{1,0:T(8,128)(2,1)S(1)}, bf16[1536,3072]{1,0:T(8,128)(2,1)}, u32[]{:S(2)}) copy-start(bf16[1536,3072]{1,0:T(8,128)(2,1)} %weight.2) | copy-start | bytes 28311556
  20.7 2.6 %copy-start.9 = (bf16[256,256]{1,0:T(8,128)(2,1)S(1)}, bf16[256,256]{1,0:T(8,128)(2,1)}, u32[]{:S(2)}) copy-start(bf16[256,256]{1,0:T(8,128)(2,1)} %get-tuple-element.31.refs_1_.bc) | copy-start | bytes 393220
  20.7 2.6 %copy-start.11 = (f32[256,128]{1,0:T(8,128)S(1)}, f32[256,128]{1,0:T(8,128)}, u32[]{:S(2)}) copy-start(f32[256,128]{1,0:T(8,128)} %get-tuple-element.32.refs_2_) | copy-start | bytes 393220
  20.7 2.6 %copy-start.12 = (f32[16,128]{1,0:T(8,128)S(1)}, f32[16,128]{1,0:T(8,128)}, u32[]{:S(2)}) copy-start(f32[16,128]{1,0:T(8,128)} %get-tuple-element.33.refs_3_.refs_1_) | copy-start | bytes 24580
  23.3 16.2 %copy-start.5 = (bf16[144,1536]{1,0:T(8,128)(2,1)S(1)}, bf16[144,1536]{1,0:T(8,128)(2,1)}, u32[]{:S(2)}) copy-start(bf16[144,1536]{1,0:T(8,128)(2,1)} %copy-done.4) | copy-start | bytes 1327108
  25.2 1.2 %copy-start.6 = (f32[256,1536]{1,0:T(8,128)}, f32[256,1536]{1,0:T(8,128)S(1)}, u32[]{:S(2)}) copy-start(f32[256,1536]{1,0:T(8,128)S(1)} %get-tuple-element.34.out_local) | copy-start | bytes 4718596
  28.0 11.5 %collective-permute-start.2 = (bf16[144,1536]{1,0:T(8,128)(2,1)S(1)}, bf16[144,1536]{1,0:T(8,128)(2,1)S(1)}, u32[]{:S(2)}, u32[]{:S(2)}) collective-permute-start(bf16[144,1536]{1,0:T(8,128)(2,1)S(1)} %get-tuple-element.38.refs_2_), channel_id=1, source_target_pairs={{0,4},{1,5},{2,6},{3,7},{4,0},{5,1},{6,2},{7,3},{8,12},{9,13},{10,... | collective-permute-start | bytes 1327112 | tf_op jit(solution)/shard_map/ppermute | solution.py:534
  40.5 15.0 %copy-start.10 = (bf16[256,256]{1,0:T(8,128)(2,1)S(1)}, bf16[256,256]{1,0:T(8,128)(2,1)}, u32[]{:S(2)}) copy-start(bf16[256,256]{1,0:T(8,128)(2,1)} %get-tuple-element.31.refs_1_.bc) | copy-start | bytes 393220
  40.5 12.7 %collective-permute-start.3 = (bf16[128,1536]{1,0:T(8,128)(2,1)}, bf16[128,1536]{1,0:T(8,128)(2,1)S(1)}, u32[]{:S(2)}, u32[]{:S(2)}) collective-permute-start(bf16[128,1536]{1,0:T(8,128)(2,1)} %get-tuple-element.41), channel_id=1, source_target_pairs={{0,1},{1,0},{2,3},{3,2},{4,5},{5,4},{6,7},{7,6},{8,9},{9,8},{10,11... | collective-permute-start | bytes 1179656 | tf_op jit(solution)/shard_map/ppermute | solution.py:534
  44.6 6.6 %collective-permute-start.7 = (bf16[64,768]{1,0:T(8,128)(2,1)S(1)}, bf16[64,768]{1,0:T(8,128)(2,1)S(1)}, u32[]{:S(2)}, u32[]{:S(2)}) collective-permute-start(bf16[64,768]{1,0:T(8,128)(2,1)S(1)} %get-tuple-element.50), channel_id=1, source_target_pairs={{0,8},{8,0},{16,24},{24,16},{1,9},{9,1},{17,25},{25,17},{2,10},{10... | collective-permute-start | bytes 294920 | tf_op jit(solution)/shard_map/ppermute | solution.py:534
  44.6 15.8 %collective-permute-start.8 = (bf16[64,768]{1,0:T(8,128)(2,1)S(1)}, bf16[64,768]{1,0:T(8,128)(2,1)S(1)}, u32[]{:S(2)}, u32[]{:S(2)}) collective-permute-start(bf16[64,768]{1,0:T(8,128)(2,1)S(1)} %get-tuple-element.51), channel_id=1, source_target_pairs={{0,16},{8,24},{16,0},{24,8},{1,17},{9,25},{17,1},{25,9},{2,18},{10... | collective-permute-start | bytes 294920 | tf_op jit(solution)/shard_map/ppermute | solution.py:534
  46.7 13.7 %collective-permute-start.9 = (bf16[64,768]{1,0:T(8,128)(2,1)S(1)}, bf16[64,768]{1,0:T(8,128)(2,1)S(1)}, u32[]{:S(2)}, u32[]{:S(2)}) collective-permute-start(bf16[64,768]{1,0:T(8,128)(2,1)S(1)} %get-tuple-element.52), channel_id=1, source_target_pairs={{0,24},{8,16},{16,8},{24,0},{1,25},{9,17},{17,9},{25,1},{2,26},{10... | collective-permute-start | bytes 294920 | tf_op jit(solution)/shard_map/ppermute | solution.py:534
  51.1 11.3 %collective-permute-start.4 = (bf16[64,768]{1,0:T(8,128)(2,1)S(1)}, bf16[64,768]{1,0:T(8,128)(2,1)S(1)}, u32[]{:S(2)}, u32[]{:S(2)}) collective-permute-start(bf16[64,768]{1,0:T(8,128)(2,1)S(1)} %get-tuple-element.46), channel_id=1, source_target_pairs={{0,8},{8,0},{16,24},{24,16},{1,9},{9,1},{17,25},{25,17},{2,10},{10... | collective-permute-start | bytes 294920 | tf_op jit(solution)/shard_map/ppermute | solution.py:534
  51.2 12.7 %collective-permute-start.5 = (bf16[64,768]{1,0:T(8,128)(2,1)S(1)}, bf16[64,768]{1,0:T(8,128)(2,1)S(1)}, u32[]{:S(2)}, u32[]{:S(2)}) collective-permute-start(bf16[64,768]{1,0:T(8,128)(2,1)S(1)} %get-tuple-element.47), channel_id=1, source_target_pairs={{0,16},{8,24},{16,0},{24,8},{1,17},{9,25},{17,1},{25,9},{2,18},{10... | collective-permute-start | bytes 294920 | tf_op jit(solution)/shard_map/ppermute | solution.py:534
  53.2 10.7 %collective-permute-start.6 = (bf16[64,768]{1,0:T(8,128)(2,1)S(1)}, bf16[64,768]{1,0:T(8,128)(2,1)S(1)}, u32[]{:S(2)}, u32[]{:S(2)}) collective-permute-start(bf16[64,768]{1,0:T(8,128)(2,1)S(1)} %get-tuple-element.48), channel_id=1, source_target_pairs={{0,24},{8,16},{16,8},{24,0},{1,25},{9,17},{17,9},{25,1},{2,26},{10... | collective-permute-start | bytes 294920 | tf_op jit(solution)/shard_map/ppermute | solution.py:534
  55.6 2.3 %copy-start.2 = (bf16[1536,1536]{1,0:T(8,128)(2,1)S(1)}, bf16[1536,1536]{1,0:T(8,128)(2,1)}, u32[]{:S(2)}) copy-start(bf16[1536,1536]{1,0:T(8,128)(2,1)} %weight.3) | copy-start | bytes 14155780
  57.9 1.4 %copy-start.7 = (f32[256,1536]{1,0:T(8,128)S(1)}, f32[256,1536]{1,0:T(8,128)}, u32[]{:S(2)}) copy-start(f32[256,1536]{1,0:T(8,128)} %copy-done.6) | copy-start | bytes 4718596
  (1 other events, 1.1 us)

commit v4 on v1

--- a/solution.py
+++ b/solution.py
@@ -11,6 +11,7 @@
 EPSILON = 1e-05
 LANES = 128
 TAIL = 16
+LOG2_E = 1.4426950408889634
 F32 = jnp.float32
 BF16 = jnp.bfloat16
 EXACT = lax.Precision.HIGHEST
@@ -72,11 +73,12 @@
 
 def head_mixes(scores, running, running_t, dt_t, x, first_head, heads, head_dim):
     length = scores.shape[0]
+    running, running_t = running * LOG2_E, running_t * LOG2_E
     outs = []
 
     def weights(head):
         spreads = running[:, head : head + 1] - running_t[head : head + 1, :]
-        return (scores * jnp.exp(jnp.minimum(spreads, 0.0)) * dt_t[head : head + 1, :]).astype(BF16)
+        return (scores * jnp.exp2(jnp.minimum(spreads, 0.0)) * dt_t[head : head + 1, :]).astype(BF16)
 
     head = 0
     while head < heads:
@@ -131,8 +133,8 @@
 
 def entry_kernel(shares, heads, state, blocks, *refs):
     here_ref, band, tokens, gain, bias, rates, dt_weight, bc_weight, weight = refs[:9]
-    normed_out, payload_out, bc_own, logits, params, own_states, other_states = refs[9:16]
-    held, dt_held, bc_held, held_weight, table, normed, payload, sems, out_sems = refs[16:]
+    normed_out, payload_out, bc_own, logits, params, own_states, other_states, band_decays = refs[9:17]
+    held, dt_held, bc_held, held_weight, table, normed, payload, sems, out_sems = refs[17:]
     frames, rows, columns, width = tokens.shape
     length = frames * columns
     count = rows * length
@@ -232,6 +234,7 @@
     tail = tail_of(decays)
     own_states[frames * half :, :] = tail
     other_states[frames * half :, :] = tail
+    band_decays[...] = tail
     for copy in outgoing:
         copy.wait()
 
@@ -373,7 +376,57 @@
         before_out[frames * rows :, :] = jnp.where(upper, before_decay * far_decay, before_decay)
 
 
-def incoming_kernel(frames, rows, columns, head_dim, band, out_local, bc, reach, own, other, out):
+def decays_of(ref):
+    return ref[-TAIL:-8, :].astype(F32) + ref[-8:, :].astype(F32)
+
+
+def places_of(band):
+    return band % 2 == 0, (band // 2) % 2 == 1, band // 4 == 1
+
+
+def cross_kernel(frames, _, band, total, first, near, far, message):
+    even, x_high, y_high = places_of(band[0])
+    own_decay, first_decay = decays_of(total), decays_of(first)
+    diagonal = decays_of(near) * decays_of(far)
+    one, zero = jnp.ones_like(own_decay), jnp.zeros_like(own_decay)
+    odd_first = jnp.where(y_high, jnp.where(x_high, one, own_decay * diagonal), zero)
+    odd_own = jnp.where(x_high & y_high, zero, one)
+    of_first = jnp.where(even, jnp.where(x_high, own_decay, one), odd_first)
+    of_own = jnp.where(even, jnp.where(x_high, one, first_decay), odd_own)
+    rows = (total.shape[0] - TAIL) // frames
+    for frame in range(frames):
+        at, row = slice(frame * rows, (frame + 1) * rows), slice(frame, frame + 1)
+        sent = of_first[row] * first[at, :].astype(F32) + of_own[row] * total[at, :].astype(F32)
+        message[at, :] = sent.astype(BF16)
+    message[frames * rows :, :] = tail_of(jnp.where(even, own_decay * first_decay, own_decay))
+
+
+def settle_kernel(frames, _, band, first, second, near, far, band_own, band_far, keep, give):
+    even, x_high, y_high = places_of(band[0])
+    first_decay, second_decay = decays_of(first), decays_of(second)
+    diagonal = decays_of(near) * decays_of(far)
+    one, zero = jnp.ones_like(first_decay), jnp.zeros_like(first_decay)
+    even_second = jnp.where(y_high, jnp.where(x_high, first_decay, one), zero)
+    odd_second = jnp.where(x_high | y_high, one, zero)
+    odd_first = jnp.where(y_high, jnp.where(x_high, second_decay, diagonal), zero)
+    of_second = jnp.where(even, even_second, odd_second)
+    of_first = jnp.where(even, jnp.where(x_high, one, zero), odd_first)
+    band_decay = jnp.where(even, decays_of(band_own), decays_of(band_far))
+    rows = keep.shape[0] // frames
+    for frame in range(frames):
+        at, row = slice(frame * rows, (frame + 1) * rows), slice(frame, frame + 1)
+        before = of_second[row] * second[at, :].astype(F32) + of_first[row] * first[at, :].astype(F32)
+        lower = jnp.where(even, band_own[at, :], band_far[at, :]).astype(F32)
+        after = band_decay[row] * before + lower
+        keep[at, :] = jnp.where(even, before, after).astype(BF16)
+        give[at, :] = jnp.where(even, after, before).astype(BF16)
+
+
+def incoming_kernel(
+    frames, rows, columns, head_dim, band, out_local, bc, reach, own, other, weight, out, held, sem
+):
+    fetch = pltpu.make_async_copy(weight, held, sem)
+    fetch.start()
     state = bc.shape[1] // 2
     half = state // 2
     inner = out.shape[1]
@@ -389,6 +442,7 @@
             here = slice(to, to + columns)
             factor = spread(reach[here, :], matrix)
             out[here, :] = out_local[here, :] + factor * dot(bc[here, state:], carried)
+    fetch.wait()
 
 
 def temporal_kernel(
@@ -457,7 +511,7 @@
         last = jnp.min(running, axis=0, keepdims=True)
         mixed = head_mixes(scores, running, running_t, dt_t, values, 0, per_group, head_dim)
         ends = jnp.concatenate([running, jnp.broadcast_to(last, (8, LANES))], axis=0)
-        reach = spread(jnp.exp(ends), matrix)
+        reach = dot(jnp.exp(ends).astype(BF16), matrix)
         mixed = mixed + reach[:size] * dot(c_proj, carried.astype(BF16))
         to_end = (jnp.exp(last - running) * dt).astype(BF16)
         scaled = (values.astype(F32) * dot(to_end, matrix)).astype(BF16)
@@ -526,6 +580,12 @@
     return lax.ppermute(value, axis, [(source, source ^ distance) for source in range(count)])
 
 
+def crossed(value, axis, even, odd):
+    count = lax.axis_size(axis)
+    pairs = [(source, source ^ (odd if source % 2 else even)) for source in range(count)]
+    return lax.ppermute(value, axis, pairs)
+
+
 def per_device(
     tokens, norm_gain, in_weight, bc_weight, dt_weight, dt_bias, decay_rate, out_gain, out_weight
 ):
@@ -549,7 +609,7 @@
     band = lax.axis_index("height").astype(jnp.int32).reshape(1)
 
     packed = (shares, sum(packing(length, group)), group)
-    normed, payload, bc_own, logits, params, own, other = call(
+    normed, payload, bc_own, logits, params, own, other, band_decays = call(
         functools.partial(entry_kernel, shares, heads, state, blocks),
         "entry",
         [
@@ -559,10 +619,11 @@
             shape_of((count, LANES), F32),
             shape_of((16, LANES), F32),
         ]
-        + [shape_of((frames * half + TAIL, inner), BF16)] * 2,
+        + [shape_of((frames * half + TAIL, inner), BF16)] * 2
+        + [shape_of((TAIL, inner), BF16)],
         [SCALAR, SCALAR, HBM, WHOLE, WHOLE, WHOLE, HBM, HBM, HBM],
         limit=LARGE,
-        outs=[HBM, HBM] + [WHOLE] * 5,
+        outs=[HBM, HBM] + [WHOLE] * 6,
         scratch_shapes=[
             pltpu.VMEM((rows, frames, columns, width), BF16),
             pltpu.VMEM((2 * heads, width), BF16),
@@ -637,6 +698,23 @@
 
     before = []
     distance = 2
+    if bands == 8:
+        near, far_decays = (swapped(band_decays, "height", distance) for distance in (6, 7))
+        first = crossed(total, "height", 2, 4)
+        message = call(
+            functools.partial(cross_kernel, frames),
+            "cross",
+            shape_of((frames * half + TAIL, inner), BF16),
+            [ANY, SCALAR] + [WHOLE] * 4,
+        )(reach, band, total, first, near, far_decays)
+        second = crossed(message, "height", 4, 2)
+        results = call(
+            functools.partial(settle_kernel, frames),
+            "settle",
+            [shape_of((frames * half, inner), BF16)] * 2,
+            [ANY, SCALAR] + [WHOLE] * 6,
+        )(reach, band, first, second, near, far_decays, own, far)
+        distance = bands
     while distance < bands:
         far_total = swapped(total, "height", distance)
         finish = distance * 2 >= bands
@@ -661,12 +739,13 @@
     keep, give = results
     came = swapped(give, "height", 1)
 
-    spatial_out = call(
+    spatial_out, held_weight = call(
         functools.partial(incoming_kernel, frames, rows, columns, head_dim),
         "spatial_incoming",
-        shape_of((count, inner), F32),
-        [SCALAR] + [WHOLE] * 5,
-    )(band, out_local, bc_own, reach, keep, came)
+        [shape_of((count, inner), F32), shape_of((inner, width), BF16)],
+        [SCALAR] + [WHOLE] * 5 + [HBM],
+        scratch_shapes=[pltpu.SemaphoreType.DMA],
+    )(band, out_local, bc_own, reach, keep, came, out_weight)
 
     mixed = []
     for part in range(parts):
@@ -684,7 +763,7 @@
                     pltpu.SemaphoreType.DMA((rows * frames,)),
                 ],
                 input_output_aliases={5 + shares: 0} if mixed else {},
-            )(here, spatial_out, gate, out_gain, out_weight, *returned[part], *mixed)
+            )(here, spatial_out, gate, out_gain, held_weight, *returned[part], *mixed)
         ]
     return mixed[0]
 

time: 65.2 us -> 64.6 us (level)
  waiting for transfers between devices: 14.6 us -> 12.5 us
  starting transfers between devices: 18.6 us -> 20 us
    ppermute x10, waiting for transfers between devices: 12.9 us -> 1 us  [swapped(): lax.ppermute(value, axis, [(source, source ^ distance) for source in rang...]
    ppermute x0 -> x2, waiting for transfers between devices: none -> 7.81 us  [crossed(): return lax.ppermute(value, axis, pairs)]
    ppermute x0 -> x2, starting transfers between devices: none -> 2.12 us  [crossed(): return lax.ppermute(value, axis, pairs)]
    all_to_all x1, waiting for transfers between devices: 1.75 us -> 3.72 us  [per_device(): lax.all_to_all(payload, 'tm', split_axis=0, concat_axis=0, tiled=True)]
    ppermute x10, starting transfers between devices: 12.5 us -> 11.9 us  [swapped(): lax.ppermute(value, axis, [(source, source ^ distance) for source in rang...]
  transfers between devices with their start and end apart: 11 -> 13, of which waited for: 4 -> 3; matrix products, arithmetic and copies ran while one was open for 0% -> 0% of each run, Pallas kernels for 20% -> 21%
where the time goes in v4:
time: 64.6 us; the launch traced here: 64.3 us
  Pallas kernels  22.7 us (35%)
  starting transfers between devices  20 us (31%)
  waiting for transfers between devices  12.5 us (19%)
  local copies, waits for them, and re-layouts  8.64 us (13%)
    ppermute x10, starting transfers between devices, swapped(): lax.ppermute(value, axis, [(source, source ^ distance) for source in rang...  11.9 us
    unnamed x28, local copies, waits for them, and re-layouts  8.64 us
    ppermute x2, waiting for transfers between devices, crossed(): return lax.ppermute(value, axis, pairs)  7.81 us
    pallas_call x1, Pallas kernels, per_device(): call(functools.partial(entry_kernel, shares, heads, state, blocks), 'entr...  7.43 us
    all_to_all x1, starting transfers between devices, per_device(): lax.all_to_all(payload, 'tm', split_axis=0, concat_axis=0, tiled=True)  6.03 us
    pallas_call x2, Pallas kernels, per_device(): call(functools.partial(temporal_kernel, part, parts, per_group, head_dim,...  4.35 us
    pallas_call x2, Pallas kernels, per_device(): call(functools.partial(exit_kernel, part, parts, shares), 'exit', shape_o...  3.93 us
    all_to_all x1, waiting for transfers between devices, per_device(): lax.all_to_all(payload, 'tm', split_axis=0, concat_axis=0, tiled=True)  3.72 us
  transfers between devices with their start and end apart: 13, of which 3 were waited for; matrix products, arithmetic and copies ran while one was open for 0% of the time, Pallas kernels for 21%

profile of v4, /device:TPU:0, one launch (start us, length us, event | category | flops | bytes accessed | tf_op | source)
XLA Modules:
  0.0 64.3 jit_solution(6751912091778429065)
XLA Ops:
  0.0 7.4 %entry.1 = (bf16[256,1536]{1,0:T(8,128)(2,1)}, bf16[4,176,768]{2,1,0:T(8,128)(2,1)}, bf16[256,256]{1,0:T(8,128)(2,1)}, f32[256,128]{1,0:T(8,128)}, f32[16,128]{1...) custom-call(s32[1]{0:T(128)} %bitcast.refs_0_, ...), custom_call_target="tpu_custom_call" | custom-call | flops 1 | bytes 1 | tf_op jit(solution)/shard_map/entry/pallas_call | solution.py:612
  8.0 6.0 %all-to-all-start = ((bf16[4,176,768]{2,1,0:T(8,128)(2,1)}), bf16[4,176,768]{2,1,0:T(8,128)(2,1)S(1)}, u32[]{:S(2)}, u32[]{:S(2)}) async-start(bf16[4,176,768]{2,1,0:T(8,128)(2,1)} %get-tuple-element.28.after.refs_4_), calls=%async_computation | async-start | bytes 2162688 | tf_op jit(solution)/shard_map/all_to_all | solution.py:643
  14.2 1.6 %collective-permute-start.1 = (bf16[144,1536]{1,0:T(8,128)(2,1)S(1)}, bf16[144,1536]{1,0:T(8,128)(2,1)S(1)}, u32[]{:S(2)}, u32[]{:S(2)}) collective-permute-start(bf16[144,1536]{1,0:T(8,128)(2,1)S(1)} %pair_total.1.total), channel_id=1, source_target_pairs={{0,2},{1,5},{2,0},{3,7},{4,6},{5,1},{6,4},{7,3},{8,10},{9,13},{10,... | collective-permute-start | bytes 1327112 | tf_op jit(solution)/shard_map/ppermute | solution.py:586
  15.8 1.0 %collective-permute-start.3 = (bf16[16,1536]{1,0:T(8,128)(2,1)}, bf16[16,1536]{1,0:T(8,128)(2,1)S(1)}, u32[]{:S(2)}, u32[]{:S(2)}) collective-permute-start(bf16[16,1536]{1,0:T(8,128)(2,1)} %get-tuple-element.37), channel_id=1, source_target_pairs={{0,7},{1,6},{2,5},{3,4},{4,3},{5,2},{6,1},{7,0},{8,15},{9,14},{10,... | collective-permute-start | bytes 147464 | tf_op jit(solution)/shard_map/ppermute | solution.py:580
  16.8 1.5 %collective-permute-start.2 = (bf16[16,1536]{1,0:T(8,128)(2,1)}, bf16[16,1536]{1,0:T(8,128)(2,1)S(1)}, u32[]{:S(2)}, u32[]{:S(2)}) collective-permute-start(bf16[16,1536]{1,0:T(8,128)(2,1)} %get-tuple-element.37), channel_id=1, source_target_pairs={{0,6},{1,7},{2,4},{3,5},{4,2},{5,3},{6,0},{7,1},{8,14},{9,15},{10,... | collective-permute-start | bytes 147464 | tf_op jit(solution)/shard_map/ppermute | solution.py:580
  18.3 3.7 %copy-done = bf16[1536,3072]{1,0:T(8,128)(2,1)S(1)} copy-done((bf16[1536,3072]{1,0:T(8,128)(2,1)S(1)}, bf16[1536,3072]{1,0:T(8,128)(2,1)}, u32[]{:S(2)}) %copy-start) | copy-done | bytes 9437208
  21.9 2.6 %gate.1.refs_0_.refs_2_ = bf16[256,1536]{1,0:T(8,128)(2,1)S(1)} custom-call(bf16[4,176,768]{2,1,0:T(8,128)(2,1)S(1)} %copy-done.1, bf16[256,1536]{1,0:T(8,128)(2,1)S(1)} %copy-done.8, bf16[1536,3072]{1,0:T(8,128)(2,1)S(1)} %copy-done), custom_call_target="tpu_custom_call" | custom-call | flops 1 | bytes 1 | tf_op jit(solution)/shard_map/gate/pallas_call | solution.py:645
  24.6 1.9 %spatial_local.1 = (f32[256,1536]{1,0:T(8,128)S(1)}, f32[256,128]{1,0:T(8,128)S(1)}) custom-call(bf16[256,1536]{1,0:T(8,128)(2,1)S(1)} %gate.1.refs_0_.refs_2_, bf16[256,256]{1,0:T(8,128)(2,1)S(1)} %copy-done.9, f32[256,128]{1,0:T(8,128)S(1)} %copy-done.11, f32[16,128]{1,0:T(8,128)S(1)} %copy-done.12, bf16[4,176,768]{2,1,0:T(8,128)(2,1)S(1)} %copy-done.1), custom_call_target="tpu_custom_call" | custom-call | flops 1 | bytes 1 | tf_op jit(solution)/shard_map/spatial_local/pallas_call | solution.py:656
  26.5 1.2 %copy-done.6 = f32[256,1536]{1,0:T(8,128)} copy-done((f32[256,1536]{1,0:T(8,128)}, f32[256,1536]{1,0:T(8,128)S(1)}, u32[]{:S(2)}) %copy-start.6) | copy-done | bytes 1572888
  28.5 7.8 %collective-permute-done.4.second = bf16[144,1536]{1,0:T(8,128)(2,1)S(1)} collective-permute-done((bf16[144,1536]{1,0:T(8,128)(2,1)S(1)}, bf16[144,1536]{1,0:T(8,128)(2,1)S(1)}, u32[]{:S(2)}, u32[]{:S(2)}) %collective-permute-start.4) | collective-permute-done | bytes 442400 | tf_op jit(solution)/shard_map/ppermute | solution.py:586
  36.3 1.1 %settle.1 = (bf16[128,1536]{1,0:T(8,128)(2,1)S(1)}, bf16[128,1536]{1,0:T(8,128)(2,1)}) custom-call(f32[256,128]{1,0:T(8,128)S(1)} %get-tuple-element.34._.reach, s32[1]{0:T(128)} %bitcast.1.refs_1_.band, bf16[144,1536]{1,0:T(8,128)(2,1)S(1)} %collective-permute-done.1.first, bf16[144,1536]{1,0:T(8,128)(2,1)S(1)} %collective-permute-done.4.second, ...), custom_call_target="tpu_custom_call" | custom-call | flops 1 | bytes 1 | tf_op jit(solution)/shard_map/settle/pallas_call | solution.py:711
  37.3 3.7 %all-to-all-done.refs_2_ = bf16[4,176,768]{2,1,0:T(8,128)(2,1)S(1)} async-done(((bf16[4,176,768]{2,1,0:T(8,128)(2,1)}), bf16[4,176,768]{2,1,0:T(8,128)(2,1)S(1)}, u32[]{:S(2)}, u32[]{:S(2)}) %all-to-all-start) | async-done | bytes 1081376 | tf_op jit(solution)/shard_map/all_to_all | solution.py:643
  41.1 2.3 %temporal.2 = (bf16[64,768]{1,0:T(8,128)(2,1)S(1)}, bf16[64,768]{1,0:T(8,128)(2,1)S(1)}, bf16[64,768]{1,0:T(8,128)(2,1)S(1)}, bf16[64,768]{1,0:T(8,128)(2,1)S(1)}, f32[128,768]{1,0:T(8,128)S(1)}) custom-call(s32[1]{0:T(128)} %bitcast.refs_0_, f32[16,128]{1,0:T(8,128)S(1)} %copy-done.12, bf16[4,176,768]{2,1,0:T(8,128)(2,1)S(1)} %all-to-all-done.refs_2_), custom_call_target="tpu_custom_call" | custom-call | flops 1 | bytes 1 | tf_op jit(solution)/shard_map/temporal/pallas_call | solution.py:672
  43.4 2.0 %collective-permute-start.10 = (bf16[64,768]{1,0:T(8,128)(2,1)S(1)}, bf16[64,768]{1,0:T(8,128)(2,1)S(1)}, u32[]{:S(2)}, u32[]{:S(2)}) collective-permute-start(bf16[64,768]{1,0:T(8,128)(2,1)S(1)} %get-tuple-element.49), channel_id=1, source_target_pairs={{0,16},{8,24},{16,0},{24,8},{1,17},{9,25},{17,1},{25,9},{2,18},{10... | collective-permute-start | bytes 294920 | tf_op jit(solution)/shard_map/ppermute | solution.py:580
  45.4 2.4 %collective-permute-start.11 = (bf16[64,768]{1,0:T(8,128)(2,1)S(1)}, bf16[64,768]{1,0:T(8,128)(2,1)S(1)}, u32[]{:S(2)}, u32[]{:S(2)}) collective-permute-start(bf16[64,768]{1,0:T(8,128)(2,1)S(1)} %get-tuple-element.50), channel_id=1, source_target_pairs={{0,24},{8,16},{16,8},{24,0},{1,25},{9,17},{17,9},{25,1},{2,26},{10... | collective-permute-start | bytes 294920 | tf_op jit(solution)/shard_map/ppermute | solution.py:580
  47.8 2.1 %temporal.3 = (bf16[64,768]{1,0:T(8,128)(2,1)S(1)}, bf16[64,768]{1,0:T(8,128)(2,1)S(1)}, bf16[64,768]{1,0:T(8,128)(2,1)S(1)}, bf16[64,768]{1,0:T(8,128)(2,1)S(1)}) custom-call(s32[1]{0:T(128)} %bitcast.refs_0_, f32[16,128]{1,0:T(8,128)S(1)} %copy-done.12, bf16[4,176,768]{2,1,0:T(8,128)(2,1)S(1)} %all-to-all-done.refs_2_, ...), custom_call_target="tpu_custom_call" | custom-call | flops 1 | bytes 1 | tf_op jit(solution)/shard_map/temporal/pallas_call | solution.py:672
  50.0 2.0 %collective-permute-start.7 = (bf16[64,768]{1,0:T(8,128)(2,1)S(1)}, bf16[64,768]{1,0:T(8,128)(2,1)S(1)}, u32[]{:S(2)}, u32[]{:S(2)}) collective-permute-start(bf16[64,768]{1,0:T(8,128)(2,1)S(1)} %get-tuple-element.45), channel_id=1, source_target_pairs={{0,16},{8,24},{16,0},{24,8},{1,17},{9,25},{17,1},{25,9},{2,18},{10... | collective-permute-start | bytes 294920 | tf_op jit(solution)/shard_map/ppermute | solution.py:580
  52.0 2.4 %collective-permute-start.8 = (bf16[64,768]{1,0:T(8,128)(2,1)S(1)}, bf16[64,768]{1,0:T(8,128)(2,1)S(1)}, u32[]{:S(2)}, u32[]{:S(2)}) collective-permute-start(bf16[64,768]{1,0:T(8,128)(2,1)S(1)} %get-tuple-element.46), channel_id=1, source_target_pairs={{0,24},{8,16},{16,8},{24,0},{1,25},{9,17},{17,9},{25,1},{2,26},{10... | collective-permute-start | bytes 294920 | tf_op jit(solution)/shard_map/ppermute | solution.py:580
  54.3 2.3 %copy-done.2 = bf16[1536,1536]{1,0:T(8,128)(2,1)S(1)} copy-done((bf16[1536,1536]{1,0:T(8,128)(2,1)S(1)}, bf16[1536,1536]{1,0:T(8,128)(2,1)}, u32[]{:S(2)}) %copy-start.2) | copy-done | bytes 4718616
  56.7 1.4 %copy-done.7 = f32[256,1536]{1,0:T(8,128)S(1)} copy-done((f32[256,1536]{1,0:T(8,128)S(1)}, f32[256,1536]{1,0:T(8,128)}, u32[]{:S(2)}) %copy-start.7) | copy-done | bytes 1572888
  58.1 1.1 %spatial_incoming.1 = (f32[256,1536]{1,0:T(8,128)S(1)}, bf16[1536,1536]{1,0:T(8,128)(2,1)S(1)}) custom-call(s32[1]{0:T(128)} %bitcast.1.refs_1_.band, f32[256,1536]{1,0:T(8,128)S(1)} %copy-done.7, bf16[256,256]{1,0:T(8,128)(2,1)S(1)} %copy-done.10, f32[256,128]{1,0:T(8,128)S(1)} %get-tuple-element.34._.reach, bf16[128,1536]{1,0:T(8,128)(2,1)S(1)} %get-tuple-element.38.own, ...), custom_call_target="tpu_custom_call" | custom-call | flops 1 | bytes 1 | tf_op jit(solution)/shard_map/spatial_incoming/pallas_call | solution.py:742
  59.2 2.0 %exit.2.refs_9_ = bf16[2,2,64,1536]{3,2,1,0:T(8,128)(2,1)} custom-call(s32[1]{0:T(128)} %bitcast.refs_0_, f32[256,1536]{1,0:T(8,128)S(1)} %get-tuple-element.40.refs_1_, bf16[256,1536]{1,0:T(8,128)(2,1)S(1)} %gate.1.refs_0_.refs_2_, f32[1536]{0:T(1024)S(1)} %copy-done.13, bf16[1536,1536]{1,0:T(8,128)(2,1)S(1)} %get-tuple-element.41.refs_4_, ...), custom_call_target="tpu_custom_call" | custom-call | flops 1 | bytes 1 | tf_op jit(solution)/shard_map/exit/pallas_call | solution.py:753
  61.2 1.0 %collective-permute-done.7.refs_7_ = bf16[64,768]{1,0:T(8,128)(2,1)S(1)} collective-permute-done((bf16[64,768]{1,0:T(8,128)(2,1)S(1)}, bf16[64,768]{1,0:T(8,128)(2,1)S(1)}, u32[]{:S(2)}, u32[]{:S(2)}) %collective-permute-start.7) | collective-permute-done | bytes 98336 | tf_op jit(solution)/shard_map/ppermute | solution.py:580
  62.2 2.0 %exit.3 = bf16[2,2,64,1536]{3,2,1,0:T(8,128)(2,1)} custom-call(s32[1]{0:T(128)} %bitcast.refs_0_, f32[256,1536]{1,0:T(8,128)S(1)} %get-tuple-element.40.refs_1_, bf16[256,1536]{1,0:T(8,128)(2,1)S(1)} %gate.1.refs_0_.refs_2_, f32[1536]{0:T(1024)S(1)} %copy-done.13, bf16[1536,1536]{1,0:T(8,128)(2,1)S(1)} %get-tuple-element.41.refs_4_, ...), custom_call_target="tpu_custom_call", output_to_operand_aliasing={{}: (9, {})} | custom-call | flops 1 | bytes 1 | tf_op jit(solution)/shard_map/exit/pallas_call | solution.py:753
  (41 shorter events, 1.7 us)
Async XLA Ops:
  7.4 6.6 %copy-start.3 = (bf16[144,1536]{1,0:T(8,128)(2,1)S(1)}, bf16[144,1536]{1,0:T(8,128)(2,1)}, u32[]{:S(2)}) copy-start(bf16[144,1536]{1,0:T(8,128)(2,1)} %get-tuple-element.35.own.band_own) | copy-start | bytes 1327108
  7.4 6.6 %collective-permute-start = (bf16[144,1536]{1,0:T(8,128)(2,1)}, bf16[144,1536]{1,0:T(8,128)(2,1)S(1)}, u32[]{:S(2)}, u32[]{:S(2)}) collective-permute-start(bf16[144,1536]{1,0:T(8,128)(2,1)} %get-tuple-element.36), channel_id=1, source_target_pairs={{0,1},{1,0},{2,3},{3,2},{4,5},{5,4},{6,7},{7,6},{8,9},{9,8},{10,11... | collective-permute-start | bytes 1327112 | tf_op jit(solution)/shard_map/ppermute | solution.py:580
  8.0 10.3 %copy-start.1 = (bf16[4,176,768]{2,1,0:T(8,128)(2,1)S(1)}, bf16[4,176,768]{2,1,0:T(8,128)(2,1)}, u32[]{:S(2)}) copy-start(bf16[4,176,768]{2,1,0:T(8,128)(2,1)} %get-tuple-element.28.after.refs_4_) | copy-start | bytes 3244036
  8.0 33.1 %all-to-all-start = ((bf16[4,176,768]{2,1,0:T(8,128)(2,1)}), bf16[4,176,768]{2,1,0:T(8,128)(2,1)S(1)}, u32[]{:S(2)}, u32[]{:S(2)}) async-start(bf16[4,176,768]{2,1,0:T(8,128)(2,1)} %get-tuple-element.28.after.refs_4_), calls=%async_computation | async-start | bytes 2162688 | tf_op jit(solution)/shard_map/all_to_all | solution.py:643
  14.0 4.2 %copy-start.8 = (bf16[256,1536]{1,0:T(8,128)(2,1)S(1)}, bf16[256,1536]{1,0:T(8,128)(2,1)}, u32[]{:S(2)}) copy-start(bf16[256,1536]{1,0:T(8,128)(2,1)} %get-tuple-element.29.normed) | copy-start | bytes 2359300
  14.0 4.2 %copy-start.4 = (bf16[144,1536]{1,0:T(8,128)(2,1)}, bf16[144,1536]{1,0:T(8,128)(2,1)S(1)}, u32[]{:S(2)}) copy-start(bf16[144,1536]{1,0:T(8,128)(2,1)S(1)} %collective-permute-done.far.band_far) | copy-start | bytes 1327108
  14.2 13.5 %collective-permute-start.1 = (bf16[144,1536]{1,0:T(8,128)(2,1)S(1)}, bf16[144,1536]{1,0:T(8,128)(2,1)S(1)}, u32[]{:S(2)}, u32[]{:S(2)}) collective-permute-start(bf16[144,1536]{1,0:T(8,128)(2,1)S(1)} %pair_total.1.total), channel_id=1, source_target_pairs={{0,2},{1,5},{2,0},{3,7},{4,6},{5,1},{6,4},{7,3},{8,10},{9,13},{10,... | collective-permute-start | bytes 1327112 | tf_op jit(solution)/shard_map/ppermute | solution.py:586
  15.8 11.9 %collective-permute-start.3 = (bf16[16,1536]{1,0:T(8,128)(2,1)}, bf16[16,1536]{1,0:T(8,128)(2,1)S(1)}, u32[]{:S(2)}, u32[]{:S(2)}) collective-permute-start(bf16[16,1536]{1,0:T(8,128)(2,1)} %get-tuple-element.37), channel_id=1, source_target_pairs={{0,7},{1,6},{2,5},{3,4},{4,3},{5,2},{6,1},{7,0},{8,15},{9,14},{10,... | collective-permute-start | bytes 147464 | tf_op jit(solution)/shard_map/ppermute | solution.py:580
  16.8 10.9 %collective-permute-start.2 = (bf16[16,1536]{1,0:T(8,128)(2,1)}, bf16[16,1536]{1,0:T(8,128)(2,1)S(1)}, u32[]{:S(2)}, u32[]{:S(2)}) collective-permute-start(bf16[16,1536]{1,0:T(8,128)(2,1)} %get-tuple-element.37), channel_id=1, source_target_pairs={{0,6},{1,7},{2,4},{3,5},{4,2},{5,3},{6,0},{7,1},{8,14},{9,15},{10,... | collective-permute-start | bytes 147464 | tf_op jit(solution)/shard_map/ppermute | solution.py:580
  18.2 3.7 %copy-start = (bf16[1536,3072]{1,0:T(8,128)(2,1)S(1)}, bf16[1536,3072]{1,0:T(8,128)(2,1)}, u32[]{:S(2)}) copy-start(bf16[1536,3072]{1,0:T(8,128)(2,1)} %weight.2) | copy-start | bytes 28311556
  21.9 2.6 %copy-start.9 = (bf16[256,256]{1,0:T(8,128)(2,1)S(1)}, bf16[256,256]{1,0:T(8,128)(2,1)}, u32[]{:S(2)}) copy-start(bf16[256,256]{1,0:T(8,128)(2,1)} %get-tuple-element.30.refs_1_.bc) | copy-start | bytes 393220
  21.9 2.6 %copy-start.11 = (f32[256,128]{1,0:T(8,128)S(1)}, f32[256,128]{1,0:T(8,128)}, u32[]{:S(2)}) copy-start(f32[256,128]{1,0:T(8,128)} %get-tuple-element.31.refs_2_) | copy-start | bytes 393220
  21.9 2.6 %copy-start.12 = (f32[16,128]{1,0:T(8,128)S(1)}, f32[16,128]{1,0:T(8,128)}, u32[]{:S(2)}) copy-start(f32[16,128]{1,0:T(8,128)} %get-tuple-element.32.refs_3_.refs_1_) | copy-start | bytes 24580
  24.6 11.7 %copy-start.5 = (bf16[144,1536]{1,0:T(8,128)(2,1)S(1)}, bf16[144,1536]{1,0:T(8,128)(2,1)}, u32[]{:S(2)}) copy-start(bf16[144,1536]{1,0:T(8,128)(2,1)} %copy-done.4) | copy-start | bytes 1327108
  27.9 8.4 %collective-permute-start.4 = (bf16[144,1536]{1,0:T(8,128)(2,1)S(1)}, bf16[144,1536]{1,0:T(8,128)(2,1)S(1)}, u32[]{:S(2)}, u32[]{:S(2)}) collective-permute-start(bf16[144,1536]{1,0:T(8,128)(2,1)S(1)} %cross.1), channel_id=1, source_target_pairs={{0,4},{1,3},{2,6},{3,1},{4,0},{5,7},{6,2},{7,5},{8,12},{9,11},{10,... | collective-permute-start | bytes 1327112 | tf_op jit(solution)/shard_map/ppermute | solution.py:586
  37.3 17.0 %copy-start.10 = (bf16[256,256]{1,0:T(8,128)(2,1)S(1)}, bf16[256,256]{1,0:T(8,128)(2,1)}, u32[]{:S(2)}) copy-start(bf16[256,256]{1,0:T(8,128)(2,1)} %get-tuple-element.30.refs_1_.bc) | copy-start | bytes 393220
  37.3 14.6 %collective-permute-start.5 = (bf16[128,1536]{1,0:T(8,128)(2,1)}, bf16[128,1536]{1,0:T(8,128)(2,1)S(1)}, u32[]{:S(2)}, u32[]{:S(2)}) collective-permute-start(bf16[128,1536]{1,0:T(8,128)(2,1)} %get-tuple-element.39), channel_id=1, source_target_pairs={{0,1},{1,0},{2,3},{3,2},{4,5},{5,4},{6,7},{7,6},{8,9},{9,8},{10,11... | collective-permute-start | bytes 1179656 | tf_op jit(solution)/shard_map/ppermute | solution.py:580
  43.3 6.6 %collective-permute-start.9 = (bf16[64,768]{1,0:T(8,128)(2,1)S(1)}, bf16[64,768]{1,0:T(8,128)(2,1)S(1)}, u32[]{:S(2)}, u32[]{:S(2)}) collective-permute-start(bf16[64,768]{1,0:T(8,128)(2,1)S(1)} %get-tuple-element.48), channel_id=1, source_target_pairs={{0,8},{8,0},{16,24},{24,16},{1,9},{9,1},{17,25},{25,17},{2,10},{10... | collective-permute-start | bytes 294920 | tf_op jit(solution)/shard_map/ppermute | solution.py:580
  43.4 15.8 %collective-permute-start.10 = (bf16[64,768]{1,0:T(8,128)(2,1)S(1)}, bf16[64,768]{1,0:T(8,128)(2,1)S(1)}, u32[]{:S(2)}, u32[]{:S(2)}) collective-permute-start(bf16[64,768]{1,0:T(8,128)(2,1)S(1)} %get-tuple-element.49), channel_id=1, source_target_pairs={{0,16},{8,24},{16,0},{24,8},{1,17},{9,25},{17,1},{25,9},{2,18},{10... | collective-permute-start | bytes 294920 | tf_op jit(solution)/shard_map/ppermute | solution.py:580
  45.4 13.8 %collective-permute-start.11 = (bf16[64,768]{1,0:T(8,128)(2,1)S(1)}, bf16[64,768]{1,0:T(8,128)(2,1)S(1)}, u32[]{:S(2)}, u32[]{:S(2)}) collective-permute-start(bf16[64,768]{1,0:T(8,128)(2,1)S(1)} %get-tuple-element.50), channel_id=1, source_target_pairs={{0,24},{8,16},{16,8},{24,0},{1,25},{9,17},{17,9},{25,1},{2,26},{10... | collective-permute-start | bytes 294920 | tf_op jit(solution)/shard_map/ppermute | solution.py:580
  49.9 11.3 %collective-permute-start.6 = (bf16[64,768]{1,0:T(8,128)(2,1)S(1)}, bf16[64,768]{1,0:T(8,128)(2,1)S(1)}, u32[]{:S(2)}, u32[]{:S(2)}) collective-permute-start(bf16[64,768]{1,0:T(8,128)(2,1)S(1)} %get-tuple-element.44), channel_id=1, source_target_pairs={{0,8},{8,0},{16,24},{24,16},{1,9},{9,1},{17,25},{25,17},{2,10},{10... | collective-permute-start | bytes 294920 | tf_op jit(solution)/shard_map/ppermute | solution.py:580
  50.0 12.2 %collective-permute-start.7 = (bf16[64,768]{1,0:T(8,128)(2,1)S(1)}, bf16[64,768]{1,0:T(8,128)(2,1)S(1)}, u32[]{:S(2)}, u32[]{:S(2)}) collective-permute-start(bf16[64,768]{1,0:T(8,128)(2,1)S(1)} %get-tuple-element.45), channel_id=1, source_target_pairs={{0,16},{8,24},{16,0},{24,8},{1,17},{9,25},{17,1},{25,9},{2,18},{10... | collective-permute-start | bytes 294920 | tf_op jit(solution)/shard_map/ppermute | solution.py:580
  52.0 10.2 %collective-permute-start.8 = (bf16[64,768]{1,0:T(8,128)(2,1)S(1)}, bf16[64,768]{1,0:T(8,128)(2,1)S(1)}, u32[]{:S(2)}, u32[]{:S(2)}) collective-permute-start(bf16[64,768]{1,0:T(8,128)(2,1)S(1)} %get-tuple-element.46), channel_id=1, source_target_pairs={{0,24},{8,16},{16,8},{24,0},{1,25},{9,17},{17,9},{25,1},{2,26},{10... | collective-permute-start | bytes 294920 | tf_op jit(solution)/shard_map/ppermute | solution.py:580
  54.3 2.3 %copy-start.2 = (bf16[1536,1536]{1,0:T(8,128)(2,1)S(1)}, bf16[1536,1536]{1,0:T(8,128)(2,1)}, u32[]{:S(2)}) copy-start(bf16[1536,1536]{1,0:T(8,128)(2,1)} %weight.3) | copy-start | bytes 14155780
  (3 other events, 3.7 us)

commit v5 on v4

--- a/solution.py
+++ b/solution.py
@@ -107,6 +107,10 @@
         )
         for index in range(blocks)
     ]
+
+
+def rank_of(device):
+    return device ^ (device >> 1)
 
 
 def packing(length, group):
@@ -199,7 +203,7 @@
         for inside in range(0, block, group):
             part = (at + inside) // group
             for row in range(rows):
-                piece = part * rows + row
+                piece = rank_of(part * rows + row)
                 here = slice(row * length, (row + 1) * length)
                 payload[piece, :length, :] = values[here, inside : inside + group]
                 pack_rest(
@@ -264,7 +268,7 @@
 def frame_x(payload, part, frame, rows, columns):
     return jnp.concatenate(
         [
-            payload[part * rows + row, frame * columns : (frame + 1) * columns, :]
+            payload[rank_of(part * rows + row), frame * columns : (frame + 1) * columns, :]
             for row in range(rows)
         ],
         axis=0,
@@ -462,7 +466,7 @@
     eye = eye.astype(BF16)
 
     def came(distance):
-        return payload.at[here ^ distance]
+        return payload.at[rank_of(here ^ distance)]
 
     for distance in range(shares):
         b_proj, c_proj, logits = unpacked_rest(came(distance), length)
@@ -640,7 +644,15 @@
     def sent(parts):
         return [parts[0]] + [swapped(parts[d], "tm", d) for d in range(1, shares)]
 
-    received = lax.all_to_all(payload, "tm", split_axis=0, concat_axis=0, tiled=True)
+    line = [rank_of(device) for device in range(shares)]
+    received = lax.all_to_all(
+        payload,
+        "tm",
+        split_axis=0,
+        concat_axis=0,
+        tiled=True,
+        axis_index_groups=[[line.index(rank) for rank in range(shares)]],
+    )
     far = swapped(other, "height", 1)
     gate = call(
         functools.partial(gate_kernel, blocks),

time: 64.6 us -> 64.5 us (level)
  starting transfers between devices: 20 us -> 22.5 us
  waiting for transfers between devices: 12.5 us -> 10 us
    all_to_all x1, waiting for transfers between devices: 3.72 us -> 0.01 us  [per_device(): lax.all_to_all(payload, 'tm', split_axis=0, concat_axis=0, tiled=True, ax...]
    ppermute x10, starting transfers between devices: 11.9 us -> 14.3 us  [swapped(): lax.ppermute(value, axis, [(source, source ^ distance) for source in rang...]
    ppermute x10, waiting for transfers between devices: 1 us -> 2.23 us  [swapped(): lax.ppermute(value, axis, [(source, source ^ distance) for source in rang...]
  transfers between devices with their start and end apart: 13 -> 13, of which waited for: 3 -> 2; matrix products, arithmetic and copies ran while one was open for 0% -> 0% of each run, Pallas kernels for 21% -> 21%
where the time goes in v5:
time: 64.5 us; the launch traced here: 64.2 us
  Pallas kernels  22.7 us (35%)
  starting transfers between devices  22.5 us (35%)
  waiting for transfers between devices  10 us (16%)
  local copies, waits for them, and re-layouts  8.64 us (13%)
    ppermute x10, starting transfers between devices, swapped(): lax.ppermute(value, axis, [(source, source ^ distance) for source in rang...  14.3 us
    unnamed x28, local copies, waits for them, and re-layouts  8.64 us
    ppermute x2, waiting for transfers between devices, crossed(): return lax.ppermute(value, axis, pairs)  7.8 us
    pallas_call x1, Pallas kernels, per_device(): call(functools.partial(entry_kernel, shares, heads, state, blocks), 'entr...  7.43 us
    all_to_all x1, starting transfers between devices, per_device(): lax.all_to_all(payload, 'tm', split_axis=0, concat_axis=0, tiled=True, ax...  6.03 us
    pallas_call x2, Pallas kernels, per_device(): call(functools.partial(temporal_kernel, part, parts, per_group, head_dim,...  4.34 us
    pallas_call x2, Pallas kernels, per_device(): call(functools.partial(exit_kernel, part, parts, shares), 'exit', shape_o...  3.93 us
    pallas_call x1, Pallas kernels, per_device(): call(functools.partial(gate_kernel, blocks), 'gate', shape_of((count, inn...  2.59 us
  transfers between devices with their start and end apart: 13, of which 2 were waited for; matrix products, arithmetic and copies ran while one was open for 0% of the time, Pallas kernels for 21%

profile of v5, /device:TPU:0, one launch (start us, length us, event | category | flops | bytes accessed | tf_op | source)
XLA Modules:
  0.0 64.2 jit_solution(16982232145505381253)
XLA Ops:
  0.0 7.4 %entry.1 = (bf16[256,1536]{1,0:T(8,128)(2,1)}, bf16[4,176,768]{2,1,0:T(8,128)(2,1)}, bf16[256,256]{1,0:T(8,128)(2,1)}, f32[256,128]{1,0:T(8,128)}, f32[16,128]{1...) custom-call(s32[1]{0:T(128)} %bitcast.refs_0_, ...), custom_call_target="tpu_custom_call" | custom-call | flops 1 | bytes 1 | tf_op jit(solution)/shard_map/entry/pallas_call | solution.py:616
  8.0 6.0 %all-to-all-start = ((bf16[4,176,768]{2,1,0:T(8,128)(2,1)}), bf16[4,176,768]{2,1,0:T(8,128)(2,1)S(1)}, u32[]{:S(2)}, u32[]{:S(2)}) async-start(bf16[4,176,768]{2,1,0:T(8,128)(2,1)} %get-tuple-element.28.after.refs_4_), calls=%async_computation | async-start | bytes 2162688 | tf_op jit(solution)/shard_map/all_to_all | solution.py:648
  14.2 1.6 %collective-permute-start.1 = (bf16[144,1536]{1,0:T(8,128)(2,1)S(1)}, bf16[144,1536]{1,0:T(8,128)(2,1)S(1)}, u32[]{:S(2)}, u32[]{:S(2)}) collective-permute-start(bf16[144,1536]{1,0:T(8,128)(2,1)S(1)} %pair_total.1.total), channel_id=1, source_target_pairs={{0,2},{1,5},{2,0},{3,7},{4,6},{5,1},{6,4},{7,3},{8,10},{9,13},{10,... | collective-permute-start | bytes 1327112 | tf_op jit(solution)/shard_map/ppermute | solution.py:590
  15.8 1.0 %collective-permute-start.3 = (bf16[16,1536]{1,0:T(8,128)(2,1)}, bf16[16,1536]{1,0:T(8,128)(2,1)S(1)}, u32[]{:S(2)}, u32[]{:S(2)}) collective-permute-start(bf16[16,1536]{1,0:T(8,128)(2,1)} %get-tuple-element.37), channel_id=1, source_target_pairs={{0,7},{1,6},{2,5},{3,4},{4,3},{5,2},{6,1},{7,0},{8,15},{9,14},{10,... | collective-permute-start | bytes 147464 | tf_op jit(solution)/shard_map/ppermute | solution.py:584
  16.8 1.5 %collective-permute-start.2 = (bf16[16,1536]{1,0:T(8,128)(2,1)}, bf16[16,1536]{1,0:T(8,128)(2,1)S(1)}, u32[]{:S(2)}, u32[]{:S(2)}) collective-permute-start(bf16[16,1536]{1,0:T(8,128)(2,1)} %get-tuple-element.37), channel_id=1, source_target_pairs={{0,6},{1,7},{2,4},{3,5},{4,2},{5,3},{6,0},{7,1},{8,14},{9,15},{10,... | collective-permute-start | bytes 147464 | tf_op jit(solution)/shard_map/ppermute | solution.py:584
  18.3 3.7 %copy-done = bf16[1536,3072]{1,0:T(8,128)(2,1)S(1)} copy-done((bf16[1536,3072]{1,0:T(8,128)(2,1)S(1)}, bf16[1536,3072]{1,0:T(8,128)(2,1)}, u32[]{:S(2)}) %copy-start) | copy-done | bytes 9437208
  21.9 2.6 %gate.1.refs_0_.refs_2_ = bf16[256,1536]{1,0:T(8,128)(2,1)S(1)} custom-call(bf16[4,176,768]{2,1,0:T(8,128)(2,1)S(1)} %copy-done.1, bf16[256,1536]{1,0:T(8,128)(2,1)S(1)} %copy-done.8, bf16[1536,3072]{1,0:T(8,128)(2,1)S(1)} %copy-done), custom_call_target="tpu_custom_call" | custom-call | flops 1 | bytes 1 | tf_op jit(solution)/shard_map/gate/pallas_call | solution.py:657
  24.6 1.9 %spatial_local.1 = (f32[256,1536]{1,0:T(8,128)S(1)}, f32[256,128]{1,0:T(8,128)S(1)}) custom-call(bf16[256,1536]{1,0:T(8,128)(2,1)S(1)} %gate.1.refs_0_.refs_2_, bf16[256,256]{1,0:T(8,128)(2,1)S(1)} %copy-done.9, f32[256,128]{1,0:T(8,128)S(1)} %copy-done.11, f32[16,128]{1,0:T(8,128)S(1)} %copy-done.12, bf16[4,176,768]{2,1,0:T(8,128)(2,1)S(1)} %copy-done.1), custom_call_target="tpu_custom_call" | custom-call | flops 1 | bytes 1 | tf_op jit(solution)/shard_map/spatial_local/pallas_call | solution.py:668
  26.5 1.2 %copy-done.6 = f32[256,1536]{1,0:T(8,128)} copy-done((f32[256,1536]{1,0:T(8,128)}, f32[256,1536]{1,0:T(8,128)S(1)}, u32[]{:S(2)}) %copy-start.6) | copy-done | bytes 1572888
  28.5 7.8 %collective-permute-done.4.second = bf16[144,1536]{1,0:T(8,128)(2,1)S(1)} collective-permute-done((bf16[144,1536]{1,0:T(8,128)(2,1)S(1)}, bf16[144,1536]{1,0:T(8,128)(2,1)S(1)}, u32[]{:S(2)}, u32[]{:S(2)}) %collective-permute-start.4) | collective-permute-done | bytes 442400 | tf_op jit(solution)/shard_map/ppermute | solution.py:590
  36.3 1.1 %settle.1 = (bf16[128,1536]{1,0:T(8,128)(2,1)S(1)}, bf16[128,1536]{1,0:T(8,128)(2,1)}) custom-call(f32[256,128]{1,0:T(8,128)S(1)} %get-tuple-element.34._.reach, s32[1]{0:T(128)} %bitcast.1.refs_1_.band, bf16[144,1536]{1,0:T(8,128)(2,1)S(1)} %collective-permute-done.1.first, bf16[144,1536]{1,0:T(8,128)(2,1)S(1)} %collective-permute-done.4.second, ...), custom_call_target="tpu_custom_call" | custom-call | flops 1 | bytes 1 | tf_op jit(solution)/shard_map/settle/pallas_call | solution.py:723
  37.3 2.3 %temporal.2 = (bf16[64,768]{1,0:T(8,128)(2,1)S(1)}, bf16[64,768]{1,0:T(8,128)(2,1)S(1)}, bf16[64,768]{1,0:T(8,128)(2,1)S(1)}, bf16[64,768]{1,0:T(8,128)(2,1)S(1)}, f32[128,768]{1,0:T(8,128)S(1)}) custom-call(s32[1]{0:T(128)} %bitcast.refs_0_, f32[16,128]{1,0:T(8,128)S(1)} %copy-done.12, bf16[4,176,768]{2,1,0:T(8,128)(2,1)S(1)} %all-to-all-done.refs_2_), custom_call_target="tpu_custom_call" | custom-call | flops 1 | bytes 1 | tf_op jit(solution)/shard_map/temporal/pallas_call | solution.py:684
  39.6 4.4 %collective-permute-start.9 = (bf16[64,768]{1,0:T(8,128)(2,1)S(1)}, bf16[64,768]{1,0:T(8,128)(2,1)S(1)}, u32[]{:S(2)}, u32[]{:S(2)}) collective-permute-start(bf16[64,768]{1,0:T(8,128)(2,1)S(1)} %get-tuple-element.48), channel_id=1, source_target_pairs={{0,8},{8,0},{16,24},{24,16},{1,9},{9,1},{17,25},{25,17},{2,10},{10... | collective-permute-start | bytes 294920 | tf_op jit(solution)/shard_map/ppermute | solution.py:584
  44.1 2.4 %collective-permute-start.11 = (bf16[64,768]{1,0:T(8,128)(2,1)S(1)}, bf16[64,768]{1,0:T(8,128)(2,1)S(1)}, u32[]{:S(2)}, u32[]{:S(2)}) collective-permute-start(bf16[64,768]{1,0:T(8,128)(2,1)S(1)} %get-tuple-element.50), channel_id=1, source_target_pairs={{0,24},{8,16},{16,8},{24,0},{1,25},{9,17},{17,9},{25,1},{2,26},{10... | collective-permute-start | bytes 294920 | tf_op jit(solution)/shard_map/ppermute | solution.py:584
  46.5 2.1 %temporal.3 = (bf16[64,768]{1,0:T(8,128)(2,1)S(1)}, bf16[64,768]{1,0:T(8,128)(2,1)S(1)}, bf16[64,768]{1,0:T(8,128)(2,1)S(1)}, bf16[64,768]{1,0:T(8,128)(2,1)S(1)}) custom-call(s32[1]{0:T(128)} %bitcast.refs_0_, f32[16,128]{1,0:T(8,128)S(1)} %copy-done.12, bf16[4,176,768]{2,1,0:T(8,128)(2,1)S(1)} %all-to-all-done.refs_2_, ...), custom_call_target="tpu_custom_call" | custom-call | flops 1 | bytes 1 | tf_op jit(solution)/shard_map/temporal/pallas_call | solution.py:684
  48.5 1.1 %collective-permute-start.6 = (bf16[64,768]{1,0:T(8,128)(2,1)S(1)}, bf16[64,768]{1,0:T(8,128)(2,1)S(1)}, u32[]{:S(2)}, u32[]{:S(2)}) collective-permute-start(bf16[64,768]{1,0:T(8,128)(2,1)S(1)} %get-tuple-element.44), channel_id=1, source_target_pairs={{0,8},{8,0},{16,24},{24,16},{1,9},{9,1},{17,25},{25,17},{2,10},{10... | collective-permute-start | bytes 294920 | tf_op jit(solution)/shard_map/ppermute | solution.py:584
  49.7 1.0 %collective-permute-start.7 = (bf16[64,768]{1,0:T(8,128)(2,1)S(1)}, bf16[64,768]{1,0:T(8,128)(2,1)S(1)}, u32[]{:S(2)}, u32[]{:S(2)}) collective-permute-start(bf16[64,768]{1,0:T(8,128)(2,1)S(1)} %get-tuple-element.45), channel_id=1, source_target_pairs={{0,16},{8,24},{16,0},{24,8},{1,17},{9,25},{17,1},{25,9},{2,18},{10... | collective-permute-start | bytes 294920 | tf_op jit(solution)/shard_map/ppermute | solution.py:584
  50.6 2.4 %collective-permute-start.8 = (bf16[64,768]{1,0:T(8,128)(2,1)S(1)}, bf16[64,768]{1,0:T(8,128)(2,1)S(1)}, u32[]{:S(2)}, u32[]{:S(2)}) collective-permute-start(bf16[64,768]{1,0:T(8,128)(2,1)S(1)} %get-tuple-element.46), channel_id=1, source_target_pairs={{0,24},{8,16},{16,8},{24,0},{1,25},{9,17},{17,9},{25,1},{2,26},{10... | collective-permute-start | bytes 294920 | tf_op jit(solution)/shard_map/ppermute | solution.py:584
  53.0 2.3 %copy-done.2 = bf16[1536,1536]{1,0:T(8,128)(2,1)S(1)} copy-done((bf16[1536,1536]{1,0:T(8,128)(2,1)S(1)}, bf16[1536,1536]{1,0:T(8,128)(2,1)}, u32[]{:S(2)}) %copy-start.2) | copy-done | bytes 4718616
  55.4 1.4 %copy-done.7 = f32[256,1536]{1,0:T(8,128)S(1)} copy-done((f32[256,1536]{1,0:T(8,128)S(1)}, f32[256,1536]{1,0:T(8,128)}, u32[]{:S(2)}) %copy-start.7) | copy-done | bytes 1572888
  56.8 1.1 %spatial_incoming.1 = (f32[256,1536]{1,0:T(8,128)S(1)}, bf16[1536,1536]{1,0:T(8,128)(2,1)S(1)}) custom-call(s32[1]{0:T(128)} %bitcast.1.refs_1_.band, f32[256,1536]{1,0:T(8,128)S(1)} %copy-done.7, bf16[256,256]{1,0:T(8,128)(2,1)S(1)} %copy-done.10, f32[256,128]{1,0:T(8,128)S(1)} %get-tuple-element.34._.reach, bf16[128,1536]{1,0:T(8,128)(2,1)S(1)} %get-tuple-element.38.own, ...), custom_call_target="tpu_custom_call" | custom-call | flops 1 | bytes 1 | tf_op jit(solution)/shard_map/spatial_incoming/pallas_call | solution.py:754
  57.9 2.0 %exit.2.refs_9_ = bf16[2,2,64,1536]{3,2,1,0:T(8,128)(2,1)} custom-call(s32[1]{0:T(128)} %bitcast.refs_0_, f32[256,1536]{1,0:T(8,128)S(1)} %get-tuple-element.40.refs_1_, bf16[256,1536]{1,0:T(8,128)(2,1)S(1)} %gate.1.refs_0_.refs_2_, f32[1536]{0:T(1024)S(1)} %copy-done.13, bf16[1536,1536]{1,0:T(8,128)(2,1)S(1)} %get-tuple-element.41.refs_4_, ...), custom_call_target="tpu_custom_call" | custom-call | flops 1 | bytes 1 | tf_op jit(solution)/shard_map/exit/pallas_call | solution.py:765
  59.9 2.2 %collective-permute-done.7.refs_7_ = bf16[64,768]{1,0:T(8,128)(2,1)S(1)} collective-permute-done((bf16[64,768]{1,0:T(8,128)(2,1)S(1)}, bf16[64,768]{1,0:T(8,128)(2,1)S(1)}, u32[]{:S(2)}, u32[]{:S(2)}) %collective-permute-start.7) | collective-permute-done | bytes 98336 | tf_op jit(solution)/shard_map/ppermute | solution.py:584
  62.1 2.0 %exit.3 = bf16[2,2,64,1536]{3,2,1,0:T(8,128)(2,1)} custom-call(s32[1]{0:T(128)} %bitcast.refs_0_, f32[256,1536]{1,0:T(8,128)S(1)} %get-tuple-element.40.refs_1_, bf16[256,1536]{1,0:T(8,128)(2,1)S(1)} %gate.1.refs_0_.refs_2_, f32[1536]{0:T(1024)S(1)} %copy-done.13, bf16[1536,1536]{1,0:T(8,128)(2,1)S(1)} %get-tuple-element.41.refs_4_, ...), custom_call_target="tpu_custom_call", output_to_operand_aliasing={{}: (9, {})} | custom-call | flops 1 | bytes 1 | tf_op jit(solution)/shard_map/exit/pallas_call | solution.py:765
  (41 shorter events, 1.6 us)
Async XLA Ops:
  7.4 6.6 %copy-start.3 = (bf16[144,1536]{1,0:T(8,128)(2,1)S(1)}, bf16[144,1536]{1,0:T(8,128)(2,1)}, u32[]{:S(2)}) copy-start(bf16[144,1536]{1,0:T(8,128)(2,1)} %get-tuple-element.35.own.band_own) | copy-start | bytes 1327108
  7.5 6.6 %collective-permute-start = (bf16[144,1536]{1,0:T(8,128)(2,1)}, bf16[144,1536]{1,0:T(8,128)(2,1)S(1)}, u32[]{:S(2)}, u32[]{:S(2)}) collective-permute-start(bf16[144,1536]{1,0:T(8,128)(2,1)} %get-tuple-element.36), channel_id=1, source_target_pairs={{0,1},{1,0},{2,3},{3,2},{4,5},{5,4},{6,7},{7,6},{8,9},{9,8},{10,11... | collective-permute-start | bytes 1327112 | tf_op jit(solution)/shard_map/ppermute | solution.py:584
  8.0 10.3 %copy-start.1 = (bf16[4,176,768]{2,1,0:T(8,128)(2,1)S(1)}, bf16[4,176,768]{2,1,0:T(8,128)(2,1)}, u32[]{:S(2)}) copy-start(bf16[4,176,768]{2,1,0:T(8,128)(2,1)} %get-tuple-element.28.after.refs_4_) | copy-start | bytes 3244036
  8.0 29.4 %all-to-all-start = ((bf16[4,176,768]{2,1,0:T(8,128)(2,1)}), bf16[4,176,768]{2,1,0:T(8,128)(2,1)S(1)}, u32[]{:S(2)}, u32[]{:S(2)}) async-start(bf16[4,176,768]{2,1,0:T(8,128)(2,1)} %get-tuple-element.28.after.refs_4_), calls=%async_computation | async-start | bytes 2162688 | tf_op jit(solution)/shard_map/all_to_all | solution.py:648
  14.0 4.2 %copy-start.8 = (bf16[256,1536]{1,0:T(8,128)(2,1)S(1)}, bf16[256,1536]{1,0:T(8,128)(2,1)}, u32[]{:S(2)}) copy-start(bf16[256,1536]{1,0:T(8,128)(2,1)} %get-tuple-element.29.normed) | copy-start | bytes 2359300
  14.0 4.2 %copy-start.4 = (bf16[144,1536]{1,0:T(8,128)(2,1)}, bf16[144,1536]{1,0:T(8,128)(2,1)S(1)}, u32[]{:S(2)}) copy-start(bf16[144,1536]{1,0:T(8,128)(2,1)S(1)} %collective-permute-done.far.band_far) | copy-start | bytes 1327108
  14.2 13.5 %collective-permute-start.1 = (bf16[144,1536]{1,0:T(8,128)(2,1)S(1)}, bf16[144,1536]{1,0:T(8,128)(2,1)S(1)}, u32[]{:S(2)}, u32[]{:S(2)}) collective-permute-start(bf16[144,1536]{1,0:T(8,128)(2,1)S(1)} %pair_total.1.total), channel_id=1, source_target_pairs={{0,2},{1,5},{2,0},{3,7},{4,6},{5,1},{6,4},{7,3},{8,10},{9,13},{10,... | collective-permute-start | bytes 1327112 | tf_op jit(solution)/shard_map/ppermute | solution.py:590
  15.8 11.9 %collective-permute-start.3 = (bf16[16,1536]{1,0:T(8,128)(2,1)}, bf16[16,1536]{1,0:T(8,128)(2,1)S(1)}, u32[]{:S(2)}, u32[]{:S(2)}) collective-permute-start(bf16[16,1536]{1,0:T(8,128)(2,1)} %get-tuple-element.37), channel_id=1, source_target_pairs={{0,7},{1,6},{2,5},{3,4},{4,3},{5,2},{6,1},{7,0},{8,15},{9,14},{10,... | collective-permute-start | bytes 147464 | tf_op jit(solution)/shard_map/ppermute | solution.py:584
  16.8 10.9 %collective-permute-start.2 = (bf16[16,1536]{1,0:T(8,128)(2,1)}, bf16[16,1536]{1,0:T(8,128)(2,1)S(1)}, u32[]{:S(2)}, u32[]{:S(2)}) collective-permute-start(bf16[16,1536]{1,0:T(8,128)(2,1)} %get-tuple-element.37), channel_id=1, source_target_pairs={{0,6},{1,7},{2,4},{3,5},{4,2},{5,3},{6,0},{7,1},{8,14},{9,15},{10,... | collective-permute-start | bytes 147464 | tf_op jit(solution)/shard_map/ppermute | solution.py:584
  18.3 3.7 %copy-start = (bf16[1536,3072]{1,0:T(8,128)(2,1)S(1)}, bf16[1536,3072]{1,0:T(8,128)(2,1)}, u32[]{:S(2)}) copy-start(bf16[1536,3072]{1,0:T(8,128)(2,1)} %weight.2) | copy-start | bytes 28311556
  21.9 2.6 %copy-start.9 = (bf16[256,256]{1,0:T(8,128)(2,1)S(1)}, bf16[256,256]{1,0:T(8,128)(2,1)}, u32[]{:S(2)}) copy-start(bf16[256,256]{1,0:T(8,128)(2,1)} %get-tuple-element.30.refs_1_.bc) | copy-start | bytes 393220
  21.9 2.6 %copy-start.11 = (f32[256,128]{1,0:T(8,128)S(1)}, f32[256,128]{1,0:T(8,128)}, u32[]{:S(2)}) copy-start(f32[256,128]{1,0:T(8,128)} %get-tuple-element.31.refs_2_) | copy-start | bytes 393220
  21.9 2.6 %copy-start.12 = (f32[16,128]{1,0:T(8,128)S(1)}, f32[16,128]{1,0:T(8,128)}, u32[]{:S(2)}) copy-start(f32[16,128]{1,0:T(8,128)} %get-tuple-element.32.refs_3_.refs_1_) | copy-start | bytes 24580
  24.6 11.7 %copy-start.5 = (bf16[144,1536]{1,0:T(8,128)(2,1)S(1)}, bf16[144,1536]{1,0:T(8,128)(2,1)}, u32[]{:S(2)}) copy-start(bf16[144,1536]{1,0:T(8,128)(2,1)} %copy-done.4) | copy-start | bytes 1327108
  27.9 8.4 %collective-permute-start.4 = (bf16[144,1536]{1,0:T(8,128)(2,1)S(1)}, bf16[144,1536]{1,0:T(8,128)(2,1)S(1)}, u32[]{:S(2)}, u32[]{:S(2)}) collective-permute-start(bf16[144,1536]{1,0:T(8,128)(2,1)S(1)} %cross.1), channel_id=1, source_target_pairs={{0,4},{1,3},{2,6},{3,1},{4,0},{5,7},{6,2},{7,5},{8,12},{9,11},{10,... | collective-permute-start | bytes 1327112 | tf_op jit(solution)/shard_map/ppermute | solution.py:590
  37.3 15.7 %copy-start.10 = (bf16[256,256]{1,0:T(8,128)(2,1)S(1)}, bf16[256,256]{1,0:T(8,128)(2,1)}, u32[]{:S(2)}) copy-start(bf16[256,256]{1,0:T(8,128)(2,1)} %get-tuple-element.30.refs_1_.bc) | copy-start | bytes 393220
  37.3 13.3 %collective-permute-start.5 = (bf16[128,1536]{1,0:T(8,128)(2,1)}, bf16[128,1536]{1,0:T(8,128)(2,1)S(1)}, u32[]{:S(2)}, u32[]{:S(2)}) collective-permute-start(bf16[128,1536]{1,0:T(8,128)(2,1)} %get-tuple-element.39), channel_id=1, source_target_pairs={{0,1},{1,0},{2,3},{3,2},{4,5},{5,4},{6,7},{7,6},{8,9},{9,8},{10,11... | collective-permute-start | bytes 1179656 | tf_op jit(solution)/shard_map/ppermute | solution.py:584
  39.6 10.0 %collective-permute-start.9 = (bf16[64,768]{1,0:T(8,128)(2,1)S(1)}, bf16[64,768]{1,0:T(8,128)(2,1)S(1)}, u32[]{:S(2)}, u32[]{:S(2)}) collective-permute-start(bf16[64,768]{1,0:T(8,128)(2,1)S(1)} %get-tuple-element.48), channel_id=1, source_target_pairs={{0,8},{8,0},{16,24},{24,16},{1,9},{9,1},{17,25},{25,17},{2,10},{10... | collective-permute-start | bytes 294920 | tf_op jit(solution)/shard_map/ppermute | solution.py:584
  44.0 13.8 %collective-permute-start.10 = (bf16[64,768]{1,0:T(8,128)(2,1)S(1)}, bf16[64,768]{1,0:T(8,128)(2,1)S(1)}, u32[]{:S(2)}, u32[]{:S(2)}) collective-permute-start(bf16[64,768]{1,0:T(8,128)(2,1)S(1)} %get-tuple-element.49), channel_id=1, source_target_pairs={{0,16},{8,24},{16,0},{24,8},{1,17},{9,25},{17,1},{25,9},{2,18},{10... | collective-permute-start | bytes 294920 | tf_op jit(solution)/shard_map/ppermute | solution.py:584
  44.1 13.8 %collective-permute-start.11 = (bf16[64,768]{1,0:T(8,128)(2,1)S(1)}, bf16[64,768]{1,0:T(8,128)(2,1)S(1)}, u32[]{:S(2)}, u32[]{:S(2)}) collective-permute-start(bf16[64,768]{1,0:T(8,128)(2,1)S(1)} %get-tuple-element.50), channel_id=1, source_target_pairs={{0,24},{8,16},{16,8},{24,0},{1,25},{9,17},{17,9},{25,1},{2,26},{10... | collective-permute-start | bytes 294920 | tf_op jit(solution)/shard_map/ppermute | solution.py:584
  48.5 11.3 %collective-permute-start.6 = (bf16[64,768]{1,0:T(8,128)(2,1)S(1)}, bf16[64,768]{1,0:T(8,128)(2,1)S(1)}, u32[]{:S(2)}, u32[]{:S(2)}) collective-permute-start(bf16[64,768]{1,0:T(8,128)(2,1)S(1)} %get-tuple-element.44), channel_id=1, source_target_pairs={{0,8},{8,0},{16,24},{24,16},{1,9},{9,1},{17,25},{25,17},{2,10},{10... | collective-permute-start | bytes 294920 | tf_op jit(solution)/shard_map/ppermute | solution.py:584
  49.7 12.4 %collective-permute-start.7 = (bf16[64,768]{1,0:T(8,128)(2,1)S(1)}, bf16[64,768]{1,0:T(8,128)(2,1)S(1)}, u32[]{:S(2)}, u32[]{:S(2)}) collective-permute-start(bf16[64,768]{1,0:T(8,128)(2,1)S(1)} %get-tuple-element.45), channel_id=1, source_target_pairs={{0,16},{8,24},{16,0},{24,8},{1,17},{9,25},{17,1},{25,9},{2,18},{10... | collective-permute-start | bytes 294920 | tf_op jit(solution)/shard_map/ppermute | solution.py:584
  50.6 11.4 %collective-permute-start.8 = (bf16[64,768]{1,0:T(8,128)(2,1)S(1)}, bf16[64,768]{1,0:T(8,128)(2,1)S(1)}, u32[]{:S(2)}, u32[]{:S(2)}) collective-permute-start(bf16[64,768]{1,0:T(8,128)(2,1)S(1)} %get-tuple-element.46), channel_id=1, source_target_pairs={{0,24},{8,16},{16,8},{24,0},{1,25},{9,17},{17,9},{25,1},{2,26},{10... | collective-permute-start | bytes 294920 | tf_op jit(solution)/shard_map/ppermute | solution.py:584
  53.0 2.3 %copy-start.2 = (bf16[1536,1536]{1,0:T(8,128)(2,1)S(1)}, bf16[1536,1536]{1,0:T(8,128)(2,1)}, u32[]{:S(2)}) copy-start(bf16[1536,1536]{1,0:T(8,128)(2,1)} %weight.3) | copy-start | bytes 14155780
  (3 other events, 3.7 us)

commit v6 on v5

--- a/solution.py
+++ b/solution.py
@@ -311,7 +311,7 @@
             mixed = head_mixes(
                 scores, running, running_t, dt_t, values, piece * per_group, per_group, head_dim
             )
-            stored(out, mixed, frame, slice(piece * group, (piece + 1) * group))
+            stored(out, mixed.astype(BF16), frame, slice(piece * group, (piece + 1) * group))
 
 
 def tail_of(decays):
@@ -426,11 +426,7 @@
         give[at, :] = jnp.where(even, after, before).astype(BF16)
 
 
-def incoming_kernel(
-    frames, rows, columns, head_dim, band, out_local, bc, reach, own, other, weight, out, held, sem
-):
-    fetch = pltpu.make_async_copy(weight, held, sem)
-    fetch.start()
+def incoming_kernel(frames, rows, columns, head_dim, band, out_local, bc, reach, own, other, out):
     state = bc.shape[1] // 2
     half = state // 2
     inner = out.shape[1]
@@ -445,8 +441,7 @@
             to = (row * frames + frame) * columns
             here = slice(to, to + columns)
             factor = spread(reach[here, :], matrix)
-            out[here, :] = out_local[here, :] + factor * dot(bc[here, state:], carried)
-    fetch.wait()
+            out[here, :] = out_local[here, :].astype(F32) + factor * dot(bc[here, state:], carried)
 
 
 def temporal_kernel(
@@ -455,6 +450,7 @@
     here_ref, params, payload = refs[:3]
     rest = list(refs[3:])
     carried_in = rest.pop(0) if part > 0 else None
+    del rest[:part]
     outs, rest = rest[:shares], rest[shares:]
     carried_out = rest.pop(0) if part + 1 < parts else None
     b_all, c_all, dt_all, decay_all = rest
@@ -536,8 +532,9 @@
     _, part_len, group = temporal.shape
     groups = shares // rows
     inner = groups * group
-    for distance in range(shares):
-        temporal[here[0] ^ distance] = refs[5 + distance][...]
+    for index in range(shares):
+        distance = (shares - index) % shares
+        temporal[here[0] ^ distance] = refs[5 + index][...]
 
     def own(ref, row, at):
         return jnp.concatenate(
@@ -642,7 +639,8 @@
     )(here, band, tokens, norm_gain, dt_bias, decay_rate, dt_weight.T, bc_weight, in_weight)
 
     def sent(parts):
-        return [parts[0]] + [swapped(parts[d], "tm", d) for d in range(1, shares)]
+        moved = {d: swapped(parts[d], "tm", d) for d in range(shares - 1, 0, -1)}
+        return [parts[0]] + list(moved.values())
 
     line = [rank_of(device) for device in range(shares)]
     received = lax.all_to_all(
@@ -668,7 +666,7 @@
     out_local, reach = call(
         functools.partial(local_kernel, frames, rows, columns, head_dim, groups),
         "spatial_local",
-        [shape_of((count, inner), F32), shape_of((count, LANES), F32)],
+        [shape_of((count, inner), BF16), shape_of((count, LANES), F32)],
         [ANY] + [WHOLE] * 4,
     )(gate, bc_own, logits, params, payload)
 
@@ -678,36 +676,6 @@
         shape_of((frames * half + TAIL, inner), BF16),
         [SCALAR, WHOLE, WHOLE],
     )(band, own, far)
-    returned, carried = [], []
-    for part in range(parts):
-        more = [shape_of((state, group), F32)] if part + 1 < parts else []
-        results = call(
-            functools.partial(
-                temporal_kernel,
-                part,
-                parts,
-                per_group,
-                head_dim,
-                rows,
-                frames,
-                columns,
-                chunk_cols,
-                shares,
-                state,
-            ),
-            "temporal",
-            [shape_of((part_len, group), BF16)] * shares + more,
-            [SCALAR] + [WHOLE] * (2 + len(carried)),
-            scratch_shapes=[
-                pltpu.VMEM((shares, part_len, state), BF16),
-                pltpu.VMEM((shares, part_len, state), BF16),
-                pltpu.VMEM((shares, part_len, LANES), F32),
-                pltpu.VMEM((shares, part_len, LANES), F32),
-            ],
-        )(here, params, received, *carried)
-        returned.append(sent(results[:shares]))
-        carried = results[shares:]
-
     before = []
     distance = 2
     if bands == 8:
@@ -751,13 +719,42 @@
     keep, give = results
     came = swapped(give, "height", 1)
 
-    spatial_out, held_weight = call(
+    spatial_out = call(
         functools.partial(incoming_kernel, frames, rows, columns, head_dim),
         "spatial_incoming",
-        [shape_of((count, inner), F32), shape_of((inner, width), BF16)],
-        [SCALAR] + [WHOLE] * 5 + [HBM],
-        scratch_shapes=[pltpu.SemaphoreType.DMA],
-    )(band, out_local, bc_own, reach, keep, came, out_weight)
+        shape_of((count, inner), F32),
+        [SCALAR] + [WHOLE] * 5,
+    )(band, out_local, bc_own, reach, keep, came)
+
+    returned, carried = [], []
+    for part in range(parts):
+        more = [shape_of((state, group), F32)] if part + 1 < parts else []
+        results = call(
+            functools.partial(
+                temporal_kernel,
+                part,
+                parts,
+                per_group,
+                head_dim,
+                rows,
+                frames,
+                columns,
+                chunk_cols,
+                shares,
+                state,
+            ),
+            "temporal",
+            [shape_of((part_len, group), BF16)] * shares + more,
+            [SCALAR] + [WHOLE] * (2 + len(carried)) + [ANY] * part,
+            scratch_shapes=[
+                pltpu.VMEM((shares, part_len, state), BF16),
+                pltpu.VMEM((shares, part_len, state), BF16),
+                pltpu.VMEM((shares, part_len, LANES), F32),
+                pltpu.VMEM((shares, part_len, LANES), F32),
+            ],
+        )(here, params, received, *carried, *([spatial_out] * part))
+        returned.append(sent(results[:shares]))
+        carried = results[shares:]
 
     mixed = []
     for part in range(parts):
@@ -775,7 +772,7 @@
                     pltpu.SemaphoreType.DMA((rows * frames,)),
                 ],
                 input_output_aliases={5 + shares: 0} if mixed else {},
-            )(here, spatial_out, gate, out_gain, held_weight, *returned[part], *mixed)
+            )(here, spatial_out, gate, out_gain, out_weight, *returned[part], *mixed)
         ]
     return mixed[0]
 

time: 64.5 us -> 63.9 us (level)
  local copies, waits for them, and re-layouts: 8.64 us -> 7.84 us
  Pallas kernels: 22.7 us -> 23.4 us
  starting transfers between devices: 22.5 us -> 21.8 us
    unnamed x28 -> x32, local copies, waits for them, and re-layouts: 8.64 us -> 7.84 us
    pallas_call x1, Pallas kernels: 1.08 us -> 1.75 us  [per_device(): call(functools.partial(incoming_kernel, frames, rows, columns, head_dim),...]
    ppermute x10, starting transfers between devices: 14.3 us -> 13.6 us  [swapped(): lax.ppermute(value, axis, [(source, source ^ distance) for source in rang...]
  transfers between devices with their start and end apart: 13 -> 13, of which waited for: 2 -> 2; matrix products, arithmetic and copies ran while one was open for 0% -> 0% of each run, Pallas kernels for 21% -> 22%
where the time goes in v6:
time: 63.9 us; the launch traced here: 63.6 us
  Pallas kernels  23.4 us (37%)
  starting transfers between devices  21.8 us (34%)
  waiting for transfers between devices  10.1 us (16%)
  local copies, waits for them, and re-layouts  7.84 us (12%)
    ppermute x10, starting transfers between devices, swapped(): lax.ppermute(value, axis, [(source, source ^ distance) for source in rang...  13.6 us
    unnamed x32, local copies, waits for them, and re-layouts  7.84 us
    ppermute x2, waiting for transfers between devices, crossed(): return lax.ppermute(value, axis, pairs)  7.79 us
    pallas_call x1, Pallas kernels, per_device(): call(functools.partial(entry_kernel, shares, heads, state, blocks), 'entr...  7.42 us
    all_to_all x1, starting transfers between devices, per_device(): lax.all_to_all(payload, 'tm', split_axis=0, concat_axis=0, tiled=True, ax...  6.03 us
    pallas_call x2, Pallas kernels, per_device(): call(functools.partial(temporal_kernel, part, parts, per_group, head_dim,...  4.35 us
    pallas_call x2, Pallas kernels, per_device(): call(functools.partial(exit_kernel, part, parts, shares), 'exit', shape_o...  3.92 us
    pallas_call x1, Pallas kernels, per_device(): call(functools.partial(gate_kernel, blocks), 'gate', shape_of((count, inn...  2.59 us
  transfers between devices with their start and end apart: 13, of which 2 were waited for; matrix products, arithmetic and copies ran while one was open for 0% of the time, Pallas kernels for 22%

profile of v6, /device:TPU:0, one launch (start us, length us, event | category | flops | bytes accessed | tf_op | source)
XLA Modules:
  0.0 63.6 jit_solution(3621087022340132596)
XLA Ops:
  0.0 7.4 %entry.1 = (bf16[256,1536]{1,0:T(8,128)(2,1)}, bf16[4,176,768]{2,1,0:T(8,128)(2,1)}, bf16[256,256]{1,0:T(8,128)(2,1)}, f32[256,128]{1,0:T(8,128)}, f32[16,128]{1...) custom-call(s32[1]{0:T(128)} %bitcast.refs_0_, ...), custom_call_target="tpu_custom_call" | custom-call | flops 1 | bytes 1 | tf_op jit(solution)/shard_map/entry/pallas_call | solution.py:613
  8.0 6.0 %all-to-all-start = ((bf16[4,176,768]{2,1,0:T(8,128)(2,1)}), bf16[4,176,768]{2,1,0:T(8,128)(2,1)S(1)}, u32[]{:S(2)}, u32[]{:S(2)}) async-start(bf16[4,176,768]{2,1,0:T(8,128)(2,1)} %get-tuple-element.26.after.refs_4_), calls=%async_computation | async-start | bytes 2162688 | tf_op jit(solution)/shard_map/all_to_all | solution.py:646
  14.2 1.6 %collective-permute-start.1 = (bf16[144,1536]{1,0:T(8,128)(2,1)S(1)}, bf16[144,1536]{1,0:T(8,128)(2,1)S(1)}, u32[]{:S(2)}, u32[]{:S(2)}) collective-permute-start(bf16[144,1536]{1,0:T(8,128)(2,1)S(1)} %pair_total.1.total), channel_id=1, source_target_pairs={{0,2},{1,5},{2,0},{3,7},{4,6},{5,1},{6,4},{7,3},{8,10},{9,13},{10,... | collective-permute-start | bytes 1327112 | tf_op jit(solution)/shard_map/ppermute | solution.py:587
  15.8 1.5 %collective-permute-start.2 = (bf16[16,1536]{1,0:T(8,128)(2,1)}, bf16[16,1536]{1,0:T(8,128)(2,1)S(1)}, u32[]{:S(2)}, u32[]{:S(2)}) collective-permute-start(bf16[16,1536]{1,0:T(8,128)(2,1)} %get-tuple-element.35), channel_id=1, source_target_pairs={{0,6},{1,7},{2,4},{3,5},{4,2},{5,3},{6,0},{7,1},{8,14},{9,15},{10,... | collective-permute-start | bytes 147464 | tf_op jit(solution)/shard_map/ppermute | solution.py:581
  17.3 0.7 %collective-permute-start.3 = (bf16[16,1536]{1,0:T(8,128)(2,1)}, bf16[16,1536]{1,0:T(8,128)(2,1)S(1)}, u32[]{:S(2)}, u32[]{:S(2)}) collective-permute-start(bf16[16,1536]{1,0:T(8,128)(2,1)} %get-tuple-element.35), channel_id=1, source_target_pairs={{0,7},{1,6},{2,5},{3,4},{4,3},{5,2},{6,1},{7,0},{8,15},{9,14},{10,... | collective-permute-start | bytes 147464 | tf_op jit(solution)/shard_map/ppermute | solution.py:581
  18.0 3.7 %copy-done = bf16[1536,3072]{1,0:T(8,128)(2,1)S(1)} copy-done((bf16[1536,3072]{1,0:T(8,128)(2,1)S(1)}, bf16[1536,3072]{1,0:T(8,128)(2,1)}, u32[]{:S(2)}) %copy-start) | copy-done | bytes 9437208
  21.7 2.6 %gate.1.refs_0_.refs_2_ = bf16[256,1536]{1,0:T(8,128)(2,1)S(1)} custom-call(bf16[4,176,768]{2,1,0:T(8,128)(2,1)S(1)} %copy-done.2, bf16[256,1536]{1,0:T(8,128)(2,1)S(1)} %copy-done.6, bf16[1536,3072]{1,0:T(8,128)(2,1)S(1)} %copy-done), custom_call_target="tpu_custom_call" | custom-call | flops 1 | bytes 1 | tf_op jit(solution)/shard_map/gate/pallas_call | solution.py:655
  24.3 1.9 %spatial_local.1 = (bf16[256,1536]{1,0:T(8,128)(2,1)S(1)}, f32[256,128]{1,0:T(8,128)S(1)}) custom-call(bf16[256,1536]{1,0:T(8,128)(2,1)S(1)} %gate.1.refs_0_.refs_2_, bf16[256,256]{1,0:T(8,128)(2,1)S(1)} %copy-done.9, f32[256,128]{1,0:T(8,128)S(1)} %copy-done.13, f32[16,128]{1,0:T(8,128)S(1)} %copy-done.14, bf16[4,176,768]{2,1,0:T(8,128)(2,1)S(1)} %copy-done.2), custom_call_target="tpu_custom_call" | custom-call | flops 1 | bytes 1 | tf_op jit(solution)/shard_map/spatial_local/pallas_call | solution.py:666
  27.0 7.8 %collective-permute-done.4.second = bf16[144,1536]{1,0:T(8,128)(2,1)S(1)} collective-permute-done((bf16[144,1536]{1,0:T(8,128)(2,1)S(1)}, bf16[144,1536]{1,0:T(8,128)(2,1)S(1)}, u32[]{:S(2)}, u32[]{:S(2)}) %collective-permute-start.4) | collective-permute-done | bytes 442400 | tf_op jit(solution)/shard_map/ppermute | solution.py:587
  34.8 1.1 %settle.1 = (bf16[128,1536]{1,0:T(8,128)(2,1)S(1)}, bf16[128,1536]{1,0:T(8,128)(2,1)}) custom-call(f32[256,128]{1,0:T(8,128)S(1)} %get-tuple-element.32._.reach, s32[1]{0:T(128)} %bitcast.1.refs_1_.band, bf16[144,1536]{1,0:T(8,128)(2,1)S(1)} %collective-permute-done.1.first, bf16[144,1536]{1,0:T(8,128)(2,1)S(1)} %collective-permute-done.4.second, ...), custom_call_target="tpu_custom_call" | custom-call | flops 1 | bytes 1 | tf_op jit(solution)/shard_map/settle/pallas_call | solution.py:691
  35.9 0.8 %copy-done.11 = bf16[128,1536]{1,0:T(8,128)(2,1)} copy-done((bf16[128,1536]{1,0:T(8,128)(2,1)}, bf16[128,1536]{1,0:T(8,128)(2,1)S(1)}, u32[]{:S(2)}) %copy-start.11) | copy-done | bytes 393240
  36.7 2.3 %temporal.2 = (bf16[64,768]{1,0:T(8,128)(2,1)S(1)}, bf16[64,768]{1,0:T(8,128)(2,1)S(1)}, bf16[64,768]{1,0:T(8,128)(2,1)S(1)}, bf16[64,768]{1,0:T(8,128)(2,1)S(1)}, f32[128,768]{1,0:T(8,128)S(1)}) custom-call(s32[1]{0:T(128)} %bitcast.refs_0_, f32[16,128]{1,0:T(8,128)S(1)} %copy-done.14, bf16[4,176,768]{2,1,0:T(8,128)(2,1)S(1)} %all-to-all-done.refs_2_), custom_call_target="tpu_custom_call" | custom-call | flops 1 | bytes 1 | tf_op jit(solution)/shard_map/temporal/pallas_call | solution.py:732
  39.0 3.7 %collective-permute-start.9 = (bf16[64,768]{1,0:T(8,128)(2,1)S(1)}, bf16[64,768]{1,0:T(8,128)(2,1)S(1)}, u32[]{:S(2)}, u32[]{:S(2)}) collective-permute-start(bf16[64,768]{1,0:T(8,128)(2,1)S(1)} %get-tuple-element.44), channel_id=1, source_target_pairs={{0,24},{8,16},{16,8},{24,0},{1,25},{9,17},{17,9},{25,1},{2,26},{10... | collective-permute-start | bytes 294920 | tf_op jit(solution)/shard_map/ppermute | solution.py:581
  42.7 2.8 %collective-permute-start.10 = (bf16[64,768]{1,0:T(8,128)(2,1)S(1)}, bf16[64,768]{1,0:T(8,128)(2,1)S(1)}, u32[]{:S(2)}, u32[]{:S(2)}) collective-permute-start(bf16[64,768]{1,0:T(8,128)(2,1)S(1)} %get-tuple-element.45), channel_id=1, source_target_pairs={{0,16},{8,24},{16,0},{24,8},{1,17},{9,25},{17,1},{25,9},{2,18},{10... | collective-permute-start | bytes 294920 | tf_op jit(solution)/shard_map/ppermute | solution.py:581
  45.5 1.0 %copy-done.12 = bf16[128,1536]{1,0:T(8,128)(2,1)S(1)} copy-done((bf16[128,1536]{1,0:T(8,128)(2,1)S(1)}, bf16[128,1536]{1,0:T(8,128)(2,1)}, u32[]{:S(2)}) %copy-start.12) | copy-done | bytes 393240
  46.5 1.8 %spatial_incoming.1.refs_4_.refs_1_ = f32[256,1536]{1,0:T(8,128)S(1)} custom-call(s32[1]{0:T(128)} %bitcast.1.refs_1_.band, bf16[256,1536]{1,0:T(8,128)(2,1)S(1)} %copy-done.8, bf16[256,256]{1,0:T(8,128)(2,1)S(1)} %copy-done.10, f32[256,128]{1,0:T(8,128)S(1)} %get-tuple-element.32._.reach, bf16[128,1536]{1,0:T(8,128)(2,1)S(1)} %copy-done.12, ...), custom_call_target="tpu_custom_call" | custom-call | flops 1 | bytes 1 | tf_op jit(solution)/shard_map/spatial_incoming/pallas_call | solution.py:722
  48.3 2.1 %temporal.3 = (bf16[64,768]{1,0:T(8,128)(2,1)S(1)}, bf16[64,768]{1,0:T(8,128)(2,1)S(1)}, bf16[64,768]{1,0:T(8,128)(2,1)S(1)}, bf16[64,768]{1,0:T(8,128)(2,1)S(1)}) custom-call(s32[1]{0:T(128)} %bitcast.refs_0_, f32[16,128]{1,0:T(8,128)S(1)} %copy-done.14, bf16[4,176,768]{2,1,0:T(8,128)(2,1)S(1)} %all-to-all-done.refs_2_, ...), custom_call_target="tpu_custom_call" | custom-call | flops 1 | bytes 1 | tf_op jit(solution)/shard_map/temporal/pallas_call | solution.py:732
  50.4 1.7 %collective-permute-start.6 = (bf16[64,768]{1,0:T(8,128)(2,1)S(1)}, bf16[64,768]{1,0:T(8,128)(2,1)S(1)}, u32[]{:S(2)}, u32[]{:S(2)}) collective-permute-start(bf16[64,768]{1,0:T(8,128)(2,1)S(1)} %get-tuple-element.40), channel_id=1, source_target_pairs={{0,24},{8,16},{16,8},{24,0},{1,25},{9,17},{17,9},{25,1},{2,26},{10... | collective-permute-start | bytes 294920 | tf_op jit(solution)/shard_map/ppermute | solution.py:581
  52.0 1.9 %collective-permute-start.7 = (bf16[64,768]{1,0:T(8,128)(2,1)S(1)}, bf16[64,768]{1,0:T(8,128)(2,1)S(1)}, u32[]{:S(2)}, u32[]{:S(2)}) collective-permute-start(bf16[64,768]{1,0:T(8,128)(2,1)S(1)} %get-tuple-element.41), channel_id=1, source_target_pairs={{0,16},{8,24},{16,0},{24,8},{1,17},{9,25},{17,1},{25,9},{2,18},{10... | collective-permute-start | bytes 294920 | tf_op jit(solution)/shard_map/ppermute | solution.py:581
  53.9 0.9 %collective-permute-start.8 = (bf16[64,768]{1,0:T(8,128)(2,1)S(1)}, bf16[64,768]{1,0:T(8,128)(2,1)S(1)}, u32[]{:S(2)}, u32[]{:S(2)}) collective-permute-start(bf16[64,768]{1,0:T(8,128)(2,1)S(1)} %get-tuple-element.42), channel_id=1, source_target_pairs={{0,8},{8,0},{16,24},{24,16},{1,9},{9,1},{17,25},{25,17},{2,10},{10... | collective-permute-start | bytes 294920 | tf_op jit(solution)/shard_map/ppermute | solution.py:581
  54.8 2.3 %copy-done.1 = bf16[1536,1536]{1,0:T(8,128)(2,1)S(1)} copy-done((bf16[1536,1536]{1,0:T(8,128)(2,1)S(1)}, bf16[1536,1536]{1,0:T(8,128)(2,1)}, u32[]{:S(2)}) %copy-start.1) | copy-done | bytes 4718616
  57.2 2.0 %exit.2.refs_9_ = bf16[2,2,64,1536]{3,2,1,0:T(8,128)(2,1)} custom-call(s32[1]{0:T(128)} %bitcast.refs_0_, f32[256,1536]{1,0:T(8,128)S(1)} %spatial_incoming.1.refs_4_.refs_1_, bf16[256,1536]{1,0:T(8,128)(2,1)S(1)} %gate.1.refs_0_.refs_2_, f32[1536]{0:T(1024)S(1)} %copy-done.15, bf16[1536,1536]{1,0:T(8,128)(2,1)S(1)} %copy-done.1, ...), custom_call_target="tpu_custom_call" | custom-call | flops 1 | bytes 1 | tf_op jit(solution)/shard_map/exit/pallas_call | solution.py:762
  59.1 2.3 %collective-permute-done.7.refs_7_ = bf16[64,768]{1,0:T(8,128)(2,1)S(1)} collective-permute-done((bf16[64,768]{1,0:T(8,128)(2,1)S(1)}, bf16[64,768]{1,0:T(8,128)(2,1)S(1)}, u32[]{:S(2)}, u32[]{:S(2)}) %collective-permute-start.7) | collective-permute-done | bytes 98336 | tf_op jit(solution)/shard_map/ppermute | solution.py:581
  61.4 2.0 %exit.3 = bf16[2,2,64,1536]{3,2,1,0:T(8,128)(2,1)} custom-call(s32[1]{0:T(128)} %bitcast.refs_0_, f32[256,1536]{1,0:T(8,128)S(1)} %spatial_incoming.1.refs_4_.refs_1_, bf16[256,1536]{1,0:T(8,128)(2,1)S(1)} %gate.1.refs_0_.refs_2_, f32[1536]{0:T(1024)S(1)} %copy-done.15, bf16[1536,1536]{1,0:T(8,128)(2,1)S(1)} %copy-done.1, ...), custom_call_target="tpu_custom_call", output_to_operand_aliasing={{}: (9, {})} | custom-call | flops 1 | bytes 1 | tf_op jit(solution)/shard_map/exit/pallas_call | solution.py:762
  (45 shorter events, 1.6 us)
Async XLA Ops:
  7.4 6.6 %copy-start.3 = (bf16[144,1536]{1,0:T(8,128)(2,1)S(1)}, bf16[144,1536]{1,0:T(8,128)(2,1)}, u32[]{:S(2)}) copy-start(bf16[144,1536]{1,0:T(8,128)(2,1)} %get-tuple-element.33.own.band_own) | copy-start | bytes 1327108
  7.4 6.6 %collective-permute-start = (bf16[144,1536]{1,0:T(8,128)(2,1)}, bf16[144,1536]{1,0:T(8,128)(2,1)S(1)}, u32[]{:S(2)}, u32[]{:S(2)}) collective-permute-start(bf16[144,1536]{1,0:T(8,128)(2,1)} %get-tuple-element.34), channel_id=1, source_target_pairs={{0,1},{1,0},{2,3},{3,2},{4,5},{5,4},{6,7},{7,6},{8,9},{9,8},{10,11... | collective-permute-start | bytes 1327112 | tf_op jit(solution)/shard_map/ppermute | solution.py:581
  8.0 10.0 %copy-start.2 = (bf16[4,176,768]{2,1,0:T(8,128)(2,1)S(1)}, bf16[4,176,768]{2,1,0:T(8,128)(2,1)}, u32[]{:S(2)}) copy-start(bf16[4,176,768]{2,1,0:T(8,128)(2,1)} %get-tuple-element.26.after.refs_4_) | copy-start | bytes 3244036
  8.0 28.8 %all-to-all-start = ((bf16[4,176,768]{2,1,0:T(8,128)(2,1)}), bf16[4,176,768]{2,1,0:T(8,128)(2,1)S(1)}, u32[]{:S(2)}, u32[]{:S(2)}) async-start(bf16[4,176,768]{2,1,0:T(8,128)(2,1)} %get-tuple-element.26.after.refs_4_), calls=%async_computation | async-start | bytes 2162688 | tf_op jit(solution)/shard_map/all_to_all | solution.py:646
  14.0 4.0 %copy-start.6 = (bf16[256,1536]{1,0:T(8,128)(2,1)S(1)}, bf16[256,1536]{1,0:T(8,128)(2,1)}, u32[]{:S(2)}) copy-start(bf16[256,1536]{1,0:T(8,128)(2,1)} %get-tuple-element.27.normed) | copy-start | bytes 2359300
  14.0 4.0 %copy-start.4 = (bf16[144,1536]{1,0:T(8,128)(2,1)}, bf16[144,1536]{1,0:T(8,128)(2,1)S(1)}, u32[]{:S(2)}) copy-start(bf16[144,1536]{1,0:T(8,128)(2,1)S(1)} %collective-permute-done.far.band_far) | copy-start | bytes 1327108
  14.2 12.0 %collective-permute-start.1 = (bf16[144,1536]{1,0:T(8,128)(2,1)S(1)}, bf16[144,1536]{1,0:T(8,128)(2,1)S(1)}, u32[]{:S(2)}, u32[]{:S(2)}) collective-permute-start(bf16[144,1536]{1,0:T(8,128)(2,1)S(1)} %pair_total.1.total), channel_id=1, source_target_pairs={{0,2},{1,5},{2,0},{3,7},{4,6},{5,1},{6,4},{7,3},{8,10},{9,13},{10,... | collective-permute-start | bytes 1327112 | tf_op jit(solution)/shard_map/ppermute | solution.py:587
  15.8 10.5 %collective-permute-start.2 = (bf16[16,1536]{1,0:T(8,128)(2,1)}, bf16[16,1536]{1,0:T(8,128)(2,1)S(1)}, u32[]{:S(2)}, u32[]{:S(2)}) collective-permute-start(bf16[16,1536]{1,0:T(8,128)(2,1)} %get-tuple-element.35), channel_id=1, source_target_pairs={{0,6},{1,7},{2,4},{3,5},{4,2},{5,3},{6,0},{7,1},{8,14},{9,15},{10,... | collective-permute-start | bytes 147464 | tf_op jit(solution)/shard_map/ppermute | solution.py:581
  17.3 9.0 %collective-permute-start.3 = (bf16[16,1536]{1,0:T(8,128)(2,1)}, bf16[16,1536]{1,0:T(8,128)(2,1)S(1)}, u32[]{:S(2)}, u32[]{:S(2)}) collective-permute-start(bf16[16,1536]{1,0:T(8,128)(2,1)} %get-tuple-element.35), channel_id=1, source_target_pairs={{0,7},{1,6},{2,5},{3,4},{4,3},{5,2},{6,1},{7,0},{8,15},{9,14},{10,... | collective-permute-start | bytes 147464 | tf_op jit(solution)/shard_map/ppermute | solution.py:581
  18.0 3.7 %copy-start = (bf16[1536,3072]{1,0:T(8,128)(2,1)S(1)}, bf16[1536,3072]{1,0:T(8,128)(2,1)}, u32[]{:S(2)}) copy-start(bf16[1536,3072]{1,0:T(8,128)(2,1)} %weight.1) | copy-start | bytes 28311556
  21.7 2.6 %copy-start.14 = (f32[16,128]{1,0:T(8,128)S(1)}, f32[16,128]{1,0:T(8,128)}, u32[]{:S(2)}) copy-start(f32[16,128]{1,0:T(8,128)} %get-tuple-element.30.refs_3_.refs_1_) | copy-start | bytes 24580
  24.3 10.6 %copy-start.5 = (bf16[144,1536]{1,0:T(8,128)(2,1)S(1)}, bf16[144,1536]{1,0:T(8,128)(2,1)}, u32[]{:S(2)}) copy-start(bf16[144,1536]{1,0:T(8,128)(2,1)} %copy-done.4) | copy-start | bytes 1327108
  26.2 9.7 %copy-start.7 = (bf16[256,1536]{1,0:T(8,128)(2,1)}, bf16[256,1536]{1,0:T(8,128)(2,1)S(1)}, u32[]{:S(2)}) copy-start(bf16[256,1536]{1,0:T(8,128)(2,1)S(1)} %get-tuple-element.31.out_local) | copy-start | bytes 2359300
  26.5 19.0 %copy-start.10 = (bf16[256,256]{1,0:T(8,128)(2,1)S(1)}, bf16[256,256]{1,0:T(8,128)(2,1)}, u32[]{:S(2)}) copy-start(bf16[256,256]{1,0:T(8,128)(2,1)} %get-tuple-element.28.refs_1_.bc) | copy-start | bytes 393220
  26.5 8.4 %collective-permute-start.4 = (bf16[144,1536]{1,0:T(8,128)(2,1)S(1)}, bf16[144,1536]{1,0:T(8,128)(2,1)S(1)}, u32[]{:S(2)}, u32[]{:S(2)}) collective-permute-start(bf16[144,1536]{1,0:T(8,128)(2,1)S(1)} %cross.1), channel_id=1, source_target_pairs={{0,4},{1,3},{2,6},{3,1},{4,0},{5,7},{6,2},{7,5},{8,12},{9,11},{10,... | collective-permute-start | bytes 1327112 | tf_op jit(solution)/shard_map/ppermute | solution.py:587
  36.7 8.8 %copy-start.8 = (bf16[256,1536]{1,0:T(8,128)(2,1)S(1)}, bf16[256,1536]{1,0:T(8,128)(2,1)}, u32[]{:S(2)}) copy-start(bf16[256,1536]{1,0:T(8,128)(2,1)} %copy-done.7) | copy-start | bytes 2359300
  36.7 8.8 %collective-permute-start.5 = (bf16[128,1536]{1,0:T(8,128)(2,1)}, bf16[128,1536]{1,0:T(8,128)(2,1)}, u32[]{:S(2)}, u32[]{:S(2)}) collective-permute-start(bf16[128,1536]{1,0:T(8,128)(2,1)} %get-tuple-element.37), channel_id=1, source_target_pairs={{0,1},{1,0},{2,3},{3,2},{4,5},{5,4},{6,7},{7,6},{8,9},{9,8},{10,11... | collective-permute-start | bytes 1179656 | tf_op jit(solution)/shard_map/ppermute | solution.py:581
  39.0 14.9 %collective-permute-start.9 = (bf16[64,768]{1,0:T(8,128)(2,1)S(1)}, bf16[64,768]{1,0:T(8,128)(2,1)S(1)}, u32[]{:S(2)}, u32[]{:S(2)}) collective-permute-start(bf16[64,768]{1,0:T(8,128)(2,1)S(1)} %get-tuple-element.44), channel_id=1, source_target_pairs={{0,24},{8,16},{16,8},{24,0},{1,25},{9,17},{17,9},{25,1},{2,26},{10... | collective-permute-start | bytes 294920 | tf_op jit(solution)/shard_map/ppermute | solution.py:581
  42.7 12.1 %collective-permute-start.10 = (bf16[64,768]{1,0:T(8,128)(2,1)S(1)}, bf16[64,768]{1,0:T(8,128)(2,1)S(1)}, u32[]{:S(2)}, u32[]{:S(2)}) collective-permute-start(bf16[64,768]{1,0:T(8,128)(2,1)S(1)} %get-tuple-element.45), channel_id=1, source_target_pairs={{0,16},{8,24},{16,0},{24,8},{1,17},{9,25},{17,1},{25,9},{2,18},{10... | collective-permute-start | bytes 294920 | tf_op jit(solution)/shard_map/ppermute | solution.py:581
  45.5 9.3 %collective-permute-start.11 = (bf16[64,768]{1,0:T(8,128)(2,1)S(1)}, bf16[64,768]{1,0:T(8,128)(2,1)S(1)}, u32[]{:S(2)}, u32[]{:S(2)}) collective-permute-start(bf16[64,768]{1,0:T(8,128)(2,1)S(1)} %get-tuple-element.46), channel_id=1, source_target_pairs={{0,8},{8,0},{16,24},{24,16},{1,9},{9,1},{17,25},{25,17},{2,10},{10... | collective-permute-start | bytes 294920 | tf_op jit(solution)/shard_map/ppermute | solution.py:581
  48.3 6.6 %copy-start.15 = (f32[1536]{0:T(1024)S(1)}, f32[1536]{0:T(1024)}, u32[]{:S(2)}) copy-start(f32[1536]{0:T(1024)} %refs_3_.5) | copy-start | bytes 18436
  50.4 8.8 %collective-permute-start.6 = (bf16[64,768]{1,0:T(8,128)(2,1)S(1)}, bf16[64,768]{1,0:T(8,128)(2,1)S(1)}, u32[]{:S(2)}, u32[]{:S(2)}) collective-permute-start(bf16[64,768]{1,0:T(8,128)(2,1)S(1)} %get-tuple-element.40), channel_id=1, source_target_pairs={{0,24},{8,16},{16,8},{24,0},{1,25},{9,17},{17,9},{25,1},{2,26},{10... | collective-permute-start | bytes 294920 | tf_op jit(solution)/shard_map/ppermute | solution.py:581
  52.0 9.4 %collective-permute-start.7 = (bf16[64,768]{1,0:T(8,128)(2,1)S(1)}, bf16[64,768]{1,0:T(8,128)(2,1)S(1)}, u32[]{:S(2)}, u32[]{:S(2)}) collective-permute-start(bf16[64,768]{1,0:T(8,128)(2,1)S(1)} %get-tuple-element.41), channel_id=1, source_target_pairs={{0,16},{8,24},{16,0},{24,8},{1,17},{9,25},{17,1},{25,9},{2,18},{10... | collective-permute-start | bytes 294920 | tf_op jit(solution)/shard_map/ppermute | solution.py:581
  53.9 7.5 %collective-permute-start.8 = (bf16[64,768]{1,0:T(8,128)(2,1)S(1)}, bf16[64,768]{1,0:T(8,128)(2,1)S(1)}, u32[]{:S(2)}, u32[]{:S(2)}) collective-permute-start(bf16[64,768]{1,0:T(8,128)(2,1)S(1)} %get-tuple-element.42), channel_id=1, source_target_pairs={{0,8},{8,0},{16,24},{24,16},{1,9},{9,1},{17,25},{25,17},{2,10},{10... | collective-permute-start | bytes 294920 | tf_op jit(solution)/shard_map/ppermute | solution.py:581
  (5 other events, 9.3 us)

commit v7 on v6

--- a/solution.py
+++ b/solution.py
@@ -185,8 +185,7 @@
     outgoing[0].start()
     dt_copy.wait()
     logits[:, : 2 * heads] = dot_nt(normed[...], dt_held[...]).astype(BF16).astype(F32)
-    dt_heads = dot_nt(dt_held[heads:, :], normed[...])
-    dt_heads = jnp.concatenate([dt_heads, jnp.zeros((TAIL, count), F32)], axis=0).astype(BF16)
+    dt_heads = jnp.transpose(logits[...]).astype(BF16)[heads : 2 * heads + TAIL]
     bc_copy.wait()
     bc = dot(normed[...], bc_held[...]).astype(BF16)
     bc_own[...] = bc[:, : 2 * state]
@@ -195,44 +194,44 @@
         for frame in range(frames)
     ]
 
-    block = held_weight.shape[1] // blocks
-    for index, copy in enumerate(copies):
-        copy.wait()
-        at = index * block
-        values = dot(normed[...], held_weight[:, at : at + block]).astype(BF16)
-        for inside in range(0, block, group):
-            part = (at + inside) // group
-            for row in range(rows):
-                piece = rank_of(part * rows + row)
-                here = slice(row * length, (row + 1) * length)
-                payload[piece, :length, :] = values[here, inside : inside + group]
-                pack_rest(
-                    payload.at[piece],
-                    length,
-                    bc[here, 2 * state : 3 * state],
-                    bc[here, 3 * state :],
-                    dt_heads[part * per_group : part * per_group + TAIL, here],
-                )
-                outgoing.append(
-                    pltpu.make_async_copy(
-                        payload.at[piece], payload_out.at[piece], out_sems.at[1 + piece]
-                    )
-                )
-                outgoing[-1].start()
     half = state // 2
     head_dim = groups * group // heads
     mine = band[0] % 2 == 0
-    for frame in range(frames):
-        b_proj = frame_of(bc_own, frame, rows, frames, columns)[:, :state]
-        for part in range(groups):
-            at = slice(part * group, (part + 1) * group)
+    b_frames = [frame_of(bc_own, frame, rows, frames, columns)[:, :state] for frame in range(frames)]
+    block = held_weight.shape[1] // blocks
+    waits = list(copies)
+    for part in range(groups):
+        for at in range(0, group, block):
+            waits.pop(0).wait()
+            from_col = part * group + at
+            values = dot(normed[...], held_weight[:, from_col : from_col + block]).astype(BF16)
+            for row in range(rows):
+                payload[rank_of(part * rows + row), :length, at : at + block] = values[
+                    row * length : (row + 1) * length
+                ]
+        for row in range(rows):
+            piece = rank_of(part * rows + row)
+            here = slice(row * length, (row + 1) * length)
+            pack_rest(
+                payload.at[piece],
+                length,
+                bc[here, 2 * state : 3 * state],
+                bc[here, 3 * state :],
+                dt_heads[part * per_group : part * per_group + TAIL, here],
+            )
+            outgoing.append(
+                pltpu.make_async_copy(payload.at[piece], payload_out.at[piece], out_sems.at[1 + piece])
+            )
+            outgoing[-1].start()
+        cols = slice(part * group, (part + 1) * group)
+        matrix = spread_matrix(part * per_group, group, head_dim)
+        for frame in range(frames):
             values = frame_x(payload, part, frame, rows, columns)
-            matrix = spread_matrix(part * per_group, group, head_dim)
             scaled = (values.astype(F32) * dot(scan[frame][0], matrix)).astype(BF16)
-            fresh = dot_tn(b_proj, scaled).astype(BF16)
+            fresh = dot_tn(b_frames[frame], scaled).astype(BF16)
             at_rows = slice(frame * half, (frame + 1) * half)
-            own_states[at_rows, at] = jnp.where(mine, fresh[:half], fresh[half:])
-            other_states[at_rows, at] = jnp.where(mine, fresh[half:], fresh[:half])
+            own_states[at_rows, cols] = jnp.where(mine, fresh[:half], fresh[half:])
+            other_states[at_rows, cols] = jnp.where(mine, fresh[half:], fresh[:half])
     whole = [decay for _, decay in scan] + [jnp.zeros((8 - frames, LANES), F32)]
     decays = spread(jnp.concatenate(whole, axis=0), spread_matrix(0, groups * group, head_dim))
     tail = tail_of(decays)
@@ -604,7 +603,8 @@
     count = rows * length
     half = state // 2
     chunk_cols = 16
-    blocks = parts = 2
+    parts = 2
+    blocks = inner // (2 * LANES) if group % (2 * LANES) == 0 else groups
     part_len = length // parts
     here = lax.axis_index("tm").astype(jnp.int32).reshape(1)
     band = lax.axis_index("height").astype(jnp.int32).reshape(1)
@@ -653,13 +653,13 @@
     )
     far = swapped(other, "height", 1)
     gate = call(
-        functools.partial(gate_kernel, blocks),
+        functools.partial(gate_kernel, 2),
         "gate",
         shape_of((count, inner), BF16),
         [ANY, WHOLE, HBM],
         scratch_shapes=[
             pltpu.VMEM((width, inner), BF16),
-            pltpu.SemaphoreType.DMA((blocks,)),
+            pltpu.SemaphoreType.DMA((2,)),
         ],
     )(payload, normed, in_weight)
 

time: 63.9 us -> 66.2 us (1.036)
  Pallas kernels: 23.4 us -> 25.7 us
    pallas_call x1, Pallas kernels: 7.42 us -> 9.69 us  [per_device(): call(functools.partial(entry_kernel, shares, heads, state, blocks), 'entr...]
  transfers between devices with their start and end apart: 13 -> 13, of which waited for: 2 -> 2; matrix products, arithmetic and copies ran while one was open for 0% -> 0% of each run, Pallas kernels for 22% -> 21%
where the time goes in v7:
time: 66.2 us; the launch traced here: 65.8 us
  Pallas kernels  25.7 us (39%)
  starting transfers between devices  21.8 us (33%)
  waiting for transfers between devices  10.1 us (15%)
  local copies, waits for them, and re-layouts  7.84 us (12%)
    ppermute x10, starting transfers between devices, swapped(): lax.ppermute(value, axis, [(source, source ^ distance) for source in rang...  13.6 us
    pallas_call x1, Pallas kernels, per_device(): call(functools.partial(entry_kernel, shares, heads, state, blocks), 'entr...  9.69 us
    unnamed x32, local copies, waits for them, and re-layouts  7.84 us
    ppermute x2, waiting for transfers between devices, crossed(): return lax.ppermute(value, axis, pairs)  7.8 us
    all_to_all x1, starting transfers between devices, per_device(): lax.all_to_all(payload, 'tm', split_axis=0, concat_axis=0, tiled=True, ax...  6.03 us
    pallas_call x2, Pallas kernels, per_device(): call(functools.partial(temporal_kernel, part, parts, per_group, head_dim,...  4.36 us
    pallas_call x2, Pallas kernels, per_device(): call(functools.partial(exit_kernel, part, parts, shares), 'exit', shape_o...  3.92 us
    pallas_call x1, Pallas kernels, per_device(): call(functools.partial(gate_kernel, 2), 'gate', shape_of((count, inner),...  2.59 us
  transfers between devices with their start and end apart: 13, of which 2 were waited for; matrix products, arithmetic and copies ran while one was open for 0% of the time, Pallas kernels for 21%

profile of v7, /device:TPU:0, one launch (start us, length us, event | category | flops | bytes accessed | tf_op | source)
XLA Modules:
  0.0 65.8 jit_solution(15524423936075718792)
XLA Ops:
  0.0 9.7 %entry.1 = (bf16[256,1536]{1,0:T(8,128)(2,1)}, bf16[4,176,768]{2,1,0:T(8,128)(2,1)}, bf16[256,256]{1,0:T(8,128)(2,1)}, f32[256,128]{1,0:T(8,128)}, f32[16,128]{1...) custom-call(s32[1]{0:T(128)} %bitcast.refs_0_, ...), custom_call_target="tpu_custom_call" | custom-call | flops 1 | bytes 1 | tf_op jit(solution)/shard_map/entry/pallas_call | solution.py:613
  10.2 6.0 %all-to-all-start = ((bf16[4,176,768]{2,1,0:T(8,128)(2,1)}), bf16[4,176,768]{2,1,0:T(8,128)(2,1)S(1)}, u32[]{:S(2)}, u32[]{:S(2)}) async-start(bf16[4,176,768]{2,1,0:T(8,128)(2,1)} %get-tuple-element.26.after.refs_4_), calls=%async_computation | async-start | bytes 2162688 | tf_op jit(solution)/shard_map/all_to_all | solution.py:646
  16.5 1.6 %collective-permute-start.1 = (bf16[144,1536]{1,0:T(8,128)(2,1)S(1)}, bf16[144,1536]{1,0:T(8,128)(2,1)S(1)}, u32[]{:S(2)}, u32[]{:S(2)}) collective-permute-start(bf16[144,1536]{1,0:T(8,128)(2,1)S(1)} %pair_total.1.total), channel_id=1, source_target_pairs={{0,2},{1,5},{2,0},{3,7},{4,6},{5,1},{6,4},{7,3},{8,10},{9,13},{10,... | collective-permute-start | bytes 1327112 | tf_op jit(solution)/shard_map/ppermute | solution.py:586
  18.0 1.5 %collective-permute-start.2 = (bf16[16,1536]{1,0:T(8,128)(2,1)}, bf16[16,1536]{1,0:T(8,128)(2,1)S(1)}, u32[]{:S(2)}, u32[]{:S(2)}) collective-permute-start(bf16[16,1536]{1,0:T(8,128)(2,1)} %get-tuple-element.35), channel_id=1, source_target_pairs={{0,6},{1,7},{2,4},{3,5},{4,2},{5,3},{6,0},{7,1},{8,14},{9,15},{10,... | collective-permute-start | bytes 147464 | tf_op jit(solution)/shard_map/ppermute | solution.py:580
  19.5 0.7 %collective-permute-start.3 = (bf16[16,1536]{1,0:T(8,128)(2,1)}, bf16[16,1536]{1,0:T(8,128)(2,1)S(1)}, u32[]{:S(2)}, u32[]{:S(2)}) collective-permute-start(bf16[16,1536]{1,0:T(8,128)(2,1)} %get-tuple-element.35), channel_id=1, source_target_pairs={{0,7},{1,6},{2,5},{3,4},{4,3},{5,2},{6,1},{7,0},{8,15},{9,14},{10,... | collective-permute-start | bytes 147464 | tf_op jit(solution)/shard_map/ppermute | solution.py:580
  20.2 3.7 %copy-done = bf16[1536,3072]{1,0:T(8,128)(2,1)S(1)} copy-done((bf16[1536,3072]{1,0:T(8,128)(2,1)S(1)}, bf16[1536,3072]{1,0:T(8,128)(2,1)}, u32[]{:S(2)}) %copy-start) | copy-done | bytes 9437208
  23.9 2.6 %gate.1.refs_0_.refs_2_ = bf16[256,1536]{1,0:T(8,128)(2,1)S(1)} custom-call(bf16[4,176,768]{2,1,0:T(8,128)(2,1)S(1)} %copy-done.2, bf16[256,1536]{1,0:T(8,128)(2,1)S(1)} %copy-done.6, bf16[1536,3072]{1,0:T(8,128)(2,1)S(1)} %copy-done), custom_call_target="tpu_custom_call" | custom-call | flops 1 | bytes 1 | tf_op jit(solution)/shard_map/gate/pallas_call | solution.py:655
  26.6 1.9 %spatial_local.1 = (bf16[256,1536]{1,0:T(8,128)(2,1)S(1)}, f32[256,128]{1,0:T(8,128)S(1)}) custom-call(bf16[256,1536]{1,0:T(8,128)(2,1)S(1)} %gate.1.refs_0_.refs_2_, bf16[256,256]{1,0:T(8,128)(2,1)S(1)} %copy-done.9, f32[256,128]{1,0:T(8,128)S(1)} %copy-done.13, f32[16,128]{1,0:T(8,128)S(1)} %copy-done.14, bf16[4,176,768]{2,1,0:T(8,128)(2,1)S(1)} %copy-done.2), custom_call_target="tpu_custom_call" | custom-call | flops 1 | bytes 1 | tf_op jit(solution)/shard_map/spatial_local/pallas_call | solution.py:666
  29.3 7.8 %collective-permute-done.4.second = bf16[144,1536]{1,0:T(8,128)(2,1)S(1)} collective-permute-done((bf16[144,1536]{1,0:T(8,128)(2,1)S(1)}, bf16[144,1536]{1,0:T(8,128)(2,1)S(1)}, u32[]{:S(2)}, u32[]{:S(2)}) %collective-permute-start.4) | collective-permute-done | bytes 442400 | tf_op jit(solution)/shard_map/ppermute | solution.py:586
  37.1 1.1 %settle.1 = (bf16[128,1536]{1,0:T(8,128)(2,1)S(1)}, bf16[128,1536]{1,0:T(8,128)(2,1)}) custom-call(f32[256,128]{1,0:T(8,128)S(1)} %get-tuple-element.32._.reach, s32[1]{0:T(128)} %bitcast.1.refs_1_.band, bf16[144,1536]{1,0:T(8,128)(2,1)S(1)} %collective-permute-done.1.first, bf16[144,1536]{1,0:T(8,128)(2,1)S(1)} %collective-permute-done.4.second, ...), custom_call_target="tpu_custom_call" | custom-call | flops 1 | bytes 1 | tf_op jit(solution)/shard_map/settle/pallas_call | solution.py:691
  38.2 0.8 %copy-done.11 = bf16[128,1536]{1,0:T(8,128)(2,1)} copy-done((bf16[128,1536]{1,0:T(8,128)(2,1)}, bf16[128,1536]{1,0:T(8,128)(2,1)S(1)}, u32[]{:S(2)}) %copy-start.11) | copy-done | bytes 393240
  39.0 2.3 %temporal.2 = (bf16[64,768]{1,0:T(8,128)(2,1)S(1)}, bf16[64,768]{1,0:T(8,128)(2,1)S(1)}, bf16[64,768]{1,0:T(8,128)(2,1)S(1)}, bf16[64,768]{1,0:T(8,128)(2,1)S(1)}, f32[128,768]{1,0:T(8,128)S(1)}) custom-call(s32[1]{0:T(128)} %bitcast.refs_0_, f32[16,128]{1,0:T(8,128)S(1)} %copy-done.14, bf16[4,176,768]{2,1,0:T(8,128)(2,1)S(1)} %all-to-all-done.refs_2_), custom_call_target="tpu_custom_call" | custom-call | flops 1 | bytes 1 | tf_op jit(solution)/shard_map/temporal/pallas_call | solution.py:732
  41.3 3.7 %collective-permute-start.9 = (bf16[64,768]{1,0:T(8,128)(2,1)S(1)}, bf16[64,768]{1,0:T(8,128)(2,1)S(1)}, u32[]{:S(2)}, u32[]{:S(2)}) collective-permute-start(bf16[64,768]{1,0:T(8,128)(2,1)S(1)} %get-tuple-element.44), channel_id=1, source_target_pairs={{0,24},{8,16},{16,8},{24,0},{1,25},{9,17},{17,9},{25,1},{2,26},{10... | collective-permute-start | bytes 294920 | tf_op jit(solution)/shard_map/ppermute | solution.py:580
  45.0 2.8 %collective-permute-start.10 = (bf16[64,768]{1,0:T(8,128)(2,1)S(1)}, bf16[64,768]{1,0:T(8,128)(2,1)S(1)}, u32[]{:S(2)}, u32[]{:S(2)}) collective-permute-start(bf16[64,768]{1,0:T(8,128)(2,1)S(1)} %get-tuple-element.45), channel_id=1, source_target_pairs={{0,16},{8,24},{16,0},{24,8},{1,17},{9,25},{17,1},{25,9},{2,18},{10... | collective-permute-start | bytes 294920 | tf_op jit(solution)/shard_map/ppermute | solution.py:580
  47.8 1.0 %copy-done.12 = bf16[128,1536]{1,0:T(8,128)(2,1)S(1)} copy-done((bf16[128,1536]{1,0:T(8,128)(2,1)S(1)}, bf16[128,1536]{1,0:T(8,128)(2,1)}, u32[]{:S(2)}) %copy-start.12) | copy-done | bytes 393240
  48.8 1.8 %spatial_incoming.1.refs_4_.refs_1_ = f32[256,1536]{1,0:T(8,128)S(1)} custom-call(s32[1]{0:T(128)} %bitcast.1.refs_1_.band, bf16[256,1536]{1,0:T(8,128)(2,1)S(1)} %copy-done.8, bf16[256,256]{1,0:T(8,128)(2,1)S(1)} %copy-done.10, f32[256,128]{1,0:T(8,128)S(1)} %get-tuple-element.32._.reach, bf16[128,1536]{1,0:T(8,128)(2,1)S(1)} %copy-done.12, ...), custom_call_target="tpu_custom_call" | custom-call | flops 1 | bytes 1 | tf_op jit(solution)/shard_map/spatial_incoming/pallas_call | solution.py:722
  50.5 2.1 %temporal.3 = (bf16[64,768]{1,0:T(8,128)(2,1)S(1)}, bf16[64,768]{1,0:T(8,128)(2,1)S(1)}, bf16[64,768]{1,0:T(8,128)(2,1)S(1)}, bf16[64,768]{1,0:T(8,128)(2,1)S(1)}) custom-call(s32[1]{0:T(128)} %bitcast.refs_0_, f32[16,128]{1,0:T(8,128)S(1)} %copy-done.14, bf16[4,176,768]{2,1,0:T(8,128)(2,1)S(1)} %all-to-all-done.refs_2_, ...), custom_call_target="tpu_custom_call" | custom-call | flops 1 | bytes 1 | tf_op jit(solution)/shard_map/temporal/pallas_call | solution.py:732
  52.6 1.7 %collective-permute-start.6 = (bf16[64,768]{1,0:T(8,128)(2,1)S(1)}, bf16[64,768]{1,0:T(8,128)(2,1)S(1)}, u32[]{:S(2)}, u32[]{:S(2)}) collective-permute-start(bf16[64,768]{1,0:T(8,128)(2,1)S(1)} %get-tuple-element.40), channel_id=1, source_target_pairs={{0,24},{8,16},{16,8},{24,0},{1,25},{9,17},{17,9},{25,1},{2,26},{10... | collective-permute-start | bytes 294920 | tf_op jit(solution)/shard_map/ppermute | solution.py:580
  54.3 1.9 %collective-permute-start.7 = (bf16[64,768]{1,0:T(8,128)(2,1)S(1)}, bf16[64,768]{1,0:T(8,128)(2,1)S(1)}, u32[]{:S(2)}, u32[]{:S(2)}) collective-permute-start(bf16[64,768]{1,0:T(8,128)(2,1)S(1)} %get-tuple-element.41), channel_id=1, source_target_pairs={{0,16},{8,24},{16,0},{24,8},{1,17},{9,25},{17,1},{25,9},{2,18},{10... | collective-permute-start | bytes 294920 | tf_op jit(solution)/shard_map/ppermute | solution.py:580
  56.2 0.9 %collective-permute-start.8 = (bf16[64,768]{1,0:T(8,128)(2,1)S(1)}, bf16[64,768]{1,0:T(8,128)(2,1)S(1)}, u32[]{:S(2)}, u32[]{:S(2)}) collective-permute-start(bf16[64,768]{1,0:T(8,128)(2,1)S(1)} %get-tuple-element.42), channel_id=1, source_target_pairs={{0,8},{8,0},{16,24},{24,16},{1,9},{9,1},{17,25},{25,17},{2,10},{10... | collective-permute-start | bytes 294920 | tf_op jit(solution)/shard_map/ppermute | solution.py:580
  57.1 2.3 %copy-done.1 = bf16[1536,1536]{1,0:T(8,128)(2,1)S(1)} copy-done((bf16[1536,1536]{1,0:T(8,128)(2,1)S(1)}, bf16[1536,1536]{1,0:T(8,128)(2,1)}, u32[]{:S(2)}) %copy-start.1) | copy-done | bytes 4718616
  59.4 2.0 %exit.2.refs_9_ = bf16[2,2,64,1536]{3,2,1,0:T(8,128)(2,1)} custom-call(s32[1]{0:T(128)} %bitcast.refs_0_, f32[256,1536]{1,0:T(8,128)S(1)} %spatial_incoming.1.refs_4_.refs_1_, bf16[256,1536]{1,0:T(8,128)(2,1)S(1)} %gate.1.refs_0_.refs_2_, f32[1536]{0:T(1024)S(1)} %copy-done.15, bf16[1536,1536]{1,0:T(8,128)(2,1)S(1)} %copy-done.1, ...), custom_call_target="tpu_custom_call" | custom-call | flops 1 | bytes 1 | tf_op jit(solution)/shard_map/exit/pallas_call | solution.py:762
  61.4 2.3 %collective-permute-done.7.refs_7_ = bf16[64,768]{1,0:T(8,128)(2,1)S(1)} collective-permute-done((bf16[64,768]{1,0:T(8,128)(2,1)S(1)}, bf16[64,768]{1,0:T(8,128)(2,1)S(1)}, u32[]{:S(2)}, u32[]{:S(2)}) %collective-permute-start.7) | collective-permute-done | bytes 98336 | tf_op jit(solution)/shard_map/ppermute | solution.py:580
  63.7 2.0 %exit.3 = bf16[2,2,64,1536]{3,2,1,0:T(8,128)(2,1)} custom-call(s32[1]{0:T(128)} %bitcast.refs_0_, f32[256,1536]{1,0:T(8,128)S(1)} %spatial_incoming.1.refs_4_.refs_1_, bf16[256,1536]{1,0:T(8,128)(2,1)S(1)} %gate.1.refs_0_.refs_2_, f32[1536]{0:T(1024)S(1)} %copy-done.15, bf16[1536,1536]{1,0:T(8,128)(2,1)S(1)} %copy-done.1, ...), custom_call_target="tpu_custom_call", output_to_operand_aliasing={{}: (9, {})} | custom-call | flops 1 | bytes 1 | tf_op jit(solution)/shard_map/exit/pallas_call | solution.py:762
  (45 shorter events, 1.6 us)
Async XLA Ops:
  9.7 6.6 %copy-start.3 = (bf16[144,1536]{1,0:T(8,128)(2,1)S(1)}, bf16[144,1536]{1,0:T(8,128)(2,1)}, u32[]{:S(2)}) copy-start(bf16[144,1536]{1,0:T(8,128)(2,1)} %get-tuple-element.33.own.band_own) | copy-start | bytes 1327108
  9.7 6.6 %collective-permute-start = (bf16[144,1536]{1,0:T(8,128)(2,1)}, bf16[144,1536]{1,0:T(8,128)(2,1)S(1)}, u32[]{:S(2)}, u32[]{:S(2)}) collective-permute-start(bf16[144,1536]{1,0:T(8,128)(2,1)} %get-tuple-element.34), channel_id=1, source_target_pairs={{0,1},{1,0},{2,3},{3,2},{4,5},{5,4},{6,7},{7,6},{8,9},{9,8},{10,11... | collective-permute-start | bytes 1327112 | tf_op jit(solution)/shard_map/ppermute | solution.py:580
  10.2 10.0 %copy-start.2 = (bf16[4,176,768]{2,1,0:T(8,128)(2,1)S(1)}, bf16[4,176,768]{2,1,0:T(8,128)(2,1)}, u32[]{:S(2)}) copy-start(bf16[4,176,768]{2,1,0:T(8,128)(2,1)} %get-tuple-element.26.after.refs_4_) | copy-start | bytes 3244036
  10.2 28.8 %all-to-all-start = ((bf16[4,176,768]{2,1,0:T(8,128)(2,1)}), bf16[4,176,768]{2,1,0:T(8,128)(2,1)S(1)}, u32[]{:S(2)}, u32[]{:S(2)}) async-start(bf16[4,176,768]{2,1,0:T(8,128)(2,1)} %get-tuple-element.26.after.refs_4_), calls=%async_computation | async-start | bytes 2162688 | tf_op jit(solution)/shard_map/all_to_all | solution.py:646
  16.3 4.0 %copy-start.6 = (bf16[256,1536]{1,0:T(8,128)(2,1)S(1)}, bf16[256,1536]{1,0:T(8,128)(2,1)}, u32[]{:S(2)}) copy-start(bf16[256,1536]{1,0:T(8,128)(2,1)} %get-tuple-element.27.normed) | copy-start | bytes 2359300
  16.3 4.0 %copy-start.4 = (bf16[144,1536]{1,0:T(8,128)(2,1)}, bf16[144,1536]{1,0:T(8,128)(2,1)S(1)}, u32[]{:S(2)}) copy-start(bf16[144,1536]{1,0:T(8,128)(2,1)S(1)} %collective-permute-done.far.band_far) | copy-start | bytes 1327108
  16.5 12.0 %collective-permute-start.1 = (bf16[144,1536]{1,0:T(8,128)(2,1)S(1)}, bf16[144,1536]{1,0:T(8,128)(2,1)S(1)}, u32[]{:S(2)}, u32[]{:S(2)}) collective-permute-start(bf16[144,1536]{1,0:T(8,128)(2,1)S(1)} %pair_total.1.total), channel_id=1, source_target_pairs={{0,2},{1,5},{2,0},{3,7},{4,6},{5,1},{6,4},{7,3},{8,10},{9,13},{10,... | collective-permute-start | bytes 1327112 | tf_op jit(solution)/shard_map/ppermute | solution.py:586
  18.0 10.5 %collective-permute-start.2 = (bf16[16,1536]{1,0:T(8,128)(2,1)}, bf16[16,1536]{1,0:T(8,128)(2,1)S(1)}, u32[]{:S(2)}, u32[]{:S(2)}) collective-permute-start(bf16[16,1536]{1,0:T(8,128)(2,1)} %get-tuple-element.35), channel_id=1, source_target_pairs={{0,6},{1,7},{2,4},{3,5},{4,2},{5,3},{6,0},{7,1},{8,14},{9,15},{10,... | collective-permute-start | bytes 147464 | tf_op jit(solution)/shard_map/ppermute | solution.py:580
  19.5 9.0 %collective-permute-start.3 = (bf16[16,1536]{1,0:T(8,128)(2,1)}, bf16[16,1536]{1,0:T(8,128)(2,1)S(1)}, u32[]{:S(2)}, u32[]{:S(2)}) collective-permute-start(bf16[16,1536]{1,0:T(8,128)(2,1)} %get-tuple-element.35), channel_id=1, source_target_pairs={{0,7},{1,6},{2,5},{3,4},{4,3},{5,2},{6,1},{7,0},{8,15},{9,14},{10,... | collective-permute-start | bytes 147464 | tf_op jit(solution)/shard_map/ppermute | solution.py:580
  20.2 3.7 %copy-start = (bf16[1536,3072]{1,0:T(8,128)(2,1)S(1)}, bf16[1536,3072]{1,0:T(8,128)(2,1)}, u32[]{:S(2)}) copy-start(bf16[1536,3072]{1,0:T(8,128)(2,1)} %weight.1) | copy-start | bytes 28311556
  23.9 2.6 %copy-start.14 = (f32[16,128]{1,0:T(8,128)S(1)}, f32[16,128]{1,0:T(8,128)}, u32[]{:S(2)}) copy-start(f32[16,128]{1,0:T(8,128)} %get-tuple-element.30.refs_3_.refs_1_) | copy-start | bytes 24580
  26.5 10.6 %copy-start.5 = (bf16[144,1536]{1,0:T(8,128)(2,1)S(1)}, bf16[144,1536]{1,0:T(8,128)(2,1)}, u32[]{:S(2)}) copy-start(bf16[144,1536]{1,0:T(8,128)(2,1)} %copy-done.4) | copy-start | bytes 1327108
  28.5 9.7 %copy-start.7 = (bf16[256,1536]{1,0:T(8,128)(2,1)}, bf16[256,1536]{1,0:T(8,128)(2,1)S(1)}, u32[]{:S(2)}) copy-start(bf16[256,1536]{1,0:T(8,128)(2,1)S(1)} %get-tuple-element.31.out_local) | copy-start | bytes 2359300
  28.7 19.0 %copy-start.10 = (bf16[256,256]{1,0:T(8,128)(2,1)S(1)}, bf16[256,256]{1,0:T(8,128)(2,1)}, u32[]{:S(2)}) copy-start(bf16[256,256]{1,0:T(8,128)(2,1)} %get-tuple-element.28.refs_1_.bc) | copy-start | bytes 393220
  28.7 8.4 %collective-permute-start.4 = (bf16[144,1536]{1,0:T(8,128)(2,1)S(1)}, bf16[144,1536]{1,0:T(8,128)(2,1)S(1)}, u32[]{:S(2)}, u32[]{:S(2)}) collective-permute-start(bf16[144,1536]{1,0:T(8,128)(2,1)S(1)} %cross.1), channel_id=1, source_target_pairs={{0,4},{1,3},{2,6},{3,1},{4,0},{5,7},{6,2},{7,5},{8,12},{9,11},{10,... | collective-permute-start | bytes 1327112 | tf_op jit(solution)/shard_map/ppermute | solution.py:586
  39.0 8.8 %copy-start.8 = (bf16[256,1536]{1,0:T(8,128)(2,1)S(1)}, bf16[256,1536]{1,0:T(8,128)(2,1)}, u32[]{:S(2)}) copy-start(bf16[256,1536]{1,0:T(8,128)(2,1)} %copy-done.7) | copy-start | bytes 2359300
  39.0 8.8 %collective-permute-start.5 = (bf16[128,1536]{1,0:T(8,128)(2,1)}, bf16[128,1536]{1,0:T(8,128)(2,1)}, u32[]{:S(2)}, u32[]{:S(2)}) collective-permute-start(bf16[128,1536]{1,0:T(8,128)(2,1)} %get-tuple-element.37), channel_id=1, source_target_pairs={{0,1},{1,0},{2,3},{3,2},{4,5},{5,4},{6,7},{7,6},{8,9},{9,8},{10,11... | collective-permute-start | bytes 1179656 | tf_op jit(solution)/shard_map/ppermute | solution.py:580
  41.3 14.9 %collective-permute-start.9 = (bf16[64,768]{1,0:T(8,128)(2,1)S(1)}, bf16[64,768]{1,0:T(8,128)(2,1)S(1)}, u32[]{:S(2)}, u32[]{:S(2)}) collective-permute-start(bf16[64,768]{1,0:T(8,128)(2,1)S(1)} %get-tuple-element.44), channel_id=1, source_target_pairs={{0,24},{8,16},{16,8},{24,0},{1,25},{9,17},{17,9},{25,1},{2,26},{10... | collective-permute-start | bytes 294920 | tf_op jit(solution)/shard_map/ppermute | solution.py:580
  45.0 12.1 %collective-permute-start.10 = (bf16[64,768]{1,0:T(8,128)(2,1)S(1)}, bf16[64,768]{1,0:T(8,128)(2,1)S(1)}, u32[]{:S(2)}, u32[]{:S(2)}) collective-permute-start(bf16[64,768]{1,0:T(8,128)(2,1)S(1)} %get-tuple-element.45), channel_id=1, source_target_pairs={{0,16},{8,24},{16,0},{24,8},{1,17},{9,25},{17,1},{25,9},{2,18},{10... | collective-permute-start | bytes 294920 | tf_op jit(solution)/shard_map/ppermute | solution.py:580
  47.7 9.3 %collective-permute-start.11 = (bf16[64,768]{1,0:T(8,128)(2,1)S(1)}, bf16[64,768]{1,0:T(8,128)(2,1)S(1)}, u32[]{:S(2)}, u32[]{:S(2)}) collective-permute-start(bf16[64,768]{1,0:T(8,128)(2,1)S(1)} %get-tuple-element.46), channel_id=1, source_target_pairs={{0,8},{8,0},{16,24},{24,16},{1,9},{9,1},{17,25},{25,17},{2,10},{10... | collective-permute-start | bytes 294920 | tf_op jit(solution)/shard_map/ppermute | solution.py:580
  50.5 6.6 %copy-start.15 = (f32[1536]{0:T(1024)S(1)}, f32[1536]{0:T(1024)}, u32[]{:S(2)}) copy-start(f32[1536]{0:T(1024)} %refs_3_.5) | copy-start | bytes 18436
  52.6 8.8 %collective-permute-start.6 = (bf16[64,768]{1,0:T(8,128)(2,1)S(1)}, bf16[64,768]{1,0:T(8,128)(2,1)S(1)}, u32[]{:S(2)}, u32[]{:S(2)}) collective-permute-start(bf16[64,768]{1,0:T(8,128)(2,1)S(1)} %get-tuple-element.40), channel_id=1, source_target_pairs={{0,24},{8,16},{16,8},{24,0},{1,25},{9,17},{17,9},{25,1},{2,26},{10... | collective-permute-start | bytes 294920 | tf_op jit(solution)/shard_map/ppermute | solution.py:580
  54.3 9.4 %collective-permute-start.7 = (bf16[64,768]{1,0:T(8,128)(2,1)S(1)}, bf16[64,768]{1,0:T(8,128)(2,1)S(1)}, u32[]{:S(2)}, u32[]{:S(2)}) collective-permute-start(bf16[64,768]{1,0:T(8,128)(2,1)S(1)} %get-tuple-element.41), channel_id=1, source_target_pairs={{0,16},{8,24},{16,0},{24,8},{1,17},{9,25},{17,1},{25,9},{2,18},{10... | collective-permute-start | bytes 294920 | tf_op jit(solution)/shard_map/ppermute | solution.py:580
  56.2 7.5 %collective-permute-start.8 = (bf16[64,768]{1,0:T(8,128)(2,1)S(1)}, bf16[64,768]{1,0:T(8,128)(2,1)S(1)}, u32[]{:S(2)}, u32[]{:S(2)}) collective-permute-start(bf16[64,768]{1,0:T(8,128)(2,1)S(1)} %get-tuple-element.42), channel_id=1, source_target_pairs={{0,8},{8,0},{16,24},{24,16},{1,9},{9,1},{17,25},{25,17},{2,10},{10... | collective-permute-start | bytes 294920 | tf_op jit(solution)/shard_map/ppermute | solution.py:580
  (5 other events, 9.3 us)

commit v8 on v6

--- a/solution.py
+++ b/solution.py
@@ -185,8 +185,7 @@
     outgoing[0].start()
     dt_copy.wait()
     logits[:, : 2 * heads] = dot_nt(normed[...], dt_held[...]).astype(BF16).astype(F32)
-    dt_heads = dot_nt(dt_held[heads:, :], normed[...])
-    dt_heads = jnp.concatenate([dt_heads, jnp.zeros((TAIL, count), F32)], axis=0).astype(BF16)
+    dt_heads = jnp.transpose(logits[...]).astype(BF16)[heads : 2 * heads + TAIL]
     bc_copy.wait()
     bc = dot(normed[...], bc_held[...]).astype(BF16)
     bc_own[...] = bc[:, : 2 * state]
@@ -222,19 +221,21 @@
     half = state // 2
     head_dim = groups * group // heads
     mine = band[0] % 2 == 0
+    matrix = spread_matrix(0, groups * group, head_dim)
+    factors = dot(jnp.concatenate([factor for factor, _ in scan], axis=0), matrix)
+    span = rows * columns
     for frame in range(frames):
         b_proj = frame_of(bc_own, frame, rows, frames, columns)[:, :state]
-        for part in range(groups):
-            at = slice(part * group, (part + 1) * group)
-            values = frame_x(payload, part, frame, rows, columns)
-            matrix = spread_matrix(part * per_group, group, head_dim)
-            scaled = (values.astype(F32) * dot(scan[frame][0], matrix)).astype(BF16)
-            fresh = dot_tn(b_proj, scaled).astype(BF16)
-            at_rows = slice(frame * half, (frame + 1) * half)
-            own_states[at_rows, at] = jnp.where(mine, fresh[:half], fresh[half:])
-            other_states[at_rows, at] = jnp.where(mine, fresh[half:], fresh[:half])
+        values = jnp.concatenate(
+            [frame_x(payload, part, frame, rows, columns) for part in range(groups)], axis=1
+        )
+        scaled = (values.astype(F32) * factors[frame * span : (frame + 1) * span]).astype(BF16)
+        fresh = dot_tn(b_proj, scaled).astype(BF16)
+        at_rows = slice(frame * half, (frame + 1) * half)
+        own_states[at_rows, :] = jnp.where(mine, fresh[:half], fresh[half:])
+        other_states[at_rows, :] = jnp.where(mine, fresh[half:], fresh[:half])
     whole = [decay for _, decay in scan] + [jnp.zeros((8 - frames, LANES), F32)]
-    decays = spread(jnp.concatenate(whole, axis=0), spread_matrix(0, groups * group, head_dim))
+    decays = spread(jnp.concatenate(whole, axis=0), matrix)
     tail = tail_of(decays)
     own_states[frames * half :, :] = tail
     other_states[frames * half :, :] = tail
@@ -511,11 +512,11 @@
         last = jnp.min(running, axis=0, keepdims=True)
         mixed = head_mixes(scores, running, running_t, dt_t, values, 0, per_group, head_dim)
         ends = jnp.concatenate([running, jnp.broadcast_to(last, (8, LANES))], axis=0)
-        reach = dot(jnp.exp(ends).astype(BF16), matrix)
-        mixed = mixed + reach[:size] * dot(c_proj, carried.astype(BF16))
-        to_end = (jnp.exp(last - running) * dt).astype(BF16)
-        scaled = (values.astype(F32) * dot(to_end, matrix)).astype(BF16)
-        carried = reach[size : size + 1, :] * carried + dot_tn(b_proj, scaled)
+        to_end = jnp.exp(last - running) * dt
+        factors = dot(jnp.concatenate([jnp.exp(ends), to_end], axis=0).astype(BF16), matrix)
+        mixed = mixed + factors[:size] * dot(c_proj, carried.astype(BF16))
+        scaled = (values.astype(F32) * factors[size + 8 :]).astype(BF16)
+        carried = factors[size : size + 1, :] * carried + dot_tn(b_proj, scaled)
         mixed = mixed.astype(BF16)
         for index, (source, frame) in enumerate(places):
             to = frame * part_cols + chunk * chunk_cols

time: 63.9 us -> 63.9 us (level)
  no operation moved by 1% of the time
where the time goes in v8:
time: 63.9 us; the launch traced here: 63.5 us
  Pallas kernels  23.4 us (37%)
  starting transfers between devices  21.8 us (34%)
  waiting for transfers between devices  10.1 us (16%)
  local copies, waits for them, and re-layouts  7.84 us (12%)
    ppermute x10, starting transfers between devices, swapped(): lax.ppermute(value, axis, [(source, source ^ distance) for source in rang...  13.6 us
    unnamed x32, local copies, waits for them, and re-layouts  7.84 us
    ppermute x2, waiting for transfers between devices, crossed(): return lax.ppermute(value, axis, pairs)  7.81 us
    pallas_call x1, Pallas kernels, per_device(): call(functools.partial(entry_kernel, shares, heads, state, blocks), 'entr...  7.5 us
    all_to_all x1, starting transfers between devices, per_device(): lax.all_to_all(payload, 'tm', split_axis=0, concat_axis=0, tiled=True, ax...  6.03 us
    pallas_call x2, Pallas kernels, per_device(): call(functools.partial(temporal_kernel, part, parts, per_group, head_dim,...  4.26 us
    pallas_call x2, Pallas kernels, per_device(): call(functools.partial(exit_kernel, part, parts, shares), 'exit', shape_o...  3.92 us
    pallas_call x1, Pallas kernels, per_device(): call(functools.partial(gate_kernel, blocks), 'gate', shape_of((count, inn...  2.59 us
  transfers between devices with their start and end apart: 13, of which 2 were waited for; matrix products, arithmetic and copies ran while one was open for 0% of the time, Pallas kernels for 22%

profile of v8, /device:TPU:0, one launch (start us, length us, event | category | flops | bytes accessed | tf_op | source)
XLA Modules:
  0.0 63.5 jit_solution(1881264839518837283)
XLA Ops:
  0.0 7.5 %entry.1 = (bf16[256,1536]{1,0:T(8,128)(2,1)}, bf16[4,176,768]{2,1,0:T(8,128)(2,1)}, bf16[256,256]{1,0:T(8,128)(2,1)}, f32[256,128]{1,0:T(8,128)}, f32[16,128]{1...) custom-call(s32[1]{0:T(128)} %bitcast.refs_0_, ...), custom_call_target="tpu_custom_call" | custom-call | flops 1 | bytes 1 | tf_op jit(solution)/shard_map/entry/pallas_call | solution.py:614
  8.0 6.0 %all-to-all-start = ((bf16[4,176,768]{2,1,0:T(8,128)(2,1)}), bf16[4,176,768]{2,1,0:T(8,128)(2,1)S(1)}, u32[]{:S(2)}, u32[]{:S(2)}) async-start(bf16[4,176,768]{2,1,0:T(8,128)(2,1)} %get-tuple-element.26.after.refs_4_), calls=%async_computation | async-start | bytes 2162688 | tf_op jit(solution)/shard_map/all_to_all | solution.py:647
  14.3 1.6 %collective-permute-start.1 = (bf16[144,1536]{1,0:T(8,128)(2,1)S(1)}, bf16[144,1536]{1,0:T(8,128)(2,1)S(1)}, u32[]{:S(2)}, u32[]{:S(2)}) collective-permute-start(bf16[144,1536]{1,0:T(8,128)(2,1)S(1)} %pair_total.1.total), channel_id=1, source_target_pairs={{0,2},{1,5},{2,0},{3,7},{4,6},{5,1},{6,4},{7,3},{8,10},{9,13},{10,... | collective-permute-start | bytes 1327112 | tf_op jit(solution)/shard_map/ppermute | solution.py:588
  15.8 1.5 %collective-permute-start.2 = (bf16[16,1536]{1,0:T(8,128)(2,1)}, bf16[16,1536]{1,0:T(8,128)(2,1)S(1)}, u32[]{:S(2)}, u32[]{:S(2)}) collective-permute-start(bf16[16,1536]{1,0:T(8,128)(2,1)} %get-tuple-element.35), channel_id=1, source_target_pairs={{0,6},{1,7},{2,4},{3,5},{4,2},{5,3},{6,0},{7,1},{8,14},{9,15},{10,... | collective-permute-start | bytes 147464 | tf_op jit(solution)/shard_map/ppermute | solution.py:582
  17.3 0.7 %collective-permute-start.3 = (bf16[16,1536]{1,0:T(8,128)(2,1)}, bf16[16,1536]{1,0:T(8,128)(2,1)S(1)}, u32[]{:S(2)}, u32[]{:S(2)}) collective-permute-start(bf16[16,1536]{1,0:T(8,128)(2,1)} %get-tuple-element.35), channel_id=1, source_target_pairs={{0,7},{1,6},{2,5},{3,4},{4,3},{5,2},{6,1},{7,0},{8,15},{9,14},{10,... | collective-permute-start | bytes 147464 | tf_op jit(solution)/shard_map/ppermute | solution.py:582
  18.1 3.7 %copy-done = bf16[1536,3072]{1,0:T(8,128)(2,1)S(1)} copy-done((bf16[1536,3072]{1,0:T(8,128)(2,1)S(1)}, bf16[1536,3072]{1,0:T(8,128)(2,1)}, u32[]{:S(2)}) %copy-start) | copy-done | bytes 9437208
  21.7 2.6 %gate.1.refs_0_.refs_2_ = bf16[256,1536]{1,0:T(8,128)(2,1)S(1)} custom-call(bf16[4,176,768]{2,1,0:T(8,128)(2,1)S(1)} %copy-done.2, bf16[256,1536]{1,0:T(8,128)(2,1)S(1)} %copy-done.6, bf16[1536,3072]{1,0:T(8,128)(2,1)S(1)} %copy-done), custom_call_target="tpu_custom_call" | custom-call | flops 1 | bytes 1 | tf_op jit(solution)/shard_map/gate/pallas_call | solution.py:656
  24.4 1.9 %spatial_local.1 = (bf16[256,1536]{1,0:T(8,128)(2,1)S(1)}, f32[256,128]{1,0:T(8,128)S(1)}) custom-call(bf16[256,1536]{1,0:T(8,128)(2,1)S(1)} %gate.1.refs_0_.refs_2_, bf16[256,256]{1,0:T(8,128)(2,1)S(1)} %copy-done.9, f32[256,128]{1,0:T(8,128)S(1)} %copy-done.13, f32[16,128]{1,0:T(8,128)S(1)} %copy-done.14, bf16[4,176,768]{2,1,0:T(8,128)(2,1)S(1)} %copy-done.2), custom_call_target="tpu_custom_call" | custom-call | flops 1 | bytes 1 | tf_op jit(solution)/shard_map/spatial_local/pallas_call | solution.py:667
  27.1 7.8 %collective-permute-done.4.second = bf16[144,1536]{1,0:T(8,128)(2,1)S(1)} collective-permute-done((bf16[144,1536]{1,0:T(8,128)(2,1)S(1)}, bf16[144,1536]{1,0:T(8,128)(2,1)S(1)}, u32[]{:S(2)}, u32[]{:S(2)}) %collective-permute-start.4) | collective-permute-done | bytes 442400 | tf_op jit(solution)/shard_map/ppermute | solution.py:588
  34.9 1.1 %settle.1 = (bf16[128,1536]{1,0:T(8,128)(2,1)S(1)}, bf16[128,1536]{1,0:T(8,128)(2,1)}) custom-call(f32[256,128]{1,0:T(8,128)S(1)} %get-tuple-element.32._.reach, s32[1]{0:T(128)} %bitcast.1.refs_1_.band, bf16[144,1536]{1,0:T(8,128)(2,1)S(1)} %collective-permute-done.1.first, bf16[144,1536]{1,0:T(8,128)(2,1)S(1)} %collective-permute-done.4.second, ...), custom_call_target="tpu_custom_call" | custom-call | flops 1 | bytes 1 | tf_op jit(solution)/shard_map/settle/pallas_call | solution.py:692
  36.0 0.8 %copy-done.11 = bf16[128,1536]{1,0:T(8,128)(2,1)} copy-done((bf16[128,1536]{1,0:T(8,128)(2,1)}, bf16[128,1536]{1,0:T(8,128)(2,1)S(1)}, u32[]{:S(2)}) %copy-start.11) | copy-done | bytes 393240
  36.8 2.3 %temporal.2 = (bf16[64,768]{1,0:T(8,128)(2,1)S(1)}, bf16[64,768]{1,0:T(8,128)(2,1)S(1)}, bf16[64,768]{1,0:T(8,128)(2,1)S(1)}, bf16[64,768]{1,0:T(8,128)(2,1)S(1)}, f32[128,768]{1,0:T(8,128)S(1)}) custom-call(s32[1]{0:T(128)} %bitcast.refs_0_, f32[16,128]{1,0:T(8,128)S(1)} %copy-done.14, bf16[4,176,768]{2,1,0:T(8,128)(2,1)S(1)} %all-to-all-done.refs_2_), custom_call_target="tpu_custom_call" | custom-call | flops 1 | bytes 1 | tf_op jit(solution)/shard_map/temporal/pallas_call | solution.py:733
  39.1 3.7 %collective-permute-start.9 = (bf16[64,768]{1,0:T(8,128)(2,1)S(1)}, bf16[64,768]{1,0:T(8,128)(2,1)S(1)}, u32[]{:S(2)}, u32[]{:S(2)}) collective-permute-start(bf16[64,768]{1,0:T(8,128)(2,1)S(1)} %get-tuple-element.44), channel_id=1, source_target_pairs={{0,24},{8,16},{16,8},{24,0},{1,25},{9,17},{17,9},{25,1},{2,26},{10... | collective-permute-start | bytes 294920 | tf_op jit(solution)/shard_map/ppermute | solution.py:582
  42.9 2.7 %collective-permute-start.10 = (bf16[64,768]{1,0:T(8,128)(2,1)S(1)}, bf16[64,768]{1,0:T(8,128)(2,1)S(1)}, u32[]{:S(2)}, u32[]{:S(2)}) collective-permute-start(bf16[64,768]{1,0:T(8,128)(2,1)S(1)} %get-tuple-element.45), channel_id=1, source_target_pairs={{0,16},{8,24},{16,0},{24,8},{1,17},{9,25},{17,1},{25,9},{2,18},{10... | collective-permute-start | bytes 294920 | tf_op jit(solution)/shard_map/ppermute | solution.py:582
  45.6 1.0 %copy-done.12 = bf16[128,1536]{1,0:T(8,128)(2,1)S(1)} copy-done((bf16[128,1536]{1,0:T(8,128)(2,1)S(1)}, bf16[128,1536]{1,0:T(8,128)(2,1)}, u32[]{:S(2)}) %copy-start.12) | copy-done | bytes 393240
  46.6 1.8 %spatial_incoming.1.refs_4_.refs_1_ = f32[256,1536]{1,0:T(8,128)S(1)} custom-call(s32[1]{0:T(128)} %bitcast.1.refs_1_.band, bf16[256,1536]{1,0:T(8,128)(2,1)S(1)} %copy-done.8, bf16[256,256]{1,0:T(8,128)(2,1)S(1)} %copy-done.10, f32[256,128]{1,0:T(8,128)S(1)} %get-tuple-element.32._.reach, bf16[128,1536]{1,0:T(8,128)(2,1)S(1)} %copy-done.12, ...), custom_call_target="tpu_custom_call" | custom-call | flops 1 | bytes 1 | tf_op jit(solution)/shard_map/spatial_incoming/pallas_call | solution.py:723
  48.4 2.0 %temporal.3 = (bf16[64,768]{1,0:T(8,128)(2,1)S(1)}, bf16[64,768]{1,0:T(8,128)(2,1)S(1)}, bf16[64,768]{1,0:T(8,128)(2,1)S(1)}, bf16[64,768]{1,0:T(8,128)(2,1)S(1)}) custom-call(s32[1]{0:T(128)} %bitcast.refs_0_, f32[16,128]{1,0:T(8,128)S(1)} %copy-done.14, bf16[4,176,768]{2,1,0:T(8,128)(2,1)S(1)} %all-to-all-done.refs_2_, ...), custom_call_target="tpu_custom_call" | custom-call | flops 1 | bytes 1 | tf_op jit(solution)/shard_map/temporal/pallas_call | solution.py:733
  50.3 1.7 %collective-permute-start.6 = (bf16[64,768]{1,0:T(8,128)(2,1)S(1)}, bf16[64,768]{1,0:T(8,128)(2,1)S(1)}, u32[]{:S(2)}, u32[]{:S(2)}) collective-permute-start(bf16[64,768]{1,0:T(8,128)(2,1)S(1)} %get-tuple-element.40), channel_id=1, source_target_pairs={{0,24},{8,16},{16,8},{24,0},{1,25},{9,17},{17,9},{25,1},{2,26},{10... | collective-permute-start | bytes 294920 | tf_op jit(solution)/shard_map/ppermute | solution.py:582
  52.1 1.8 %collective-permute-start.7 = (bf16[64,768]{1,0:T(8,128)(2,1)S(1)}, bf16[64,768]{1,0:T(8,128)(2,1)S(1)}, u32[]{:S(2)}, u32[]{:S(2)}) collective-permute-start(bf16[64,768]{1,0:T(8,128)(2,1)S(1)} %get-tuple-element.41), channel_id=1, source_target_pairs={{0,16},{8,24},{16,0},{24,8},{1,17},{9,25},{17,1},{25,9},{2,18},{10... | collective-permute-start | bytes 294920 | tf_op jit(solution)/shard_map/ppermute | solution.py:582
  53.9 0.9 %collective-permute-start.8 = (bf16[64,768]{1,0:T(8,128)(2,1)S(1)}, bf16[64,768]{1,0:T(8,128)(2,1)S(1)}, u32[]{:S(2)}, u32[]{:S(2)}) collective-permute-start(bf16[64,768]{1,0:T(8,128)(2,1)S(1)} %get-tuple-element.42), channel_id=1, source_target_pairs={{0,8},{8,0},{16,24},{24,16},{1,9},{9,1},{17,25},{25,17},{2,10},{10... | collective-permute-start | bytes 294920 | tf_op jit(solution)/shard_map/ppermute | solution.py:582
  54.8 2.3 %copy-done.1 = bf16[1536,1536]{1,0:T(8,128)(2,1)S(1)} copy-done((bf16[1536,1536]{1,0:T(8,128)(2,1)S(1)}, bf16[1536,1536]{1,0:T(8,128)(2,1)}, u32[]{:S(2)}) %copy-start.1) | copy-done | bytes 4718616
  57.1 2.0 %exit.2.refs_9_ = bf16[2,2,64,1536]{3,2,1,0:T(8,128)(2,1)} custom-call(s32[1]{0:T(128)} %bitcast.refs_0_, f32[256,1536]{1,0:T(8,128)S(1)} %spatial_incoming.1.refs_4_.refs_1_, bf16[256,1536]{1,0:T(8,128)(2,1)S(1)} %gate.1.refs_0_.refs_2_, f32[1536]{0:T(1024)S(1)} %copy-done.15, bf16[1536,1536]{1,0:T(8,128)(2,1)S(1)} %copy-done.1, ...), custom_call_target="tpu_custom_call" | custom-call | flops 1 | bytes 1 | tf_op jit(solution)/shard_map/exit/pallas_call | solution.py:763
  59.1 2.3 %collective-permute-done.7.refs_7_ = bf16[64,768]{1,0:T(8,128)(2,1)S(1)} collective-permute-done((bf16[64,768]{1,0:T(8,128)(2,1)S(1)}, bf16[64,768]{1,0:T(8,128)(2,1)S(1)}, u32[]{:S(2)}, u32[]{:S(2)}) %collective-permute-start.7) | collective-permute-done | bytes 98336 | tf_op jit(solution)/shard_map/ppermute | solution.py:582
  61.4 2.0 %exit.3 = bf16[2,2,64,1536]{3,2,1,0:T(8,128)(2,1)} custom-call(s32[1]{0:T(128)} %bitcast.refs_0_, f32[256,1536]{1,0:T(8,128)S(1)} %spatial_incoming.1.refs_4_.refs_1_, bf16[256,1536]{1,0:T(8,128)(2,1)S(1)} %gate.1.refs_0_.refs_2_, f32[1536]{0:T(1024)S(1)} %copy-done.15, bf16[1536,1536]{1,0:T(8,128)(2,1)S(1)} %copy-done.1, ...), custom_call_target="tpu_custom_call", output_to_operand_aliasing={{}: (9, {})} | custom-call | flops 1 | bytes 1 | tf_op jit(solution)/shard_map/exit/pallas_call | solution.py:763
  (45 shorter events, 1.6 us)
Async XLA Ops:
  7.5 6.6 %copy-start.3 = (bf16[144,1536]{1,0:T(8,128)(2,1)S(1)}, bf16[144,1536]{1,0:T(8,128)(2,1)}, u32[]{:S(2)}) copy-start(bf16[144,1536]{1,0:T(8,128)(2,1)} %get-tuple-element.33.own.band_own) | copy-start | bytes 1327108
  7.5 6.6 %collective-permute-start = (bf16[144,1536]{1,0:T(8,128)(2,1)}, bf16[144,1536]{1,0:T(8,128)(2,1)S(1)}, u32[]{:S(2)}, u32[]{:S(2)}) collective-permute-start(bf16[144,1536]{1,0:T(8,128)(2,1)} %get-tuple-element.34), channel_id=1, source_target_pairs={{0,1},{1,0},{2,3},{3,2},{4,5},{5,4},{6,7},{7,6},{8,9},{9,8},{10,11... | collective-permute-start | bytes 1327112 | tf_op jit(solution)/shard_map/ppermute | solution.py:582
  8.0 10.0 %copy-start.2 = (bf16[4,176,768]{2,1,0:T(8,128)(2,1)S(1)}, bf16[4,176,768]{2,1,0:T(8,128)(2,1)}, u32[]{:S(2)}) copy-start(bf16[4,176,768]{2,1,0:T(8,128)(2,1)} %get-tuple-element.26.after.refs_4_) | copy-start | bytes 3244036
  8.0 28.8 %all-to-all-start = ((bf16[4,176,768]{2,1,0:T(8,128)(2,1)}), bf16[4,176,768]{2,1,0:T(8,128)(2,1)S(1)}, u32[]{:S(2)}, u32[]{:S(2)}) async-start(bf16[4,176,768]{2,1,0:T(8,128)(2,1)} %get-tuple-element.26.after.refs_4_), calls=%async_computation | async-start | bytes 2162688 | tf_op jit(solution)/shard_map/all_to_all | solution.py:647
  14.1 4.0 %copy-start.6 = (bf16[256,1536]{1,0:T(8,128)(2,1)S(1)}, bf16[256,1536]{1,0:T(8,128)(2,1)}, u32[]{:S(2)}) copy-start(bf16[256,1536]{1,0:T(8,128)(2,1)} %get-tuple-element.27.normed) | copy-start | bytes 2359300
  14.1 4.0 %copy-start.4 = (bf16[144,1536]{1,0:T(8,128)(2,1)}, bf16[144,1536]{1,0:T(8,128)(2,1)S(1)}, u32[]{:S(2)}) copy-start(bf16[144,1536]{1,0:T(8,128)(2,1)S(1)} %collective-permute-done.far.band_far) | copy-start | bytes 1327108
  14.3 12.0 %collective-permute-start.1 = (bf16[144,1536]{1,0:T(8,128)(2,1)S(1)}, bf16[144,1536]{1,0:T(8,128)(2,1)S(1)}, u32[]{:S(2)}, u32[]{:S(2)}) collective-permute-start(bf16[144,1536]{1,0:T(8,128)(2,1)S(1)} %pair_total.1.total), channel_id=1, source_target_pairs={{0,2},{1,5},{2,0},{3,7},{4,6},{5,1},{6,4},{7,3},{8,10},{9,13},{10,... | collective-permute-start | bytes 1327112 | tf_op jit(solution)/shard_map/ppermute | solution.py:588
  15.8 10.5 %collective-permute-start.2 = (bf16[16,1536]{1,0:T(8,128)(2,1)}, bf16[16,1536]{1,0:T(8,128)(2,1)S(1)}, u32[]{:S(2)}, u32[]{:S(2)}) collective-permute-start(bf16[16,1536]{1,0:T(8,128)(2,1)} %get-tuple-element.35), channel_id=1, source_target_pairs={{0,6},{1,7},{2,4},{3,5},{4,2},{5,3},{6,0},{7,1},{8,14},{9,15},{10,... | collective-permute-start | bytes 147464 | tf_op jit(solution)/shard_map/ppermute | solution.py:582
  17.3 9.0 %collective-permute-start.3 = (bf16[16,1536]{1,0:T(8,128)(2,1)}, bf16[16,1536]{1,0:T(8,128)(2,1)S(1)}, u32[]{:S(2)}, u32[]{:S(2)}) collective-permute-start(bf16[16,1536]{1,0:T(8,128)(2,1)} %get-tuple-element.35), channel_id=1, source_target_pairs={{0,7},{1,6},{2,5},{3,4},{4,3},{5,2},{6,1},{7,0},{8,15},{9,14},{10,... | collective-permute-start | bytes 147464 | tf_op jit(solution)/shard_map/ppermute | solution.py:582
  18.0 3.7 %copy-start = (bf16[1536,3072]{1,0:T(8,128)(2,1)S(1)}, bf16[1536,3072]{1,0:T(8,128)(2,1)}, u32[]{:S(2)}) copy-start(bf16[1536,3072]{1,0:T(8,128)(2,1)} %weight.1) | copy-start | bytes 28311556
  21.7 2.6 %copy-start.14 = (f32[16,128]{1,0:T(8,128)S(1)}, f32[16,128]{1,0:T(8,128)}, u32[]{:S(2)}) copy-start(f32[16,128]{1,0:T(8,128)} %get-tuple-element.30.refs_3_.refs_1_) | copy-start | bytes 24580
  24.4 10.6 %copy-start.5 = (bf16[144,1536]{1,0:T(8,128)(2,1)S(1)}, bf16[144,1536]{1,0:T(8,128)(2,1)}, u32[]{:S(2)}) copy-start(bf16[144,1536]{1,0:T(8,128)(2,1)} %copy-done.4) | copy-start | bytes 1327108
  26.3 9.7 %copy-start.7 = (bf16[256,1536]{1,0:T(8,128)(2,1)}, bf16[256,1536]{1,0:T(8,128)(2,1)S(1)}, u32[]{:S(2)}) copy-start(bf16[256,1536]{1,0:T(8,128)(2,1)S(1)} %get-tuple-element.31.out_local) | copy-start | bytes 2359300
  26.5 19.1 %copy-start.10 = (bf16[256,256]{1,0:T(8,128)(2,1)S(1)}, bf16[256,256]{1,0:T(8,128)(2,1)}, u32[]{:S(2)}) copy-start(bf16[256,256]{1,0:T(8,128)(2,1)} %get-tuple-element.28.refs_1_.bc) | copy-start | bytes 393220
  26.5 8.4 %collective-permute-start.4 = (bf16[144,1536]{1,0:T(8,128)(2,1)S(1)}, bf16[144,1536]{1,0:T(8,128)(2,1)S(1)}, u32[]{:S(2)}, u32[]{:S(2)}) collective-permute-start(bf16[144,1536]{1,0:T(8,128)(2,1)S(1)} %cross.1), channel_id=1, source_target_pairs={{0,4},{1,3},{2,6},{3,1},{4,0},{5,7},{6,2},{7,5},{8,12},{9,11},{10,... | collective-permute-start | bytes 1327112 | tf_op jit(solution)/shard_map/ppermute | solution.py:588
  36.8 8.8 %copy-start.8 = (bf16[256,1536]{1,0:T(8,128)(2,1)S(1)}, bf16[256,1536]{1,0:T(8,128)(2,1)}, u32[]{:S(2)}) copy-start(bf16[256,1536]{1,0:T(8,128)(2,1)} %copy-done.7) | copy-start | bytes 2359300
  36.8 8.8 %collective-permute-start.5 = (bf16[128,1536]{1,0:T(8,128)(2,1)}, bf16[128,1536]{1,0:T(8,128)(2,1)}, u32[]{:S(2)}, u32[]{:S(2)}) collective-permute-start(bf16[128,1536]{1,0:T(8,128)(2,1)} %get-tuple-element.37), channel_id=1, source_target_pairs={{0,1},{1,0},{2,3},{3,2},{4,5},{5,4},{6,7},{7,6},{8,9},{9,8},{10,11... | collective-permute-start | bytes 1179656 | tf_op jit(solution)/shard_map/ppermute | solution.py:582
  39.1 14.8 %collective-permute-start.9 = (bf16[64,768]{1,0:T(8,128)(2,1)S(1)}, bf16[64,768]{1,0:T(8,128)(2,1)S(1)}, u32[]{:S(2)}, u32[]{:S(2)}) collective-permute-start(bf16[64,768]{1,0:T(8,128)(2,1)S(1)} %get-tuple-element.44), channel_id=1, source_target_pairs={{0,24},{8,16},{16,8},{24,0},{1,25},{9,17},{17,9},{25,1},{2,26},{10... | collective-permute-start | bytes 294920 | tf_op jit(solution)/shard_map/ppermute | solution.py:582
  42.9 11.9 %collective-permute-start.10 = (bf16[64,768]{1,0:T(8,128)(2,1)S(1)}, bf16[64,768]{1,0:T(8,128)(2,1)S(1)}, u32[]{:S(2)}, u32[]{:S(2)}) collective-permute-start(bf16[64,768]{1,0:T(8,128)(2,1)S(1)} %get-tuple-element.45), channel_id=1, source_target_pairs={{0,16},{8,24},{16,0},{24,8},{1,17},{9,25},{17,1},{25,9},{2,18},{10... | collective-permute-start | bytes 294920 | tf_op jit(solution)/shard_map/ppermute | solution.py:582
  45.6 9.2 %collective-permute-start.11 = (bf16[64,768]{1,0:T(8,128)(2,1)S(1)}, bf16[64,768]{1,0:T(8,128)(2,1)S(1)}, u32[]{:S(2)}, u32[]{:S(2)}) collective-permute-start(bf16[64,768]{1,0:T(8,128)(2,1)S(1)} %get-tuple-element.46), channel_id=1, source_target_pairs={{0,8},{8,0},{16,24},{24,16},{1,9},{9,1},{17,25},{25,17},{2,10},{10... | collective-permute-start | bytes 294920 | tf_op jit(solution)/shard_map/ppermute | solution.py:582
  48.4 6.4 %copy-start.15 = (f32[1536]{0:T(1024)S(1)}, f32[1536]{0:T(1024)}, u32[]{:S(2)}) copy-start(f32[1536]{0:T(1024)} %refs_3_.5) | copy-start | bytes 18436
  50.3 8.8 %collective-permute-start.6 = (bf16[64,768]{1,0:T(8,128)(2,1)S(1)}, bf16[64,768]{1,0:T(8,128)(2,1)S(1)}, u32[]{:S(2)}, u32[]{:S(2)}) collective-permute-start(bf16[64,768]{1,0:T(8,128)(2,1)S(1)} %get-tuple-element.40), channel_id=1, source_target_pairs={{0,24},{8,16},{16,8},{24,0},{1,25},{9,17},{17,9},{25,1},{2,26},{10... | collective-permute-start | bytes 294920 | tf_op jit(solution)/shard_map/ppermute | solution.py:582
  52.1 9.4 %collective-permute-start.7 = (bf16[64,768]{1,0:T(8,128)(2,1)S(1)}, bf16[64,768]{1,0:T(8,128)(2,1)S(1)}, u32[]{:S(2)}, u32[]{:S(2)}) collective-permute-start(bf16[64,768]{1,0:T(8,128)(2,1)S(1)} %get-tuple-element.41), channel_id=1, source_target_pairs={{0,16},{8,24},{16,0},{24,8},{1,17},{9,25},{17,1},{25,9},{2,18},{10... | collective-permute-start | bytes 294920 | tf_op jit(solution)/shard_map/ppermute | solution.py:582
  53.9 7.5 %collective-permute-start.8 = (bf16[64,768]{1,0:T(8,128)(2,1)S(1)}, bf16[64,768]{1,0:T(8,128)(2,1)S(1)}, u32[]{:S(2)}, u32[]{:S(2)}) collective-permute-start(bf16[64,768]{1,0:T(8,128)(2,1)S(1)} %get-tuple-element.42), channel_id=1, source_target_pairs={{0,8},{8,0},{16,24},{24,16},{1,9},{9,1},{17,25},{25,17},{2,10},{10... | collective-permute-start | bytes 294920 | tf_op jit(solution)/shard_map/ppermute | solution.py:582
  (5 other events, 9.3 us)

commit v9 on v8

--- a/solution.py
+++ b/solution.py
@@ -109,8 +109,9 @@
     ]
 
 
-def rank_of(device):
-    return device ^ (device >> 1)
+def rank_of(device, shares):
+    code = device ^ (device >> 1)
+    return (shares - code) % shares if isinstance(device, int) else lax.rem(shares - code, shares)
 
 
 def packing(length, group):
@@ -202,7 +203,7 @@
         for inside in range(0, block, group):
             part = (at + inside) // group
             for row in range(rows):
-                piece = rank_of(part * rows + row)
+                piece = rank_of(part * rows + row, shares)
                 here = slice(row * length, (row + 1) * length)
                 payload[piece, :length, :] = values[here, inside : inside + group]
                 pack_rest(
@@ -267,9 +268,10 @@
 
 
 def frame_x(payload, part, frame, rows, columns):
+    shares = payload.shape[0]
     return jnp.concatenate(
         [
-            payload[rank_of(part * rows + row), frame * columns : (frame + 1) * columns, :]
+            payload[rank_of(part * rows + row, shares), frame * columns : (frame + 1) * columns, :]
             for row in range(rows)
         ],
         axis=0,
@@ -289,7 +291,8 @@
 
 
 def local_kernel(frames, rows, columns, head_dim, groups, *refs):
-    after, bc, logits, params, x, out, reach = refs
+    after, bc, logits, params, x, out, reach, done = refs
+    done[...] = jnp.zeros_like(done)
     length = rows * columns
     group = x.shape[2]
     state = bc.shape[1] // 2
@@ -463,7 +466,7 @@
     eye = eye.astype(BF16)
 
     def came(distance):
-        return payload.at[rank_of(here ^ distance)]
+        return payload.at[rank_of(here ^ distance, shares)]
 
     for distance in range(shares):
         b_proj, c_proj, logits = unpacked_rest(came(distance), length)
@@ -643,7 +646,7 @@
         moved = {d: swapped(parts[d], "tm", d) for d in range(shares - 1, 0, -1)}
         return [parts[0]] + list(moved.values())
 
-    line = [rank_of(device) for device in range(shares)]
+    line = [rank_of(device, shares) for device in range(shares)]
     received = lax.all_to_all(
         payload,
         "tm",
@@ -664,10 +667,10 @@
         ],
     )(payload, normed, in_weight)
 
-    out_local, reach = call(
+    out_local, reach, done = call(
         functools.partial(local_kernel, frames, rows, columns, head_dim, groups),
         "spatial_local",
-        [shape_of((count, inner), BF16), shape_of((count, LANES), F32)],
+        [shape_of((count, inner), BF16), shape_of((count, LANES), F32), shape_of((8, LANES), F32)],
         [ANY] + [WHOLE] * 4,
     )(gate, bc_own, logits, params, payload)
 
@@ -687,19 +690,19 @@
             "cross",
             shape_of((frames * half + TAIL, inner), BF16),
             [ANY, SCALAR] + [WHOLE] * 4,
-        )(reach, band, total, first, near, far_decays)
+        )(done, band, total, first, near, far_decays)
         second = crossed(message, "height", 4, 2)
         results = call(
             functools.partial(settle_kernel, frames),
             "settle",
             [shape_of((frames * half, inner), BF16)] * 2,
             [ANY, SCALAR] + [WHOLE] * 6,
-        )(reach, band, first, second, near, far_decays, own, far)
+        )(done, band, first, second, near, far_decays, own, far)
         distance = bands
     while distance < bands:
         far_total = swapped(total, "height", distance)
         finish = distance * 2 >= bands
-        operands = [reach, band, total, far_total] + before + ([own, far] if finish else [])
+        operands = [done, band, total, far_total] + before + ([own, far] if finish else [])
         outs = (
             [shape_of((frames * half, inner), BF16)] * 2
             if finish

time: 63.9 us -> 63.9 us (level)
    unnamed x32 -> x34, local copies, waits for them, and re-layouts: 7.84 us -> 7.83 us
where the time goes in v9:
time: 63.9 us; the launch traced here: 63.5 us
  Pallas kernels  23.4 us (37%)
  starting transfers between devices  21.8 us (34%)
  waiting for transfers between devices  10.1 us (16%)
  local copies, waits for them, and re-layouts  7.83 us (12%)
    ppermute x10, starting transfers between devices, swapped(): lax.ppermute(value, axis, [(source, source ^ distance) for source in rang...  13.6 us
    unnamed x34, local copies, waits for them, and re-layouts  7.83 us
    ppermute x2, waiting for transfers between devices, crossed(): return lax.ppermute(value, axis, pairs)  7.8 us
    pallas_call x1, Pallas kernels, per_device(): call(functools.partial(entry_kernel, shares, heads, state, blocks), 'entr...  7.49 us
    all_to_all x1, starting transfers between devices, per_device(): lax.all_to_all(payload, 'tm', split_axis=0, concat_axis=0, tiled=True, ax...  6.03 us
    pallas_call x2, Pallas kernels, per_device(): call(functools.partial(temporal_kernel, part, parts, per_group, head_dim,...  4.27 us
    pallas_call x2, Pallas kernels, per_device(): call(functools.partial(exit_kernel, part, parts, shares), 'exit', shape_o...  3.93 us
    pallas_call x1, Pallas kernels, per_device(): call(functools.partial(gate_kernel, blocks), 'gate', shape_of((count, inn...  2.59 us
  transfers between devices with their start and end apart: 13, of which 2 were waited for; matrix products, arithmetic and copies ran while one was open for 0% of the time, Pallas kernels for 22%

profile of v9, /device:TPU:0, one launch (start us, length us, event | category | flops | bytes accessed | tf_op | source)
XLA Modules:
  0.0 63.5 jit_solution(5250728040261842319)
XLA Ops:
  0.0 7.5 %entry.1 = (bf16[256,1536]{1,0:T(8,128)(2,1)}, bf16[4,176,768]{2,1,0:T(8,128)(2,1)}, bf16[256,256]{1,0:T(8,128)(2,1)}, f32[256,128]{1,0:T(8,128)}, f32[16,128]{1...) custom-call(s32[1]{0:T(128)} %bitcast.refs_0_, ...), custom_call_target="tpu_custom_call" | custom-call | flops 1 | bytes 1 | tf_op jit(solution)/shard_map/entry/pallas_call | solution.py:617
  8.0 6.0 %all-to-all-start = ((bf16[4,176,768]{2,1,0:T(8,128)(2,1)}), bf16[4,176,768]{2,1,0:T(8,128)(2,1)S(1)}, u32[]{:S(2)}, u32[]{:S(2)}) async-start(bf16[4,176,768]{2,1,0:T(8,128)(2,1)} %get-tuple-element.27.after.refs_4_), calls=%async_computation | async-start | bytes 2162688 | tf_op jit(solution)/shard_map/all_to_all | solution.py:650
  14.3 1.6 %collective-permute-start.1 = (bf16[144,1536]{1,0:T(8,128)(2,1)S(1)}, bf16[144,1536]{1,0:T(8,128)(2,1)S(1)}, u32[]{:S(2)}, u32[]{:S(2)}) collective-permute-start(bf16[144,1536]{1,0:T(8,128)(2,1)S(1)} %pair_total.1.total), channel_id=1, source_target_pairs={{0,2},{1,5},{2,0},{3,7},{4,6},{5,1},{6,4},{7,3},{8,10},{9,13},{10,... | collective-permute-start | bytes 1327112 | tf_op jit(solution)/shard_map/ppermute | solution.py:591
  15.8 1.5 %collective-permute-start.2 = (bf16[16,1536]{1,0:T(8,128)(2,1)}, bf16[16,1536]{1,0:T(8,128)(2,1)S(1)}, u32[]{:S(2)}, u32[]{:S(2)}) collective-permute-start(bf16[16,1536]{1,0:T(8,128)(2,1)} %get-tuple-element.37), channel_id=1, source_target_pairs={{0,6},{1,7},{2,4},{3,5},{4,2},{5,3},{6,0},{7,1},{8,14},{9,15},{10,... | collective-permute-start | bytes 147464 | tf_op jit(solution)/shard_map/ppermute | solution.py:585
  17.3 0.7 %collective-permute-start.3 = (bf16[16,1536]{1,0:T(8,128)(2,1)}, bf16[16,1536]{1,0:T(8,128)(2,1)S(1)}, u32[]{:S(2)}, u32[]{:S(2)}) collective-permute-start(bf16[16,1536]{1,0:T(8,128)(2,1)} %get-tuple-element.37), channel_id=1, source_target_pairs={{0,7},{1,6},{2,5},{3,4},{4,3},{5,2},{6,1},{7,0},{8,15},{9,14},{10,... | collective-permute-start | bytes 147464 | tf_op jit(solution)/shard_map/ppermute | solution.py:585
  18.0 3.7 %copy-done = bf16[1536,3072]{1,0:T(8,128)(2,1)S(1)} copy-done((bf16[1536,3072]{1,0:T(8,128)(2,1)S(1)}, bf16[1536,3072]{1,0:T(8,128)(2,1)}, u32[]{:S(2)}) %copy-start) | copy-done | bytes 9437208
  21.7 2.6 %gate.1.refs_0_.refs_2_ = bf16[256,1536]{1,0:T(8,128)(2,1)S(1)} custom-call(bf16[4,176,768]{2,1,0:T(8,128)(2,1)S(1)} %copy-done.2, bf16[256,1536]{1,0:T(8,128)(2,1)S(1)} %copy-done.6, bf16[1536,3072]{1,0:T(8,128)(2,1)S(1)} %copy-done), custom_call_target="tpu_custom_call" | custom-call | flops 1 | bytes 1 | tf_op jit(solution)/shard_map/gate/pallas_call | solution.py:659
  24.4 1.9 %spatial_local.1 = (bf16[256,1536]{1,0:T(8,128)(2,1)S(1)}, f32[256,128]{1,0:T(8,128)S(1)}, f32[8,128]{1,0:T(8,128)S(1)}) custom-call(bf16[256,1536]{1,0:T(8,128)(2,1)S(1)} %gate.1.refs_0_.refs_2_, bf16[256,256]{1,0:T(8,128)(2,1)S(1)} %copy-done.9, f32[256,128]{1,0:T(8,128)S(1)} %copy-done.14, f32[16,128]{1,0:T(8,128)S(1)} %copy-done.15, ...), custom_call_target="tpu_custom_call" | custom-call | flops 1 | bytes 1 | tf_op jit(solution)/shard_map/spatial_local/pallas_call | solution.py:670
  27.1 7.8 %collective-permute-done.4.second = bf16[144,1536]{1,0:T(8,128)(2,1)S(1)} collective-permute-done((bf16[144,1536]{1,0:T(8,128)(2,1)S(1)}, bf16[144,1536]{1,0:T(8,128)(2,1)S(1)}, u32[]{:S(2)}, u32[]{:S(2)}) %collective-permute-start.4) | collective-permute-done | bytes 442400 | tf_op jit(solution)/shard_map/ppermute | solution.py:591
  34.9 1.1 %settle.1 = (bf16[128,1536]{1,0:T(8,128)(2,1)S(1)}, bf16[128,1536]{1,0:T(8,128)(2,1)}) custom-call(f32[8,128]{1,0:T(8,128)S(1)} %get-tuple-element.34._, s32[1]{0:T(128)} %bitcast.1.refs_1_.band, bf16[144,1536]{1,0:T(8,128)(2,1)S(1)} %collective-permute-done.1.first, bf16[144,1536]{1,0:T(8,128)(2,1)S(1)} %collective-permute-done.4.second, ...), custom_call_target="tpu_custom_call" | custom-call | flops 1 | bytes 1 | tf_op jit(solution)/shard_map/settle/pallas_call | solution.py:695
  36.0 0.8 %copy-done.10 = bf16[128,1536]{1,0:T(8,128)(2,1)} copy-done((bf16[128,1536]{1,0:T(8,128)(2,1)}, bf16[128,1536]{1,0:T(8,128)(2,1)S(1)}, u32[]{:S(2)}) %copy-start.10) | copy-done | bytes 393240
  36.8 2.3 %temporal.2 = (bf16[64,768]{1,0:T(8,128)(2,1)S(1)}, bf16[64,768]{1,0:T(8,128)(2,1)S(1)}, bf16[64,768]{1,0:T(8,128)(2,1)S(1)}, bf16[64,768]{1,0:T(8,128)(2,1)S(1)}, f32[128,768]{1,0:T(8,128)S(1)}) custom-call(s32[1]{0:T(128)} %bitcast.refs_0_, f32[16,128]{1,0:T(8,128)S(1)} %copy-done.15, bf16[4,176,768]{2,1,0:T(8,128)(2,1)S(1)} %all-to-all-done.refs_2_), custom_call_target="tpu_custom_call" | custom-call | flops 1 | bytes 1 | tf_op jit(solution)/shard_map/temporal/pallas_call | solution.py:736
  39.1 3.7 %collective-permute-start.9 = (bf16[64,768]{1,0:T(8,128)(2,1)S(1)}, bf16[64,768]{1,0:T(8,128)(2,1)S(1)}, u32[]{:S(2)}, u32[]{:S(2)}) collective-permute-start(bf16[64,768]{1,0:T(8,128)(2,1)S(1)} %get-tuple-element.46), channel_id=1, source_target_pairs={{0,24},{8,16},{16,8},{24,0},{1,25},{9,17},{17,9},{25,1},{2,26},{10... | collective-permute-start | bytes 294920 | tf_op jit(solution)/shard_map/ppermute | solution.py:585
  42.8 2.7 %collective-permute-start.10 = (bf16[64,768]{1,0:T(8,128)(2,1)S(1)}, bf16[64,768]{1,0:T(8,128)(2,1)S(1)}, u32[]{:S(2)}, u32[]{:S(2)}) collective-permute-start(bf16[64,768]{1,0:T(8,128)(2,1)S(1)} %get-tuple-element.47), channel_id=1, source_target_pairs={{0,16},{8,24},{16,0},{24,8},{1,17},{9,25},{17,1},{25,9},{2,18},{10... | collective-permute-start | bytes 294920 | tf_op jit(solution)/shard_map/ppermute | solution.py:585
  45.6 1.0 %copy-done.11 = bf16[128,1536]{1,0:T(8,128)(2,1)S(1)} copy-done((bf16[128,1536]{1,0:T(8,128)(2,1)S(1)}, bf16[128,1536]{1,0:T(8,128)(2,1)}, u32[]{:S(2)}) %copy-start.11) | copy-done | bytes 393240
  46.5 1.8 %spatial_incoming.1.refs_4_.refs_1_ = f32[256,1536]{1,0:T(8,128)S(1)} custom-call(s32[1]{0:T(128)} %bitcast.1.refs_1_.band, bf16[256,1536]{1,0:T(8,128)(2,1)S(1)} %copy-done.8, bf16[256,256]{1,0:T(8,128)(2,1)S(1)} %copy-done.9, f32[256,128]{1,0:T(8,128)S(1)} %copy-done.13, bf16[128,1536]{1,0:T(8,128)(2,1)S(1)} %copy-done.11, ...), custom_call_target="tpu_custom_call" | custom-call | flops 1 | bytes 1 | tf_op jit(solution)/shard_map/spatial_incoming/pallas_call | solution.py:726
  48.3 2.0 %temporal.3 = (bf16[64,768]{1,0:T(8,128)(2,1)S(1)}, bf16[64,768]{1,0:T(8,128)(2,1)S(1)}, bf16[64,768]{1,0:T(8,128)(2,1)S(1)}, bf16[64,768]{1,0:T(8,128)(2,1)S(1)}) custom-call(s32[1]{0:T(128)} %bitcast.refs_0_, f32[16,128]{1,0:T(8,128)S(1)} %copy-done.15, bf16[4,176,768]{2,1,0:T(8,128)(2,1)S(1)} %all-to-all-done.refs_2_, ...), custom_call_target="tpu_custom_call" | custom-call | flops 1 | bytes 1 | tf_op jit(solution)/shard_map/temporal/pallas_call | solution.py:736
  50.3 1.7 %collective-permute-start.6 = (bf16[64,768]{1,0:T(8,128)(2,1)S(1)}, bf16[64,768]{1,0:T(8,128)(2,1)S(1)}, u32[]{:S(2)}, u32[]{:S(2)}) collective-permute-start(bf16[64,768]{1,0:T(8,128)(2,1)S(1)} %get-tuple-element.42), channel_id=1, source_target_pairs={{0,24},{8,16},{16,8},{24,0},{1,25},{9,17},{17,9},{25,1},{2,26},{10... | collective-permute-start | bytes 294920 | tf_op jit(solution)/shard_map/ppermute | solution.py:585
  52.0 1.8 %collective-permute-start.7 = (bf16[64,768]{1,0:T(8,128)(2,1)S(1)}, bf16[64,768]{1,0:T(8,128)(2,1)S(1)}, u32[]{:S(2)}, u32[]{:S(2)}) collective-permute-start(bf16[64,768]{1,0:T(8,128)(2,1)S(1)} %get-tuple-element.43), channel_id=1, source_target_pairs={{0,16},{8,24},{16,0},{24,8},{1,17},{9,25},{17,1},{25,9},{2,18},{10... | collective-permute-start | bytes 294920 | tf_op jit(solution)/shard_map/ppermute | solution.py:585
  53.8 0.9 %collective-permute-start.8 = (bf16[64,768]{1,0:T(8,128)(2,1)S(1)}, bf16[64,768]{1,0:T(8,128)(2,1)S(1)}, u32[]{:S(2)}, u32[]{:S(2)}) collective-permute-start(bf16[64,768]{1,0:T(8,128)(2,1)S(1)} %get-tuple-element.44), channel_id=1, source_target_pairs={{0,8},{8,0},{16,24},{24,16},{1,9},{9,1},{17,25},{25,17},{2,10},{10... | collective-permute-start | bytes 294920 | tf_op jit(solution)/shard_map/ppermute | solution.py:585
  54.8 2.3 %copy-done.1 = bf16[1536,1536]{1,0:T(8,128)(2,1)S(1)} copy-done((bf16[1536,1536]{1,0:T(8,128)(2,1)S(1)}, bf16[1536,1536]{1,0:T(8,128)(2,1)}, u32[]{:S(2)}) %copy-start.1) | copy-done | bytes 4718616
  57.1 2.0 %exit.2.refs_9_ = bf16[2,2,64,1536]{3,2,1,0:T(8,128)(2,1)} custom-call(s32[1]{0:T(128)} %bitcast.refs_0_, f32[256,1536]{1,0:T(8,128)S(1)} %spatial_incoming.1.refs_4_.refs_1_, bf16[256,1536]{1,0:T(8,128)(2,1)S(1)} %gate.1.refs_0_.refs_2_, f32[1536]{0:T(1024)S(1)} %copy-done.16, bf16[1536,1536]{1,0:T(8,128)(2,1)S(1)} %copy-done.1, ...), custom_call_target="tpu_custom_call" | custom-call | flops 1 | bytes 1 | tf_op jit(solution)/shard_map/exit/pallas_call | solution.py:766
  59.1 2.3 %collective-permute-done.7.refs_7_ = bf16[64,768]{1,0:T(8,128)(2,1)S(1)} collective-permute-done((bf16[64,768]{1,0:T(8,128)(2,1)S(1)}, bf16[64,768]{1,0:T(8,128)(2,1)S(1)}, u32[]{:S(2)}, u32[]{:S(2)}) %collective-permute-start.7) | collective-permute-done | bytes 98336 | tf_op jit(solution)/shard_map/ppermute | solution.py:585
  61.4 2.0 %exit.3 = bf16[2,2,64,1536]{3,2,1,0:T(8,128)(2,1)} custom-call(s32[1]{0:T(128)} %bitcast.refs_0_, f32[256,1536]{1,0:T(8,128)S(1)} %spatial_incoming.1.refs_4_.refs_1_, bf16[256,1536]{1,0:T(8,128)(2,1)S(1)} %gate.1.refs_0_.refs_2_, f32[1536]{0:T(1024)S(1)} %copy-done.16, bf16[1536,1536]{1,0:T(8,128)(2,1)S(1)} %copy-done.1, ...), custom_call_target="tpu_custom_call", output_to_operand_aliasing={{}: (9, {})} | custom-call | flops 1 | bytes 1 | tf_op jit(solution)/shard_map/exit/pallas_call | solution.py:766
  (47 shorter events, 1.6 us)
Async XLA Ops:
  7.5 6.6 %copy-start.3 = (bf16[144,1536]{1,0:T(8,128)(2,1)S(1)}, bf16[144,1536]{1,0:T(8,128)(2,1)}, u32[]{:S(2)}) copy-start(bf16[144,1536]{1,0:T(8,128)(2,1)} %get-tuple-element.35.own.band_own) | copy-start | bytes 1327108
  7.5 6.6 %collective-permute-start = (bf16[144,1536]{1,0:T(8,128)(2,1)}, bf16[144,1536]{1,0:T(8,128)(2,1)S(1)}, u32[]{:S(2)}, u32[]{:S(2)}) collective-permute-start(bf16[144,1536]{1,0:T(8,128)(2,1)} %get-tuple-element.36), channel_id=1, source_target_pairs={{0,1},{1,0},{2,3},{3,2},{4,5},{5,4},{6,7},{7,6},{8,9},{9,8},{10,11... | collective-permute-start | bytes 1327112 | tf_op jit(solution)/shard_map/ppermute | solution.py:585
  8.0 10.0 %copy-start.2 = (bf16[4,176,768]{2,1,0:T(8,128)(2,1)S(1)}, bf16[4,176,768]{2,1,0:T(8,128)(2,1)}, u32[]{:S(2)}) copy-start(bf16[4,176,768]{2,1,0:T(8,128)(2,1)} %get-tuple-element.27.after.refs_4_) | copy-start | bytes 3244036
  8.0 28.7 %all-to-all-start = ((bf16[4,176,768]{2,1,0:T(8,128)(2,1)}), bf16[4,176,768]{2,1,0:T(8,128)(2,1)S(1)}, u32[]{:S(2)}, u32[]{:S(2)}) async-start(bf16[4,176,768]{2,1,0:T(8,128)(2,1)} %get-tuple-element.27.after.refs_4_), calls=%async_computation | async-start | bytes 2162688 | tf_op jit(solution)/shard_map/all_to_all | solution.py:650
  14.1 4.0 %copy-start.6 = (bf16[256,1536]{1,0:T(8,128)(2,1)S(1)}, bf16[256,1536]{1,0:T(8,128)(2,1)}, u32[]{:S(2)}) copy-start(bf16[256,1536]{1,0:T(8,128)(2,1)} %get-tuple-element.28.normed) | copy-start | bytes 2359300
  14.1 4.0 %copy-start.4 = (bf16[144,1536]{1,0:T(8,128)(2,1)}, bf16[144,1536]{1,0:T(8,128)(2,1)S(1)}, u32[]{:S(2)}) copy-start(bf16[144,1536]{1,0:T(8,128)(2,1)S(1)} %collective-permute-done.far.band_far) | copy-start | bytes 1327108
  14.3 12.1 %collective-permute-start.1 = (bf16[144,1536]{1,0:T(8,128)(2,1)S(1)}, bf16[144,1536]{1,0:T(8,128)(2,1)S(1)}, u32[]{:S(2)}, u32[]{:S(2)}) collective-permute-start(bf16[144,1536]{1,0:T(8,128)(2,1)S(1)} %pair_total.1.total), channel_id=1, source_target_pairs={{0,2},{1,5},{2,0},{3,7},{4,6},{5,1},{6,4},{7,3},{8,10},{9,13},{10,... | collective-permute-start | bytes 1327112 | tf_op jit(solution)/shard_map/ppermute | solution.py:591
  15.8 10.5 %collective-permute-start.2 = (bf16[16,1536]{1,0:T(8,128)(2,1)}, bf16[16,1536]{1,0:T(8,128)(2,1)S(1)}, u32[]{:S(2)}, u32[]{:S(2)}) collective-permute-start(bf16[16,1536]{1,0:T(8,128)(2,1)} %get-tuple-element.37), channel_id=1, source_target_pairs={{0,6},{1,7},{2,4},{3,5},{4,2},{5,3},{6,0},{7,1},{8,14},{9,15},{10,... | collective-permute-start | bytes 147464 | tf_op jit(solution)/shard_map/ppermute | solution.py:585
  17.3 9.0 %collective-permute-start.3 = (bf16[16,1536]{1,0:T(8,128)(2,1)}, bf16[16,1536]{1,0:T(8,128)(2,1)S(1)}, u32[]{:S(2)}, u32[]{:S(2)}) collective-permute-start(bf16[16,1536]{1,0:T(8,128)(2,1)} %get-tuple-element.37), channel_id=1, source_target_pairs={{0,7},{1,6},{2,5},{3,4},{4,3},{5,2},{6,1},{7,0},{8,15},{9,14},{10,... | collective-permute-start | bytes 147464 | tf_op jit(solution)/shard_map/ppermute | solution.py:585
  18.0 3.7 %copy-start = (bf16[1536,3072]{1,0:T(8,128)(2,1)S(1)}, bf16[1536,3072]{1,0:T(8,128)(2,1)}, u32[]{:S(2)}) copy-start(bf16[1536,3072]{1,0:T(8,128)(2,1)} %weight.1) | copy-start | bytes 28311556
  21.7 2.6 %copy-start.15 = (f32[16,128]{1,0:T(8,128)S(1)}, f32[16,128]{1,0:T(8,128)}, u32[]{:S(2)}) copy-start(f32[16,128]{1,0:T(8,128)} %get-tuple-element.31.refs_3_.refs_1_) | copy-start | bytes 24580
  24.4 10.6 %copy-start.5 = (bf16[144,1536]{1,0:T(8,128)(2,1)S(1)}, bf16[144,1536]{1,0:T(8,128)(2,1)}, u32[]{:S(2)}) copy-start(bf16[144,1536]{1,0:T(8,128)(2,1)} %copy-done.4) | copy-start | bytes 1327108
  26.3 9.7 %copy-start.7 = (bf16[256,1536]{1,0:T(8,128)(2,1)}, bf16[256,1536]{1,0:T(8,128)(2,1)S(1)}, u32[]{:S(2)}) copy-start(bf16[256,1536]{1,0:T(8,128)(2,1)S(1)} %get-tuple-element.32.out_local) | copy-start | bytes 2359300
  26.5 8.4 %collective-permute-start.4 = (bf16[144,1536]{1,0:T(8,128)(2,1)S(1)}, bf16[144,1536]{1,0:T(8,128)(2,1)S(1)}, u32[]{:S(2)}, u32[]{:S(2)}) collective-permute-start(bf16[144,1536]{1,0:T(8,128)(2,1)S(1)} %cross.1), channel_id=1, source_target_pairs={{0,4},{1,3},{2,6},{3,1},{4,0},{5,7},{6,2},{7,5},{8,12},{9,11},{10,... | collective-permute-start | bytes 1327112 | tf_op jit(solution)/shard_map/ppermute | solution.py:591
  34.9 10.6 %copy-start.13 = (f32[256,128]{1,0:T(8,128)S(1)}, f32[256,128]{1,0:T(8,128)}, u32[]{:S(2)}) copy-start(f32[256,128]{1,0:T(8,128)} %copy-done.12) | copy-start | bytes 393220
  36.8 8.8 %copy-start.8 = (bf16[256,1536]{1,0:T(8,128)(2,1)S(1)}, bf16[256,1536]{1,0:T(8,128)(2,1)}, u32[]{:S(2)}) copy-start(bf16[256,1536]{1,0:T(8,128)(2,1)} %copy-done.7) | copy-start | bytes 2359300
  36.8 8.8 %collective-permute-start.5 = (bf16[128,1536]{1,0:T(8,128)(2,1)}, bf16[128,1536]{1,0:T(8,128)(2,1)}, u32[]{:S(2)}, u32[]{:S(2)}) collective-permute-start(bf16[128,1536]{1,0:T(8,128)(2,1)} %get-tuple-element.39), channel_id=1, source_target_pairs={{0,1},{1,0},{2,3},{3,2},{4,5},{5,4},{6,7},{7,6},{8,9},{9,8},{10,11... | collective-permute-start | bytes 1179656 | tf_op jit(solution)/shard_map/ppermute | solution.py:585
  39.1 14.8 %collective-permute-start.9 = (bf16[64,768]{1,0:T(8,128)(2,1)S(1)}, bf16[64,768]{1,0:T(8,128)(2,1)S(1)}, u32[]{:S(2)}, u32[]{:S(2)}) collective-permute-start(bf16[64,768]{1,0:T(8,128)(2,1)S(1)} %get-tuple-element.46), channel_id=1, source_target_pairs={{0,24},{8,16},{16,8},{24,0},{1,25},{9,17},{17,9},{25,1},{2,26},{10... | collective-permute-start | bytes 294920 | tf_op jit(solution)/shard_map/ppermute | solution.py:585
  42.8 12.0 %collective-permute-start.10 = (bf16[64,768]{1,0:T(8,128)(2,1)S(1)}, bf16[64,768]{1,0:T(8,128)(2,1)S(1)}, u32[]{:S(2)}, u32[]{:S(2)}) collective-permute-start(bf16[64,768]{1,0:T(8,128)(2,1)S(1)} %get-tuple-element.47), channel_id=1, source_target_pairs={{0,16},{8,24},{16,0},{24,8},{1,17},{9,25},{17,1},{25,9},{2,18},{10... | collective-permute-start | bytes 294920 | tf_op jit(solution)/shard_map/ppermute | solution.py:585
  45.5 9.2 %collective-permute-start.11 = (bf16[64,768]{1,0:T(8,128)(2,1)S(1)}, bf16[64,768]{1,0:T(8,128)(2,1)S(1)}, u32[]{:S(2)}, u32[]{:S(2)}) collective-permute-start(bf16[64,768]{1,0:T(8,128)(2,1)S(1)} %get-tuple-element.48), channel_id=1, source_target_pairs={{0,8},{8,0},{16,24},{24,16},{1,9},{9,1},{17,25},{25,17},{2,10},{10... | collective-permute-start | bytes 294920 | tf_op jit(solution)/shard_map/ppermute | solution.py:585
  48.3 6.4 %copy-start.16 = (f32[1536]{0:T(1024)S(1)}, f32[1536]{0:T(1024)}, u32[]{:S(2)}) copy-start(f32[1536]{0:T(1024)} %refs_3_.5) | copy-start | bytes 18436
  50.3 8.8 %collective-permute-start.6 = (bf16[64,768]{1,0:T(8,128)(2,1)S(1)}, bf16[64,768]{1,0:T(8,128)(2,1)S(1)}, u32[]{:S(2)}, u32[]{:S(2)}) collective-permute-start(bf16[64,768]{1,0:T(8,128)(2,1)S(1)} %get-tuple-element.42), channel_id=1, source_target_pairs={{0,24},{8,16},{16,8},{24,0},{1,25},{9,17},{17,9},{25,1},{2,26},{10... | collective-permute-start | bytes 294920 | tf_op jit(solution)/shard_map/ppermute | solution.py:585
  52.0 9.4 %collective-permute-start.7 = (bf16[64,768]{1,0:T(8,128)(2,1)S(1)}, bf16[64,768]{1,0:T(8,128)(2,1)S(1)}, u32[]{:S(2)}, u32[]{:S(2)}) collective-permute-start(bf16[64,768]{1,0:T(8,128)(2,1)S(1)} %get-tuple-element.43), channel_id=1, source_target_pairs={{0,16},{8,24},{16,0},{24,8},{1,17},{9,25},{17,1},{25,9},{2,18},{10... | collective-permute-start | bytes 294920 | tf_op jit(solution)/shard_map/ppermute | solution.py:585
  53.8 7.5 %collective-permute-start.8 = (bf16[64,768]{1,0:T(8,128)(2,1)S(1)}, bf16[64,768]{1,0:T(8,128)(2,1)S(1)}, u32[]{:S(2)}, u32[]{:S(2)}) collective-permute-start(bf16[64,768]{1,0:T(8,128)(2,1)S(1)} %get-tuple-element.44), channel_id=1, source_target_pairs={{0,8},{8,0},{16,24},{24,16},{1,9},{9,1},{17,25},{25,17},{2,10},{10... | collective-permute-start | bytes 294920 | tf_op jit(solution)/shard_map/ppermute | solution.py:585
  (6 other events, 10.2 us)

commit v10 on v9

--- a/solution.py
+++ b/solution.py
@@ -157,11 +157,11 @@
     first = rows * frames
     dt_copy = pltpu.make_async_copy(dt_weight, dt_held, sems.at[first])
     dt_copy.start()
-    bc_copy = pltpu.make_async_copy(bc_weight, bc_held, sems.at[first + 1])
-    bc_copy.start()
     copies = column_copies(weight, held_weight, sems, first + 2, 0, blocks)
     for copy in copies:
         copy.start()
+    bc_copy = pltpu.make_async_copy(bc_weight, bc_held, sems.at[first + 1])
+    bc_copy.start()
 
     table[...] = jnp.zeros_like(table)
     table[0:1, : 2 * heads] = bias[...].reshape(1, 2 * heads)
@@ -187,13 +187,16 @@
     dt_copy.wait()
     logits[:, : 2 * heads] = dot_nt(normed[...], dt_held[...]).astype(BF16).astype(F32)
     dt_heads = jnp.transpose(logits[...]).astype(BF16)[heads : 2 * heads + TAIL]
-    bc_copy.wait()
-    bc = dot(normed[...], bc_held[...]).astype(BF16)
-    bc_own[...] = bc[:, : 2 * state]
     scan = [
         end_factors(frame_of(logits, frame, rows, frames, columns), params, rows * columns)
         for frame in range(frames)
     ]
+
+    def leave(piece, at, sem):
+        outgoing.append(
+            pltpu.make_async_copy(payload.at[piece, at], payload_out.at[piece, at], out_sems.at[sem])
+        )
+        outgoing[-1].start()
 
     block = held_weight.shape[1] // blocks
     for index, copy in enumerate(copies):
@@ -201,24 +204,25 @@
         at = index * block
         values = dot(normed[...], held_weight[:, at : at + block]).astype(BF16)
         for inside in range(0, block, group):
-            part = (at + inside) // group
             for row in range(rows):
-                piece = rank_of(part * rows + row, shares)
-                here = slice(row * length, (row + 1) * length)
-                payload[piece, :length, :] = values[here, inside : inside + group]
-                pack_rest(
-                    payload.at[piece],
-                    length,
-                    bc[here, 2 * state : 3 * state],
-                    bc[here, 3 * state :],
-                    dt_heads[part * per_group : part * per_group + TAIL, here],
-                )
-                outgoing.append(
-                    pltpu.make_async_copy(
-                        payload.at[piece], payload_out.at[piece], out_sems.at[1 + piece]
-                    )
-                )
-                outgoing[-1].start()
+                piece = rank_of((at + inside) // group * rows + row, shares)
+                payload[piece, :length, :] = values[row * length : (row + 1) * length, inside : inside + group]
+                leave(piece, pl.ds(0, length), 1 + piece)
+    bc_copy.wait()
+    bc = dot(normed[...], bc_held[...]).astype(BF16)
+    bc_own[...] = bc[:, : 2 * state]
+    for part in range(groups):
+        for row in range(rows):
+            piece = rank_of(part * rows + row, shares)
+            here = slice(row * length, (row + 1) * length)
+            pack_rest(
+                payload.at[piece],
+                length,
+                bc[here, 2 * state : 3 * state],
+                bc[here, 3 * state :],
+                dt_heads[part * per_group : part * per_group + TAIL, here],
+            )
+            leave(piece, pl.ds(length, payload.shape[1] - length), 1 + shares + piece)
     half = state // 2
     head_dim = groups * group // heads
     mine = band[0] % 2 == 0
@@ -638,7 +642,7 @@
             pltpu.VMEM((count, width), BF16),
             pltpu.VMEM(packed, BF16),
             pltpu.SemaphoreType.DMA((rows * frames + 2 + blocks,)),
-            pltpu.SemaphoreType.DMA((1 + shares,)),
+            pltpu.SemaphoreType.DMA((1 + 2 * shares,)),
         ],
     )(here, band, tokens, norm_gain, dt_bias, decay_rate, dt_weight.T, bc_weight, in_weight)
 

time: 63.9 us -> 63.9 us (level)
  no operation moved by 1% of the time
where the time goes in v10:
time: 63.9 us; the launch traced here: 63.5 us
  Pallas kernels  23.4 us (37%)
  starting transfers between devices  21.8 us (34%)
  waiting for transfers between devices  10.1 us (16%)
  local copies, waits for them, and re-layouts  7.83 us (12%)
    ppermute x10, starting transfers between devices, swapped(): lax.ppermute(value, axis, [(source, source ^ distance) for source in rang...  13.6 us
    unnamed x34, local copies, waits for them, and re-layouts  7.83 us
    ppermute x2, waiting for transfers between devices, crossed(): return lax.ppermute(value, axis, pairs)  7.8 us
    pallas_call x1, Pallas kernels, per_device(): call(functools.partial(entry_kernel, shares, heads, state, blocks), 'entr...  7.52 us
    all_to_all x1, starting transfers between devices, per_device(): lax.all_to_all(payload, 'tm', split_axis=0, concat_axis=0, tiled=True, ax...  6.03 us
    pallas_call x2, Pallas kernels, per_device(): call(functools.partial(temporal_kernel, part, parts, per_group, head_dim,...  4.27 us
    pallas_call x2, Pallas kernels, per_device(): call(functools.partial(exit_kernel, part, parts, shares), 'exit', shape_o...  3.92 us
    pallas_call x1, Pallas kernels, per_device(): call(functools.partial(gate_kernel, blocks), 'gate', shape_of((count, inn...  2.59 us
  transfers between devices with their start and end apart: 13, of which 2 were waited for; matrix products, arithmetic and copies ran while one was open for 0% of the time, Pallas kernels for 22%

profile of v10, /device:TPU:0, one launch (start us, length us, event | category | flops | bytes accessed | tf_op | source)
XLA Modules:
  0.0 63.5 jit_solution(5110630837957924805)
XLA Ops:
  0.0 7.5 %entry.1 = (bf16[256,1536]{1,0:T(8,128)(2,1)}, bf16[4,176,768]{2,1,0:T(8,128)(2,1)}, bf16[256,256]{1,0:T(8,128)(2,1)}, f32[256,128]{1,0:T(8,128)}, f32[16,128]{1...) custom-call(s32[1]{0:T(128)} %bitcast.refs_0_, ...), custom_call_target="tpu_custom_call" | custom-call | flops 1 | bytes 1 | tf_op jit(solution)/shard_map/entry/pallas_call | solution.py:621
  8.1 6.0 %all-to-all-start = ((bf16[4,176,768]{2,1,0:T(8,128)(2,1)}), bf16[4,176,768]{2,1,0:T(8,128)(2,1)S(1)}, u32[]{:S(2)}, u32[]{:S(2)}) async-start(bf16[4,176,768]{2,1,0:T(8,128)(2,1)} %get-tuple-element.27.after.refs_4_), calls=%async_computation | async-start | bytes 2162688 | tf_op jit(solution)/shard_map/all_to_all | solution.py:654
  14.3 1.6 %collective-permute-start.1 = (bf16[144,1536]{1,0:T(8,128)(2,1)S(1)}, bf16[144,1536]{1,0:T(8,128)(2,1)S(1)}, u32[]{:S(2)}, u32[]{:S(2)}) collective-permute-start(bf16[144,1536]{1,0:T(8,128)(2,1)S(1)} %pair_total.1.total), channel_id=1, source_target_pairs={{0,2},{1,5},{2,0},{3,7},{4,6},{5,1},{6,4},{7,3},{8,10},{9,13},{10,... | collective-permute-start | bytes 1327112 | tf_op jit(solution)/shard_map/ppermute | solution.py:595
  15.9 1.5 %collective-permute-start.2 = (bf16[16,1536]{1,0:T(8,128)(2,1)}, bf16[16,1536]{1,0:T(8,128)(2,1)S(1)}, u32[]{:S(2)}, u32[]{:S(2)}) collective-permute-start(bf16[16,1536]{1,0:T(8,128)(2,1)} %get-tuple-element.37), channel_id=1, source_target_pairs={{0,6},{1,7},{2,4},{3,5},{4,2},{5,3},{6,0},{7,1},{8,14},{9,15},{10,... | collective-permute-start | bytes 147464 | tf_op jit(solution)/shard_map/ppermute | solution.py:589
  17.3 0.7 %collective-permute-start.3 = (bf16[16,1536]{1,0:T(8,128)(2,1)}, bf16[16,1536]{1,0:T(8,128)(2,1)S(1)}, u32[]{:S(2)}, u32[]{:S(2)}) collective-permute-start(bf16[16,1536]{1,0:T(8,128)(2,1)} %get-tuple-element.37), channel_id=1, source_target_pairs={{0,7},{1,6},{2,5},{3,4},{4,3},{5,2},{6,1},{7,0},{8,15},{9,14},{10,... | collective-permute-start | bytes 147464 | tf_op jit(solution)/shard_map/ppermute | solution.py:589
  18.1 3.7 %copy-done = bf16[1536,3072]{1,0:T(8,128)(2,1)S(1)} copy-done((bf16[1536,3072]{1,0:T(8,128)(2,1)S(1)}, bf16[1536,3072]{1,0:T(8,128)(2,1)}, u32[]{:S(2)}) %copy-start) | copy-done | bytes 9437208
  21.7 2.6 %gate.1.refs_0_.refs_2_ = bf16[256,1536]{1,0:T(8,128)(2,1)S(1)} custom-call(bf16[4,176,768]{2,1,0:T(8,128)(2,1)S(1)} %copy-done.2, bf16[256,1536]{1,0:T(8,128)(2,1)S(1)} %copy-done.6, bf16[1536,3072]{1,0:T(8,128)(2,1)S(1)} %copy-done), custom_call_target="tpu_custom_call" | custom-call | flops 1 | bytes 1 | tf_op jit(solution)/shard_map/gate/pallas_call | solution.py:663
  24.4 1.9 %spatial_local.1 = (bf16[256,1536]{1,0:T(8,128)(2,1)S(1)}, f32[256,128]{1,0:T(8,128)S(1)}, f32[8,128]{1,0:T(8,128)S(1)}) custom-call(bf16[256,1536]{1,0:T(8,128)(2,1)S(1)} %gate.1.refs_0_.refs_2_, bf16[256,256]{1,0:T(8,128)(2,1)S(1)} %copy-done.9, f32[256,128]{1,0:T(8,128)S(1)} %copy-done.14, f32[16,128]{1,0:T(8,128)S(1)} %copy-done.15, ...), custom_call_target="tpu_custom_call" | custom-call | flops 1 | bytes 1 | tf_op jit(solution)/shard_map/spatial_local/pallas_call | solution.py:674
  27.1 7.8 %collective-permute-done.4.second = bf16[144,1536]{1,0:T(8,128)(2,1)S(1)} collective-permute-done((bf16[144,1536]{1,0:T(8,128)(2,1)S(1)}, bf16[144,1536]{1,0:T(8,128)(2,1)S(1)}, u32[]{:S(2)}, u32[]{:S(2)}) %collective-permute-start.4) | collective-permute-done | bytes 442400 | tf_op jit(solution)/shard_map/ppermute | solution.py:595
  34.9 1.1 %settle.1 = (bf16[128,1536]{1,0:T(8,128)(2,1)S(1)}, bf16[128,1536]{1,0:T(8,128)(2,1)}) custom-call(f32[8,128]{1,0:T(8,128)S(1)} %get-tuple-element.34._, s32[1]{0:T(128)} %bitcast.1.refs_1_.band, bf16[144,1536]{1,0:T(8,128)(2,1)S(1)} %collective-permute-done.1.first, bf16[144,1536]{1,0:T(8,128)(2,1)S(1)} %collective-permute-done.4.second, ...), custom_call_target="tpu_custom_call" | custom-call | flops 1 | bytes 1 | tf_op jit(solution)/shard_map/settle/pallas_call | solution.py:699
  36.0 0.8 %copy-done.10 = bf16[128,1536]{1,0:T(8,128)(2,1)} copy-done((bf16[128,1536]{1,0:T(8,128)(2,1)}, bf16[128,1536]{1,0:T(8,128)(2,1)S(1)}, u32[]{:S(2)}) %copy-start.10) | copy-done | bytes 393240
  36.8 2.3 %temporal.2 = (bf16[64,768]{1,0:T(8,128)(2,1)S(1)}, bf16[64,768]{1,0:T(8,128)(2,1)S(1)}, bf16[64,768]{1,0:T(8,128)(2,1)S(1)}, bf16[64,768]{1,0:T(8,128)(2,1)S(1)}, f32[128,768]{1,0:T(8,128)S(1)}) custom-call(s32[1]{0:T(128)} %bitcast.refs_0_, f32[16,128]{1,0:T(8,128)S(1)} %copy-done.15, bf16[4,176,768]{2,1,0:T(8,128)(2,1)S(1)} %all-to-all-done.refs_2_), custom_call_target="tpu_custom_call" | custom-call | flops 1 | bytes 1 | tf_op jit(solution)/shard_map/temporal/pallas_call | solution.py:740
  39.1 3.7 %collective-permute-start.9 = (bf16[64,768]{1,0:T(8,128)(2,1)S(1)}, bf16[64,768]{1,0:T(8,128)(2,1)S(1)}, u32[]{:S(2)}, u32[]{:S(2)}) collective-permute-start(bf16[64,768]{1,0:T(8,128)(2,1)S(1)} %get-tuple-element.46), channel_id=1, source_target_pairs={{0,24},{8,16},{16,8},{24,0},{1,25},{9,17},{17,9},{25,1},{2,26},{10... | collective-permute-start | bytes 294920 | tf_op jit(solution)/shard_map/ppermute | solution.py:589
  42.8 2.7 %collective-permute-start.10 = (bf16[64,768]{1,0:T(8,128)(2,1)S(1)}, bf16[64,768]{1,0:T(8,128)(2,1)S(1)}, u32[]{:S(2)}, u32[]{:S(2)}) collective-permute-start(bf16[64,768]{1,0:T(8,128)(2,1)S(1)} %get-tuple-element.47), channel_id=1, source_target_pairs={{0,16},{8,24},{16,0},{24,8},{1,17},{9,25},{17,1},{25,9},{2,18},{10... | collective-permute-start | bytes 294920 | tf_op jit(solution)/shard_map/ppermute | solution.py:589
  45.6 1.0 %copy-done.11 = bf16[128,1536]{1,0:T(8,128)(2,1)S(1)} copy-done((bf16[128,1536]{1,0:T(8,128)(2,1)S(1)}, bf16[128,1536]{1,0:T(8,128)(2,1)}, u32[]{:S(2)}) %copy-start.11) | copy-done | bytes 393240
  46.6 1.8 %spatial_incoming.1.refs_4_.refs_1_ = f32[256,1536]{1,0:T(8,128)S(1)} custom-call(s32[1]{0:T(128)} %bitcast.1.refs_1_.band, bf16[256,1536]{1,0:T(8,128)(2,1)S(1)} %copy-done.8, bf16[256,256]{1,0:T(8,128)(2,1)S(1)} %copy-done.9, f32[256,128]{1,0:T(8,128)S(1)} %copy-done.13, bf16[128,1536]{1,0:T(8,128)(2,1)S(1)} %copy-done.11, ...), custom_call_target="tpu_custom_call" | custom-call | flops 1 | bytes 1 | tf_op jit(solution)/shard_map/spatial_incoming/pallas_call | solution.py:730
  48.3 2.0 %temporal.3 = (bf16[64,768]{1,0:T(8,128)(2,1)S(1)}, bf16[64,768]{1,0:T(8,128)(2,1)S(1)}, bf16[64,768]{1,0:T(8,128)(2,1)S(1)}, bf16[64,768]{1,0:T(8,128)(2,1)S(1)}) custom-call(s32[1]{0:T(128)} %bitcast.refs_0_, f32[16,128]{1,0:T(8,128)S(1)} %copy-done.15, bf16[4,176,768]{2,1,0:T(8,128)(2,1)S(1)} %all-to-all-done.refs_2_, ...), custom_call_target="tpu_custom_call" | custom-call | flops 1 | bytes 1 | tf_op jit(solution)/shard_map/temporal/pallas_call | solution.py:740
  50.3 1.7 %collective-permute-start.6 = (bf16[64,768]{1,0:T(8,128)(2,1)S(1)}, bf16[64,768]{1,0:T(8,128)(2,1)S(1)}, u32[]{:S(2)}, u32[]{:S(2)}) collective-permute-start(bf16[64,768]{1,0:T(8,128)(2,1)S(1)} %get-tuple-element.42), channel_id=1, source_target_pairs={{0,24},{8,16},{16,8},{24,0},{1,25},{9,17},{17,9},{25,1},{2,26},{10... | collective-permute-start | bytes 294920 | tf_op jit(solution)/shard_map/ppermute | solution.py:589
  52.0 1.9 %collective-permute-start.7 = (bf16[64,768]{1,0:T(8,128)(2,1)S(1)}, bf16[64,768]{1,0:T(8,128)(2,1)S(1)}, u32[]{:S(2)}, u32[]{:S(2)}) collective-permute-start(bf16[64,768]{1,0:T(8,128)(2,1)S(1)} %get-tuple-element.43), channel_id=1, source_target_pairs={{0,16},{8,24},{16,0},{24,8},{1,17},{9,25},{17,1},{25,9},{2,18},{10... | collective-permute-start | bytes 294920 | tf_op jit(solution)/shard_map/ppermute | solution.py:589
  53.9 0.9 %collective-permute-start.8 = (bf16[64,768]{1,0:T(8,128)(2,1)S(1)}, bf16[64,768]{1,0:T(8,128)(2,1)S(1)}, u32[]{:S(2)}, u32[]{:S(2)}) collective-permute-start(bf16[64,768]{1,0:T(8,128)(2,1)S(1)} %get-tuple-element.44), channel_id=1, source_target_pairs={{0,8},{8,0},{16,24},{24,16},{1,9},{9,1},{17,25},{25,17},{2,10},{10... | collective-permute-start | bytes 294920 | tf_op jit(solution)/shard_map/ppermute | solution.py:589
  54.8 2.3 %copy-done.1 = bf16[1536,1536]{1,0:T(8,128)(2,1)S(1)} copy-done((bf16[1536,1536]{1,0:T(8,128)(2,1)S(1)}, bf16[1536,1536]{1,0:T(8,128)(2,1)}, u32[]{:S(2)}) %copy-start.1) | copy-done | bytes 4718616
  57.1 2.0 %exit.2.refs_9_ = bf16[2,2,64,1536]{3,2,1,0:T(8,128)(2,1)} custom-call(s32[1]{0:T(128)} %bitcast.refs_0_, f32[256,1536]{1,0:T(8,128)S(1)} %spatial_incoming.1.refs_4_.refs_1_, bf16[256,1536]{1,0:T(8,128)(2,1)S(1)} %gate.1.refs_0_.refs_2_, f32[1536]{0:T(1024)S(1)} %copy-done.16, bf16[1536,1536]{1,0:T(8,128)(2,1)S(1)} %copy-done.1, ...), custom_call_target="tpu_custom_call" | custom-call | flops 1 | bytes 1 | tf_op jit(solution)/shard_map/exit/pallas_call | solution.py:770
  59.1 2.3 %collective-permute-done.7.refs_7_ = bf16[64,768]{1,0:T(8,128)(2,1)S(1)} collective-permute-done((bf16[64,768]{1,0:T(8,128)(2,1)S(1)}, bf16[64,768]{1,0:T(8,128)(2,1)S(1)}, u32[]{:S(2)}, u32[]{:S(2)}) %collective-permute-start.7) | collective-permute-done | bytes 98336 | tf_op jit(solution)/shard_map/ppermute | solution.py:589
  61.4 2.0 %exit.3 = bf16[2,2,64,1536]{3,2,1,0:T(8,128)(2,1)} custom-call(s32[1]{0:T(128)} %bitcast.refs_0_, f32[256,1536]{1,0:T(8,128)S(1)} %spatial_incoming.1.refs_4_.refs_1_, bf16[256,1536]{1,0:T(8,128)(2,1)S(1)} %gate.1.refs_0_.refs_2_, f32[1536]{0:T(1024)S(1)} %copy-done.16, bf16[1536,1536]{1,0:T(8,128)(2,1)S(1)} %copy-done.1, ...), custom_call_target="tpu_custom_call", output_to_operand_aliasing={{}: (9, {})} | custom-call | flops 1 | bytes 1 | tf_op jit(solution)/shard_map/exit/pallas_call | solution.py:770
  (47 shorter events, 1.6 us)
Async XLA Ops:
  7.5 6.6 %copy-start.3 = (bf16[144,1536]{1,0:T(8,128)(2,1)S(1)}, bf16[144,1536]{1,0:T(8,128)(2,1)}, u32[]{:S(2)}) copy-start(bf16[144,1536]{1,0:T(8,128)(2,1)} %get-tuple-element.35.own.band_own) | copy-start | bytes 1327108
  7.5 6.6 %collective-permute-start = (bf16[144,1536]{1,0:T(8,128)(2,1)}, bf16[144,1536]{1,0:T(8,128)(2,1)S(1)}, u32[]{:S(2)}, u32[]{:S(2)}) collective-permute-start(bf16[144,1536]{1,0:T(8,128)(2,1)} %get-tuple-element.36), channel_id=1, source_target_pairs={{0,1},{1,0},{2,3},{3,2},{4,5},{5,4},{6,7},{7,6},{8,9},{9,8},{10,11... | collective-permute-start | bytes 1327112 | tf_op jit(solution)/shard_map/ppermute | solution.py:589
  8.1 10.0 %copy-start.2 = (bf16[4,176,768]{2,1,0:T(8,128)(2,1)S(1)}, bf16[4,176,768]{2,1,0:T(8,128)(2,1)}, u32[]{:S(2)}) copy-start(bf16[4,176,768]{2,1,0:T(8,128)(2,1)} %get-tuple-element.27.after.refs_4_) | copy-start | bytes 3244036
  8.1 28.7 %all-to-all-start = ((bf16[4,176,768]{2,1,0:T(8,128)(2,1)}), bf16[4,176,768]{2,1,0:T(8,128)(2,1)S(1)}, u32[]{:S(2)}, u32[]{:S(2)}) async-start(bf16[4,176,768]{2,1,0:T(8,128)(2,1)} %get-tuple-element.27.after.refs_4_), calls=%async_computation | async-start | bytes 2162688 | tf_op jit(solution)/shard_map/all_to_all | solution.py:654
  14.1 4.0 %copy-start.6 = (bf16[256,1536]{1,0:T(8,128)(2,1)S(1)}, bf16[256,1536]{1,0:T(8,128)(2,1)}, u32[]{:S(2)}) copy-start(bf16[256,1536]{1,0:T(8,128)(2,1)} %get-tuple-element.28.normed) | copy-start | bytes 2359300
  14.1 4.0 %copy-start.4 = (bf16[144,1536]{1,0:T(8,128)(2,1)}, bf16[144,1536]{1,0:T(8,128)(2,1)S(1)}, u32[]{:S(2)}) copy-start(bf16[144,1536]{1,0:T(8,128)(2,1)S(1)} %collective-permute-done.far.band_far) | copy-start | bytes 1327108
  14.3 12.1 %collective-permute-start.1 = (bf16[144,1536]{1,0:T(8,128)(2,1)S(1)}, bf16[144,1536]{1,0:T(8,128)(2,1)S(1)}, u32[]{:S(2)}, u32[]{:S(2)}) collective-permute-start(bf16[144,1536]{1,0:T(8,128)(2,1)S(1)} %pair_total.1.total), channel_id=1, source_target_pairs={{0,2},{1,5},{2,0},{3,7},{4,6},{5,1},{6,4},{7,3},{8,10},{9,13},{10,... | collective-permute-start | bytes 1327112 | tf_op jit(solution)/shard_map/ppermute | solution.py:595
  15.9 10.5 %collective-permute-start.2 = (bf16[16,1536]{1,0:T(8,128)(2,1)}, bf16[16,1536]{1,0:T(8,128)(2,1)S(1)}, u32[]{:S(2)}, u32[]{:S(2)}) collective-permute-start(bf16[16,1536]{1,0:T(8,128)(2,1)} %get-tuple-element.37), channel_id=1, source_target_pairs={{0,6},{1,7},{2,4},{3,5},{4,2},{5,3},{6,0},{7,1},{8,14},{9,15},{10,... | collective-permute-start | bytes 147464 | tf_op jit(solution)/shard_map/ppermute | solution.py:589
  17.3 9.0 %collective-permute-start.3 = (bf16[16,1536]{1,0:T(8,128)(2,1)}, bf16[16,1536]{1,0:T(8,128)(2,1)S(1)}, u32[]{:S(2)}, u32[]{:S(2)}) collective-permute-start(bf16[16,1536]{1,0:T(8,128)(2,1)} %get-tuple-element.37), channel_id=1, source_target_pairs={{0,7},{1,6},{2,5},{3,4},{4,3},{5,2},{6,1},{7,0},{8,15},{9,14},{10,... | collective-permute-start | bytes 147464 | tf_op jit(solution)/shard_map/ppermute | solution.py:589
  18.1 3.7 %copy-start = (bf16[1536,3072]{1,0:T(8,128)(2,1)S(1)}, bf16[1536,3072]{1,0:T(8,128)(2,1)}, u32[]{:S(2)}) copy-start(bf16[1536,3072]{1,0:T(8,128)(2,1)} %weight.1) | copy-start | bytes 28311556
  21.7 2.6 %copy-start.15 = (f32[16,128]{1,0:T(8,128)S(1)}, f32[16,128]{1,0:T(8,128)}, u32[]{:S(2)}) copy-start(f32[16,128]{1,0:T(8,128)} %get-tuple-element.31.refs_3_.refs_1_) | copy-start | bytes 24580
  24.4 10.6 %copy-start.5 = (bf16[144,1536]{1,0:T(8,128)(2,1)S(1)}, bf16[144,1536]{1,0:T(8,128)(2,1)}, u32[]{:S(2)}) copy-start(bf16[144,1536]{1,0:T(8,128)(2,1)} %copy-done.4) | copy-start | bytes 1327108
  26.3 9.7 %copy-start.7 = (bf16[256,1536]{1,0:T(8,128)(2,1)}, bf16[256,1536]{1,0:T(8,128)(2,1)S(1)}, u32[]{:S(2)}) copy-start(bf16[256,1536]{1,0:T(8,128)(2,1)S(1)} %get-tuple-element.32.out_local) | copy-start | bytes 2359300
  26.6 8.4 %collective-permute-start.4 = (bf16[144,1536]{1,0:T(8,128)(2,1)S(1)}, bf16[144,1536]{1,0:T(8,128)(2,1)S(1)}, u32[]{:S(2)}, u32[]{:S(2)}) collective-permute-start(bf16[144,1536]{1,0:T(8,128)(2,1)S(1)} %cross.1), channel_id=1, source_target_pairs={{0,4},{1,3},{2,6},{3,1},{4,0},{5,7},{6,2},{7,5},{8,12},{9,11},{10,... | collective-permute-start | bytes 1327112 | tf_op jit(solution)/shard_map/ppermute | solution.py:595
  34.9 10.6 %copy-start.13 = (f32[256,128]{1,0:T(8,128)S(1)}, f32[256,128]{1,0:T(8,128)}, u32[]{:S(2)}) copy-start(f32[256,128]{1,0:T(8,128)} %copy-done.12) | copy-start | bytes 393220
  36.8 8.8 %copy-start.8 = (bf16[256,1536]{1,0:T(8,128)(2,1)S(1)}, bf16[256,1536]{1,0:T(8,128)(2,1)}, u32[]{:S(2)}) copy-start(bf16[256,1536]{1,0:T(8,128)(2,1)} %copy-done.7) | copy-start | bytes 2359300
  36.8 8.8 %collective-permute-start.5 = (bf16[128,1536]{1,0:T(8,128)(2,1)}, bf16[128,1536]{1,0:T(8,128)(2,1)}, u32[]{:S(2)}, u32[]{:S(2)}) collective-permute-start(bf16[128,1536]{1,0:T(8,128)(2,1)} %get-tuple-element.39), channel_id=1, source_target_pairs={{0,1},{1,0},{2,3},{3,2},{4,5},{5,4},{6,7},{7,6},{8,9},{9,8},{10,11... | collective-permute-start | bytes 1179656 | tf_op jit(solution)/shard_map/ppermute | solution.py:589
  39.1 14.8 %collective-permute-start.9 = (bf16[64,768]{1,0:T(8,128)(2,1)S(1)}, bf16[64,768]{1,0:T(8,128)(2,1)S(1)}, u32[]{:S(2)}, u32[]{:S(2)}) collective-permute-start(bf16[64,768]{1,0:T(8,128)(2,1)S(1)} %get-tuple-element.46), channel_id=1, source_target_pairs={{0,24},{8,16},{16,8},{24,0},{1,25},{9,17},{17,9},{25,1},{2,26},{10... | collective-permute-start | bytes 294920 | tf_op jit(solution)/shard_map/ppermute | solution.py:589
  42.8 12.0 %collective-permute-start.10 = (bf16[64,768]{1,0:T(8,128)(2,1)S(1)}, bf16[64,768]{1,0:T(8,128)(2,1)S(1)}, u32[]{:S(2)}, u32[]{:S(2)}) collective-permute-start(bf16[64,768]{1,0:T(8,128)(2,1)S(1)} %get-tuple-element.47), channel_id=1, source_target_pairs={{0,16},{8,24},{16,0},{24,8},{1,17},{9,25},{17,1},{25,9},{2,18},{10... | collective-permute-start | bytes 294920 | tf_op jit(solution)/shard_map/ppermute | solution.py:589
  45.6 9.2 %collective-permute-start.11 = (bf16[64,768]{1,0:T(8,128)(2,1)S(1)}, bf16[64,768]{1,0:T(8,128)(2,1)S(1)}, u32[]{:S(2)}, u32[]{:S(2)}) collective-permute-start(bf16[64,768]{1,0:T(8,128)(2,1)S(1)} %get-tuple-element.48), channel_id=1, source_target_pairs={{0,8},{8,0},{16,24},{24,16},{1,9},{9,1},{17,25},{25,17},{2,10},{10... | collective-permute-start | bytes 294920 | tf_op jit(solution)/shard_map/ppermute | solution.py:589
  48.3 6.4 %copy-start.16 = (f32[1536]{0:T(1024)S(1)}, f32[1536]{0:T(1024)}, u32[]{:S(2)}) copy-start(f32[1536]{0:T(1024)} %refs_3_.5) | copy-start | bytes 18436
  50.3 8.8 %collective-permute-start.6 = (bf16[64,768]{1,0:T(8,128)(2,1)S(1)}, bf16[64,768]{1,0:T(8,128)(2,1)S(1)}, u32[]{:S(2)}, u32[]{:S(2)}) collective-permute-start(bf16[64,768]{1,0:T(8,128)(2,1)S(1)} %get-tuple-element.42), channel_id=1, source_target_pairs={{0,24},{8,16},{16,8},{24,0},{1,25},{9,17},{17,9},{25,1},{2,26},{10... | collective-permute-start | bytes 294920 | tf_op jit(solution)/shard_map/ppermute | solution.py:589
  52.0 9.4 %collective-permute-start.7 = (bf16[64,768]{1,0:T(8,128)(2,1)S(1)}, bf16[64,768]{1,0:T(8,128)(2,1)S(1)}, u32[]{:S(2)}, u32[]{:S(2)}) collective-permute-start(bf16[64,768]{1,0:T(8,128)(2,1)S(1)} %get-tuple-element.43), channel_id=1, source_target_pairs={{0,16},{8,24},{16,0},{24,8},{1,17},{9,25},{17,1},{25,9},{2,18},{10... | collective-permute-start | bytes 294920 | tf_op jit(solution)/shard_map/ppermute | solution.py:589
  53.9 7.5 %collective-permute-start.8 = (bf16[64,768]{1,0:T(8,128)(2,1)S(1)}, bf16[64,768]{1,0:T(8,128)(2,1)S(1)}, u32[]{:S(2)}, u32[]{:S(2)}) collective-permute-start(bf16[64,768]{1,0:T(8,128)(2,1)S(1)} %get-tuple-element.44), channel_id=1, source_target_pairs={{0,8},{8,0},{16,24},{24,16},{1,9},{9,1},{17,25},{25,17},{2,10},{10... | collective-permute-start | bytes 294920 | tf_op jit(solution)/shard_map/ppermute | solution.py:589
  (6 other events, 10.2 us)

commit v11 on v8

--- a/solution.py
+++ b/solution.py
@@ -253,7 +253,8 @@
     for index, copy in enumerate(copies):
         copy.wait()
         at = slice(index * block, (index + 1) * block)
-        out[:, at] = dot(normed[...], held_weight[:, at]).astype(BF16)
+        gates = dot(normed[...], held_weight[:, at]).astype(BF16).astype(F32)
+        out[:, at] = (gates / (1.0 + jnp.exp(-gates))).astype(BF16)
 
 
 def frame_of(ref, frame, rows, frames, columns):
@@ -552,27 +553,31 @@
         kept = []
         for index in range(groups):
             at = slice(index * group, (index + 1) * group)
-            gates = own(gate, row, at).astype(F32)
             gated = own(spatial, row, at) + temporal[index * rows + row].astype(F32)
-            gated = gated * (gates / (1.0 + jnp.exp(-gates)))
+            gated = gated * own(gate, row, at).astype(F32)
             total = total + jnp.sum(gated * gated, axis=1, keepdims=True)
             kept.append(gated)
         scale = lax.rsqrt(total / inner + EPSILON)
         for index, gated in enumerate(kept):
             at = slice(index * group, (index + 1) * group)
             normed[row * part_len : (row + 1) * part_len, at] = (gated * scale * gains[:, at]).astype(BF16)
-    mixed[...] = dot(normed[...], weight[...]).astype(BF16)
-    copies = [
-        pltpu.make_async_copy(
-            mixed.at[pl.ds((row * frames + frame) * part_cols, part_cols), :],
-            out.at[frame, row, pl.ds(part * part_cols, part_cols), :],
-            sems.at[row * frames + frame],
-        )
-        for row in range(rows)
-        for frame in range(frames)
-    ]
-    for copy in copies:
-        copy.start()
+    copies = []
+    width = mixed.shape[1] // 2
+    for side in range(2):
+        cols = pl.ds(side * width, width)
+        mixed[:, side * width : (side + 1) * width] = dot(
+            normed[...], weight[:, side * width : (side + 1) * width]
+        ).astype(BF16)
+        for row in range(rows):
+            for frame in range(frames):
+                copies.append(
+                    pltpu.make_async_copy(
+                        mixed.at[pl.ds((row * frames + frame) * part_cols, part_cols), cols],
+                        out.at[frame, row, pl.ds(part * part_cols, part_cols), cols],
+                        sems.at[len(copies)],
+                    )
+                )
+                copies[-1].start()
     for copy in copies:
         copy.wait()
 
@@ -770,7 +775,7 @@
                     pltpu.VMEM((shares, part_len, group), BF16),
                     pltpu.VMEM((rows * part_len, inner), BF16),
                     pltpu.VMEM((rows * part_len, width), BF16),
-                    pltpu.SemaphoreType.DMA((rows * frames,)),
+                    pltpu.SemaphoreType.DMA((2 * rows * frames,)),
                 ],
                 input_output_aliases={5 + shares: 0} if mixed else {},
             )(here, spatial_out, gate, out_gain, out_weight, *returned[part], *mixed)

time: 63.9 us -> 63.7 us (level)
  no operation moved by 1% of the time
where the time goes in v11:
time: 63.7 us; the launch traced here: 63.3 us
  Pallas kernels  23 us (36%)
  starting transfers between devices  21.7 us (34%)
  waiting for transfers between devices  10.3 us (16%)
  local copies, waits for them, and re-layouts  7.84 us (12%)
    ppermute x10, starting transfers between devices, swapped(): lax.ppermute(value, axis, [(source, source ^ distance) for source in rang...  13.6 us
    unnamed x32, local copies, waits for them, and re-layouts  7.84 us
    ppermute x2, waiting for transfers between devices, crossed(): return lax.ppermute(value, axis, pairs)  7.81 us
    pallas_call x1, Pallas kernels, per_device(): call(functools.partial(entry_kernel, shares, heads, state, blocks), 'entr...  7.5 us
    all_to_all x1, starting transfers between devices, per_device(): lax.all_to_all(payload, 'tm', split_axis=0, concat_axis=0, tiled=True, ax...  6.03 us
    pallas_call x2, Pallas kernels, per_device(): call(functools.partial(temporal_kernel, part, parts, per_group, head_dim,...  4.26 us
    pallas_call x2, Pallas kernels, per_device(): call(functools.partial(exit_kernel, part, parts, shares), 'exit', shape_o...  3.5 us
    pallas_call x1, Pallas kernels, per_device(): call(functools.partial(gate_kernel, blocks), 'gate', shape_of((count, inn...  2.65 us
  transfers between devices with their start and end apart: 13, of which 2 were waited for; matrix products, arithmetic and copies ran while one was open for 0% of the time, Pallas kernels for 22%

profile of v11, /device:TPU:0, one launch (start us, length us, event | category | flops | bytes accessed | tf_op | source)
XLA Modules:
  0.0 63.3 jit_solution(13314803088954826703)
XLA Ops:
  0.0 7.5 %entry.1 = (bf16[256,1536]{1,0:T(8,128)(2,1)}, bf16[4,176,768]{2,1,0:T(8,128)(2,1)}, bf16[256,256]{1,0:T(8,128)(2,1)}, f32[256,128]{1,0:T(8,128)}, f32[16,128]{1...) custom-call(s32[1]{0:T(128)} %bitcast.refs_0_, ...), custom_call_target="tpu_custom_call" | custom-call | flops 1 | bytes 1 | tf_op jit(solution)/shard_map/entry/pallas_call | solution.py:619
  8.0 6.0 %all-to-all-start = ((bf16[4,176,768]{2,1,0:T(8,128)(2,1)}), bf16[4,176,768]{2,1,0:T(8,128)(2,1)S(1)}, u32[]{:S(2)}, u32[]{:S(2)}) async-start(bf16[4,176,768]{2,1,0:T(8,128)(2,1)} %get-tuple-element.26.after.refs_4_), calls=%async_computation | async-start | bytes 2162688 | tf_op jit(solution)/shard_map/all_to_all | solution.py:652
  14.3 1.6 %collective-permute-start.1 = (bf16[144,1536]{1,0:T(8,128)(2,1)S(1)}, bf16[144,1536]{1,0:T(8,128)(2,1)S(1)}, u32[]{:S(2)}, u32[]{:S(2)}) collective-permute-start(bf16[144,1536]{1,0:T(8,128)(2,1)S(1)} %pair_total.1.total), channel_id=1, source_target_pairs={{0,2},{1,5},{2,0},{3,7},{4,6},{5,1},{6,4},{7,3},{8,10},{9,13},{10,... | collective-permute-start | bytes 1327112 | tf_op jit(solution)/shard_map/ppermute | solution.py:593
  15.8 1.5 %collective-permute-start.2 = (bf16[16,1536]{1,0:T(8,128)(2,1)}, bf16[16,1536]{1,0:T(8,128)(2,1)S(1)}, u32[]{:S(2)}, u32[]{:S(2)}) collective-permute-start(bf16[16,1536]{1,0:T(8,128)(2,1)} %get-tuple-element.35), channel_id=1, source_target_pairs={{0,6},{1,7},{2,4},{3,5},{4,2},{5,3},{6,0},{7,1},{8,14},{9,15},{10,... | collective-permute-start | bytes 147464 | tf_op jit(solution)/shard_map/ppermute | solution.py:587
  17.3 0.7 %collective-permute-start.3 = (bf16[16,1536]{1,0:T(8,128)(2,1)}, bf16[16,1536]{1,0:T(8,128)(2,1)S(1)}, u32[]{:S(2)}, u32[]{:S(2)}) collective-permute-start(bf16[16,1536]{1,0:T(8,128)(2,1)} %get-tuple-element.35), channel_id=1, source_target_pairs={{0,7},{1,6},{2,5},{3,4},{4,3},{5,2},{6,1},{7,0},{8,15},{9,14},{10,... | collective-permute-start | bytes 147464 | tf_op jit(solution)/shard_map/ppermute | solution.py:587
  18.1 3.7 %copy-done = bf16[1536,3072]{1,0:T(8,128)(2,1)S(1)} copy-done((bf16[1536,3072]{1,0:T(8,128)(2,1)S(1)}, bf16[1536,3072]{1,0:T(8,128)(2,1)}, u32[]{:S(2)}) %copy-start) | copy-done | bytes 9437208
  21.7 2.6 %gate.1.refs_0_.refs_2_ = bf16[256,1536]{1,0:T(8,128)(2,1)S(1)} custom-call(bf16[4,176,768]{2,1,0:T(8,128)(2,1)S(1)} %copy-done.2, bf16[256,1536]{1,0:T(8,128)(2,1)S(1)} %copy-done.6, bf16[1536,3072]{1,0:T(8,128)(2,1)S(1)} %copy-done), custom_call_target="tpu_custom_call" | custom-call | flops 1 | bytes 1 | tf_op jit(solution)/shard_map/gate/pallas_call | solution.py:661
  24.4 1.9 %spatial_local.1 = (bf16[256,1536]{1,0:T(8,128)(2,1)S(1)}, f32[256,128]{1,0:T(8,128)S(1)}) custom-call(bf16[256,1536]{1,0:T(8,128)(2,1)S(1)} %gate.1.refs_0_.refs_2_, bf16[256,256]{1,0:T(8,128)(2,1)S(1)} %copy-done.9, f32[256,128]{1,0:T(8,128)S(1)} %copy-done.13, f32[16,128]{1,0:T(8,128)S(1)} %copy-done.14, bf16[4,176,768]{2,1,0:T(8,128)(2,1)S(1)} %copy-done.2), custom_call_target="tpu_custom_call" | custom-call | flops 1 | bytes 1 | tf_op jit(solution)/shard_map/spatial_local/pallas_call | solution.py:672
  27.2 7.8 %collective-permute-done.4.second = bf16[144,1536]{1,0:T(8,128)(2,1)S(1)} collective-permute-done((bf16[144,1536]{1,0:T(8,128)(2,1)S(1)}, bf16[144,1536]{1,0:T(8,128)(2,1)S(1)}, u32[]{:S(2)}, u32[]{:S(2)}) %collective-permute-start.4) | collective-permute-done | bytes 442400 | tf_op jit(solution)/shard_map/ppermute | solution.py:593
  35.0 1.1 %settle.1 = (bf16[128,1536]{1,0:T(8,128)(2,1)S(1)}, bf16[128,1536]{1,0:T(8,128)(2,1)}) custom-call(f32[256,128]{1,0:T(8,128)S(1)} %get-tuple-element.32._.reach, s32[1]{0:T(128)} %bitcast.1.refs_1_.band, bf16[144,1536]{1,0:T(8,128)(2,1)S(1)} %collective-permute-done.1.first, bf16[144,1536]{1,0:T(8,128)(2,1)S(1)} %collective-permute-done.4.second, ...), custom_call_target="tpu_custom_call" | custom-call | flops 1 | bytes 1 | tf_op jit(solution)/shard_map/settle/pallas_call | solution.py:697
  36.1 0.8 %copy-done.11 = bf16[128,1536]{1,0:T(8,128)(2,1)} copy-done((bf16[128,1536]{1,0:T(8,128)(2,1)}, bf16[128,1536]{1,0:T(8,128)(2,1)S(1)}, u32[]{:S(2)}) %copy-start.11) | copy-done | bytes 393240
  36.9 2.3 %temporal.2 = (bf16[64,768]{1,0:T(8,128)(2,1)S(1)}, bf16[64,768]{1,0:T(8,128)(2,1)S(1)}, bf16[64,768]{1,0:T(8,128)(2,1)S(1)}, bf16[64,768]{1,0:T(8,128)(2,1)S(1)}, f32[128,768]{1,0:T(8,128)S(1)}) custom-call(s32[1]{0:T(128)} %bitcast.refs_0_, f32[16,128]{1,0:T(8,128)S(1)} %copy-done.14, bf16[4,176,768]{2,1,0:T(8,128)(2,1)S(1)} %all-to-all-done.refs_2_), custom_call_target="tpu_custom_call" | custom-call | flops 1 | bytes 1 | tf_op jit(solution)/shard_map/temporal/pallas_call | solution.py:738
  39.2 3.7 %collective-permute-start.9 = (bf16[64,768]{1,0:T(8,128)(2,1)S(1)}, bf16[64,768]{1,0:T(8,128)(2,1)S(1)}, u32[]{:S(2)}, u32[]{:S(2)}) collective-permute-start(bf16[64,768]{1,0:T(8,128)(2,1)S(1)} %get-tuple-element.44), channel_id=1, source_target_pairs={{0,24},{8,16},{16,8},{24,0},{1,25},{9,17},{17,9},{25,1},{2,26},{10... | collective-permute-start | bytes 294920 | tf_op jit(solution)/shard_map/ppermute | solution.py:587
  42.9 2.7 %collective-permute-start.10 = (bf16[64,768]{1,0:T(8,128)(2,1)S(1)}, bf16[64,768]{1,0:T(8,128)(2,1)S(1)}, u32[]{:S(2)}, u32[]{:S(2)}) collective-permute-start(bf16[64,768]{1,0:T(8,128)(2,1)S(1)} %get-tuple-element.45), channel_id=1, source_target_pairs={{0,16},{8,24},{16,0},{24,8},{1,17},{9,25},{17,1},{25,9},{2,18},{10... | collective-permute-start | bytes 294920 | tf_op jit(solution)/shard_map/ppermute | solution.py:587
  45.6 1.0 %copy-done.12 = bf16[128,1536]{1,0:T(8,128)(2,1)S(1)} copy-done((bf16[128,1536]{1,0:T(8,128)(2,1)S(1)}, bf16[128,1536]{1,0:T(8,128)(2,1)}, u32[]{:S(2)}) %copy-start.12) | copy-done | bytes 393240
  46.6 1.8 %spatial_incoming.1.refs_4_.refs_1_ = f32[256,1536]{1,0:T(8,128)S(1)} custom-call(s32[1]{0:T(128)} %bitcast.1.refs_1_.band, bf16[256,1536]{1,0:T(8,128)(2,1)S(1)} %copy-done.8, bf16[256,256]{1,0:T(8,128)(2,1)S(1)} %copy-done.10, f32[256,128]{1,0:T(8,128)S(1)} %get-tuple-element.32._.reach, bf16[128,1536]{1,0:T(8,128)(2,1)S(1)} %copy-done.12, ...), custom_call_target="tpu_custom_call" | custom-call | flops 1 | bytes 1 | tf_op jit(solution)/shard_map/spatial_incoming/pallas_call | solution.py:728
  48.4 2.0 %temporal.3 = (bf16[64,768]{1,0:T(8,128)(2,1)S(1)}, bf16[64,768]{1,0:T(8,128)(2,1)S(1)}, bf16[64,768]{1,0:T(8,128)(2,1)S(1)}, bf16[64,768]{1,0:T(8,128)(2,1)S(1)}) custom-call(s32[1]{0:T(128)} %bitcast.refs_0_, f32[16,128]{1,0:T(8,128)S(1)} %copy-done.14, bf16[4,176,768]{2,1,0:T(8,128)(2,1)S(1)} %all-to-all-done.refs_2_, ...), custom_call_target="tpu_custom_call" | custom-call | flops 1 | bytes 1 | tf_op jit(solution)/shard_map/temporal/pallas_call | solution.py:738
  50.3 1.7 %collective-permute-start.6 = (bf16[64,768]{1,0:T(8,128)(2,1)S(1)}, bf16[64,768]{1,0:T(8,128)(2,1)S(1)}, u32[]{:S(2)}, u32[]{:S(2)}) collective-permute-start(bf16[64,768]{1,0:T(8,128)(2,1)S(1)} %get-tuple-element.40), channel_id=1, source_target_pairs={{0,24},{8,16},{16,8},{24,0},{1,25},{9,17},{17,9},{25,1},{2,26},{10... | collective-permute-start | bytes 294920 | tf_op jit(solution)/shard_map/ppermute | solution.py:587
  52.1 1.8 %collective-permute-start.7 = (bf16[64,768]{1,0:T(8,128)(2,1)S(1)}, bf16[64,768]{1,0:T(8,128)(2,1)S(1)}, u32[]{:S(2)}, u32[]{:S(2)}) collective-permute-start(bf16[64,768]{1,0:T(8,128)(2,1)S(1)} %get-tuple-element.41), channel_id=1, source_target_pairs={{0,16},{8,24},{16,0},{24,8},{1,17},{9,25},{17,1},{25,9},{2,18},{10... | collective-permute-start | bytes 294920 | tf_op jit(solution)/shard_map/ppermute | solution.py:587
  53.9 0.9 %collective-permute-start.8 = (bf16[64,768]{1,0:T(8,128)(2,1)S(1)}, bf16[64,768]{1,0:T(8,128)(2,1)S(1)}, u32[]{:S(2)}, u32[]{:S(2)}) collective-permute-start(bf16[64,768]{1,0:T(8,128)(2,1)S(1)} %get-tuple-element.42), channel_id=1, source_target_pairs={{0,8},{8,0},{16,24},{24,16},{1,9},{9,1},{17,25},{25,17},{2,10},{10... | collective-permute-start | bytes 294920 | tf_op jit(solution)/shard_map/ppermute | solution.py:587
  54.8 2.3 %copy-done.1 = bf16[1536,1536]{1,0:T(8,128)(2,1)S(1)} copy-done((bf16[1536,1536]{1,0:T(8,128)(2,1)S(1)}, bf16[1536,1536]{1,0:T(8,128)(2,1)}, u32[]{:S(2)}) %copy-start.1) | copy-done | bytes 4718616
  57.1 1.7 %exit.2.refs_9_ = bf16[2,2,64,1536]{3,2,1,0:T(8,128)(2,1)} custom-call(s32[1]{0:T(128)} %bitcast.refs_0_, f32[256,1536]{1,0:T(8,128)S(1)} %spatial_incoming.1.refs_4_.refs_1_, bf16[256,1536]{1,0:T(8,128)(2,1)S(1)} %gate.1.refs_0_.refs_2_, f32[1536]{0:T(1024)S(1)} %copy-done.15, bf16[1536,1536]{1,0:T(8,128)(2,1)S(1)} %copy-done.1, ...), custom_call_target="tpu_custom_call" | custom-call | flops 1 | bytes 1 | tf_op jit(solution)/shard_map/exit/pallas_call | solution.py:768
  58.9 2.5 %collective-permute-done.7.refs_7_ = bf16[64,768]{1,0:T(8,128)(2,1)S(1)} collective-permute-done((bf16[64,768]{1,0:T(8,128)(2,1)S(1)}, bf16[64,768]{1,0:T(8,128)(2,1)S(1)}, u32[]{:S(2)}, u32[]{:S(2)}) %collective-permute-start.7) | collective-permute-done | bytes 98336 | tf_op jit(solution)/shard_map/ppermute | solution.py:587
  61.4 1.7 %exit.3 = bf16[2,2,64,1536]{3,2,1,0:T(8,128)(2,1)} custom-call(s32[1]{0:T(128)} %bitcast.refs_0_, f32[256,1536]{1,0:T(8,128)S(1)} %spatial_incoming.1.refs_4_.refs_1_, bf16[256,1536]{1,0:T(8,128)(2,1)S(1)} %gate.1.refs_0_.refs_2_, f32[1536]{0:T(1024)S(1)} %copy-done.15, bf16[1536,1536]{1,0:T(8,128)(2,1)S(1)} %copy-done.1, ...), custom_call_target="tpu_custom_call", output_to_operand_aliasing={{}: (9, {})} | custom-call | flops 1 | bytes 1 | tf_op jit(solution)/shard_map/exit/pallas_call | solution.py:768
  (45 shorter events, 1.6 us)
Async XLA Ops:
  7.5 6.6 %copy-start.3 = (bf16[144,1536]{1,0:T(8,128)(2,1)S(1)}, bf16[144,1536]{1,0:T(8,128)(2,1)}, u32[]{:S(2)}) copy-start(bf16[144,1536]{1,0:T(8,128)(2,1)} %get-tuple-element.33.own.band_own) | copy-start | bytes 1327108
  7.5 6.6 %collective-permute-start = (bf16[144,1536]{1,0:T(8,128)(2,1)}, bf16[144,1536]{1,0:T(8,128)(2,1)S(1)}, u32[]{:S(2)}, u32[]{:S(2)}) collective-permute-start(bf16[144,1536]{1,0:T(8,128)(2,1)} %get-tuple-element.34), channel_id=1, source_target_pairs={{0,1},{1,0},{2,3},{3,2},{4,5},{5,4},{6,7},{7,6},{8,9},{9,8},{10,11... | collective-permute-start | bytes 1327112 | tf_op jit(solution)/shard_map/ppermute | solution.py:587
  8.0 10.0 %copy-start.2 = (bf16[4,176,768]{2,1,0:T(8,128)(2,1)S(1)}, bf16[4,176,768]{2,1,0:T(8,128)(2,1)}, u32[]{:S(2)}) copy-start(bf16[4,176,768]{2,1,0:T(8,128)(2,1)} %get-tuple-element.26.after.refs_4_) | copy-start | bytes 3244036
  8.0 28.8 %all-to-all-start = ((bf16[4,176,768]{2,1,0:T(8,128)(2,1)}), bf16[4,176,768]{2,1,0:T(8,128)(2,1)S(1)}, u32[]{:S(2)}, u32[]{:S(2)}) async-start(bf16[4,176,768]{2,1,0:T(8,128)(2,1)} %get-tuple-element.26.after.refs_4_), calls=%async_computation | async-start | bytes 2162688 | tf_op jit(solution)/shard_map/all_to_all | solution.py:652
  14.1 4.0 %copy-start.6 = (bf16[256,1536]{1,0:T(8,128)(2,1)S(1)}, bf16[256,1536]{1,0:T(8,128)(2,1)}, u32[]{:S(2)}) copy-start(bf16[256,1536]{1,0:T(8,128)(2,1)} %get-tuple-element.27.normed) | copy-start | bytes 2359300
  14.1 4.0 %copy-start.4 = (bf16[144,1536]{1,0:T(8,128)(2,1)}, bf16[144,1536]{1,0:T(8,128)(2,1)S(1)}, u32[]{:S(2)}) copy-start(bf16[144,1536]{1,0:T(8,128)(2,1)S(1)} %collective-permute-done.far.band_far) | copy-start | bytes 1327108
  14.3 12.1 %collective-permute-start.1 = (bf16[144,1536]{1,0:T(8,128)(2,1)S(1)}, bf16[144,1536]{1,0:T(8,128)(2,1)S(1)}, u32[]{:S(2)}, u32[]{:S(2)}) collective-permute-start(bf16[144,1536]{1,0:T(8,128)(2,1)S(1)} %pair_total.1.total), channel_id=1, source_target_pairs={{0,2},{1,5},{2,0},{3,7},{4,6},{5,1},{6,4},{7,3},{8,10},{9,13},{10,... | collective-permute-start | bytes 1327112 | tf_op jit(solution)/shard_map/ppermute | solution.py:593
  15.8 10.5 %collective-permute-start.2 = (bf16[16,1536]{1,0:T(8,128)(2,1)}, bf16[16,1536]{1,0:T(8,128)(2,1)S(1)}, u32[]{:S(2)}, u32[]{:S(2)}) collective-permute-start(bf16[16,1536]{1,0:T(8,128)(2,1)} %get-tuple-element.35), channel_id=1, source_target_pairs={{0,6},{1,7},{2,4},{3,5},{4,2},{5,3},{6,0},{7,1},{8,14},{9,15},{10,... | collective-permute-start | bytes 147464 | tf_op jit(solution)/shard_map/ppermute | solution.py:587
  17.3 9.0 %collective-permute-start.3 = (bf16[16,1536]{1,0:T(8,128)(2,1)}, bf16[16,1536]{1,0:T(8,128)(2,1)S(1)}, u32[]{:S(2)}, u32[]{:S(2)}) collective-permute-start(bf16[16,1536]{1,0:T(8,128)(2,1)} %get-tuple-element.35), channel_id=1, source_target_pairs={{0,7},{1,6},{2,5},{3,4},{4,3},{5,2},{6,1},{7,0},{8,15},{9,14},{10,... | collective-permute-start | bytes 147464 | tf_op jit(solution)/shard_map/ppermute | solution.py:587
  18.0 3.7 %copy-start = (bf16[1536,3072]{1,0:T(8,128)(2,1)S(1)}, bf16[1536,3072]{1,0:T(8,128)(2,1)}, u32[]{:S(2)}) copy-start(bf16[1536,3072]{1,0:T(8,128)(2,1)} %weight.1) | copy-start | bytes 28311556
  21.7 2.7 %copy-start.14 = (f32[16,128]{1,0:T(8,128)S(1)}, f32[16,128]{1,0:T(8,128)}, u32[]{:S(2)}) copy-start(f32[16,128]{1,0:T(8,128)} %get-tuple-element.30.refs_3_.refs_1_) | copy-start | bytes 24580
  24.4 10.6 %copy-start.5 = (bf16[144,1536]{1,0:T(8,128)(2,1)S(1)}, bf16[144,1536]{1,0:T(8,128)(2,1)}, u32[]{:S(2)}) copy-start(bf16[144,1536]{1,0:T(8,128)(2,1)} %copy-done.4) | copy-start | bytes 1327108
  26.3 9.7 %copy-start.7 = (bf16[256,1536]{1,0:T(8,128)(2,1)}, bf16[256,1536]{1,0:T(8,128)(2,1)S(1)}, u32[]{:S(2)}) copy-start(bf16[256,1536]{1,0:T(8,128)(2,1)S(1)} %get-tuple-element.31.out_local) | copy-start | bytes 2359300
  26.6 19.0 %copy-start.10 = (bf16[256,256]{1,0:T(8,128)(2,1)S(1)}, bf16[256,256]{1,0:T(8,128)(2,1)}, u32[]{:S(2)}) copy-start(bf16[256,256]{1,0:T(8,128)(2,1)} %get-tuple-element.28.refs_1_.bc) | copy-start | bytes 393220
  26.6 8.4 %collective-permute-start.4 = (bf16[144,1536]{1,0:T(8,128)(2,1)S(1)}, bf16[144,1536]{1,0:T(8,128)(2,1)S(1)}, u32[]{:S(2)}, u32[]{:S(2)}) collective-permute-start(bf16[144,1536]{1,0:T(8,128)(2,1)S(1)} %cross.1), channel_id=1, source_target_pairs={{0,4},{1,3},{2,6},{3,1},{4,0},{5,7},{6,2},{7,5},{8,12},{9,11},{10,... | collective-permute-start | bytes 1327112 | tf_op jit(solution)/shard_map/ppermute | solution.py:593
  36.9 8.7 %copy-start.8 = (bf16[256,1536]{1,0:T(8,128)(2,1)S(1)}, bf16[256,1536]{1,0:T(8,128)(2,1)}, u32[]{:S(2)}) copy-start(bf16[256,1536]{1,0:T(8,128)(2,1)} %copy-done.7) | copy-start | bytes 2359300
  36.9 8.7 %collective-permute-start.5 = (bf16[128,1536]{1,0:T(8,128)(2,1)}, bf16[128,1536]{1,0:T(8,128)(2,1)}, u32[]{:S(2)}, u32[]{:S(2)}) collective-permute-start(bf16[128,1536]{1,0:T(8,128)(2,1)} %get-tuple-element.37), channel_id=1, source_target_pairs={{0,1},{1,0},{2,3},{3,2},{4,5},{5,4},{6,7},{7,6},{8,9},{9,8},{10,11... | collective-permute-start | bytes 1179656 | tf_op jit(solution)/shard_map/ppermute | solution.py:587
  39.2 14.7 %collective-permute-start.9 = (bf16[64,768]{1,0:T(8,128)(2,1)S(1)}, bf16[64,768]{1,0:T(8,128)(2,1)S(1)}, u32[]{:S(2)}, u32[]{:S(2)}) collective-permute-start(bf16[64,768]{1,0:T(8,128)(2,1)S(1)} %get-tuple-element.44), channel_id=1, source_target_pairs={{0,24},{8,16},{16,8},{24,0},{1,25},{9,17},{17,9},{25,1},{2,26},{10... | collective-permute-start | bytes 294920 | tf_op jit(solution)/shard_map/ppermute | solution.py:587
  42.9 11.9 %collective-permute-start.10 = (bf16[64,768]{1,0:T(8,128)(2,1)S(1)}, bf16[64,768]{1,0:T(8,128)(2,1)S(1)}, u32[]{:S(2)}, u32[]{:S(2)}) collective-permute-start(bf16[64,768]{1,0:T(8,128)(2,1)S(1)} %get-tuple-element.45), channel_id=1, source_target_pairs={{0,16},{8,24},{16,0},{24,8},{1,17},{9,25},{17,1},{25,9},{2,18},{10... | collective-permute-start | bytes 294920 | tf_op jit(solution)/shard_map/ppermute | solution.py:587
  45.6 9.2 %collective-permute-start.11 = (bf16[64,768]{1,0:T(8,128)(2,1)S(1)}, bf16[64,768]{1,0:T(8,128)(2,1)S(1)}, u32[]{:S(2)}, u32[]{:S(2)}) collective-permute-start(bf16[64,768]{1,0:T(8,128)(2,1)S(1)} %get-tuple-element.46), channel_id=1, source_target_pairs={{0,8},{8,0},{16,24},{24,16},{1,9},{9,1},{17,25},{25,17},{2,10},{10... | collective-permute-start | bytes 294920 | tf_op jit(solution)/shard_map/ppermute | solution.py:587
  48.4 6.4 %copy-start.15 = (f32[1536]{0:T(1024)S(1)}, f32[1536]{0:T(1024)}, u32[]{:S(2)}) copy-start(f32[1536]{0:T(1024)} %refs_3_.5) | copy-start | bytes 18436
  50.3 8.6 %collective-permute-start.6 = (bf16[64,768]{1,0:T(8,128)(2,1)S(1)}, bf16[64,768]{1,0:T(8,128)(2,1)S(1)}, u32[]{:S(2)}, u32[]{:S(2)}) collective-permute-start(bf16[64,768]{1,0:T(8,128)(2,1)S(1)} %get-tuple-element.40), channel_id=1, source_target_pairs={{0,24},{8,16},{16,8},{24,0},{1,25},{9,17},{17,9},{25,1},{2,26},{10... | collective-permute-start | bytes 294920 | tf_op jit(solution)/shard_map/ppermute | solution.py:587
  52.1 9.3 %collective-permute-start.7 = (bf16[64,768]{1,0:T(8,128)(2,1)S(1)}, bf16[64,768]{1,0:T(8,128)(2,1)S(1)}, u32[]{:S(2)}, u32[]{:S(2)}) collective-permute-start(bf16[64,768]{1,0:T(8,128)(2,1)S(1)} %get-tuple-element.41), channel_id=1, source_target_pairs={{0,16},{8,24},{16,0},{24,8},{1,17},{9,25},{17,1},{25,9},{2,18},{10... | collective-permute-start | bytes 294920 | tf_op jit(solution)/shard_map/ppermute | solution.py:587
  53.9 7.5 %collective-permute-start.8 = (bf16[64,768]{1,0:T(8,128)(2,1)S(1)}, bf16[64,768]{1,0:T(8,128)(2,1)S(1)}, u32[]{:S(2)}, u32[]{:S(2)}) collective-permute-start(bf16[64,768]{1,0:T(8,128)(2,1)S(1)} %get-tuple-element.42), channel_id=1, source_target_pairs={{0,8},{8,0},{16,24},{24,16},{1,9},{9,1},{17,25},{25,17},{2,10},{10... | collective-permute-start | bytes 294920 | tf_op jit(solution)/shard_map/ppermute | solution.py:587
  (5 other events, 9.5 us)

commit v12 on v11

--- a/solution.py
+++ b/solution.py
@@ -758,7 +758,7 @@
                 pltpu.VMEM((shares, part_len, LANES), F32),
                 pltpu.VMEM((shares, part_len, LANES), F32),
             ],
-        )(here, params, received, *carried, *([spatial_out] * part))
+        )(here, params, received, *carried, *([came] * part))
         returned.append(sent(results[:shares]))
         carried = results[shares:]
 

time: 63.7 us -> 63.7 us (level)
  waiting for transfers between devices: 10.3 us -> 12.3 us
  local copies, waits for them, and re-layouts: 7.84 us -> 6.81 us
  Pallas kernels: 23 us -> 22.1 us
    ppermute x10, waiting for transfers between devices: 2.52 us -> 4.54 us  [swapped(): lax.ppermute(value, axis, [(source, source ^ distance) for source in rang...]
    unnamed x32, local copies, waits for them, and re-layouts: 7.84 us -> 6.81 us
    pallas_call x1, Pallas kernels: 1.75 us -> 0.79 us  [per_device(): call(functools.partial(incoming_kernel, frames, rows, columns, head_dim),...]
  transfers between devices with their start and end apart: 13 -> 13, of which waited for: 2 -> 2; matrix products, arithmetic and copies ran while one was open for 0% -> 0% of each run, Pallas kernels for 22% -> 20%
where the time goes in v12:
time: 63.7 us; the launch traced here: 63.4 us
  Pallas kernels  22.1 us (35%)
  starting transfers between devices  21.7 us (34%)
  waiting for transfers between devices  12.3 us (19%)
  local copies, waits for them, and re-layouts  6.81 us (11%)
    ppermute x10, starting transfers between devices, swapped(): lax.ppermute(value, axis, [(source, source ^ distance) for source in rang...  13.6 us
    ppermute x2, waiting for transfers between devices, crossed(): return lax.ppermute(value, axis, pairs)  7.81 us
    pallas_call x1, Pallas kernels, per_device(): call(functools.partial(entry_kernel, shares, heads, state, blocks), 'entr...  7.49 us
    unnamed x32, local copies, waits for them, and re-layouts  6.81 us
    all_to_all x1, starting transfers between devices, per_device(): lax.all_to_all(payload, 'tm', split_axis=0, concat_axis=0, tiled=True, ax...  6.03 us
    ppermute x10, waiting for transfers between devices, swapped(): lax.ppermute(value, axis, [(source, source ^ distance) for source in rang...  4.54 us
    pallas_call x2, Pallas kernels, per_device(): call(functools.partial(temporal_kernel, part, parts, per_group, head_dim,...  4.26 us
    pallas_call x2, Pallas kernels, per_device(): call(functools.partial(exit_kernel, part, parts, shares), 'exit', shape_o...  3.49 us
  transfers between devices with their start and end apart: 13, of which 2 were waited for; matrix products, arithmetic and copies ran while one was open for 0% of the time, Pallas kernels for 20%

profile of v12, /device:TPU:0, one launch (start us, length us, event | category | flops | bytes accessed | tf_op | source)
XLA Modules:
  0.0 63.4 jit_solution(15531680864202158849)
XLA Ops:
  0.0 7.5 %entry.1 = (bf16[256,1536]{1,0:T(8,128)(2,1)}, bf16[4,176,768]{2,1,0:T(8,128)(2,1)}, bf16[256,256]{1,0:T(8,128)(2,1)}, f32[256,128]{1,0:T(8,128)}, f32[16,128]{1...) custom-call(s32[1]{0:T(128)} %bitcast.refs_0_, ...), custom_call_target="tpu_custom_call" | custom-call | flops 1 | bytes 1 | tf_op jit(solution)/shard_map/entry/pallas_call | solution.py:619
  8.0 6.0 %all-to-all-start = ((bf16[4,176,768]{2,1,0:T(8,128)(2,1)}), bf16[4,176,768]{2,1,0:T(8,128)(2,1)S(1)}, u32[]{:S(2)}, u32[]{:S(2)}) async-start(bf16[4,176,768]{2,1,0:T(8,128)(2,1)} %get-tuple-element.26.after.refs_4_), calls=%async_computation | async-start | bytes 2162688 | tf_op jit(solution)/shard_map/all_to_all | solution.py:652
  14.3 1.6 %collective-permute-start.1 = (bf16[144,1536]{1,0:T(8,128)(2,1)S(1)}, bf16[144,1536]{1,0:T(8,128)(2,1)S(1)}, u32[]{:S(2)}, u32[]{:S(2)}) collective-permute-start(bf16[144,1536]{1,0:T(8,128)(2,1)S(1)} %pair_total.1.total), channel_id=1, source_target_pairs={{0,2},{1,5},{2,0},{3,7},{4,6},{5,1},{6,4},{7,3},{8,10},{9,13},{10,... | collective-permute-start | bytes 1327112 | tf_op jit(solution)/shard_map/ppermute | solution.py:593
  15.8 1.5 %collective-permute-start.2 = (bf16[16,1536]{1,0:T(8,128)(2,1)}, bf16[16,1536]{1,0:T(8,128)(2,1)S(1)}, u32[]{:S(2)}, u32[]{:S(2)}) collective-permute-start(bf16[16,1536]{1,0:T(8,128)(2,1)} %get-tuple-element.35), channel_id=1, source_target_pairs={{0,6},{1,7},{2,4},{3,5},{4,2},{5,3},{6,0},{7,1},{8,14},{9,15},{10,... | collective-permute-start | bytes 147464 | tf_op jit(solution)/shard_map/ppermute | solution.py:587
  17.3 0.7 %collective-permute-start.3 = (bf16[16,1536]{1,0:T(8,128)(2,1)}, bf16[16,1536]{1,0:T(8,128)(2,1)S(1)}, u32[]{:S(2)}, u32[]{:S(2)}) collective-permute-start(bf16[16,1536]{1,0:T(8,128)(2,1)} %get-tuple-element.35), channel_id=1, source_target_pairs={{0,7},{1,6},{2,5},{3,4},{4,3},{5,2},{6,1},{7,0},{8,15},{9,14},{10,... | collective-permute-start | bytes 147464 | tf_op jit(solution)/shard_map/ppermute | solution.py:587
  18.0 3.7 %copy-done = bf16[1536,3072]{1,0:T(8,128)(2,1)S(1)} copy-done((bf16[1536,3072]{1,0:T(8,128)(2,1)S(1)}, bf16[1536,3072]{1,0:T(8,128)(2,1)}, u32[]{:S(2)}) %copy-start) | copy-done | bytes 9437208
  21.7 2.6 %gate.1.refs_0_.refs_2_ = bf16[256,1536]{1,0:T(8,128)(2,1)S(1)} custom-call(bf16[4,176,768]{2,1,0:T(8,128)(2,1)S(1)} %copy-done.2, bf16[256,1536]{1,0:T(8,128)(2,1)S(1)} %copy-done.6, bf16[1536,3072]{1,0:T(8,128)(2,1)S(1)} %copy-done), custom_call_target="tpu_custom_call" | custom-call | flops 1 | bytes 1 | tf_op jit(solution)/shard_map/gate/pallas_call | solution.py:661
  24.4 1.9 %spatial_local.1 = (bf16[256,1536]{1,0:T(8,128)(2,1)S(1)}, f32[256,128]{1,0:T(8,128)S(1)}) custom-call(bf16[256,1536]{1,0:T(8,128)(2,1)S(1)} %gate.1.refs_0_.refs_2_, bf16[256,256]{1,0:T(8,128)(2,1)S(1)} %copy-done.9, f32[256,128]{1,0:T(8,128)S(1)} %copy-done.13, f32[16,128]{1,0:T(8,128)S(1)} %copy-done.14, bf16[4,176,768]{2,1,0:T(8,128)(2,1)S(1)} %copy-done.2), custom_call_target="tpu_custom_call" | custom-call | flops 1 | bytes 1 | tf_op jit(solution)/shard_map/spatial_local/pallas_call | solution.py:672
  26.6 0.6 collective-permute-start.4
  27.2 7.8 %collective-permute-done.4.second = bf16[144,1536]{1,0:T(8,128)(2,1)S(1)} collective-permute-done((bf16[144,1536]{1,0:T(8,128)(2,1)S(1)}, bf16[144,1536]{1,0:T(8,128)(2,1)S(1)}, u32[]{:S(2)}, u32[]{:S(2)}) %collective-permute-start.4) | collective-permute-done | bytes 442400 | tf_op jit(solution)/shard_map/ppermute | solution.py:593
  35.0 1.1 %settle.1 = (bf16[128,1536]{1,0:T(8,128)(2,1)S(1)}, bf16[128,1536]{1,0:T(8,128)(2,1)}) custom-call(f32[256,128]{1,0:T(8,128)S(1)} %get-tuple-element.32._.reach, s32[1]{0:T(128)} %bitcast.1.refs_1_.band, bf16[144,1536]{1,0:T(8,128)(2,1)S(1)} %collective-permute-done.1.first, bf16[144,1536]{1,0:T(8,128)(2,1)S(1)} %collective-permute-done.4.second, ...), custom_call_target="tpu_custom_call" | custom-call | flops 1 | bytes 1 | tf_op jit(solution)/shard_map/settle/pallas_call | solution.py:697
  36.1 0.7 %copy-done.11 = bf16[128,1536]{1,0:T(8,128)(2,1)} copy-done((bf16[128,1536]{1,0:T(8,128)(2,1)}, bf16[128,1536]{1,0:T(8,128)(2,1)S(1)}, u32[]{:S(2)}) %copy-start.11) | copy-done | bytes 393240
  36.9 2.3 %temporal.2 = (bf16[64,768]{1,0:T(8,128)(2,1)S(1)}, bf16[64,768]{1,0:T(8,128)(2,1)S(1)}, bf16[64,768]{1,0:T(8,128)(2,1)S(1)}, bf16[64,768]{1,0:T(8,128)(2,1)S(1)}, f32[128,768]{1,0:T(8,128)S(1)}) custom-call(s32[1]{0:T(128)} %bitcast.refs_0_, f32[16,128]{1,0:T(8,128)S(1)} %copy-done.14, bf16[4,176,768]{2,1,0:T(8,128)(2,1)S(1)} %all-to-all-done.refs_2_), custom_call_target="tpu_custom_call" | custom-call | flops 1 | bytes 1 | tf_op jit(solution)/shard_map/temporal/pallas_call | solution.py:738
  39.2 3.7 %collective-permute-start.9 = (bf16[64,768]{1,0:T(8,128)(2,1)S(1)}, bf16[64,768]{1,0:T(8,128)(2,1)S(1)}, u32[]{:S(2)}, u32[]{:S(2)}) collective-permute-start(bf16[64,768]{1,0:T(8,128)(2,1)S(1)} %get-tuple-element.44), channel_id=1, source_target_pairs={{0,24},{8,16},{16,8},{24,0},{1,25},{9,17},{17,9},{25,1},{2,26},{10... | collective-permute-start | bytes 294920 | tf_op jit(solution)/shard_map/ppermute | solution.py:587
  42.9 2.7 %collective-permute-start.10 = (bf16[64,768]{1,0:T(8,128)(2,1)S(1)}, bf16[64,768]{1,0:T(8,128)(2,1)S(1)}, u32[]{:S(2)}, u32[]{:S(2)}) collective-permute-start(bf16[64,768]{1,0:T(8,128)(2,1)S(1)} %get-tuple-element.45), channel_id=1, source_target_pairs={{0,16},{8,24},{16,0},{24,8},{1,17},{9,25},{17,1},{25,9},{2,18},{10... | collective-permute-start | bytes 294920 | tf_op jit(solution)/shard_map/ppermute | solution.py:587
  45.6 2.0 %temporal.3 = (bf16[64,768]{1,0:T(8,128)(2,1)S(1)}, bf16[64,768]{1,0:T(8,128)(2,1)S(1)}, bf16[64,768]{1,0:T(8,128)(2,1)S(1)}, bf16[64,768]{1,0:T(8,128)(2,1)S(1)}) custom-call(s32[1]{0:T(128)} %bitcast.refs_0_, f32[16,128]{1,0:T(8,128)S(1)} %copy-done.14, bf16[4,176,768]{2,1,0:T(8,128)(2,1)S(1)} %all-to-all-done.refs_2_, ...), custom_call_target="tpu_custom_call" | custom-call | flops 1 | bytes 1 | tf_op jit(solution)/shard_map/temporal/pallas_call | solution.py:738
  47.5 1.7 %collective-permute-start.6 = (bf16[64,768]{1,0:T(8,128)(2,1)S(1)}, bf16[64,768]{1,0:T(8,128)(2,1)S(1)}, u32[]{:S(2)}, u32[]{:S(2)}) collective-permute-start(bf16[64,768]{1,0:T(8,128)(2,1)S(1)} %get-tuple-element.40), channel_id=1, source_target_pairs={{0,24},{8,16},{16,8},{24,0},{1,25},{9,17},{17,9},{25,1},{2,26},{10... | collective-permute-start | bytes 294920 | tf_op jit(solution)/shard_map/ppermute | solution.py:587
  49.3 1.8 %collective-permute-start.7 = (bf16[64,768]{1,0:T(8,128)(2,1)S(1)}, bf16[64,768]{1,0:T(8,128)(2,1)S(1)}, u32[]{:S(2)}, u32[]{:S(2)}) collective-permute-start(bf16[64,768]{1,0:T(8,128)(2,1)S(1)} %get-tuple-element.41), channel_id=1, source_target_pairs={{0,16},{8,24},{16,0},{24,8},{1,17},{9,25},{17,1},{25,9},{2,18},{10... | collective-permute-start | bytes 294920 | tf_op jit(solution)/shard_map/ppermute | solution.py:587
  51.1 0.9 %collective-permute-start.8 = (bf16[64,768]{1,0:T(8,128)(2,1)S(1)}, bf16[64,768]{1,0:T(8,128)(2,1)S(1)}, u32[]{:S(2)}, u32[]{:S(2)}) collective-permute-start(bf16[64,768]{1,0:T(8,128)(2,1)S(1)} %get-tuple-element.42), channel_id=1, source_target_pairs={{0,8},{8,0},{16,24},{24,16},{1,9},{9,1},{17,25},{25,17},{2,10},{10... | collective-permute-start | bytes 294920 | tf_op jit(solution)/shard_map/ppermute | solution.py:587
  52.0 0.8 %spatial_incoming.1.refs_1_ = f32[256,1536]{1,0:T(8,128)S(1)} custom-call(s32[1]{0:T(128)} %bitcast.1.refs_1_.band, bf16[256,1536]{1,0:T(8,128)(2,1)S(1)} %copy-done.8, bf16[256,256]{1,0:T(8,128)(2,1)S(1)} %copy-done.10, f32[256,128]{1,0:T(8,128)S(1)} %get-tuple-element.32._.reach, bf16[128,1536]{1,0:T(8,128)(2,1)S(1)} %copy-done.12, ...), custom_call_target="tpu_custom_call" | custom-call | flops 1 | bytes 1 | tf_op jit(solution)/shard_map/spatial_incoming/pallas_call | solution.py:728
  52.8 4.5 %collective-permute-done.10.refs_7_ = bf16[64,768]{1,0:T(8,128)(2,1)S(1)} collective-permute-done((bf16[64,768]{1,0:T(8,128)(2,1)S(1)}, bf16[64,768]{1,0:T(8,128)(2,1)S(1)}, u32[]{:S(2)}, u32[]{:S(2)}) %collective-permute-start.10) | collective-permute-done | bytes 98336 | tf_op jit(solution)/shard_map/ppermute | solution.py:587
  57.3 2.3 %copy-done.1 = bf16[1536,1536]{1,0:T(8,128)(2,1)S(1)} copy-done((bf16[1536,1536]{1,0:T(8,128)(2,1)S(1)}, bf16[1536,1536]{1,0:T(8,128)(2,1)}, u32[]{:S(2)}) %copy-start.1) | copy-done | bytes 4718616
  59.7 1.7 %exit.2.refs_9_ = bf16[2,2,64,1536]{3,2,1,0:T(8,128)(2,1)} custom-call(s32[1]{0:T(128)} %bitcast.refs_0_, f32[256,1536]{1,0:T(8,128)S(1)} %spatial_incoming.1.refs_1_, bf16[256,1536]{1,0:T(8,128)(2,1)S(1)} %gate.1.refs_0_.refs_2_, f32[1536]{0:T(1024)S(1)} %copy-done.15, bf16[1536,1536]{1,0:T(8,128)(2,1)S(1)} %copy-done.1, ...), custom_call_target="tpu_custom_call" | custom-call | flops 1 | bytes 1 | tf_op jit(solution)/shard_map/exit/pallas_call | solution.py:768
  61.5 1.8 %exit.3 = bf16[2,2,64,1536]{3,2,1,0:T(8,128)(2,1)} custom-call(s32[1]{0:T(128)} %bitcast.refs_0_, f32[256,1536]{1,0:T(8,128)S(1)} %spatial_incoming.1.refs_1_, bf16[256,1536]{1,0:T(8,128)(2,1)S(1)} %gate.1.refs_0_.refs_2_, f32[1536]{0:T(1024)S(1)} %copy-done.15, bf16[1536,1536]{1,0:T(8,128)(2,1)S(1)} %copy-done.1, ...), custom_call_target="tpu_custom_call", output_to_operand_aliasing={{}: (9, {})} | custom-call | flops 1 | bytes 1 | tf_op jit(solution)/shard_map/exit/pallas_call | solution.py:768
  (45 shorter events, 1.0 us)
Async XLA Ops:
  7.5 6.6 %copy-start.3 = (bf16[144,1536]{1,0:T(8,128)(2,1)S(1)}, bf16[144,1536]{1,0:T(8,128)(2,1)}, u32[]{:S(2)}) copy-start(bf16[144,1536]{1,0:T(8,128)(2,1)} %get-tuple-element.33.own.band_own) | copy-start | bytes 1327108
  7.5 6.6 %collective-permute-start = (bf16[144,1536]{1,0:T(8,128)(2,1)}, bf16[144,1536]{1,0:T(8,128)(2,1)S(1)}, u32[]{:S(2)}, u32[]{:S(2)}) collective-permute-start(bf16[144,1536]{1,0:T(8,128)(2,1)} %get-tuple-element.34), channel_id=1, source_target_pairs={{0,1},{1,0},{2,3},{3,2},{4,5},{5,4},{6,7},{7,6},{8,9},{9,8},{10,11... | collective-permute-start | bytes 1327112 | tf_op jit(solution)/shard_map/ppermute | solution.py:587
  8.0 10.0 %copy-start.2 = (bf16[4,176,768]{2,1,0:T(8,128)(2,1)S(1)}, bf16[4,176,768]{2,1,0:T(8,128)(2,1)}, u32[]{:S(2)}) copy-start(bf16[4,176,768]{2,1,0:T(8,128)(2,1)} %get-tuple-element.26.after.refs_4_) | copy-start | bytes 3244036
  8.0 28.8 %all-to-all-start = ((bf16[4,176,768]{2,1,0:T(8,128)(2,1)}), bf16[4,176,768]{2,1,0:T(8,128)(2,1)S(1)}, u32[]{:S(2)}, u32[]{:S(2)}) async-start(bf16[4,176,768]{2,1,0:T(8,128)(2,1)} %get-tuple-element.26.after.refs_4_), calls=%async_computation | async-start | bytes 2162688 | tf_op jit(solution)/shard_map/all_to_all | solution.py:652
  14.1 4.0 %copy-start.6 = (bf16[256,1536]{1,0:T(8,128)(2,1)S(1)}, bf16[256,1536]{1,0:T(8,128)(2,1)}, u32[]{:S(2)}) copy-start(bf16[256,1536]{1,0:T(8,128)(2,1)} %get-tuple-element.27.normed) | copy-start | bytes 2359300
  14.1 4.0 %copy-start.4 = (bf16[144,1536]{1,0:T(8,128)(2,1)}, bf16[144,1536]{1,0:T(8,128)(2,1)S(1)}, u32[]{:S(2)}) copy-start(bf16[144,1536]{1,0:T(8,128)(2,1)S(1)} %collective-permute-done.far.band_far) | copy-start | bytes 1327108
  14.3 12.1 %collective-permute-start.1 = (bf16[144,1536]{1,0:T(8,128)(2,1)S(1)}, bf16[144,1536]{1,0:T(8,128)(2,1)S(1)}, u32[]{:S(2)}, u32[]{:S(2)}) collective-permute-start(bf16[144,1536]{1,0:T(8,128)(2,1)S(1)} %pair_total.1.total), channel_id=1, source_target_pairs={{0,2},{1,5},{2,0},{3,7},{4,6},{5,1},{6,4},{7,3},{8,10},{9,13},{10,... | collective-permute-start | bytes 1327112 | tf_op jit(solution)/shard_map/ppermute | solution.py:593
  15.8 10.5 %collective-permute-start.2 = (bf16[16,1536]{1,0:T(8,128)(2,1)}, bf16[16,1536]{1,0:T(8,128)(2,1)S(1)}, u32[]{:S(2)}, u32[]{:S(2)}) collective-permute-start(bf16[16,1536]{1,0:T(8,128)(2,1)} %get-tuple-element.35), channel_id=1, source_target_pairs={{0,6},{1,7},{2,4},{3,5},{4,2},{5,3},{6,0},{7,1},{8,14},{9,15},{10,... | collective-permute-start | bytes 147464 | tf_op jit(solution)/shard_map/ppermute | solution.py:587
  17.3 9.0 %collective-permute-start.3 = (bf16[16,1536]{1,0:T(8,128)(2,1)}, bf16[16,1536]{1,0:T(8,128)(2,1)S(1)}, u32[]{:S(2)}, u32[]{:S(2)}) collective-permute-start(bf16[16,1536]{1,0:T(8,128)(2,1)} %get-tuple-element.35), channel_id=1, source_target_pairs={{0,7},{1,6},{2,5},{3,4},{4,3},{5,2},{6,1},{7,0},{8,15},{9,14},{10,... | collective-permute-start | bytes 147464 | tf_op jit(solution)/shard_map/ppermute | solution.py:587
  18.0 3.7 %copy-start = (bf16[1536,3072]{1,0:T(8,128)(2,1)S(1)}, bf16[1536,3072]{1,0:T(8,128)(2,1)}, u32[]{:S(2)}) copy-start(bf16[1536,3072]{1,0:T(8,128)(2,1)} %weight.1) | copy-start | bytes 28311556
  24.4 10.5 %copy-start.5 = (bf16[144,1536]{1,0:T(8,128)(2,1)S(1)}, bf16[144,1536]{1,0:T(8,128)(2,1)}, u32[]{:S(2)}) copy-start(bf16[144,1536]{1,0:T(8,128)(2,1)} %copy-done.4) | copy-start | bytes 1327108
  26.3 9.7 %copy-start.7 = (bf16[256,1536]{1,0:T(8,128)(2,1)}, bf16[256,1536]{1,0:T(8,128)(2,1)S(1)}, u32[]{:S(2)}) copy-start(bf16[256,1536]{1,0:T(8,128)(2,1)S(1)} %get-tuple-element.31.out_local) | copy-start | bytes 2359300
  26.6 8.4 %collective-permute-start.4 = (bf16[144,1536]{1,0:T(8,128)(2,1)S(1)}, bf16[144,1536]{1,0:T(8,128)(2,1)S(1)}, u32[]{:S(2)}, u32[]{:S(2)}) collective-permute-start(bf16[144,1536]{1,0:T(8,128)(2,1)S(1)} %cross.1), channel_id=1, source_target_pairs={{0,4},{1,3},{2,6},{3,1},{4,0},{5,7},{6,2},{7,5},{8,12},{9,11},{10,... | collective-permute-start | bytes 1327112 | tf_op jit(solution)/shard_map/ppermute | solution.py:593
  36.8 15.2 %copy-start.10 = (bf16[256,256]{1,0:T(8,128)(2,1)S(1)}, bf16[256,256]{1,0:T(8,128)(2,1)}, u32[]{:S(2)}) copy-start(bf16[256,256]{1,0:T(8,128)(2,1)} %get-tuple-element.28.refs_1_.bc) | copy-start | bytes 393220
  36.8 8.8 %collective-permute-start.5 = (bf16[128,1536]{1,0:T(8,128)(2,1)}, bf16[128,1536]{1,0:T(8,128)(2,1)S(1)}, u32[]{:S(2)}, u32[]{:S(2)}) collective-permute-start(bf16[128,1536]{1,0:T(8,128)(2,1)} %get-tuple-element.37), channel_id=1, source_target_pairs={{0,1},{1,0},{2,3},{3,2},{4,5},{5,4},{6,7},{7,6},{8,9},{9,8},{10,11... | collective-permute-start | bytes 1179656 | tf_op jit(solution)/shard_map/ppermute | solution.py:587
  36.8 15.2 %copy-start.8 = (bf16[256,1536]{1,0:T(8,128)(2,1)S(1)}, bf16[256,1536]{1,0:T(8,128)(2,1)}, u32[]{:S(2)}) copy-start(bf16[256,1536]{1,0:T(8,128)(2,1)} %copy-done.7) | copy-start | bytes 2359300
  36.9 15.2 %copy-start.12 = (bf16[128,1536]{1,0:T(8,128)(2,1)S(1)}, bf16[128,1536]{1,0:T(8,128)(2,1)}, u32[]{:S(2)}) copy-start(bf16[128,1536]{1,0:T(8,128)(2,1)} %copy-done.11) | copy-start | bytes 1179652
  39.2 11.9 %collective-permute-start.9 = (bf16[64,768]{1,0:T(8,128)(2,1)S(1)}, bf16[64,768]{1,0:T(8,128)(2,1)S(1)}, u32[]{:S(2)}, u32[]{:S(2)}) collective-permute-start(bf16[64,768]{1,0:T(8,128)(2,1)S(1)} %get-tuple-element.44), channel_id=1, source_target_pairs={{0,24},{8,16},{16,8},{24,0},{1,25},{9,17},{17,9},{25,1},{2,26},{10... | collective-permute-start | bytes 294920 | tf_op jit(solution)/shard_map/ppermute | solution.py:587
  42.9 14.5 %collective-permute-start.10 = (bf16[64,768]{1,0:T(8,128)(2,1)S(1)}, bf16[64,768]{1,0:T(8,128)(2,1)S(1)}, u32[]{:S(2)}, u32[]{:S(2)}) collective-permute-start(bf16[64,768]{1,0:T(8,128)(2,1)S(1)} %get-tuple-element.45), channel_id=1, source_target_pairs={{0,16},{8,24},{16,0},{24,8},{1,17},{9,25},{17,1},{25,9},{2,18},{10... | collective-permute-start | bytes 294920 | tf_op jit(solution)/shard_map/ppermute | solution.py:587
  45.6 11.8 %collective-permute-start.11 = (bf16[64,768]{1,0:T(8,128)(2,1)S(1)}, bf16[64,768]{1,0:T(8,128)(2,1)S(1)}, u32[]{:S(2)}, u32[]{:S(2)}) collective-permute-start(bf16[64,768]{1,0:T(8,128)(2,1)S(1)} %get-tuple-element.46), channel_id=1, source_target_pairs={{0,8},{8,0},{16,24},{24,16},{1,9},{9,1},{17,25},{25,17},{2,10},{10... | collective-permute-start | bytes 294920 | tf_op jit(solution)/shard_map/ppermute | solution.py:587
  47.5 13.9 %collective-permute-start.6 = (bf16[64,768]{1,0:T(8,128)(2,1)S(1)}, bf16[64,768]{1,0:T(8,128)(2,1)S(1)}, u32[]{:S(2)}, u32[]{:S(2)}) collective-permute-start(bf16[64,768]{1,0:T(8,128)(2,1)S(1)} %get-tuple-element.40), channel_id=1, source_target_pairs={{0,24},{8,16},{16,8},{24,0},{1,25},{9,17},{17,9},{25,1},{2,26},{10... | collective-permute-start | bytes 294920 | tf_op jit(solution)/shard_map/ppermute | solution.py:587
  49.3 12.2 %collective-permute-start.7 = (bf16[64,768]{1,0:T(8,128)(2,1)S(1)}, bf16[64,768]{1,0:T(8,128)(2,1)S(1)}, u32[]{:S(2)}, u32[]{:S(2)}) collective-permute-start(bf16[64,768]{1,0:T(8,128)(2,1)S(1)} %get-tuple-element.41), channel_id=1, source_target_pairs={{0,16},{8,24},{16,0},{24,8},{1,17},{9,25},{17,1},{25,9},{2,18},{10... | collective-permute-start | bytes 294920 | tf_op jit(solution)/shard_map/ppermute | solution.py:587
  51.1 10.4 %collective-permute-start.8 = (bf16[64,768]{1,0:T(8,128)(2,1)S(1)}, bf16[64,768]{1,0:T(8,128)(2,1)S(1)}, u32[]{:S(2)}, u32[]{:S(2)}) collective-permute-start(bf16[64,768]{1,0:T(8,128)(2,1)S(1)} %get-tuple-element.42), channel_id=1, source_target_pairs={{0,8},{8,0},{16,24},{24,16},{1,9},{9,1},{17,25},{25,17},{2,10},{10... | collective-permute-start | bytes 294920 | tf_op jit(solution)/shard_map/ppermute | solution.py:587
  52.0 5.3 %copy-start.15 = (f32[1536]{0:T(1024)S(1)}, f32[1536]{0:T(1024)}, u32[]{:S(2)}) copy-start(f32[1536]{0:T(1024)} %refs_3_.5) | copy-start | bytes 18436
  (5 other events, 11.1 us)
